TPU v7x, 32 devices: a whole 2x2x4 slice. The times are simulated.
32 devices in a mesh: row: 8 (over z, x), col: 4 (over y, core).
Axes of the slice: x: 2, y: 2, z: 4, core: 2. Of those that a mesh axis runs over, the one named last changes fastest.
Arguments:
- cotangent: bfloat16 [1536, 1536], P('row', 'col'), may hold values from -9 to 9, as said below
- saved_panels: bfloat16 [3, 1536, 256], P(None, ('row', 'col')), may hold values from -0.15625 to 0.15625
- upstream: bfloat16 [3, 1536, 256], P(None, ('row', 'col')), may hold values from -6 to 6
- inverse_diag: float32 [3, 256, 256], replicated, as said below
- panel_tops: bfloat16 [3, 256, 256], replicated, may hold values from -0.375 to 0.375
Outputs:
- columns: bfloat16 [3, 1536, 256], P(None, ('row', 'col'))
- diag_cot: float32 [3, 256, 256], replicated
Inputs may be any that keep to these rules, and one draw needn't show every extreme that they name: `cotangent`: symmetric once its columns are reordered as in the first step. `inverse_diag`: each matrix is lower triangular with a diagonal of 0.6 to 1.2.
All inputs are finite; a program needn't handle non-finite values.
Results may differ from a plain program's by a relative error of at most 0.02.
Values may be sent and summed in bfloat16 or wider, within the bound.
No kernel may reach another device: no remote copies, remote signals or barrier semaphores. Data moves between devices by JAX's collectives and lax.ppermute only.
A program may use at most 64 MiB of HBM per device.

v0:
```python
import jax
import jax.numpy as jnp
from jax import lax
from jax.sharding import PartitionSpec as P


def finish(gram, crosses, solver, tops_list):
    highest = lax.Precision.HIGHEST
    result = -gram
    for cross, tops in zip(crosses, tops_list):
        solved = jnp.dot(cross, solver, precision=highest, preferred_element_type=jnp.float32)
        result = result + 2.0 * jnp.dot(
            tops.astype(jnp.float32).T,
            solved,
            precision=highest,
            preferred_element_type=jnp.float32,
        )
    return result


def body(cotangent, saved_panels, upstream, inverse_diag, panel_tops):
    count_panels = saved_panels.shape[0]
    contract = (((0,), (0,)), ((), ()))
    gathered_all = lax.all_gather(saved_panels, "row", axis=1, tiled=True)
    resident_all = lax.psum_scatter(
        jnp.einsum(
            "ik,pkb->ipb", cotangent, gathered_all, preferred_element_type=jnp.float32
        ).astype(jnp.bfloat16),
        "col",
        scatter_dimension=0,
        tiled=True,
    ).astype(jnp.float32)
    resident_terms = [resident_all[:, index] for index in range(count_panels)]
    columns_list = []
    diag_list = []
    for index in range(count_panels):
        panel = saved_panels[index]
        tops_list = [panel_tops[index * (index - 1) // 2 + earlier] for earlier in range(index)]
        product = resident_terms[index]
        for earlier in range(index):
            product = product + jnp.dot(
                columns_list[earlier], tops_list[earlier], preferred_element_type=jnp.float32
            )
        combined = upstream[index].astype(jnp.float32) - 2.0 * product
        columns_now = jnp.dot(
            combined,
            inverse_diag[index],
            precision=lax.Precision.HIGHEST,
            preferred_element_type=jnp.float32,
        ).astype(jnp.bfloat16)
        gram = lax.dot_general(panel, columns_now, contract, preferred_element_type=jnp.float32)
        crosses = [
            lax.dot_general(
                columns_list[earlier], panel, contract, preferred_element_type=jnp.float32
            )
            for earlier in range(index)
        ]
        columns_list.append(columns_now)
        summed = lax.psum(jnp.stack([gram] + crosses), ("row", "col"))
        diag_list.append(
            finish(
                summed[0],
                [summed[1 + earlier] for earlier in range(index)],
                inverse_diag[index],
                tops_list,
            )
        )
    diag_cot = jnp.stack(diag_list)
    return (jnp.stack(columns_list), diag_cot)


def solution(mesh):
    in_specs = (
        P("row", "col"),
        P(None, ("row", "col"), None),
        P(None, ("row", "col"), None),
        P(),
        P(),
    )
    out_specs = (P(None, ("row", "col"), None), P())
    return jax.shard_map(body, mesh=mesh, in_specs=in_specs, out_specs=out_specs, check_vma=False)
```

profile of v0, /device:TPU:0, one launch (start us, length us, event | category | flops | bytes accessed | tf_op | source)
XLA Modules:
  0.0 215.9 jit_solution(3856220369227553691)
XLA Ops:
  7.2 33.5 %all_gather.3 = bf16[3,384,256]{2,1,0:T(8,128)(2,1)S(1)} all-gather(bf16[3,48,256]{2,1,0:T(8,128)(2,1)} %param.6), channel_id=1, replica_groups=mesh['row'=8,'col'=4] {'row'}, dimensions={1}, use_global_device_ids=true | all-gather | bytes 663552 | tf_op jit(solution)/shard_map/all_gather | solution.py:24
  40.8 1.0 convolution_convert_fusion
  41.8 0.0 all-reduce.3.cloned.1.call-start
  41.9 21.4 %reduce-scatter.2.cloned.1.call-done = bf16[48,3,256]{2,0,1:T(8,128)(2,1)} async-done(((bf16[192,3,256]{2,0,1:T(8,128)(2,1)}), bf16[48,3,256]{2,0,1:T(8,128)(2,1)}) %reduce-scatter.2.cloned.1.call-update) | async-done | bytes 73744 | tf_op jit(solution)/shard_map/reduce_scatter | solution.py:25
  63.3 0.9 convert_element_type.36
  64.2 0.2 convolution_convert_fusion.3
  64.5 0.1 convolution_add_fusion.1
  64.6 0.2 fusion.11
  64.8 0.2 convolution_convert_fusion.2
  65.1 0.6 copy-done.4
  65.7 0.2 convolution_bitcast_fusion
  65.9 0.2 convolution_bitcast_fusion.4
  66.1 0.2 convolution_bitcast_fusion.1
  66.4 0.2 convolution_bitcast_fusion.3
  66.6 0.9 convolution_bitcast_fusion.5
  67.5 0.2 fusion.9
  67.7 0.2 convolution_convert_fusion.1
  67.9 0.2 convolution_bitcast_fusion.2
  68.1 0.9 pad_maximum_fusion.2
  69.0 0.9 pad_maximum_fusion
  69.9 0.6 pad_maximum_fusion.3
  70.6 132.7 %all-reduce.3.cloned.1.call-done = (f32[3,256,256]{1,2,0:T(8,128)}, f32[2,256,256]{1,2,0:T(8,128)}, f32[1,256,256]{1,2,0:T(8,128)}) async-done(((f32[3,256,256]{1,2,0:T(8,128)}, f32[2,256,256]{1,2,0:T(8,128)}, f32[1,256,256]{1,2,0:T(8,128)}), (f32[3,256,256]{1,2,0:T(8,128)}, f32[2,256,256]{1,2,0:T(8,128)}, f32[1,256,256]{1,2,0:T(8,128)})) %all-reduce.3.cloned.1.call-update) | async-done | bytes 1572880 | tf_op jit(solution)/shard_map/psum | solution.py:59
  203.3 1.6 fusion.12
  204.9 0.6 fusion.13
  205.5 0.3 copy-done.6
  205.9 0.2 copy-done.5
  206.0 0.6 fusion.15
  206.6 0.4 fusion.7
  207.0 0.4 fusion.4
  207.5 0.4 fusion.2
  207.9 0.1 pad_maximum_fusion.1
  207.9 1.1 copy.10
  (17 shorter events, 0.1 us)
Async XLA Ops:
  7.2 33.6 %copy-start = (bf16[192,384]{1,0:T(8,128)(2,1)S(1)}, bf16[192,384]{1,0:T(8,128)(2,1)}, u32[]{:S(2)}) copy-start(bf16[192,384]{1,0:T(8,128)(2,1)} %param.5) | copy-start | bytes 442372
  7.2 56.1 %reduce-scatter.2.cloned.1.call-start = ((), (), s32[]{:S(2)}) async-start(), calls=%async_computation.1 | async-start | bytes 368640 | tf_op jit(solution)/shard_map/reduce_scatter | solution.py:25
  40.8 23.5 %copy-start.1 = (f32[3,256,256]{2,1,0:T(8,128)S(1)}, f32[3,256,256]{2,1,0:T(8,128)}, u32[]{:S(2)}) copy-start(f32[3,256,256]{2,1,0:T(8,128)} %param.8) | copy-start | bytes 2359300
  41.8 22.7 %copy-start.2 = (bf16[3,256,256]{2,1,0:T(8,128)(2,1)S(1)}, bf16[3,256,256]{2,1,0:T(8,128)(2,1)}, u32[]{:S(2)}) copy-start(bf16[3,256,256]{2,1,0:T(8,128)(2,1)} %param.9) | copy-start | bytes 1179652
  41.8 22.4 %copy-start.7 = (bf16[3,48,256]{2,1,0:T(8,128)(2,1)S(1)}, bf16[3,48,256]{2,1,0:T(8,128)(2,1)}, u32[]{:S(2)}) copy-start(bf16[3,48,256]{2,1,0:T(8,128)(2,1)} %param.7) | copy-start | bytes 221188
  41.8 161.4 %all-reduce.3.cloned.1.call-start = ((), (), s32[]{:S(2)}) async-start(), calls=%async_computation.2 | async-start | bytes 3145728 | tf_op jit(solution)/shard_map/psum | solution.py:59
  64.8 0.9 copy-start.4
  203.3 1.6 copy-start.3
  204.9 1.0 copy-start.6
  204.9 1.1 copy-start.5
Sparse Core Ops, SparseCore 0:
  42.0 21.3 reduce-scatter.1
  70.4 132.8 all-reduce.2
where the time goes:
time: 216 us
  waiting for transfers between devices  154 us (71%)
  blocking collectives  33.5 us (16%)
  between operations  14.2 us (7%)
  matrix products  8.22 us (4%)
  other arithmetic  3.4 us (2%)
  local copies, waits for them, and re-layouts  2.29 us (1%)
    psum x1, waiting for transfers between devices, body(): summed = lax.psum(jnp.stack([gram] + crosses), ('row', 'col'))  133 us
    all_gather x1, blocking collectives, body(): gathered_all = lax.all_gather(saved_panels, 'row', axis=1, tiled=True)  33.5 us
    reduce_scatter x1, waiting for transfers between devices, body(): lax.psum_scatter(jnp.einsum('ik,pkb->ipb', cotangent, gathered_all, prefe...  21.4 us
  transfers between devices with their start and end apart: 2, of which 2 were waited for; matrix products, arithmetic and copies ran while one was open for 0% of the time, Pallas kernels for 0%

commit v1 on v0

v1 whole, which is shorter than its diff:
```python
import functools

import jax
import jax.numpy as jnp
from jax import lax
from jax.experimental import pallas as pl
from jax.experimental.pallas import tpu as pltpu
from jax.sharding import PartitionSpec as P

F32 = jnp.float32
BF16 = jnp.bfloat16
VMEM = pl.BlockSpec(memory_space=pltpu.VMEM)


def swap(value, axes, sizes, bits):
    dims = [sizes[axis] for axis in axes]
    pairs = []
    count = 1
    for dim in dims:
        count *= dim
    for source in range(count):
        rest, coords = source, []
        for dim in reversed(dims):
            coords.append(rest % dim)
            rest //= dim
        coords = coords[::-1]
        target = 0
        for axis, dim, coord in zip(axes, dims, coords):
            target = target * dim + (coord ^ bits.get(axis, 0))
        pairs.append((source, target))
    return lax.ppermute(value, axes, pairs)


def split(value):
    high = value.astype(BF16)
    return high, (value - high.astype(F32)).astype(BF16)


def dot(left, right):
    return jnp.dot(left, right, preferred_element_type=F32)


def dot_rows(left, right):
    return lax.dot_general(left, right, (((0,), (0,)), ((), ())), preferred_element_type=F32)


def product_kernel(order, cols, *refs):
    cot_ref, tiles, outs = refs[0], refs[1 : 1 + len(order)], refs[1 + len(order) : -2]
    joined, total = refs[-2:]
    row, col = lax.axis_index("row"), lax.axis_index("col")
    for bits_list, ref in zip(order, tiles):
        for place, bits in enumerate(bits_list):
            panels, height, width = ref.shape[-3:]
            start = pl.multiple_of((row ^ bits) * height, height)
            for panel in range(panels):
                joined[pl.ds(start, height), panel * width : (panel + 1) * width] = ref[place, panel]
    total[...] = dot(cot_ref[...], joined[...])
    height = outs[0].shape[0]
    for bits in range(cols):
        start = pl.multiple_of((col ^ bits) * height, height)
        outs[bits][...] = total[pl.ds(start, height), :].astype(outs[bits].dtype)


def panels_kernel(cols, *refs):
    parts, refs = refs[:cols], refs[cols:]
    saved_ref, upstream_ref, solver_ref, tops_ref, columns_ref, keep_ref, send_ref, diag = refs
    panels, height, width = saved_ref.shape
    product = parts[0][...]
    for part in parts[1:]:
        product = product + part[...].astype(F32)
    columns = []
    for index in range(panels):
        panel = saved_ref[index]
        appended = None
        for earlier in range(index):
            term = dot(columns[earlier], tops_ref[index * (index - 1) // 2 + earlier])
            appended = term if appended is None else appended + term
        summed = product[:, index * width : (index + 1) * width]
        if appended is not None:
            summed = summed + appended
        combined = upstream_ref[index].astype(F32) - 2.0 * summed
        high, low = split(combined)
        solver_high, solver_low = split(solver_ref[index])
        first = dot(jnp.concatenate([high, low, panel]), solver_high)
        second = dot(jnp.concatenate([high, panel]), solver_low)
        now = (first[:height] + (first[height : 2 * height] + second[:height])).astype(BF16)
        columns_ref[index] = now
        result = -dot_rows(panel, now)
        if appended is not None:
            solved_high, solved_low = split(2.0 * (first[2 * height :] + second[height:]))
            appended_high, appended_low = split(appended)
            result = result + dot_rows(
                jnp.concatenate([appended_high, appended_high, appended_low]),
                jnp.concatenate([solved_high, solved_low, solved_high]),
            )
        diag[index * width : (index + 1) * width, :] = result
        columns.append(now)
    piece = keep_ref.shape[1]
    core, spot = place_of()
    for bits in range(4):
        here = pl.multiple_of((core * 4 + (spot ^ bits)) * piece, piece)
        there = pl.multiple_of(((1 - core) * 4 + (spot ^ bits)) * piece, piece)
        keep_ref[bits] = diag[pl.ds(here, piece), :]
        send_ref[bits] = diag[pl.ds(there, piece), :].astype(BF16)


def place_of():
    row, col = lax.axis_index("row"), lax.axis_index("col")
    return col & 1, ((col >> 1) & 1) * 2 + (row & 1)


def finish_kernel(here_ref, there_ref, out_ref):
    core, spot = place_of()
    piece = here_ref.shape[1]
    for bits in range(4):
        here = pl.multiple_of((core * 4 + (spot ^ bits)) * piece, piece)
        there = pl.multiple_of(((1 - core) * 4 + (spot ^ bits)) * piece, piece)
        out_ref[pl.ds(here, piece), :] = here_ref[bits].astype(F32)
        out_ref[pl.ds(there, piece), :] = there_ref[bits].astype(F32)


def body(sizes, cotangent, saved_panels, upstream, inverse_diag, panel_tops):
    rows, cols = sizes["row"], sizes["col"]
    panels, height, width = saved_panels.shape
    limit = pltpu.CompilerParams(vmem_limit_bytes=32 * 1024 * 1024)

    order, tiles = [(0,)], [saved_panels[None]]
    far = [
        swap(saved_panels, ("row",), sizes, {"row": bits}) for bits in range(2, rows, 2)
    ]
    near = swap(saved_panels, ("row",), sizes, {"row": 1})
    order.append((1,))
    tiles.append(near[None])
    if far:
        for bits, value in zip(range(2, rows, 2), far):
            order.append((bits,))
            tiles.append(value[None])
        order.append(tuple(bits ^ 1 for bits in range(2, rows, 2)))
        tiles.append(swap(jnp.stack(far), ("row",), sizes, {"row": 1}))

    tall = cols * height
    parts = pl.pallas_call(
        functools.partial(product_kernel, order, cols),
        out_shape=[
            jax.ShapeDtypeStruct((height, panels * width), BF16 if bits else F32)
            for bits in range(cols)
        ],
        in_specs=[VMEM] * (1 + len(tiles)),
        out_specs=[VMEM] * cols,
        scratch_shapes=[
            pltpu.VMEM((rows * height, panels * width), BF16),
            pltpu.VMEM((tall, panels * width), F32),
        ],
        compiler_params=limit,
    )(cotangent, *tiles)

    parts = [parts[0]] + [
        swap(parts[bits], ("col",), sizes, {"col": bits}) for bits in range(1, cols)
    ]

    piece = panels * width // 8
    columns, keep, send = pl.pallas_call(
        functools.partial(panels_kernel, cols),
        out_shape=[
            jax.ShapeDtypeStruct(saved_panels.shape, BF16),
            jax.ShapeDtypeStruct((4, piece, width), F32),
            jax.ShapeDtypeStruct((4, piece, width), BF16),
        ],
        in_specs=[VMEM] * (cols + 4),
        out_specs=[VMEM] * 3,
        scratch_shapes=[pltpu.VMEM((panels * width, width), F32)],
        compiler_params=limit,
    )(*parts, saved_panels, upstream, inverse_diag, panel_tops)

    both = ("row", "col")
    half = keep + swap(send, ("col",), sizes, {"col": 1}).astype(F32)
    spots = [{"col": (bits >> 1) * 2, "row": bits & 1} for bits in range(4)]
    total = half[0]
    for bits in range(1, 4):
        total = total + swap(half[bits].astype(BF16), both, sizes, spots[bits]).astype(F32)
    others = [{"row": bits} for bits in (2**power for power in range(1, rows.bit_length() - 1))]
    others += [{"col": bits} for bits in (2**power for power in range(2, cols.bit_length() - 1))]
    if len(others) == 2 and "col" not in others[1]:
        mine = total.astype(BF16)
        first, second = others[0]["row"], others[1]["row"]
        from_first, from_second, from_both = [
            swap(mine, ("row",), sizes, {"row": bits}) for bits in (first, second, first ^ second)
        ]
        total = (mine.astype(F32) + from_first.astype(F32)) + (
            from_second.astype(F32) + from_both.astype(F32)
        )
    else:
        for bits in others:
            mine = total.astype(BF16)
            total = mine.astype(F32) + swap(mine, tuple(bits), sizes, bits).astype(F32)
    mine = total.astype(BF16)
    here = jnp.stack([mine] + [swap(mine, both, sizes, spots[bits]) for bits in range(1, 4)])
    there = swap(here, ("col",), sizes, {"col": 1})
    diag_cot = pl.pallas_call(
        finish_kernel,
        out_shape=jax.ShapeDtypeStruct((panels * width, width), F32),
        in_specs=[VMEM] * 2,
        out_specs=VMEM,
        compiler_params=limit,
    )(here, there)
    return columns, diag_cot.reshape(panels, width, width)


def solution(mesh):
    in_specs = (
        P("row", "col"),
        P(None, ("row", "col"), None),
        P(None, ("row", "col"), None),
        P(),
        P(),
    )
    out_specs = (P(None, ("row", "col"), None), P())
    return jax.shard_map(
        functools.partial(body, dict(mesh.shape)),
        mesh=mesh,
        in_specs=in_specs,
        out_specs=out_specs,
        check_vma=False,
    )
```

time: 216 us -> 57.8 us (0.27)
  waiting for transfers between devices: 154 us -> 28.8 us
  blocking collectives: 33.5 us -> 0 us
  starting transfers between devices: 0.08 us -> 21.4 us
  between operations: 14.2 us -> 0.72 us
  matrix products: 8.22 us -> 0 us
  other arithmetic: 3.4 us -> 0.16 us
  Pallas kernels: 0 us -> 2.85 us
    psum x1 -> x0, waiting for transfers between devices: 133 us -> none  [body(): summed = lax.psum(jnp.stack([gram] + crosses), ('row', 'col'))]
    all_gather x1 -> x0, blocking collectives: 33.5 us -> none  [body(): gathered_all = lax.all_gather(saved_panels, 'row', axis=1, tiled=True)]
    ppermute x0 -> x19, waiting for transfers between devices: none -> 28.8 us  [swap(): return lax.ppermute(value, axes, pairs)]
    ppermute x0 -> x19, starting transfers between devices: none -> 21.4 us  [swap(): return lax.ppermute(value, axes, pairs)]
    reduce_scatter x1 -> x0, waiting for transfers between devices: 21.4 us -> none  [body(): lax.psum_scatter(jnp.einsum('ik,pkb->ipb', cotangent, gathered_all, prefe...]
    dot_general x19 -> x0, matrix products: 8.22 us -> none  [the longest x3 2.81 us: finish(): jnp.dot(cross, solver, precision=highest, preferred_element_type=jnp.floa...]
    pallas_call x0 -> x3, Pallas kernels: none -> 2.85 us  [the longest x1 1.51 us: body(): pl.pallas_call(functools.partial(panels_kernel, cols), out_shape=[jax.Sha...]
    another operation x4 -> x3, other arithmetic: 2.48 us -> 0.11 us  [the longest x2 1.79 us: body(): summed = lax.psum(jnp.stack([gram] + crosses), ('row', 'col'))]
  transfers between devices with their start and end apart: 2 -> 19, of which waited for: 2 -> 17; matrix products, arithmetic and copies ran while one was open for 0% -> 0% of each run, Pallas kernels for 0% -> 0%
where the time goes in v1:
time: 57.8 us; the launch traced here: 57.5 us
  waiting for transfers between devices  28.8 us (50%)
  starting transfers between devices  21.4 us (37%)
  local copies, waits for them, and re-layouts  3.59 us (6%)
  Pallas kernels  2.85 us (5%)
  between operations  0.72 us (1%)
    ppermute x19, waiting for transfers between devices, swap(): return lax.ppermute(value, axes, pairs)  28.8 us
    ppermute x19, starting transfers between devices, swap(): return lax.ppermute(value, axes, pairs)  21.4 us
    unnamed x12, local copies, waits for them, and re-layouts  3.57 us
    pallas_call x1, Pallas kernels, body(): pl.pallas_call(functools.partial(panels_kernel, cols), out_shape=[jax.Sha...  1.51 us
  transfers between devices with their start and end apart: 19, of which 17 were waited for; matrix products, arithmetic and copies ran while one was open for 0% of the time, Pallas kernels for 0%

profile of v1, /device:TPU:0, one launch (start us, length us, event | category | flops | bytes accessed | tf_op | source)
XLA Modules:
  0.0 57.5 jit_solution(3952672731924728100)
XLA Ops:
  0.6 4.1 %collective-permute-start.2 = (bf16[3,48,256]{2,1,0:T(8,128)(2,1)}, bf16[3,48,256]{2,1,0:T(8,128)(2,1)S(1)}, u32[]{:S(2)}, u32[]{:S(2)}) collective-permute-start(bf16[3,48,256]{2,1,0:T(8,128)(2,1)} %refs_4_.1), channel_id=1, source_target_pairs={{0,16},{4,20},{8,24},{12,28},{16,0},{20,4},{24,8},{28,12},{1,17},{... | collective-permute-start | bytes 221192 | tf_op jit(solution)/shard_map/ppermute | solution.py:31
  4.7 1.6 %collective-permute-start.1 = (bf16[3,48,256]{2,1,0:T(8,128)(2,1)}, bf16[3,48,256]{2,1,0:T(8,128)(2,1)S(1)}, u32[]{:S(2)}, u32[]{:S(2)}) collective-permute-start(bf16[3,48,256]{2,1,0:T(8,128)(2,1)} %refs_4_.1), channel_id=1, source_target_pairs={{0,8},{4,12},{8,0},{12,4},{16,24},{20,28},{24,16},{28,20},{1,9},{5... | collective-permute-start | bytes 221192 | tf_op jit(solution)/shard_map/ppermute | solution.py:31
  6.3 2.0 %collective-permute-done.2 = bf16[3,48,256]{2,1,0:T(8,128)(2,1)S(1)} collective-permute-done((bf16[3,48,256]{2,1,0:T(8,128)(2,1)}, bf16[3,48,256]{2,1,0:T(8,128)(2,1)S(1)}, u32[]{:S(2)}, u32[]{:S(2)}) %collective-permute-start.2) | collective-permute-done | bytes 73760 | tf_op jit(solution)/shard_map/ppermute | solution.py:31
  8.3 1.0 %collective-permute-done.1 = bf16[3,48,256]{2,1,0:T(8,128)(2,1)S(1)} collective-permute-done((bf16[3,48,256]{2,1,0:T(8,128)(2,1)}, bf16[3,48,256]{2,1,0:T(8,128)(2,1)S(1)}, u32[]{:S(2)}, u32[]{:S(2)}) %collective-permute-start.1) | collective-permute-done | bytes 73760 | tf_op jit(solution)/shard_map/ppermute | solution.py:31
  9.3 3.4 %collective-permute-done.3 = bf16[3,48,256]{2,1,0:T(8,128)(2,1)S(1)} collective-permute-done((bf16[3,48,256]{2,1,0:T(8,128)(2,1)}, bf16[3,48,256]{2,1,0:T(8,128)(2,1)S(1)}, u32[]{:S(2)}, u32[]{:S(2)}) %collective-permute-start.3) | collective-permute-done | bytes 73760 | tf_op jit(solution)/shard_map/ppermute | solution.py:31
  12.7 1.6 %collective-permute-start.4 = (bf16[3,3,48,256]{3,2,1,0:T(8,128)(2,1)S(1)}, bf16[3,3,48,256]{3,2,1,0:T(8,128)(2,1)S(1)}, u32[]{:S(2)}, u32[]{:S(2)}) collective-permute-start(bf16[3,3,48,256]{3,2,1,0:T(8,128)(2,1)S(1)} %pad_maximum_fusion), channel_id=1, source_target_pairs={{0,4},{4,0},{8,12},{12,8},{16,20},{20,16},{24,28},{28,24},{1,5},{5... | collective-permute-start | bytes 663560 | tf_op jit(solution)/shard_map/ppermute | solution.py:31
  14.8 5.1 %collective-permute-done = bf16[3,48,256]{2,1,0:T(8,128)(2,1)S(1)} collective-permute-done((bf16[3,48,256]{2,1,0:T(8,128)(2,1)}, bf16[3,48,256]{2,1,0:T(8,128)(2,1)S(1)}, u32[]{:S(2)}, u32[]{:S(2)}) %collective-permute-start) | collective-permute-done | bytes 73760 | tf_op jit(solution)/shard_map/ppermute | solution.py:31
  19.9 0.9 %copy-done.2 = bf16[3,48,256]{2,1,0:T(8,128)(2,1)S(1)} copy-done((bf16[3,48,256]{2,1,0:T(8,128)(2,1)S(1)}, bf16[3,48,256]{2,1,0:T(8,128)(2,1)}, u32[]{:S(2)}) %copy-start.2) | copy-done | bytes 73752
  20.8 0.9 %copy-done.4 = bf16[192,384]{1,0:T(8,128)(2,1)S(1)} copy-done((bf16[192,384]{1,0:T(8,128)(2,1)S(1)}, bf16[192,384]{1,0:T(8,128)(2,1)}, u32[]{:S(2)}) %copy-start.4) | copy-done | bytes 147480
  22.2 1.6 %collective-permute-start.6 = (bf16[48,768]{1,0:T(8,128)(2,1)S(1)}, bf16[48,768]{1,0:T(8,128)(2,1)S(1)}, u32[]{:S(2)}, u32[]{:S(2)}) collective-permute-start(bf16[48,768]{1,0:T(8,128)(2,1)S(1)} %get-tuple-element.11), channel_id=1, source_target_pairs={{0,2},{1,3},{2,0},{3,1},{4,6},{5,7},{6,4},{7,5},{8,10},{9,11},{10,... | collective-permute-start | bytes 221192 | tf_op jit(solution)/shard_map/ppermute | solution.py:31
  24.1 2.9 %collective-permute-done.6.refs_2_ = bf16[48,768]{1,0:T(8,128)(2,1)S(1)} collective-permute-done((bf16[48,768]{1,0:T(8,128)(2,1)S(1)}, bf16[48,768]{1,0:T(8,128)(2,1)S(1)}, u32[]{:S(2)}, u32[]{:S(2)}) %collective-permute-start.6) | collective-permute-done | bytes 73760 | tf_op jit(solution)/shard_map/ppermute | solution.py:31
  27.0 1.2 %collective-permute-done.7.refs_3_ = bf16[48,768]{1,0:T(8,128)(2,1)S(1)} collective-permute-done((bf16[48,768]{1,0:T(8,128)(2,1)S(1)}, bf16[48,768]{1,0:T(8,128)(2,1)S(1)}, u32[]{:S(2)}, u32[]{:S(2)}) %collective-permute-start.7) | collective-permute-done | bytes 73760 | tf_op jit(solution)/shard_map/ppermute | solution.py:31
  28.3 0.9 %copy-done.3 = bf16[3,48,256]{2,1,0:T(8,128)(2,1)S(1)} copy-done((bf16[3,48,256]{2,1,0:T(8,128)(2,1)S(1)}, bf16[3,48,256]{2,1,0:T(8,128)(2,1)}, u32[]{:S(2)}) %copy-start.3) | copy-done | bytes 73752
  29.1 0.9 %copy-done.5 = bf16[3,48,256]{2,1,0:T(8,128)(2,1)S(1)} copy-done((bf16[3,48,256]{2,1,0:T(8,128)(2,1)S(1)}, bf16[3,48,256]{2,1,0:T(8,128)(2,1)}, u32[]{:S(2)}) %copy-start.5) | copy-done | bytes 73752
  30.0 1.5 %shard_map.69 = (bf16[3,48,256]{2,1,0:T(8,128)(2,1)}, f32[4,96,256]{2,1,0:T(8,128)S(1)}, bf16[4,96,256]{2,1,0:T(8,128)(2,1)S(1)}) custom-call(f32[48,768]{1,0:T(8,128)S(1)} %get-tuple-element.9.refs_0_, bf16[48,768]{1,0:T(8,128)(2,1)S(1)} %collective-permute-done.5.refs_1_, bf16[48,768]{1,0:T(8,128)(2,1)S(1)} %collective-permute-done.6.refs_2_, ...), custom_call_target="tpu_custom_call" | custom-call | tf_op jit(solution)/shard_map/pallas_call | solution.py:162
  31.6 1.3 %collective-permute-done.8 = bf16[4,96,256]{2,1,0:T(8,128)(2,1)S(1)} collective-permute-done((bf16[4,96,256]{2,1,0:T(8,128)(2,1)S(1)}, bf16[4,96,256]{2,1,0:T(8,128)(2,1)S(1)}, u32[]{:S(2)}, u32[]{:S(2)}) %collective-permute-start.8) | collective-permute-done | bytes 196640 | tf_op jit(solution)/shard_map/ppermute | solution.py:31
  33.1 1.6 %collective-permute-start.9 = (bf16[96,256]{1,0:T(8,128)(2,1)S(1)}, bf16[96,256]{1,0:T(8,128)(2,1)S(1)}, u32[]{:S(2)}, u32[]{:S(2)}) collective-permute-start(bf16[96,256]{1,0:T(8,128)(2,1)S(1)} %get-tuple-element.18), channel_id=1, source_target_pairs={{0,4},{1,5},{2,6},{3,7},{4,0},{5,1},{6,2},{7,3},{8,12},{9,13},{10,... | collective-permute-start | bytes 147464 | tf_op jit(solution)/shard_map/ppermute | solution.py:31
  34.6 1.3 %collective-permute-start.11 = (bf16[96,256]{1,0:T(8,128)(2,1)S(1)}, bf16[96,256]{1,0:T(8,128)(2,1)S(1)}, u32[]{:S(2)}, u32[]{:S(2)}) collective-permute-start(bf16[96,256]{1,0:T(8,128)(2,1)S(1)} %get-tuple-element.19), channel_id=1, source_target_pairs={{0,6},{1,7},{2,4},{3,5},{4,2},{5,3},{6,0},{7,1},{8,14},{9,15},{10,... | collective-permute-start | bytes 147464 | tf_op jit(solution)/shard_map/ppermute | solution.py:31
  35.9 0.7 %collective-permute-start.10 = (bf16[96,256]{1,0:T(8,128)(2,1)S(1)}, bf16[96,256]{1,0:T(8,128)(2,1)S(1)}, u32[]{:S(2)}, u32[]{:S(2)}) collective-permute-start(bf16[96,256]{1,0:T(8,128)(2,1)S(1)} %get-tuple-element.20), channel_id=1, source_target_pairs={{0,2},{1,3},{2,0},{3,1},{4,6},{5,7},{6,4},{7,5},{8,10},{9,11},{10,... | collective-permute-start | bytes 147464 | tf_op jit(solution)/shard_map/ppermute | solution.py:31
  37.2 2.4 %collective-permute-done.11 = bf16[96,256]{1,0:T(8,128)(2,1)S(1)} collective-permute-done((bf16[96,256]{1,0:T(8,128)(2,1)S(1)}, bf16[96,256]{1,0:T(8,128)(2,1)S(1)}, u32[]{:S(2)}, u32[]{:S(2)}) %collective-permute-start.11) | collective-permute-done | bytes 49184 | tf_op jit(solution)/shard_map/ppermute | solution.py:31
  40.2 2.4 %collective-permute-start.14 = (bf16[96,256]{1,0:T(8,128)(2,1)S(1)}, bf16[96,256]{1,0:T(8,128)(2,1)S(1)}, u32[]{:S(2)}, u32[]{:S(2)}) collective-permute-start(bf16[96,256]{1,0:T(8,128)(2,1)S(1)} %fusion.3), channel_id=1, source_target_pairs={{0,24},{4,28},{8,16},{12,20},{16,8},{20,12},{24,0},{28,4},{1,25},{... | collective-permute-start | bytes 147464 | tf_op jit(solution)/shard_map/ppermute | solution.py:31
  42.5 1.2 %collective-permute-start.13 = (bf16[96,256]{1,0:T(8,128)(2,1)S(1)}, bf16[96,256]{1,0:T(8,128)(2,1)S(1)}, u32[]{:S(2)}, u32[]{:S(2)}) collective-permute-start(bf16[96,256]{1,0:T(8,128)(2,1)S(1)} %fusion.3), channel_id=1, source_target_pairs={{0,16},{4,20},{8,24},{12,28},{16,0},{20,4},{24,8},{28,12},{1,17},{... | collective-permute-start | bytes 147464 | tf_op jit(solution)/shard_map/ppermute | solution.py:31
  43.8 0.9 %collective-permute-start.12 = (bf16[96,256]{1,0:T(8,128)(2,1)S(1)}, bf16[96,256]{1,0:T(8,128)(2,1)S(1)}, u32[]{:S(2)}, u32[]{:S(2)}) collective-permute-start(bf16[96,256]{1,0:T(8,128)(2,1)S(1)} %fusion.3), channel_id=1, source_target_pairs={{0,8},{4,12},{8,0},{12,4},{16,24},{20,28},{24,16},{28,20},{1,9},{5... | collective-permute-start | bytes 147464 | tf_op jit(solution)/shard_map/ppermute | solution.py:31
  44.6 2.1 %collective-permute-done.14 = bf16[96,256]{1,0:T(8,128)(2,1)S(1)} collective-permute-done((bf16[96,256]{1,0:T(8,128)(2,1)S(1)}, bf16[96,256]{1,0:T(8,128)(2,1)S(1)}, u32[]{:S(2)}, u32[]{:S(2)}) %collective-permute-start.14) | collective-permute-done | bytes 49184 | tf_op jit(solution)/shard_map/ppermute | solution.py:31
  46.7 0.8 %collective-permute-done.13 = bf16[96,256]{1,0:T(8,128)(2,1)S(1)} collective-permute-done((bf16[96,256]{1,0:T(8,128)(2,1)S(1)}, bf16[96,256]{1,0:T(8,128)(2,1)S(1)}, u32[]{:S(2)}, u32[]{:S(2)}) %collective-permute-start.13) | collective-permute-done | bytes 49184 | tf_op jit(solution)/shard_map/ppermute | solution.py:31
  48.1 1.8 %collective-permute-start.17 = (bf16[96,256]{1,0:T(8,128)(2,1)S(1)}, bf16[96,256]{1,0:T(8,128)(2,1)S(1)}, u32[]{:S(2)}, u32[]{:S(2)}) collective-permute-start(bf16[96,256]{1,0:T(8,128)(2,1)S(1)} %add_convert_fusion), channel_id=1, source_target_pairs={{0,6},{1,7},{2,4},{3,5},{4,2},{5,3},{6,0},{7,1},{8,14},{9,15},{10,... | collective-permute-start | bytes 147464 | tf_op jit(solution)/shard_map/ppermute | solution.py:31
  49.9 1.1 %collective-permute-start.16 = (bf16[96,256]{1,0:T(8,128)(2,1)S(1)}, bf16[96,256]{1,0:T(8,128)(2,1)S(1)}, u32[]{:S(2)}, u32[]{:S(2)}) collective-permute-start(bf16[96,256]{1,0:T(8,128)(2,1)S(1)} %add_convert_fusion), channel_id=1, source_target_pairs={{0,2},{1,3},{2,0},{3,1},{4,6},{5,7},{6,4},{7,5},{8,10},{9,11},{10,... | collective-permute-start | bytes 147464 | tf_op jit(solution)/shard_map/ppermute | solution.py:31
  51.7 1.5 %collective-permute-done.17 = bf16[96,256]{1,0:T(8,128)(2,1)S(1)} collective-permute-done((bf16[96,256]{1,0:T(8,128)(2,1)S(1)}, bf16[96,256]{1,0:T(8,128)(2,1)S(1)}, u32[]{:S(2)}, u32[]{:S(2)}) %collective-permute-start.17) | collective-permute-done | bytes 49184 | tf_op jit(solution)/shard_map/ppermute | solution.py:31
  53.2 0.8 %collective-permute-done.16 = bf16[96,256]{1,0:T(8,128)(2,1)S(1)} collective-permute-done((bf16[96,256]{1,0:T(8,128)(2,1)S(1)}, bf16[96,256]{1,0:T(8,128)(2,1)S(1)}, u32[]{:S(2)}, u32[]{:S(2)}) %collective-permute-start.16) | collective-permute-done | bytes 49184 | tf_op jit(solution)/shard_map/ppermute | solution.py:31
  54.0 1.1 %collective-permute-done.15 = bf16[96,256]{1,0:T(8,128)(2,1)S(1)} collective-permute-done((bf16[96,256]{1,0:T(8,128)(2,1)S(1)}, bf16[96,256]{1,0:T(8,128)(2,1)S(1)}, u32[]{:S(2)}, u32[]{:S(2)}) %collective-permute-start.15) | collective-permute-done | bytes 49184 | tf_op jit(solution)/shard_map/ppermute | solution.py:31
  55.2 1.4 %collective-permute-done.18.there_ref = bf16[4,96,256]{2,1,0:T(8,128)(2,1)S(1)} collective-permute-done((bf16[4,96,256]{2,1,0:T(8,128)(2,1)S(1)}, bf16[4,96,256]{2,1,0:T(8,128)(2,1)S(1)}, u32[]{:S(2)}, u32[]{:S(2)}) %collective-permute-start.18) | collective-permute-done | bytes 196640 | tf_op jit(solution)/shard_map/ppermute | solution.py:31
  56.6 0.9 %shard_map.70 = f32[768,256]{1,0:T(8,128)} custom-call(bf16[4,96,256]{2,1,0:T(8,128)(2,1)S(1)} %pad_maximum_fusion.1.here_ref, bf16[4,96,256]{2,1,0:T(8,128)(2,1)S(1)} %collective-permute-done.18.there_ref), custom_call_target="tpu_custom_call" | custom-call | tf_op jit(solution)/shard_map/pallas_call | solution.py:199
  (27 shorter events, 4.0 us)
Async XLA Ops:
  0.6 27.6 %copy-start = (f32[3,256,256]{2,1,0:T(8,128)S(1)}, f32[3,256,256]{2,1,0:T(8,128)}, u32[]{:S(2)}) copy-start(f32[3,256,256]{2,1,0:T(8,128)} %refs_6_.1) | copy-start | bytes 2359300
  0.6 7.7 %collective-permute-start.2 = (bf16[3,48,256]{2,1,0:T(8,128)(2,1)}, bf16[3,48,256]{2,1,0:T(8,128)(2,1)S(1)}, u32[]{:S(2)}, u32[]{:S(2)}) collective-permute-start(bf16[3,48,256]{2,1,0:T(8,128)(2,1)} %refs_4_.1), channel_id=1, source_target_pairs={{0,16},{4,20},{8,24},{12,28},{16,0},{20,4},{24,8},{28,12},{1,17},{... | collective-permute-start | bytes 221192 | tf_op jit(solution)/shard_map/ppermute | solution.py:31
  4.7 4.6 %collective-permute-start.1 = (bf16[3,48,256]{2,1,0:T(8,128)(2,1)}, bf16[3,48,256]{2,1,0:T(8,128)(2,1)S(1)}, u32[]{:S(2)}, u32[]{:S(2)}) collective-permute-start(bf16[3,48,256]{2,1,0:T(8,128)(2,1)} %refs_4_.1), channel_id=1, source_target_pairs={{0,8},{4,12},{8,0},{12,4},{16,24},{20,28},{24,16},{28,20},{1,9},{5... | collective-permute-start | bytes 221192 | tf_op jit(solution)/shard_map/ppermute | solution.py:31
  6.3 6.4 %collective-permute-start.3 = (bf16[3,48,256]{2,1,0:T(8,128)(2,1)}, bf16[3,48,256]{2,1,0:T(8,128)(2,1)S(1)}, u32[]{:S(2)}, u32[]{:S(2)}) collective-permute-start(bf16[3,48,256]{2,1,0:T(8,128)(2,1)} %refs_4_.1), channel_id=1, source_target_pairs={{0,24},{4,28},{8,16},{12,20},{16,8},{20,12},{24,0},{28,4},{1,25},{... | collective-permute-start | bytes 221192 | tf_op jit(solution)/shard_map/ppermute | solution.py:31
  12.7 15.5 %copy-start.1 = (bf16[3,256,256]{2,1,0:T(8,128)(2,1)S(1)}, bf16[3,256,256]{2,1,0:T(8,128)(2,1)}, u32[]{:S(2)}) copy-start(bf16[3,256,256]{2,1,0:T(8,128)(2,1)} %refs_7_.1) | copy-start | bytes 1179652
  12.7 7.2 %collective-permute-start.4 = (bf16[3,3,48,256]{3,2,1,0:T(8,128)(2,1)S(1)}, bf16[3,3,48,256]{3,2,1,0:T(8,128)(2,1)S(1)}, u32[]{:S(2)}, u32[]{:S(2)}) collective-permute-start(bf16[3,3,48,256]{3,2,1,0:T(8,128)(2,1)S(1)} %pad_maximum_fusion), channel_id=1, source_target_pairs={{0,4},{4,0},{8,12},{12,8},{16,20},{20,16},{24,28},{28,24},{1,5},{5... | collective-permute-start | bytes 663560 | tf_op jit(solution)/shard_map/ppermute | solution.py:31
  14.3 5.7 %collective-permute-start = (bf16[3,48,256]{2,1,0:T(8,128)(2,1)}, bf16[3,48,256]{2,1,0:T(8,128)(2,1)S(1)}, u32[]{:S(2)}, u32[]{:S(2)}) collective-permute-start(bf16[3,48,256]{2,1,0:T(8,128)(2,1)} %refs_4_.1), channel_id=1, source_target_pairs={{0,4},{4,0},{8,12},{12,8},{16,20},{20,16},{24,28},{28,24},{1,5},{5... | collective-permute-start | bytes 221192 | tf_op jit(solution)/shard_map/ppermute | solution.py:31
  19.9 0.9 %copy-start.2 = (bf16[3,48,256]{2,1,0:T(8,128)(2,1)S(1)}, bf16[3,48,256]{2,1,0:T(8,128)(2,1)}, u32[]{:S(2)}) copy-start(bf16[3,48,256]{2,1,0:T(8,128)(2,1)} %refs_4_.1) | copy-start | bytes 221188
  20.8 0.9 %copy-start.4 = (bf16[192,384]{1,0:T(8,128)(2,1)S(1)}, bf16[192,384]{1,0:T(8,128)(2,1)}, u32[]{:S(2)}) copy-start(bf16[192,384]{1,0:T(8,128)(2,1)} %refs_0_.1) | copy-start | bytes 442372
  22.1 1.9 %collective-permute-start.5 = (bf16[48,768]{1,0:T(8,128)(2,1)S(1)}, bf16[48,768]{1,0:T(8,128)(2,1)S(1)}, u32[]{:S(2)}, u32[]{:S(2)}) collective-permute-start(bf16[48,768]{1,0:T(8,128)(2,1)S(1)} %get-tuple-element.10), channel_id=1, source_target_pairs={{0,1},{1,0},{2,3},{3,2},{4,5},{5,4},{6,7},{7,6},{8,9},{9,8},{10,11... | collective-permute-start | bytes 221192 | tf_op jit(solution)/shard_map/ppermute | solution.py:31
  22.2 4.8 %collective-permute-start.6 = (bf16[48,768]{1,0:T(8,128)(2,1)S(1)}, bf16[48,768]{1,0:T(8,128)(2,1)S(1)}, u32[]{:S(2)}, u32[]{:S(2)}) collective-permute-start(bf16[48,768]{1,0:T(8,128)(2,1)S(1)} %get-tuple-element.11), channel_id=1, source_target_pairs={{0,2},{1,3},{2,0},{3,1},{4,6},{5,7},{6,4},{7,5},{8,10},{9,11},{10,... | collective-permute-start | bytes 221192 | tf_op jit(solution)/shard_map/ppermute | solution.py:31
  23.8 4.4 %collective-permute-start.7 = (bf16[48,768]{1,0:T(8,128)(2,1)S(1)}, bf16[48,768]{1,0:T(8,128)(2,1)S(1)}, u32[]{:S(2)}, u32[]{:S(2)}) collective-permute-start(bf16[48,768]{1,0:T(8,128)(2,1)S(1)} %get-tuple-element.12), channel_id=1, source_target_pairs={{0,3},{1,2},{2,1},{3,0},{4,7},{5,6},{6,5},{7,4},{8,11},{9,10},{10,... | collective-permute-start | bytes 221192 | tf_op jit(solution)/shard_map/ppermute | solution.py:31
  28.3 0.9 %copy-start.3 = (bf16[3,48,256]{2,1,0:T(8,128)(2,1)S(1)}, bf16[3,48,256]{2,1,0:T(8,128)(2,1)}, u32[]{:S(2)}) copy-start(bf16[3,48,256]{2,1,0:T(8,128)(2,1)} %refs_4_.1) | copy-start | bytes 221188
  29.1 0.9 %copy-start.5 = (bf16[3,48,256]{2,1,0:T(8,128)(2,1)S(1)}, bf16[3,48,256]{2,1,0:T(8,128)(2,1)}, u32[]{:S(2)}) copy-start(bf16[3,48,256]{2,1,0:T(8,128)(2,1)} %refs_5_.1) | copy-start | bytes 221188
  31.5 1.4 %collective-permute-start.8 = (bf16[4,96,256]{2,1,0:T(8,128)(2,1)S(1)}, bf16[4,96,256]{2,1,0:T(8,128)(2,1)S(1)}, u32[]{:S(2)}, u32[]{:S(2)}) collective-permute-start(bf16[4,96,256]{2,1,0:T(8,128)(2,1)S(1)} %get-tuple-element.15), channel_id=1, source_target_pairs={{0,1},{1,0},{2,3},{3,2},{4,5},{5,4},{6,7},{7,6},{8,9},{9,8},{10,11... | collective-permute-start | bytes 589832 | tf_op jit(solution)/shard_map/ppermute | solution.py:31
  33.1 4.2 %collective-permute-start.9 = (bf16[96,256]{1,0:T(8,128)(2,1)S(1)}, bf16[96,256]{1,0:T(8,128)(2,1)S(1)}, u32[]{:S(2)}, u32[]{:S(2)}) collective-permute-start(bf16[96,256]{1,0:T(8,128)(2,1)S(1)} %get-tuple-element.18), channel_id=1, source_target_pairs={{0,4},{1,5},{2,6},{3,7},{4,0},{5,1},{6,2},{7,3},{8,12},{9,13},{10,... | collective-permute-start | bytes 147464 | tf_op jit(solution)/shard_map/ppermute | solution.py:31
  34.6 5.0 %collective-permute-start.11 = (bf16[96,256]{1,0:T(8,128)(2,1)S(1)}, bf16[96,256]{1,0:T(8,128)(2,1)S(1)}, u32[]{:S(2)}, u32[]{:S(2)}) collective-permute-start(bf16[96,256]{1,0:T(8,128)(2,1)S(1)} %get-tuple-element.19), channel_id=1, source_target_pairs={{0,6},{1,7},{2,4},{3,5},{4,2},{5,3},{6,0},{7,1},{8,14},{9,15},{10,... | collective-permute-start | bytes 147464 | tf_op jit(solution)/shard_map/ppermute | solution.py:31
  35.9 4.2 %collective-permute-start.10 = (bf16[96,256]{1,0:T(8,128)(2,1)S(1)}, bf16[96,256]{1,0:T(8,128)(2,1)S(1)}, u32[]{:S(2)}, u32[]{:S(2)}) collective-permute-start(bf16[96,256]{1,0:T(8,128)(2,1)S(1)} %get-tuple-element.20), channel_id=1, source_target_pairs={{0,2},{1,3},{2,0},{3,1},{4,6},{5,7},{6,4},{7,5},{8,10},{9,11},{10,... | collective-permute-start | bytes 147464 | tf_op jit(solution)/shard_map/ppermute | solution.py:31
  40.2 6.6 %collective-permute-start.14 = (bf16[96,256]{1,0:T(8,128)(2,1)S(1)}, bf16[96,256]{1,0:T(8,128)(2,1)S(1)}, u32[]{:S(2)}, u32[]{:S(2)}) collective-permute-start(bf16[96,256]{1,0:T(8,128)(2,1)S(1)} %fusion.3), channel_id=1, source_target_pairs={{0,24},{4,28},{8,16},{12,20},{16,8},{20,12},{24,0},{28,4},{1,25},{... | collective-permute-start | bytes 147464 | tf_op jit(solution)/shard_map/ppermute | solution.py:31
  42.5 5.0 %collective-permute-start.13 = (bf16[96,256]{1,0:T(8,128)(2,1)S(1)}, bf16[96,256]{1,0:T(8,128)(2,1)S(1)}, u32[]{:S(2)}, u32[]{:S(2)}) collective-permute-start(bf16[96,256]{1,0:T(8,128)(2,1)S(1)} %fusion.3), channel_id=1, source_target_pairs={{0,16},{4,20},{8,24},{12,28},{16,0},{20,4},{24,8},{28,12},{1,17},{... | collective-permute-start | bytes 147464 | tf_op jit(solution)/shard_map/ppermute | solution.py:31
  43.8 4.3 %collective-permute-start.12 = (bf16[96,256]{1,0:T(8,128)(2,1)S(1)}, bf16[96,256]{1,0:T(8,128)(2,1)S(1)}, u32[]{:S(2)}, u32[]{:S(2)}) collective-permute-start(bf16[96,256]{1,0:T(8,128)(2,1)S(1)} %fusion.3), channel_id=1, source_target_pairs={{0,8},{4,12},{8,0},{12,4},{16,24},{20,28},{24,16},{28,20},{1,9},{5... | collective-permute-start | bytes 147464 | tf_op jit(solution)/shard_map/ppermute | solution.py:31
  48.1 5.1 %collective-permute-start.17 = (bf16[96,256]{1,0:T(8,128)(2,1)S(1)}, bf16[96,256]{1,0:T(8,128)(2,1)S(1)}, u32[]{:S(2)}, u32[]{:S(2)}) collective-permute-start(bf16[96,256]{1,0:T(8,128)(2,1)S(1)} %add_convert_fusion), channel_id=1, source_target_pairs={{0,6},{1,7},{2,4},{3,5},{4,2},{5,3},{6,0},{7,1},{8,14},{9,15},{10,... | collective-permute-start | bytes 147464 | tf_op jit(solution)/shard_map/ppermute | solution.py:31
  49.9 4.1 %collective-permute-start.16 = (bf16[96,256]{1,0:T(8,128)(2,1)S(1)}, bf16[96,256]{1,0:T(8,128)(2,1)S(1)}, u32[]{:S(2)}, u32[]{:S(2)}) collective-permute-start(bf16[96,256]{1,0:T(8,128)(2,1)S(1)} %add_convert_fusion), channel_id=1, source_target_pairs={{0,2},{1,3},{2,0},{3,1},{4,6},{5,7},{6,4},{7,5},{8,10},{9,11},{10,... | collective-permute-start | bytes 147464 | tf_op jit(solution)/shard_map/ppermute | solution.py:31
  51.0 4.1 %collective-permute-start.15 = (bf16[96,256]{1,0:T(8,128)(2,1)S(1)}, bf16[96,256]{1,0:T(8,128)(2,1)S(1)}, u32[]{:S(2)}, u32[]{:S(2)}) collective-permute-start(bf16[96,256]{1,0:T(8,128)(2,1)S(1)} %add_convert_fusion), channel_id=1, source_target_pairs={{0,4},{1,5},{2,6},{3,7},{4,0},{5,1},{6,2},{7,3},{8,12},{9,13},{10,... | collective-permute-start | bytes 147464 | tf_op jit(solution)/shard_map/ppermute | solution.py:31
  55.1 1.5 %collective-permute-start.18 = (bf16[4,96,256]{2,1,0:T(8,128)(2,1)S(1)}, bf16[4,96,256]{2,1,0:T(8,128)(2,1)S(1)}, u32[]{:S(2)}, u32[]{:S(2)}) collective-permute-start(bf16[4,96,256]{2,1,0:T(8,128)(2,1)S(1)} %pad_maximum_fusion.1.here_ref), channel_id=1, source_target_pairs={{0,1},{1,0},{2,3},{3,2},{4,5},{5,4},{6,7},{7,6},{8,9},{9,8},{10,11... | collective-permute-start | bytes 589832 | tf_op jit(solution)/shard_map/ppermute | solution.py:31

commit v2 on v1

v2 whole, which is shorter than its diff:
```python
import functools

import jax
import jax.numpy as jnp
from jax import lax
from jax.experimental import pallas as pl
from jax.experimental.pallas import tpu as pltpu
from jax.sharding import PartitionSpec as P

F32 = jnp.float32
BF16 = jnp.bfloat16
VMEM = pl.BlockSpec(memory_space=pltpu.VMEM)


def swap(value, axes, sizes, bits):
    dims = [sizes[axis] for axis in axes]
    pairs = []
    count = 1
    for dim in dims:
        count *= dim
    for source in range(count):
        rest, coords = source, []
        for dim in reversed(dims):
            coords.append(rest % dim)
            rest //= dim
        coords = coords[::-1]
        target = 0
        for axis, dim, coord in zip(axes, dims, coords):
            target = target * dim + (coord ^ bits.get(axis, 0))
        pairs.append((source, target))
    return lax.ppermute(value, axes, pairs)


def split(value):
    high = value.astype(BF16)
    return high, (value - high.astype(F32)).astype(BF16)


def dot(left, right):
    return jnp.dot(left, right, preferred_element_type=F32)


def dot_rows(left, right):
    return lax.dot_general(left, right, (((0,), (0,)), ((), ())), preferred_element_type=F32)


def prepare_kernel(cot_ref, saved_ref, upstream_ref, solver_ref, cot_out, saved_out, upstream_out, high_out, low_out):
    cot_out[...] = cot_ref[...]
    saved_out[...] = saved_ref[...]
    upstream_out[...] = upstream_ref[...]
    high, low = split(solver_ref[...])
    high_out[...] = high
    low_out[...] = low


def main_kernel(along_row, along_col, *refs):
    row_refs, refs = refs[: len(along_row)], refs[len(along_row) :]
    col_refs, refs = refs[: len(along_col)], refs[len(along_col) :]
    cot_ref, upstream_ref, high_ref, low_ref, tops_ref = refs[:5]
    columns_keep, columns_send, keep_ref, send_ref, joined, own, total, diag = refs[5:]
    row, col = lax.axis_index("row"), lax.axis_index("col")
    panels, height, width = upstream_ref.shape

    def place(target, index, tile):
        start = pl.multiple_of(index * height, height)
        for panel in range(panels):
            target[pl.ds(start, height), panel * width : (panel + 1) * width] = tile[panel]

    for bits_list, ref in zip(along_row, row_refs):
        for spot, bits in enumerate(bits_list):
            place(joined, row ^ bits, ref.at[spot])
    for bits_list, ref in zip(along_col, col_refs):
        for spot, bits in enumerate(bits_list):
            place(own, col ^ bits, ref.at[spot])
    total[...] = -2.0 * dot(cot_ref[...], joined[...])
    mine = pl.ds(pl.multiple_of(col * height, height), height)
    for index in range(panels):
        span = slice(index * width, (index + 1) * width)
        total[mine, span] += upstream_ref[index].astype(F32)

    columns = []
    tall = own.shape[0]
    for index in range(panels):
        span = slice(index * width, (index + 1) * width)
        panel = own[:, span]
        combined = total[:, span]
        appended = None
        for earlier in range(index):
            term = dot(columns[earlier], tops_ref[index * (index - 1) // 2 + earlier])
            appended = term if appended is None else appended + term
        if appended is not None:
            combined = combined - 2.0 * appended
        high, low = split(combined)
        if appended is None:
            first = dot(jnp.concatenate([high, low]), high_ref[index])
            second = dot(high, low_ref[index])
        else:
            first = dot(jnp.concatenate([high, low, panel]), high_ref[index])
            second = dot(jnp.concatenate([high, panel]), low_ref[index])
        now = first[:tall] + (first[tall : 2 * tall] + second[:tall])
        total[:, span] = now
        now = now.astype(BF16)
        columns.append(now)
        result = -dot_rows(panel, now)
        if appended is not None:
            solved = 2.0 * (first[2 * tall :] + second[tall:])
            result = result + dot_rows(appended.astype(BF16), solved.astype(BF16))
        diag[span, :] = result

    piece = keep_ref.shape[1]
    core, spot = place_of()
    for bits in range(4):
        here = pl.multiple_of((core * 4 + (spot ^ bits)) * piece, piece)
        there = pl.multiple_of(((1 - core) * 4 + (spot ^ bits)) * piece, piece)
        keep_ref[bits] = diag[pl.ds(here, piece), :]
        send_ref[bits] = diag[pl.ds(there, piece), :].astype(BF16)
    for pair in range(columns_keep.shape[0]):
        for bits, ref in ((2 * pair, columns_keep), (2 * pair + 1, columns_send)):
            tile = pl.ds(pl.multiple_of((col ^ bits) * height, height), height)
            for index in range(panels):
                ref[pair, index] = total[tile, index * width : (index + 1) * width].astype(ref.dtype)


def place_of():
    row, col = lax.axis_index("row"), lax.axis_index("col")
    return col & 1, ((col >> 1) & 1) * 2 + (row & 1)


def finish_kernel(here_ref, there_ref, out_ref):
    core, spot = place_of()
    piece = here_ref.shape[1]
    for bits in range(4):
        here = pl.multiple_of((core * 4 + (spot ^ bits)) * piece, piece)
        there = pl.multiple_of(((1 - core) * 4 + (spot ^ bits)) * piece, piece)
        out_ref[pl.ds(here, piece), :] = here_ref[bits].astype(F32)
        out_ref[pl.ds(there, piece), :] = there_ref[bits].astype(F32)


def after(value, *others):
    return lax.optimization_barrier((value, *others))[0]


def body(sizes, cotangent, saved_panels, upstream, inverse_diag, panel_tops):
    rows, cols = sizes["row"], sizes["col"]
    panels, height, width = saved_panels.shape
    limit = pltpu.CompilerParams(vmem_limit_bytes=32 * 1024 * 1024)
    tile_shape = jax.ShapeDtypeStruct(saved_panels.shape, BF16)

    far = {bits: swap(saved_panels, ("row",), sizes, {"row": bits}) for bits in range(rows - 2, 0, -2)}
    near = {1: swap(saved_panels, ("row",), sizes, {"row": 1})}
    along_col = [(0,)]
    col_tiles = [saved_panels]
    for power in range(cols.bit_length() - 1):
        have = [bits for group in along_col for bits in group]
        sent = jnp.concatenate([tile.reshape(-1, panels, height, width) for tile in col_tiles])
        along_col.append(tuple(bits ^ (1 << power) for bits in have))
        col_tiles.append(swap(sent, ("col",), sizes, {"col": 1 << power}))

    groups = [[2], [bits for bits in far if bits != 2]]
    along_row = [(0,), (1,)]
    row_tiles = [None, near[1][None]]
    for group in groups:
        if not group or group[0] not in far:
            continue
        sent = after(jnp.stack([far[bits] for bits in group]), near[1])
        for bits in group:
            along_row.append((bits,))
            row_tiles.append(far[bits][None])
        along_row.append(tuple(bits ^ 1 for bits in group))
        row_tiles.append(swap(sent, ("row",), sizes, {"row": 1}))

    cot, saved, upstream_here, high, low = pl.pallas_call(
        prepare_kernel,
        out_shape=[
            jax.ShapeDtypeStruct(cotangent.shape, BF16),
            tile_shape,
            tile_shape,
            jax.ShapeDtypeStruct(inverse_diag.shape, BF16),
            jax.ShapeDtypeStruct(inverse_diag.shape, BF16),
        ],
        in_specs=[VMEM] * 4,
        out_specs=[VMEM] * 5,
        compiler_params=limit,
    )(cotangent, saved_panels, upstream, inverse_diag)
    row_tiles[0] = saved[None]
    col_tiles[0] = saved[None]

    piece = panels * width // 8
    columns_keep, columns_send, keep, send = pl.pallas_call(
        functools.partial(main_kernel, along_row, along_col),
        out_shape=[
            jax.ShapeDtypeStruct((cols // 2, panels, height, width), F32),
            jax.ShapeDtypeStruct((cols // 2, panels, height, width), BF16),
            jax.ShapeDtypeStruct((4, piece, width), F32),
            jax.ShapeDtypeStruct((4, piece, width), BF16),
        ],
        in_specs=[VMEM] * (len(row_tiles) + len(col_tiles) + 5),
        out_specs=[VMEM] * 4,
        scratch_shapes=[
            pltpu.VMEM((rows * height, panels * width), BF16),
            pltpu.VMEM((cols * height, panels * width), BF16),
            pltpu.VMEM((cols * height, panels * width), F32),
            pltpu.VMEM((panels * width, width), F32),
        ],
        compiler_params=limit,
    )(*row_tiles, *col_tiles, cot, upstream_here, high, low, panel_tops)

    both = ("row", "col")
    half = keep + swap(send, ("col",), sizes, {"col": 1}).astype(F32)
    spots = [{"col": (bits >> 1) * 2, "row": bits & 1} for bits in range(4)]
    total = half[0]
    for bits in range(3, 0, -1):
        total = total + swap(half[bits].astype(BF16), both, sizes, spots[bits]).astype(F32)
    columns = columns_keep + swap(after(columns_send, half), ("col",), sizes, {"col": 1}).astype(F32)
    held = total
    for power in range(1, cols.bit_length() - 1):
        halves = columns.reshape(-1, 2, panels, height, width)
        sent = after(halves[:, 1].astype(BF16), held)
        columns = halves[:, 0] + swap(sent, ("col",), sizes, {"col": 1 << power}).astype(F32)
    columns = columns[0].astype(BF16)

    others = [{"row": 1 << power} for power in range(1, rows.bit_length() - 1)]
    others += [{"col": 1 << power} for power in range(2, cols.bit_length() - 1)]
    if len(others) == 2 and "col" not in others[1]:
        mine = total.astype(BF16)
        first, second = others[0]["row"], others[1]["row"]
        from_both, from_second, from_first = [
            swap(mine, ("row",), sizes, {"row": bits}) for bits in (first ^ second, second, first)
        ]
        total = (mine.astype(F32) + from_first.astype(F32)) + (
            from_second.astype(F32) + from_both.astype(F32)
        )
    else:
        for bits in others:
            mine = total.astype(BF16)
            total = mine.astype(F32) + swap(mine, tuple(bits), sizes, bits).astype(F32)
    mine = total.astype(BF16)
    here = jnp.stack([mine] + [swap(mine, both, sizes, spots[bits]) for bits in range(3, 0, -1)][::-1])
    there = swap(here, ("col",), sizes, {"col": 1})
    diag_cot = pl.pallas_call(
        finish_kernel,
        out_shape=jax.ShapeDtypeStruct((panels * width, width), F32),
        in_specs=[VMEM] * 2,
        out_specs=VMEM,
        compiler_params=limit,
    )(here, there)
    return columns, diag_cot.reshape(panels, width, width)


def solution(mesh):
    in_specs = (
        P("row", "col"),
        P(None, ("row", "col"), None),
        P(None, ("row", "col"), None),
        P(),
        P(),
    )
    out_specs = (P(None, ("row", "col"), None), P())
    return jax.shard_map(
        functools.partial(body, dict(mesh.shape)),
        mesh=mesh,
        in_specs=in_specs,
        out_specs=out_specs,
        check_vma=False,
    )
```

time: 57.8 us -> 49.4 us (0.85)
  waiting for transfers between devices: 28.8 us -> 18.3 us
  starting transfers between devices: 21.4 us -> 24.3 us
  local copies, waits for them, and re-layouts: 3.59 us -> 2 us
  other arithmetic: 0.16 us -> 0.84 us
    ppermute x19 -> x21, waiting for transfers between devices: 28.8 us -> 18.3 us  [swap(): return lax.ppermute(value, axes, pairs)]
    ppermute x19 -> x21, starting transfers between devices: 21.4 us -> 24.3 us  [swap(): return lax.ppermute(value, axes, pairs)]
    unnamed x12 -> x10, local copies, waits for them, and re-layouts: 3.57 us -> 1.98 us
    convert_element_type x0 -> x1, other arithmetic: none -> 0.65 us  [body(): columns = columns[0].astype(BF16)]
  transfers between devices with their start and end apart: 19 -> 21, of which waited for: 17 -> 12; matrix products, arithmetic and copies ran while one was open for 0% -> 2% of each run, Pallas kernels for 0% -> 0%
where the time goes in v2:
time: 49.4 us; the launch traced here: 49.2 us
  starting transfers between devices  24.3 us (49%)
  waiting for transfers between devices  18.3 us (37%)
  Pallas kernels  3.05 us (6%)
  local copies, waits for them, and re-layouts  2 us (4%)
  other arithmetic  0.84 us (2%)
  between operations  0.76 us (2%)
    ppermute x21, starting transfers between devices, swap(): return lax.ppermute(value, axes, pairs)  24.3 us
    ppermute x21, waiting for transfers between devices, swap(): return lax.ppermute(value, axes, pairs)  18.3 us
    unnamed x10, local copies, waits for them, and re-layouts  1.98 us
    pallas_call x1, Pallas kernels, body(): pl.pallas_call(functools.partial(main_kernel, along_row, along_col), out_...  1.94 us
  transfers between devices with their start and end apart: 21, of which 12 were waited for; matrix products, arithmetic and copies ran while one was open for 2% of the time, Pallas kernels for 0%

profile of v2, /device:TPU:0, one launch (start us, length us, event | category | flops | bytes accessed | tf_op | source)
XLA Modules:
  0.0 49.2 jit_solution(15595583813727700365)
XLA Ops:
  0.6 5.1 %collective-permute-start.3 = (bf16[3,48,256]{2,1,0:T(8,128)(2,1)}, bf16[3,48,256]{2,1,0:T(8,128)(2,1)S(1)}, u32[]{:S(2)}, u32[]{:S(2)}) collective-permute-start(bf16[3,48,256]{2,1,0:T(8,128)(2,1)} %saved_ref.1), channel_id=1, source_target_pairs={{0,24},{4,28},{8,16},{12,20},{16,8},{20,12},{24,0},{28,4},{1,25},{... | collective-permute-start | bytes 221192 | tf_op jit(solution)/shard_map/ppermute | solution.py:31
  5.7 0.6 %collective-permute-start.1 = (bf16[3,48,256]{2,1,0:T(8,128)(2,1)}, bf16[3,48,256]{2,1,0:T(8,128)(2,1)S(1)}, u32[]{:S(2)}, u32[]{:S(2)}) collective-permute-start(bf16[3,48,256]{2,1,0:T(8,128)(2,1)} %saved_ref.1), channel_id=1, source_target_pairs={{0,8},{4,12},{8,0},{12,4},{16,24},{20,28},{24,16},{28,20},{1,9},{5... | collective-permute-start | bytes 221192 | tf_op jit(solution)/shard_map/ppermute | solution.py:31
  6.4 1.6 %collective-permute-start = (bf16[3,48,256]{2,1,0:T(8,128)(2,1)}, bf16[3,48,256]{2,1,0:T(8,128)(2,1)S(1)}, u32[]{:S(2)}, u32[]{:S(2)}) collective-permute-start(bf16[3,48,256]{2,1,0:T(8,128)(2,1)} %saved_ref.1), channel_id=1, source_target_pairs={{0,4},{4,0},{8,12},{12,8},{16,20},{20,16},{24,28},{28,24},{1,5},{5... | collective-permute-start | bytes 221192 | tf_op jit(solution)/shard_map/ppermute | solution.py:31
  8.0 0.7 %collective-permute-done.3 = bf16[3,48,256]{2,1,0:T(8,128)(2,1)S(1)} collective-permute-done((bf16[3,48,256]{2,1,0:T(8,128)(2,1)}, bf16[3,48,256]{2,1,0:T(8,128)(2,1)S(1)}, u32[]{:S(2)}, u32[]{:S(2)}) %collective-permute-start.3) | collective-permute-done | bytes 73760 | tf_op jit(solution)/shard_map/ppermute | solution.py:31
  8.7 3.4 %collective-permute-done.4 = bf16[3,48,256]{2,1,0:T(8,128)(2,1)S(1)} collective-permute-done((bf16[3,48,256]{2,1,0:T(8,128)(2,1)}, bf16[3,48,256]{2,1,0:T(8,128)(2,1)S(1)}, u32[]{:S(2)}, u32[]{:S(2)}) %collective-permute-start.4) | collective-permute-done | bytes 73760 | tf_op jit(solution)/shard_map/ppermute | solution.py:31
  12.2 0.8 %copy-done.2 = bf16[3,48,256]{2,1,0:T(8,128)(2,1)S(1)} copy-done((bf16[3,48,256]{2,1,0:T(8,128)(2,1)S(1)}, bf16[3,48,256]{2,1,0:T(8,128)(2,1)}, u32[]{:S(2)}) %copy-start.2) | copy-done | bytes 73752
  13.1 1.6 %collective-permute-start.7 = (bf16[2,3,48,256]{3,2,1,0:T(8,128)(2,1)S(1)}, bf16[2,3,48,256]{3,2,1,0:T(8,128)(2,1)S(1)}, u32[]{:S(2)}, u32[]{:S(2)}) collective-permute-start(bf16[2,3,48,256]{3,2,1,0:T(8,128)(2,1)S(1)} %pad_maximum_fusion.2), channel_id=1, source_target_pairs={{0,2},{1,3},{2,0},{3,1},{4,6},{5,7},{6,4},{7,5},{8,10},{9,11},{10,... | collective-permute-start | bytes 442376 | tf_op jit(solution)/shard_map/ppermute | solution.py:31
  14.7 1.5 %collective-permute-start.5 = (bf16[2,3,48,256]{3,2,1,0:T(8,128)(2,1)S(1)}, bf16[2,3,48,256]{3,2,1,0:T(8,128)(2,1)S(1)}, u32[]{:S(2)}, u32[]{:S(2)}) collective-permute-start(bf16[2,3,48,256]{3,2,1,0:T(8,128)(2,1)S(1)} %pad_maximum_fusion.1), channel_id=1, source_target_pairs={{0,4},{4,0},{8,12},{12,8},{16,20},{20,16},{24,28},{28,24},{1,5},{5... | collective-permute-start | bytes 442376 | tf_op jit(solution)/shard_map/ppermute | solution.py:31
  16.2 0.5 %collective-permute-start.2 = (bf16[1,3,48,256]{3,2,1,0:T(8,128)(2,1)S(1)}, bf16[1,3,48,256]{3,2,1,0:T(8,128)(2,1)S(1)}, u32[]{:S(2)}, u32[]{:S(2)}) collective-permute-start(bf16[1,3,48,256]{3,2,1,0:T(8,128)(2,1)S(1)} %bitcast.47), channel_id=1, source_target_pairs={{0,4},{4,0},{8,12},{12,8},{16,20},{20,16},{24,28},{28,24},{1,5},{5... | collective-permute-start | bytes 221192 | tf_op jit(solution)/shard_map/ppermute | solution.py:31
  16.7 1.1 %copy-done = f32[3,256,256]{2,1,0:T(8,128)S(1)} copy-done((f32[3,256,256]{2,1,0:T(8,128)S(1)}, f32[3,256,256]{2,1,0:T(8,128)}, u32[]{:S(2)}) %copy-start) | copy-done | bytes 786456
  18.0 3.4 %collective-permute-done.2.refs_3_ = bf16[1,3,48,256]{3,2,1,0:T(8,128)(2,1)S(1)} collective-permute-done((bf16[1,3,48,256]{3,2,1,0:T(8,128)(2,1)S(1)}, bf16[1,3,48,256]{3,2,1,0:T(8,128)(2,1)S(1)}, u32[]{:S(2)}, u32[]{:S(2)}) %collective-permute-start.2) | collective-permute-done | bytes 73760 | tf_op jit(solution)/shard_map/ppermute | solution.py:31
  21.4 1.9 %shard_map.69 = (f32[2,3,48,256]{3,2,1,0:T(8,128)S(1)}, bf16[2,3,48,256]{3,2,1,0:T(8,128)(2,1)S(1)}, f32[4,96,256]{2,1,0:T(8,128)S(1)}, bf16[4,96,256]{2,1,0:T(8,128)(2,1)S(1)}) custom-call(bf16[1,3,48,256]{3,2,1,0:T(8,128)(2,1)S(1)} %bitcast.39, bf16[1,3,48,256]{3,2,1,0:T(8,128)(2,1)S(1)} %bitcast.49, bf16[1,3,48,256]{3,2,1,0:T(8,128)(2,1)S(1)} %bitcast.48, ...), custom_call_target="tpu_custom_call" | custom-call | tf_op jit(solution)/shard_map/pallas_call | solution.py:189
  23.4 1.4 %collective-permute-done.8 = bf16[4,96,256]{2,1,0:T(8,128)(2,1)S(1)} collective-permute-done((bf16[4,96,256]{2,1,0:T(8,128)(2,1)S(1)}, bf16[4,96,256]{2,1,0:T(8,128)(2,1)S(1)}, u32[]{:S(2)}, u32[]{:S(2)}) %collective-permute-start.8) | collective-permute-done | bytes 196640 | tf_op jit(solution)/shard_map/ppermute | solution.py:31
  24.9 1.5 %collective-permute-start.10 = (bf16[96,256]{1,0:T(8,128)(2,1)S(1)}, bf16[96,256]{1,0:T(8,128)(2,1)S(1)}, u32[]{:S(2)}, u32[]{:S(2)}) collective-permute-start(bf16[96,256]{1,0:T(8,128)(2,1)S(1)} %get-tuple-element.30), channel_id=1, source_target_pairs={{0,6},{1,7},{2,4},{3,5},{4,2},{5,3},{6,0},{7,1},{8,14},{9,15},{10,... | collective-permute-start | bytes 147464 | tf_op jit(solution)/shard_map/ppermute | solution.py:31
  26.4 0.4 collective-permute-start.12
  26.8 1.7 %collective-permute-start.11 = (bf16[96,256]{1,0:T(8,128)(2,1)S(1)}, bf16[96,256]{1,0:T(8,128)(2,1)S(1)}, u32[]{:S(2)}, u32[]{:S(2)}) collective-permute-start(bf16[96,256]{1,0:T(8,128)(2,1)S(1)} %get-tuple-element.32), channel_id=1, source_target_pairs={{0,2},{1,3},{2,0},{3,1},{4,6},{5,7},{6,4},{7,5},{8,10},{9,11},{10,... | collective-permute-start | bytes 147464 | tf_op jit(solution)/shard_map/ppermute | solution.py:31
  28.5 1.7 %collective-permute-done.10 = bf16[96,256]{1,0:T(8,128)(2,1)S(1)} collective-permute-done((bf16[96,256]{1,0:T(8,128)(2,1)S(1)}, bf16[96,256]{1,0:T(8,128)(2,1)S(1)}, u32[]{:S(2)}, u32[]{:S(2)}) %collective-permute-start.10) | collective-permute-done | bytes 49184 | tf_op jit(solution)/shard_map/ppermute | solution.py:31
  30.5 0.4 collective-permute-done.11
  30.9 0.5 %collective-permute-start.15 = (bf16[96,256]{1,0:T(8,128)(2,1)S(1)}, bf16[96,256]{1,0:T(8,128)(2,1)S(1)}, u32[]{:S(2)}, u32[]{:S(2)}) collective-permute-start(bf16[96,256]{1,0:T(8,128)(2,1)S(1)} %fusion.4), channel_id=1, source_target_pairs={{0,16},{4,20},{8,24},{12,28},{16,0},{20,4},{24,8},{28,12},{1,17},{... | collective-permute-start | bytes 147464 | tf_op jit(solution)/shard_map/ppermute | solution.py:31
  31.5 2.2 %collective-permute-start.14 = (bf16[96,256]{1,0:T(8,128)(2,1)S(1)}, bf16[96,256]{1,0:T(8,128)(2,1)S(1)}, u32[]{:S(2)}, u32[]{:S(2)}) collective-permute-start(bf16[96,256]{1,0:T(8,128)(2,1)S(1)} %fusion.4), channel_id=1, source_target_pairs={{0,8},{4,12},{8,0},{12,4},{16,24},{20,28},{24,16},{28,20},{1,9},{5... | collective-permute-start | bytes 147464 | tf_op jit(solution)/shard_map/ppermute | solution.py:31
  33.7 1.7 %collective-permute-start.16 = (bf16[96,256]{1,0:T(8,128)(2,1)S(1)}, bf16[96,256]{1,0:T(8,128)(2,1)S(1)}, u32[]{:S(2)}, u32[]{:S(2)}) collective-permute-start(bf16[96,256]{1,0:T(8,128)(2,1)S(1)} %fusion.4), channel_id=1, source_target_pairs={{0,24},{4,28},{8,16},{12,20},{16,8},{20,12},{24,0},{28,4},{1,25},{... | collective-permute-start | bytes 147464 | tf_op jit(solution)/shard_map/ppermute | solution.py:31
  35.4 0.9 %collective-permute-done.15 = bf16[96,256]{1,0:T(8,128)(2,1)S(1)} collective-permute-done((bf16[96,256]{1,0:T(8,128)(2,1)S(1)}, bf16[96,256]{1,0:T(8,128)(2,1)S(1)}, u32[]{:S(2)}, u32[]{:S(2)}) %collective-permute-start.15) | collective-permute-done | bytes 49184 | tf_op jit(solution)/shard_map/ppermute | solution.py:31
  36.3 3.3 %collective-permute-done.16 = bf16[96,256]{1,0:T(8,128)(2,1)S(1)} collective-permute-done((bf16[96,256]{1,0:T(8,128)(2,1)S(1)}, bf16[96,256]{1,0:T(8,128)(2,1)S(1)}, u32[]{:S(2)}, u32[]{:S(2)}) %collective-permute-start.16) | collective-permute-done | bytes 49184 | tf_op jit(solution)/shard_map/ppermute | solution.py:31
  39.6 2.5 %collective-permute-start.19 = (bf16[96,256]{1,0:T(8,128)(2,1)S(1)}, bf16[96,256]{1,0:T(8,128)(2,1)S(1)}, u32[]{:S(2)}, u32[]{:S(2)}) collective-permute-start(bf16[96,256]{1,0:T(8,128)(2,1)S(1)} %add_convert_fusion), channel_id=1, source_target_pairs={{0,6},{1,7},{2,4},{3,5},{4,2},{5,3},{6,0},{7,1},{8,14},{9,15},{10,... | collective-permute-start | bytes 147464 | tf_op jit(solution)/shard_map/ppermute | solution.py:31
  42.1 0.5 %collective-permute-start.18 = (bf16[96,256]{1,0:T(8,128)(2,1)S(1)}, bf16[96,256]{1,0:T(8,128)(2,1)S(1)}, u32[]{:S(2)}, u32[]{:S(2)}) collective-permute-start(bf16[96,256]{1,0:T(8,128)(2,1)S(1)} %add_convert_fusion), channel_id=1, source_target_pairs={{0,2},{1,3},{2,0},{3,1},{4,6},{5,7},{6,4},{7,5},{8,10},{9,11},{10,... | collective-permute-start | bytes 147464 | tf_op jit(solution)/shard_map/ppermute | solution.py:31
  42.6 0.5 %collective-permute-start.17 = (bf16[96,256]{1,0:T(8,128)(2,1)S(1)}, bf16[96,256]{1,0:T(8,128)(2,1)S(1)}, u32[]{:S(2)}, u32[]{:S(2)}) collective-permute-start(bf16[96,256]{1,0:T(8,128)(2,1)S(1)} %add_convert_fusion), channel_id=1, source_target_pairs={{0,4},{1,5},{2,6},{3,7},{4,0},{5,1},{6,2},{7,3},{8,12},{9,13},{10,... | collective-permute-start | bytes 147464 | tf_op jit(solution)/shard_map/ppermute | solution.py:31
  43.2 1.6 %collective-permute-start.13 = (bf16[1,3,48,256]{3,2,1,0:T(8,128)(2,1)S(1)}, bf16[1,3,48,256]{3,2,1,0:T(8,128)(2,1)S(1)}, u32[]{:S(2)}, u32[]{:S(2)}) collective-permute-start(bf16[1,3,48,256]{3,2,1,0:T(8,128)(2,1)S(1)} %fusion.6), channel_id=1, source_target_pairs={{0,2},{1,3},{2,0},{3,1},{4,6},{5,7},{6,4},{7,5},{8,10},{9,11},{10,... | collective-permute-start | bytes 221192 | tf_op jit(solution)/shard_map/ppermute | solution.py:31
  44.8 1.4 %collective-permute-done.18 = bf16[96,256]{1,0:T(8,128)(2,1)S(1)} collective-permute-done((bf16[96,256]{1,0:T(8,128)(2,1)S(1)}, bf16[96,256]{1,0:T(8,128)(2,1)S(1)}, u32[]{:S(2)}, u32[]{:S(2)}) %collective-permute-start.18) | collective-permute-done | bytes 49184 | tf_op jit(solution)/shard_map/ppermute | solution.py:31
  46.2 0.5 %collective-permute-done.17 = bf16[96,256]{1,0:T(8,128)(2,1)S(1)} collective-permute-done((bf16[96,256]{1,0:T(8,128)(2,1)S(1)}, bf16[96,256]{1,0:T(8,128)(2,1)S(1)}, u32[]{:S(2)}, u32[]{:S(2)}) %collective-permute-start.17) | collective-permute-done | bytes 49184 | tf_op jit(solution)/shard_map/ppermute | solution.py:31
  46.8 0.8 %collective-permute-done.13 = bf16[1,3,48,256]{3,2,1,0:T(8,128)(2,1)S(1)} collective-permute-done((bf16[1,3,48,256]{3,2,1,0:T(8,128)(2,1)S(1)}, bf16[1,3,48,256]{3,2,1,0:T(8,128)(2,1)S(1)}, u32[]{:S(2)}, u32[]{:S(2)}) %collective-permute-start.13) | collective-permute-done | bytes 73760 | tf_op jit(solution)/shard_map/ppermute | solution.py:31
  47.6 0.7 %fusion.5 = bf16[3,48,256]{2,1,0:T(8,128)(2,1)} fusion(bf16[1,3,48,256]{3,2,1,0:T(8,128)(2,1)S(1)} %collective-permute-done.13, f32[1,2,3,48,256]{4,3,2,1,0:T(8,128)S(1)} %add_bitcast_fusion), kind=kLoop, calls=%fused_computation.14 | loop fusion | flops 110592 | bytes 294912 | tf_op jit(solution)/shard_map/convert_element_type | solution.py:220
  48.3 0.9 %shard_map.70 = f32[768,256]{1,0:T(8,128)} custom-call(bf16[4,96,256]{2,1,0:T(8,128)(2,1)S(1)} %pad_maximum_fusion.here_ref, bf16[4,96,256]{2,1,0:T(8,128)(2,1)S(1)} %collective-permute-done.20.there_ref), custom_call_target="tpu_custom_call" | custom-call | tf_op jit(solution)/shard_map/pallas_call | solution.py:240
  (33 shorter events, 0.9 us)
Async XLA Ops:
  0.6 8.1 %collective-permute-start.3 = (bf16[3,48,256]{2,1,0:T(8,128)(2,1)}, bf16[3,48,256]{2,1,0:T(8,128)(2,1)S(1)}, u32[]{:S(2)}, u32[]{:S(2)}) collective-permute-start(bf16[3,48,256]{2,1,0:T(8,128)(2,1)} %saved_ref.1), channel_id=1, source_target_pairs={{0,24},{4,28},{8,16},{12,20},{16,8},{20,12},{24,0},{28,4},{1,25},{... | collective-permute-start | bytes 221192 | tf_op jit(solution)/shard_map/ppermute | solution.py:31
  5.7 6.4 %collective-permute-start.4 = (bf16[3,48,256]{2,1,0:T(8,128)(2,1)}, bf16[3,48,256]{2,1,0:T(8,128)(2,1)S(1)}, u32[]{:S(2)}, u32[]{:S(2)}) collective-permute-start(bf16[3,48,256]{2,1,0:T(8,128)(2,1)} %saved_ref.1), channel_id=1, source_target_pairs={{0,16},{4,20},{8,24},{12,28},{16,0},{20,4},{24,8},{28,12},{1,17},{... | collective-permute-start | bytes 221192 | tf_op jit(solution)/shard_map/ppermute | solution.py:31
  5.7 10.4 %collective-permute-start.1 = (bf16[3,48,256]{2,1,0:T(8,128)(2,1)}, bf16[3,48,256]{2,1,0:T(8,128)(2,1)S(1)}, u32[]{:S(2)}, u32[]{:S(2)}) collective-permute-start(bf16[3,48,256]{2,1,0:T(8,128)(2,1)} %saved_ref.1), channel_id=1, source_target_pairs={{0,8},{4,12},{8,0},{12,4},{16,24},{20,28},{24,16},{28,20},{1,9},{5... | collective-permute-start | bytes 221192 | tf_op jit(solution)/shard_map/ppermute | solution.py:31
  6.4 6.7 %collective-permute-start = (bf16[3,48,256]{2,1,0:T(8,128)(2,1)}, bf16[3,48,256]{2,1,0:T(8,128)(2,1)S(1)}, u32[]{:S(2)}, u32[]{:S(2)}) collective-permute-start(bf16[3,48,256]{2,1,0:T(8,128)(2,1)} %saved_ref.1), channel_id=1, source_target_pairs={{0,4},{4,0},{8,12},{12,8},{16,20},{20,16},{24,28},{28,24},{1,5},{5... | collective-permute-start | bytes 221192 | tf_op jit(solution)/shard_map/ppermute | solution.py:31
  8.0 4.2 %collective-permute-start.6 = (bf16[1,3,48,256]{3,2,1,0:T(8,128)(2,1)}, bf16[1,3,48,256]{3,2,1,0:T(8,128)(2,1)S(1)}, u32[]{:S(2)}, u32[]{:S(2)}) collective-permute-start(bf16[1,3,48,256]{3,2,1,0:T(8,128)(2,1)} %bitcast.41), channel_id=1, source_target_pairs={{0,1},{1,0},{2,3},{3,2},{4,5},{5,4},{6,7},{7,6},{8,9},{9,8},{10,11... | collective-permute-start | bytes 221192 | tf_op jit(solution)/shard_map/ppermute | solution.py:31
  12.2 0.9 %copy-start.2 = (bf16[3,48,256]{2,1,0:T(8,128)(2,1)S(1)}, bf16[3,48,256]{2,1,0:T(8,128)(2,1)}, u32[]{:S(2)}) copy-start(bf16[3,48,256]{2,1,0:T(8,128)(2,1)} %saved_ref.1) | copy-start | bytes 221188
  12.2 4.5 %copy-start.3 = (bf16[192,384]{1,0:T(8,128)(2,1)S(1)}, bf16[192,384]{1,0:T(8,128)(2,1)}, u32[]{:S(2)}) copy-start(bf16[192,384]{1,0:T(8,128)(2,1)} %cot_ref.1) | copy-start | bytes 442372
  12.2 4.5 %copy-start.4 = (bf16[3,48,256]{2,1,0:T(8,128)(2,1)S(1)}, bf16[3,48,256]{2,1,0:T(8,128)(2,1)}, u32[]{:S(2)}) copy-start(bf16[3,48,256]{2,1,0:T(8,128)(2,1)} %upstream_ref.1) | copy-start | bytes 221188
  13.1 8.3 %collective-permute-start.7 = (bf16[2,3,48,256]{3,2,1,0:T(8,128)(2,1)S(1)}, bf16[2,3,48,256]{3,2,1,0:T(8,128)(2,1)S(1)}, u32[]{:S(2)}, u32[]{:S(2)}) collective-permute-start(bf16[2,3,48,256]{3,2,1,0:T(8,128)(2,1)S(1)} %pad_maximum_fusion.2), channel_id=1, source_target_pairs={{0,2},{1,3},{2,0},{3,1},{4,6},{5,7},{6,4},{7,5},{8,10},{9,11},{10,... | collective-permute-start | bytes 442376 | tf_op jit(solution)/shard_map/ppermute | solution.py:31
  14.7 6.7 %collective-permute-start.5 = (bf16[2,3,48,256]{3,2,1,0:T(8,128)(2,1)S(1)}, bf16[2,3,48,256]{3,2,1,0:T(8,128)(2,1)S(1)}, u32[]{:S(2)}, u32[]{:S(2)}) collective-permute-start(bf16[2,3,48,256]{3,2,1,0:T(8,128)(2,1)S(1)} %pad_maximum_fusion.1), channel_id=1, source_target_pairs={{0,4},{4,0},{8,12},{12,8},{16,20},{20,16},{24,28},{28,24},{1,5},{5... | collective-permute-start | bytes 442376 | tf_op jit(solution)/shard_map/ppermute | solution.py:31
  16.2 5.2 %collective-permute-start.2 = (bf16[1,3,48,256]{3,2,1,0:T(8,128)(2,1)S(1)}, bf16[1,3,48,256]{3,2,1,0:T(8,128)(2,1)S(1)}, u32[]{:S(2)}, u32[]{:S(2)}) collective-permute-start(bf16[1,3,48,256]{3,2,1,0:T(8,128)(2,1)S(1)} %bitcast.47), channel_id=1, source_target_pairs={{0,4},{4,0},{8,12},{12,8},{16,20},{20,16},{24,28},{28,24},{1,5},{5... | collective-permute-start | bytes 221192 | tf_op jit(solution)/shard_map/ppermute | solution.py:31
  16.7 1.1 %copy-start = (f32[3,256,256]{2,1,0:T(8,128)S(1)}, f32[3,256,256]{2,1,0:T(8,128)}, u32[]{:S(2)}) copy-start(f32[3,256,256]{2,1,0:T(8,128)} %solver_ref.1) | copy-start | bytes 2359300
  17.8 3.5 %copy-start.1 = (bf16[3,256,256]{2,1,0:T(8,128)(2,1)S(1)}, bf16[3,256,256]{2,1,0:T(8,128)(2,1)}, u32[]{:S(2)}) copy-start(bf16[3,256,256]{2,1,0:T(8,128)(2,1)} %refs_14_.1) | copy-start | bytes 1179652
  23.3 1.5 %collective-permute-start.8 = (bf16[4,96,256]{2,1,0:T(8,128)(2,1)S(1)}, bf16[4,96,256]{2,1,0:T(8,128)(2,1)S(1)}, u32[]{:S(2)}, u32[]{:S(2)}) collective-permute-start(bf16[4,96,256]{2,1,0:T(8,128)(2,1)S(1)} %get-tuple-element.25), channel_id=1, source_target_pairs={{0,1},{1,0},{2,3},{3,2},{4,5},{5,4},{6,7},{7,6},{8,9},{9,8},{10,11... | collective-permute-start | bytes 589832 | tf_op jit(solution)/shard_map/ppermute | solution.py:31
  24.9 5.3 %collective-permute-start.10 = (bf16[96,256]{1,0:T(8,128)(2,1)S(1)}, bf16[96,256]{1,0:T(8,128)(2,1)S(1)}, u32[]{:S(2)}, u32[]{:S(2)}) collective-permute-start(bf16[96,256]{1,0:T(8,128)(2,1)S(1)} %get-tuple-element.30), channel_id=1, source_target_pairs={{0,6},{1,7},{2,4},{3,5},{4,2},{5,3},{6,0},{7,1},{8,14},{9,15},{10,... | collective-permute-start | bytes 147464 | tf_op jit(solution)/shard_map/ppermute | solution.py:31
  26.4 4.1 %collective-permute-start.12 = (bf16[96,256]{1,0:T(8,128)(2,1)S(1)}, bf16[96,256]{1,0:T(8,128)(2,1)S(1)}, u32[]{:S(2)}, u32[]{:S(2)}) collective-permute-start(bf16[96,256]{1,0:T(8,128)(2,1)S(1)} %get-tuple-element.31), channel_id=1, source_target_pairs={{0,4},{1,5},{2,6},{3,7},{4,0},{5,1},{6,2},{7,3},{8,12},{9,13},{10,... | collective-permute-start | bytes 147464 | tf_op jit(solution)/shard_map/ppermute | solution.py:31
  26.8 4.1 %collective-permute-start.11 = (bf16[96,256]{1,0:T(8,128)(2,1)S(1)}, bf16[96,256]{1,0:T(8,128)(2,1)S(1)}, u32[]{:S(2)}, u32[]{:S(2)}) collective-permute-start(bf16[96,256]{1,0:T(8,128)(2,1)S(1)} %get-tuple-element.32), channel_id=1, source_target_pairs={{0,2},{1,3},{2,0},{3,1},{4,6},{5,7},{6,4},{7,5},{8,10},{9,11},{10,... | collective-permute-start | bytes 147464 | tf_op jit(solution)/shard_map/ppermute | solution.py:31
  30.9 5.3 %collective-permute-start.15 = (bf16[96,256]{1,0:T(8,128)(2,1)S(1)}, bf16[96,256]{1,0:T(8,128)(2,1)S(1)}, u32[]{:S(2)}, u32[]{:S(2)}) collective-permute-start(bf16[96,256]{1,0:T(8,128)(2,1)S(1)} %fusion.4), channel_id=1, source_target_pairs={{0,16},{4,20},{8,24},{12,28},{16,0},{20,4},{24,8},{28,12},{1,17},{... | collective-permute-start | bytes 147464 | tf_op jit(solution)/shard_map/ppermute | solution.py:31
  31.5 4.8 %collective-permute-start.14 = (bf16[96,256]{1,0:T(8,128)(2,1)S(1)}, bf16[96,256]{1,0:T(8,128)(2,1)S(1)}, u32[]{:S(2)}, u32[]{:S(2)}) collective-permute-start(bf16[96,256]{1,0:T(8,128)(2,1)S(1)} %fusion.4), channel_id=1, source_target_pairs={{0,8},{4,12},{8,0},{12,4},{16,24},{20,28},{24,16},{28,20},{1,9},{5... | collective-permute-start | bytes 147464 | tf_op jit(solution)/shard_map/ppermute | solution.py:31
  33.7 5.9 %collective-permute-start.16 = (bf16[96,256]{1,0:T(8,128)(2,1)S(1)}, bf16[96,256]{1,0:T(8,128)(2,1)S(1)}, u32[]{:S(2)}, u32[]{:S(2)}) collective-permute-start(bf16[96,256]{1,0:T(8,128)(2,1)S(1)} %fusion.4), channel_id=1, source_target_pairs={{0,24},{4,28},{8,16},{12,20},{16,8},{20,12},{24,0},{28,4},{1,25},{... | collective-permute-start | bytes 147464 | tf_op jit(solution)/shard_map/ppermute | solution.py:31
  35.4 7.7 %collective-permute-start.9 = (bf16[2,3,48,256]{3,2,1,0:T(8,128)(2,1)S(1)}, bf16[2,3,48,256]{3,2,1,0:T(8,128)(2,1)S(1)}, u32[]{:S(2)}, u32[]{:S(2)}) collective-permute-start(bf16[2,3,48,256]{3,2,1,0:T(8,128)(2,1)S(1)} %get-tuple-element.26), channel_id=1, source_target_pairs={{0,1},{1,0},{2,3},{3,2},{4,5},{5,4},{6,7},{7,6},{8,9},{9,8},{10,11... | collective-permute-start | bytes 442376 | tf_op jit(solution)/shard_map/ppermute | solution.py:31
  39.6 5.2 %collective-permute-start.19 = (bf16[96,256]{1,0:T(8,128)(2,1)S(1)}, bf16[96,256]{1,0:T(8,128)(2,1)S(1)}, u32[]{:S(2)}, u32[]{:S(2)}) collective-permute-start(bf16[96,256]{1,0:T(8,128)(2,1)S(1)} %add_convert_fusion), channel_id=1, source_target_pairs={{0,6},{1,7},{2,4},{3,5},{4,2},{5,3},{6,0},{7,1},{8,14},{9,15},{10,... | collective-permute-start | bytes 147464 | tf_op jit(solution)/shard_map/ppermute | solution.py:31
  42.1 4.1 %collective-permute-start.18 = (bf16[96,256]{1,0:T(8,128)(2,1)S(1)}, bf16[96,256]{1,0:T(8,128)(2,1)S(1)}, u32[]{:S(2)}, u32[]{:S(2)}) collective-permute-start(bf16[96,256]{1,0:T(8,128)(2,1)S(1)} %add_convert_fusion), channel_id=1, source_target_pairs={{0,2},{1,3},{2,0},{3,1},{4,6},{5,7},{6,4},{7,5},{8,10},{9,11},{10,... | collective-permute-start | bytes 147464 | tf_op jit(solution)/shard_map/ppermute | solution.py:31
  42.6 4.1 %collective-permute-start.17 = (bf16[96,256]{1,0:T(8,128)(2,1)S(1)}, bf16[96,256]{1,0:T(8,128)(2,1)S(1)}, u32[]{:S(2)}, u32[]{:S(2)}) collective-permute-start(bf16[96,256]{1,0:T(8,128)(2,1)S(1)} %add_convert_fusion), channel_id=1, source_target_pairs={{0,4},{1,5},{2,6},{3,7},{4,0},{5,1},{6,2},{7,3},{8,12},{9,13},{10,... | collective-permute-start | bytes 147464 | tf_op jit(solution)/shard_map/ppermute | solution.py:31
  43.2 4.4 %collective-permute-start.13 = (bf16[1,3,48,256]{3,2,1,0:T(8,128)(2,1)S(1)}, bf16[1,3,48,256]{3,2,1,0:T(8,128)(2,1)S(1)}, u32[]{:S(2)}, u32[]{:S(2)}) collective-permute-start(bf16[1,3,48,256]{3,2,1,0:T(8,128)(2,1)S(1)} %fusion.6), channel_id=1, source_target_pairs={{0,2},{1,3},{2,0},{3,1},{4,6},{5,7},{6,4},{7,5},{8,10},{9,11},{10,... | collective-permute-start | bytes 221192 | tf_op jit(solution)/shard_map/ppermute | solution.py:31
  46.7 1.5 %collective-permute-start.20 = (bf16[4,96,256]{2,1,0:T(8,128)(2,1)S(1)}, bf16[4,96,256]{2,1,0:T(8,128)(2,1)S(1)}, u32[]{:S(2)}, u32[]{:S(2)}) collective-permute-start(bf16[4,96,256]{2,1,0:T(8,128)(2,1)S(1)} %pad_maximum_fusion.here_ref), channel_id=1, source_target_pairs={{0,1},{1,0},{2,3},{3,2},{4,5},{5,4},{6,7},{7,6},{8,9},{9,8},{10,11... | collective-permute-start | bytes 589832 | tf_op jit(solution)/shard_map/ppermute | solution.py:31

commit v3 on v2

--- a/solution.py
+++ b/solution.py
@@ -44,13 +44,20 @@
     return lax.dot_general(left, right, (((0,), (0,)), ((), ())), preferred_element_type=F32)
 
 
-def prepare_kernel(cot_ref, saved_ref, upstream_ref, solver_ref, cot_out, saved_out, upstream_out, high_out, low_out):
-    cot_out[...] = cot_ref[...]
-    saved_out[...] = saved_ref[...]
-    upstream_out[...] = upstream_ref[...]
-    high, low = split(solver_ref[...])
+def prepare_kernel(*refs):
+    sources, outs, (high_out, low_out, solver, sems) = refs[:5], refs[5:9], refs[9:]
+    copies = [
+        pltpu.make_async_copy(source, target, sems.at[index])
+        for index, (source, target) in enumerate(zip(sources, (solver, *outs)))
+    ]
+    for copy in copies:
+        copy.start()
+    copies[0].wait()
+    high, low = split(solver[...])
     high_out[...] = high
     low_out[...] = low
+    for copy in copies[1:]:
+        copy.wait()
 
 
 def main_kernel(along_row, along_col, *refs):
@@ -146,42 +153,40 @@
     limit = pltpu.CompilerParams(vmem_limit_bytes=32 * 1024 * 1024)
     tile_shape = jax.ShapeDtypeStruct(saved_panels.shape, BF16)
 
-    far = {bits: swap(saved_panels, ("row",), sizes, {"row": bits}) for bits in range(rows - 2, 0, -2)}
-    near = {1: swap(saved_panels, ("row",), sizes, {"row": 1})}
+    near = [bits for bits in (1, 2, 3) if bits < rows]
+    along_row, row_tiles = [(0,)], [None]
+    far = [bits for bits in range(4, rows, 4)]
+    crossed = [swap(saved_panels, ("row",), sizes, {"row": bits}) for bits in far]
+    nearby = {bits: swap(saved_panels, ("row",), sizes, {"row": bits}) for bits in near}
     along_col = [(0,)]
-    col_tiles = [saved_panels]
-    for power in range(cols.bit_length() - 1):
-        have = [bits for group in along_col for bits in group]
-        sent = jnp.concatenate([tile.reshape(-1, panels, height, width) for tile in col_tiles])
-        along_col.append(tuple(bits ^ (1 << power) for bits in have))
-        col_tiles.append(swap(sent, ("col",), sizes, {"col": 1 << power}))
-
-    groups = [[2], [bits for bits in far if bits != 2]]
-    along_row = [(0,), (1,)]
-    row_tiles = [None, near[1][None]]
-    for group in groups:
-        if not group or group[0] not in far:
-            continue
-        sent = after(jnp.stack([far[bits] for bits in group]), near[1])
-        for bits in group:
-            along_row.append((bits,))
-            row_tiles.append(far[bits][None])
-        along_row.append(tuple(bits ^ 1 for bits in group))
-        row_tiles.append(swap(sent, ("row",), sizes, {"row": 1}))
-
-    cot, saved, upstream_here, high, low = pl.pallas_call(
+    col_tiles = [None]
+    for power in list(range(1, cols.bit_length() - 1)) + [0]:
+        held = [(bits, tile) for (bits,), tile in zip(along_col, col_tiles)]
+        for bits, tile in held:
+            along_col.append((bits ^ (1 << power),))
+            sent = saved_panels if tile is None else tile[0]
+            col_tiles.append(swap(sent, ("col",), sizes, {"col": 1 << power})[None])
+    for bits in near:
+        along_row.append((bits,))
+        row_tiles.append(nearby[bits][None])
+    if far:
+        sent = jnp.stack(crossed)
+        along_row.append(tuple(far))
+        row_tiles.append(sent)
+        for bits in near:
+            along_row.append(tuple(other ^ bits for other in far))
+            row_tiles.append(swap(sent, ("row",), sizes, {"row": bits}))
+
+    arguments = (inverse_diag, cotangent, saved_panels, upstream, panel_tops)
+    halves = [jax.ShapeDtypeStruct(inverse_diag.shape, BF16)] * 2
+    cot, saved, upstream_here, tops, high, low = pl.pallas_call(
         prepare_kernel,
-        out_shape=[
-            jax.ShapeDtypeStruct(cotangent.shape, BF16),
-            tile_shape,
-            tile_shape,
-            jax.ShapeDtypeStruct(inverse_diag.shape, BF16),
-            jax.ShapeDtypeStruct(inverse_diag.shape, BF16),
-        ],
-        in_specs=[VMEM] * 4,
-        out_specs=[VMEM] * 5,
+        out_shape=[jax.ShapeDtypeStruct(value.shape, BF16) for value in arguments[1:]] + halves,
+        in_specs=[pl.BlockSpec(memory_space=pl.ANY)] * 5,
+        out_specs=[VMEM] * 6,
+        scratch_shapes=[pltpu.VMEM(inverse_diag.shape, F32), pltpu.SemaphoreType.DMA((5,))],
         compiler_params=limit,
-    )(cotangent, saved_panels, upstream, inverse_diag)
+    )(*[pltpu.with_memory_space_constraint(value, pltpu.HBM) for value in arguments])
     row_tiles[0] = saved[None]
     col_tiles[0] = saved[None]
 
@@ -203,7 +208,7 @@
             pltpu.VMEM((panels * width, width), F32),
         ],
         compiler_params=limit,
-    )(*row_tiles, *col_tiles, cot, upstream_here, high, low, panel_tops)
+    )(*row_tiles, *col_tiles, cot, upstream_here, high, low, tops)
 
     both = ("row", "col")
     half = keep + swap(send, ("col",), sizes, {"col": 1}).astype(F32)
@@ -211,31 +216,31 @@
     total = half[0]
     for bits in range(3, 0, -1):
         total = total + swap(half[bits].astype(BF16), both, sizes, spots[bits]).astype(F32)
-    columns = columns_keep + swap(after(columns_send, half), ("col",), sizes, {"col": 1}).astype(F32)
-    held = total
+    arrived = swap(after(columns_send, half), ("col",), sizes, {"col": 1})
+    columns = columns_keep + arrived.astype(F32)
+    mine = after(total.astype(BF16), arrived)
     for power in range(1, cols.bit_length() - 1):
         halves = columns.reshape(-1, 2, panels, height, width)
-        sent = after(halves[:, 1].astype(BF16), held)
-        columns = halves[:, 0] + swap(sent, ("col",), sizes, {"col": 1 << power}).astype(F32)
+        arrived = swap(after(halves[:, 1].astype(BF16), mine), ("col",), sizes, {"col": 1 << power})
+        columns = halves[:, 0] + arrived.astype(F32)
     columns = columns[0].astype(BF16)
 
     others = [{"row": 1 << power} for power in range(1, rows.bit_length() - 1)]
     others += [{"col": 1 << power} for power in range(2, cols.bit_length() - 1)]
     if len(others) == 2 and "col" not in others[1]:
-        mine = total.astype(BF16)
         first, second = others[0]["row"], others[1]["row"]
-        from_both, from_second, from_first = [
-            swap(mine, ("row",), sizes, {"row": bits}) for bits in (first ^ second, second, first)
+        from_first, from_second, from_both = [
+            swap(mine, ("row",), sizes, {"row": bits}) for bits in (first, second, first ^ second)
         ]
         total = (mine.astype(F32) + from_first.astype(F32)) + (
             from_second.astype(F32) + from_both.astype(F32)
         )
     else:
         for bits in others:
+            total = mine.astype(F32) + swap(mine, tuple(bits), sizes, bits).astype(F32)
             mine = total.astype(BF16)
-            total = mine.astype(F32) + swap(mine, tuple(bits), sizes, bits).astype(F32)
-    mine = total.astype(BF16)
-    here = jnp.stack([mine] + [swap(mine, both, sizes, spots[bits]) for bits in range(3, 0, -1)][::-1])
+    mine = after(total.astype(BF16), arrived)
+    here = jnp.stack([mine] + [swap(mine, both, sizes, spots[bits]) for bits in range(1, 4)])
     there = swap(here, ("col",), sizes, {"col": 1})
     diag_cot = pl.pallas_call(
         finish_kernel,

time: 49.4 us -> 46.8 us (0.947)
  waiting for transfers between devices: 18.3 us -> 15.9 us
  local copies, waits for them, and re-layouts: 2 us -> 0.02 us
  Pallas kernels: 3.05 us -> 4.24 us
  starting transfers between devices: 24.3 us -> 24.9 us
    ppermute x21 -> x23, waiting for transfers between devices: 18.3 us -> 15.9 us  [swap(): return lax.ppermute(value, axes, pairs)]
    unnamed x10 -> x0, local copies, waits for them, and re-layouts: 1.98 us -> none
    pallas_call x1, Pallas kernels: 0.16 us -> 1.37 us  [body(): pl.pallas_call(prepare_kernel, out_shape=[jax.ShapeDtypeStruct(value.shap...]
    ppermute x21 -> x23, starting transfers between devices: 24.3 us -> 24.9 us  [swap(): return lax.ppermute(value, axes, pairs)]
  transfers between devices with their start and end apart: 21 -> 23, of which waited for: 12 -> 15; matrix products, arithmetic and copies ran while one was open for 2% -> 2% of each run, Pallas kernels for 0% -> 3%
where the time goes in v3:
time: 46.8 us; the launch traced here: 46.7 us
  starting transfers between devices  24.9 us (53%)
  waiting for transfers between devices  15.9 us (34%)
  Pallas kernels  4.24 us (9%)
  other arithmetic  0.82 us (2%)
  between operations  0.74 us (2%)
    ppermute x23, starting transfers between devices, swap(): return lax.ppermute(value, axes, pairs)  24.9 us
    ppermute x23, waiting for transfers between devices, swap(): return lax.ppermute(value, axes, pairs)  15.9 us
    pallas_call x1, Pallas kernels, body(): pl.pallas_call(functools.partial(main_kernel, along_row, along_col), out_...  1.93 us
    pallas_call x1, Pallas kernels, body(): pl.pallas_call(prepare_kernel, out_shape=[jax.ShapeDtypeStruct(value.shap...  1.37 us
    pallas_call x1, Pallas kernels, body(): pl.pallas_call(finish_kernel, out_shape=jax.ShapeDtypeStruct((panels * wi...  0.94 us
  transfers between devices with their start and end apart: 23, of which 15 were waited for; matrix products, arithmetic and copies ran while one was open for 2% of the time, Pallas kernels for 3%

profile of v3, /device:TPU:0, one launch (start us, length us, event | category | flops | bytes accessed | tf_op | source)
XLA Modules:
  0.0 46.7 jit_solution(7820844439495774582)
XLA Ops:
  0.6 4.1 %collective-permute-start.3 = (bf16[3,48,256]{2,1,0:T(8,128)(2,1)}, bf16[3,48,256]{2,1,0:T(8,128)(2,1)S(1)}, u32[]{:S(2)}, u32[]{:S(2)}) collective-permute-start(bf16[3,48,256]{2,1,0:T(8,128)(2,1)} %refs_2_.1), channel_id=1, source_target_pairs={{0,16},{4,20},{8,24},{12,28},{16,0},{20,4},{24,8},{28,12},{1,17},{... | collective-permute-start | bytes 221192 | tf_op jit(solution)/shard_map/ppermute | solution.py:31
  4.7 2.5 %collective-permute-start.2 = (bf16[3,48,256]{2,1,0:T(8,128)(2,1)}, bf16[3,48,256]{2,1,0:T(8,128)(2,1)S(1)}, u32[]{:S(2)}, u32[]{:S(2)}) collective-permute-start(bf16[3,48,256]{2,1,0:T(8,128)(2,1)} %refs_2_.1), channel_id=1, source_target_pairs={{0,12},{4,8},{8,4},{12,0},{16,28},{20,24},{24,20},{28,16},{1,13},{... | collective-permute-start | bytes 221192 | tf_op jit(solution)/shard_map/ppermute | solution.py:31
  8.2 1.5 %collective-permute-start.7 = (bf16[3,48,256]{2,1,0:T(8,128)(2,1)}, bf16[3,48,256]{2,1,0:T(8,128)(2,1)S(1)}, u32[]{:S(2)}, u32[]{:S(2)}) collective-permute-start(bf16[3,48,256]{2,1,0:T(8,128)(2,1)} %refs_2_.1), channel_id=1, source_target_pairs={{0,2},{1,3},{2,0},{3,1},{4,6},{5,7},{6,4},{7,5},{8,10},{9,11},{10,... | collective-permute-start | bytes 221192 | tf_op jit(solution)/shard_map/ppermute | solution.py:31
  9.7 1.4 %collective-permute-done.2 = bf16[3,48,256]{2,1,0:T(8,128)(2,1)S(1)} collective-permute-done((bf16[3,48,256]{2,1,0:T(8,128)(2,1)}, bf16[3,48,256]{2,1,0:T(8,128)(2,1)S(1)}, u32[]{:S(2)}, u32[]{:S(2)}) %collective-permute-start.2) | collective-permute-done | bytes 73760 | tf_op jit(solution)/shard_map/ppermute | solution.py:31
  11.1 1.7 %collective-permute-start.6 = (bf16[1,3,48,256]{3,2,1,0:T(8,128)(2,1)S(1)}, bf16[1,3,48,256]{3,2,1,0:T(8,128)(2,1)S(1)}, u32[]{:S(2)}, u32[]{:S(2)}) collective-permute-start(bf16[1,3,48,256]{3,2,1,0:T(8,128)(2,1)S(1)} %bitcast.45), channel_id=1, source_target_pairs={{0,12},{4,8},{8,4},{12,0},{16,28},{20,24},{24,20},{28,16},{1,13},{... | collective-permute-start | bytes 221192 | tf_op jit(solution)/shard_map/ppermute | solution.py:31
  12.9 1.1 %collective-permute-start.5 = (bf16[1,3,48,256]{3,2,1,0:T(8,128)(2,1)S(1)}, bf16[1,3,48,256]{3,2,1,0:T(8,128)(2,1)S(1)}, u32[]{:S(2)}, u32[]{:S(2)}) collective-permute-start(bf16[1,3,48,256]{3,2,1,0:T(8,128)(2,1)S(1)} %bitcast.46), channel_id=1, source_target_pairs={{0,8},{4,12},{8,0},{12,4},{16,24},{20,28},{24,16},{28,20},{1,9},{5... | collective-permute-start | bytes 221192 | tf_op jit(solution)/shard_map/ppermute | solution.py:31
  13.9 0.7 %collective-permute-start.4 = (bf16[1,3,48,256]{3,2,1,0:T(8,128)(2,1)S(1)}, bf16[1,3,48,256]{3,2,1,0:T(8,128)(2,1)S(1)}, u32[]{:S(2)}, u32[]{:S(2)}) collective-permute-start(bf16[1,3,48,256]{3,2,1,0:T(8,128)(2,1)S(1)} %bitcast.47), channel_id=1, source_target_pairs={{0,4},{4,0},{8,12},{12,8},{16,20},{20,16},{24,28},{28,24},{1,5},{5... | collective-permute-start | bytes 221192 | tf_op jit(solution)/shard_map/ppermute | solution.py:31
  14.6 1.4 %shard_map.68 = (bf16[192,384]{1,0:T(8,128)(2,1)S(1)}, bf16[3,48,256]{2,1,0:T(8,128)(2,1)S(1)}, bf16[3,48,256]{2,1,0:T(8,128)(2,1)S(1)}, bf16[3,256,256]{2,1,0:T...) custom-call(f32[3,256,256]{2,1,0:T(8,128)} %refs_0_.1, bf16[192,384]{1,0:T(8,128)(2,1)} %refs_1_.1, ...), custom_call_target="tpu_custom_call" | custom-call | tf_op jit(solution)/shard_map/pallas_call | solution.py:182
  16.0 0.7 %collective-permute-done.6.refs_7_ = bf16[1,3,48,256]{3,2,1,0:T(8,128)(2,1)S(1)} collective-permute-done((bf16[1,3,48,256]{3,2,1,0:T(8,128)(2,1)S(1)}, bf16[1,3,48,256]{3,2,1,0:T(8,128)(2,1)S(1)}, u32[]{:S(2)}, u32[]{:S(2)}) %collective-permute-start.6) | collective-permute-done | bytes 73760 | tf_op jit(solution)/shard_map/ppermute | solution.py:31
  16.7 0.8 %collective-permute-done.5.refs_6_ = bf16[1,3,48,256]{3,2,1,0:T(8,128)(2,1)S(1)} collective-permute-done((bf16[1,3,48,256]{3,2,1,0:T(8,128)(2,1)S(1)}, bf16[1,3,48,256]{3,2,1,0:T(8,128)(2,1)S(1)}, u32[]{:S(2)}, u32[]{:S(2)}) %collective-permute-start.5) | collective-permute-done | bytes 73760 | tf_op jit(solution)/shard_map/ppermute | solution.py:31
  17.5 0.8 %collective-permute-done.4.refs_5_ = bf16[1,3,48,256]{3,2,1,0:T(8,128)(2,1)S(1)} collective-permute-done((bf16[1,3,48,256]{3,2,1,0:T(8,128)(2,1)S(1)}, bf16[1,3,48,256]{3,2,1,0:T(8,128)(2,1)S(1)}, u32[]{:S(2)}, u32[]{:S(2)}) %collective-permute-start.4) | collective-permute-done | bytes 73760 | tf_op jit(solution)/shard_map/ppermute | solution.py:31
  18.3 1.9 %shard_map.69 = (f32[2,3,48,256]{3,2,1,0:T(8,128)S(1)}, bf16[2,3,48,256]{3,2,1,0:T(8,128)(2,1)S(1)}, f32[4,96,256]{2,1,0:T(8,128)S(1)}, bf16[4,96,256]{2,1,0:T(8,128)(2,1)S(1)}) custom-call(bf16[1,3,48,256]{3,2,1,0:T(8,128)(2,1)S(1)} %bitcast.43, bf16[1,3,48,256]{3,2,1,0:T(8,128)(2,1)S(1)} %bitcast.51, bf16[1,3,48,256]{3,2,1,0:T(8,128)(2,1)S(1)} %bitcast.50, ...), custom_call_target="tpu_custom_call" | custom-call | tf_op jit(solution)/shard_map/pallas_call | solution.py:194
  20.3 1.4 %collective-permute-done.10 = bf16[4,96,256]{2,1,0:T(8,128)(2,1)S(1)} collective-permute-done((bf16[4,96,256]{2,1,0:T(8,128)(2,1)S(1)}, bf16[4,96,256]{2,1,0:T(8,128)(2,1)S(1)}, u32[]{:S(2)}, u32[]{:S(2)}) %collective-permute-start.10) | collective-permute-done | bytes 196640 | tf_op jit(solution)/shard_map/ppermute | solution.py:31
  21.8 1.7 %collective-permute-start.12 = (bf16[96,256]{1,0:T(8,128)(2,1)S(1)}, bf16[96,256]{1,0:T(8,128)(2,1)S(1)}, u32[]{:S(2)}, u32[]{:S(2)}) collective-permute-start(bf16[96,256]{1,0:T(8,128)(2,1)S(1)} %get-tuple-element.32), channel_id=1, source_target_pairs={{0,6},{1,7},{2,4},{3,5},{4,2},{5,3},{6,0},{7,1},{8,14},{9,15},{10,... | collective-permute-start | bytes 147464 | tf_op jit(solution)/shard_map/ppermute | solution.py:31
  23.5 1.2 %collective-permute-start.14 = (bf16[96,256]{1,0:T(8,128)(2,1)S(1)}, bf16[96,256]{1,0:T(8,128)(2,1)S(1)}, u32[]{:S(2)}, u32[]{:S(2)}) collective-permute-start(bf16[96,256]{1,0:T(8,128)(2,1)S(1)} %get-tuple-element.33), channel_id=1, source_target_pairs={{0,4},{1,5},{2,6},{3,7},{4,0},{5,1},{6,2},{7,3},{8,12},{9,13},{10,... | collective-permute-start | bytes 147464 | tf_op jit(solution)/shard_map/ppermute | solution.py:31
  24.8 0.6 %collective-permute-start.13 = (bf16[96,256]{1,0:T(8,128)(2,1)S(1)}, bf16[96,256]{1,0:T(8,128)(2,1)S(1)}, u32[]{:S(2)}, u32[]{:S(2)}) collective-permute-start(bf16[96,256]{1,0:T(8,128)(2,1)S(1)} %get-tuple-element.34), channel_id=1, source_target_pairs={{0,2},{1,3},{2,0},{3,1},{4,6},{5,7},{6,4},{7,5},{8,10},{9,11},{10,... | collective-permute-start | bytes 147464 | tf_op jit(solution)/shard_map/ppermute | solution.py:31
  25.4 1.7 %collective-permute-done.12 = bf16[96,256]{1,0:T(8,128)(2,1)S(1)} collective-permute-done((bf16[96,256]{1,0:T(8,128)(2,1)S(1)}, bf16[96,256]{1,0:T(8,128)(2,1)S(1)}, u32[]{:S(2)}, u32[]{:S(2)}) %collective-permute-start.12) | collective-permute-done | bytes 49184 | tf_op jit(solution)/shard_map/ppermute | solution.py:31
  27.6 1.2 %collective-permute-done.13 = bf16[96,256]{1,0:T(8,128)(2,1)S(1)} collective-permute-done((bf16[96,256]{1,0:T(8,128)(2,1)S(1)}, bf16[96,256]{1,0:T(8,128)(2,1)S(1)}, u32[]{:S(2)}, u32[]{:S(2)}) %collective-permute-start.13) | collective-permute-done | bytes 49184 | tf_op jit(solution)/shard_map/ppermute | solution.py:31
  28.9 2.5 %collective-permute-start.18 = (bf16[96,256]{1,0:T(8,128)(2,1)S(1)}, bf16[96,256]{1,0:T(8,128)(2,1)S(1)}, u32[]{:S(2)}, u32[]{:S(2)}) collective-permute-start(bf16[96,256]{1,0:T(8,128)(2,1)S(1)} %fusion.5), channel_id=1, source_target_pairs={{0,24},{4,28},{8,16},{12,20},{16,8},{20,12},{24,0},{28,4},{1,25},{... | collective-permute-start | bytes 147464 | tf_op jit(solution)/shard_map/ppermute | solution.py:31
  31.5 1.9 %collective-permute-start.16 = (bf16[96,256]{1,0:T(8,128)(2,1)S(1)}, bf16[96,256]{1,0:T(8,128)(2,1)S(1)}, u32[]{:S(2)}, u32[]{:S(2)}) collective-permute-start(bf16[96,256]{1,0:T(8,128)(2,1)S(1)} %fusion.5), channel_id=1, source_target_pairs={{0,8},{4,12},{8,0},{12,4},{16,24},{20,28},{24,16},{28,20},{1,9},{5... | collective-permute-start | bytes 147464 | tf_op jit(solution)/shard_map/ppermute | solution.py:31
  33.4 0.7 %collective-permute-start.15 = (bf16[1,3,48,256]{3,2,1,0:T(8,128)(2,1)S(1)}, bf16[1,3,48,256]{3,2,1,0:T(8,128)(2,1)S(1)}, u32[]{:S(2)}, u32[]{:S(2)}) collective-permute-start(bf16[1,3,48,256]{3,2,1,0:T(8,128)(2,1)S(1)} %fusion.7), channel_id=1, source_target_pairs={{0,2},{1,3},{2,0},{3,1},{4,6},{5,7},{6,4},{7,5},{8,10},{9,11},{10,... | collective-permute-start | bytes 221192 | tf_op jit(solution)/shard_map/ppermute | solution.py:31
  34.1 1.1 %collective-permute-done.18 = bf16[96,256]{1,0:T(8,128)(2,1)S(1)} collective-permute-done((bf16[96,256]{1,0:T(8,128)(2,1)S(1)}, bf16[96,256]{1,0:T(8,128)(2,1)S(1)}, u32[]{:S(2)}, u32[]{:S(2)}) %collective-permute-start.18) | collective-permute-done | bytes 49184 | tf_op jit(solution)/shard_map/ppermute | solution.py:31
  35.1 1.3 %collective-permute-done.17 = bf16[96,256]{1,0:T(8,128)(2,1)S(1)} collective-permute-done((bf16[96,256]{1,0:T(8,128)(2,1)S(1)}, bf16[96,256]{1,0:T(8,128)(2,1)S(1)}, u32[]{:S(2)}, u32[]{:S(2)}) %collective-permute-start.17) | collective-permute-done | bytes 49184 | tf_op jit(solution)/shard_map/ppermute | solution.py:31
  36.5 1.4 %collective-permute-done.15 = bf16[1,3,48,256]{3,2,1,0:T(8,128)(2,1)S(1)} collective-permute-done((bf16[1,3,48,256]{3,2,1,0:T(8,128)(2,1)S(1)}, bf16[1,3,48,256]{3,2,1,0:T(8,128)(2,1)S(1)}, u32[]{:S(2)}, u32[]{:S(2)}) %collective-permute-start.15) | collective-permute-done | bytes 73760 | tf_op jit(solution)/shard_map/ppermute | solution.py:31
  37.8 0.7 %collective-permute-start.21 = (bf16[96,256]{1,0:T(8,128)(2,1)S(1)}, bf16[96,256]{1,0:T(8,128)(2,1)S(1)}, u32[]{:S(2)}, u32[]{:S(2)}) collective-permute-start(bf16[96,256]{1,0:T(8,128)(2,1)S(1)} %add_convert_fusion), channel_id=1, source_target_pairs={{0,6},{1,7},{2,4},{3,5},{4,2},{5,3},{6,0},{7,1},{8,14},{9,15},{10,... | collective-permute-start | bytes 147464 | tf_op jit(solution)/shard_map/ppermute | solution.py:31
  38.6 1.5 %collective-permute-start.20 = (bf16[96,256]{1,0:T(8,128)(2,1)S(1)}, bf16[96,256]{1,0:T(8,128)(2,1)S(1)}, u32[]{:S(2)}, u32[]{:S(2)}) collective-permute-start(bf16[96,256]{1,0:T(8,128)(2,1)S(1)} %add_convert_fusion), channel_id=1, source_target_pairs={{0,2},{1,3},{2,0},{3,1},{4,6},{5,7},{6,4},{7,5},{8,10},{9,11},{10,... | collective-permute-start | bytes 147464 | tf_op jit(solution)/shard_map/ppermute | solution.py:31
  40.1 1.2 %collective-permute-start.19 = (bf16[96,256]{1,0:T(8,128)(2,1)S(1)}, bf16[96,256]{1,0:T(8,128)(2,1)S(1)}, u32[]{:S(2)}, u32[]{:S(2)}) collective-permute-start(bf16[96,256]{1,0:T(8,128)(2,1)S(1)} %add_convert_fusion), channel_id=1, source_target_pairs={{0,4},{1,5},{2,6},{3,7},{4,0},{5,1},{6,2},{7,3},{8,12},{9,13},{10,... | collective-permute-start | bytes 147464 | tf_op jit(solution)/shard_map/ppermute | solution.py:31
  41.3 1.6 %collective-permute-done.21 = bf16[96,256]{1,0:T(8,128)(2,1)S(1)} collective-permute-done((bf16[96,256]{1,0:T(8,128)(2,1)S(1)}, bf16[96,256]{1,0:T(8,128)(2,1)S(1)}, u32[]{:S(2)}, u32[]{:S(2)}) %collective-permute-start.21) | collective-permute-done | bytes 49184 | tf_op jit(solution)/shard_map/ppermute | solution.py:31
  43.2 1.0 %collective-permute-done.19 = bf16[96,256]{1,0:T(8,128)(2,1)S(1)} collective-permute-done((bf16[96,256]{1,0:T(8,128)(2,1)S(1)}, bf16[96,256]{1,0:T(8,128)(2,1)S(1)}, u32[]{:S(2)}, u32[]{:S(2)}) %collective-permute-start.19) | collective-permute-done | bytes 49184 | tf_op jit(solution)/shard_map/ppermute | solution.py:31
  44.3 0.6 %fusion.6 = bf16[3,48,256]{2,1,0:T(8,128)(2,1)} fusion(bf16[1,3,48,256]{3,2,1,0:T(8,128)(2,1)S(1)} %collective-permute-done.15, f32[1,2,3,48,256]{4,3,2,1,0:T(8,128)S(1)} %add_bitcast_fusion), kind=kLoop, calls=%fused_computation.13 | loop fusion | flops 110592 | bytes 294912 | tf_op jit(solution)/shard_map/convert_element_type | solution.py:226
  44.9 0.8 %collective-permute-done.22.there_ref = bf16[4,96,256]{2,1,0:T(8,128)(2,1)S(1)} collective-permute-done((bf16[4,96,256]{2,1,0:T(8,128)(2,1)S(1)}, bf16[4,96,256]{2,1,0:T(8,128)(2,1)S(1)}, u32[]{:S(2)}, u32[]{:S(2)}) %collective-permute-start.22) | collective-permute-done | bytes 196640 | tf_op jit(solution)/shard_map/ppermute | solution.py:31
  45.7 0.9 %shard_map.70 = f32[768,256]{1,0:T(8,128)} custom-call(bf16[4,96,256]{2,1,0:T(8,128)(2,1)S(1)} %pad_maximum_fusion.here_ref, bf16[4,96,256]{2,1,0:T(8,128)(2,1)S(1)} %collective-permute-done.22.there_ref), custom_call_target="tpu_custom_call" | custom-call | tf_op jit(solution)/shard_map/pallas_call | solution.py:245
  (25 shorter events, 2.2 us)
Async XLA Ops:
  0.6 9.1 %collective-permute-start.3 = (bf16[3,48,256]{2,1,0:T(8,128)(2,1)}, bf16[3,48,256]{2,1,0:T(8,128)(2,1)S(1)}, u32[]{:S(2)}, u32[]{:S(2)}) collective-permute-start(bf16[3,48,256]{2,1,0:T(8,128)(2,1)} %refs_2_.1), channel_id=1, source_target_pairs={{0,16},{4,20},{8,24},{12,28},{16,0},{20,4},{24,8},{28,12},{1,17},{... | collective-permute-start | bytes 221192 | tf_op jit(solution)/shard_map/ppermute | solution.py:31
  4.7 6.4 %collective-permute-start.2 = (bf16[3,48,256]{2,1,0:T(8,128)(2,1)}, bf16[3,48,256]{2,1,0:T(8,128)(2,1)S(1)}, u32[]{:S(2)}, u32[]{:S(2)}) collective-permute-start(bf16[3,48,256]{2,1,0:T(8,128)(2,1)} %refs_2_.1), channel_id=1, source_target_pairs={{0,12},{4,8},{8,4},{12,0},{16,28},{20,24},{24,20},{28,16},{1,13},{... | collective-permute-start | bytes 221192 | tf_op jit(solution)/shard_map/ppermute | solution.py:31
  7.2 5.6 %collective-permute-start.1 = (bf16[3,48,256]{2,1,0:T(8,128)(2,1)}, bf16[3,48,256]{2,1,0:T(8,128)(2,1)S(1)}, u32[]{:S(2)}, u32[]{:S(2)}) collective-permute-start(bf16[3,48,256]{2,1,0:T(8,128)(2,1)} %refs_2_.1), channel_id=1, source_target_pairs={{0,8},{4,12},{8,0},{12,4},{16,24},{20,28},{24,16},{28,20},{1,9},{5... | collective-permute-start | bytes 221192 | tf_op jit(solution)/shard_map/ppermute | solution.py:31
  7.7 6.2 %collective-permute-start = (bf16[3,48,256]{2,1,0:T(8,128)(2,1)}, bf16[3,48,256]{2,1,0:T(8,128)(2,1)S(1)}, u32[]{:S(2)}, u32[]{:S(2)}) collective-permute-start(bf16[3,48,256]{2,1,0:T(8,128)(2,1)} %refs_2_.1), channel_id=1, source_target_pairs={{0,4},{4,0},{8,12},{12,8},{16,20},{20,16},{24,28},{28,24},{1,5},{5... | collective-permute-start | bytes 221192 | tf_op jit(solution)/shard_map/ppermute | solution.py:31
  8.2 6.4 %collective-permute-start.7 = (bf16[3,48,256]{2,1,0:T(8,128)(2,1)}, bf16[3,48,256]{2,1,0:T(8,128)(2,1)S(1)}, u32[]{:S(2)}, u32[]{:S(2)}) collective-permute-start(bf16[3,48,256]{2,1,0:T(8,128)(2,1)} %refs_2_.1), channel_id=1, source_target_pairs={{0,2},{1,3},{2,0},{3,1},{4,6},{5,7},{6,4},{7,5},{8,10},{9,11},{10,... | collective-permute-start | bytes 221192 | tf_op jit(solution)/shard_map/ppermute | solution.py:31
  9.7 6.3 %collective-permute-start.8 = (bf16[3,48,256]{2,1,0:T(8,128)(2,1)}, bf16[3,48,256]{2,1,0:T(8,128)(2,1)S(1)}, u32[]{:S(2)}, u32[]{:S(2)}) collective-permute-start(bf16[3,48,256]{2,1,0:T(8,128)(2,1)} %refs_2_.1), channel_id=1, source_target_pairs={{0,1},{1,0},{2,3},{3,2},{4,5},{5,4},{6,7},{7,6},{8,9},{9,8},{10,11... | collective-permute-start | bytes 221192 | tf_op jit(solution)/shard_map/ppermute | solution.py:31
  11.1 5.6 %collective-permute-start.6 = (bf16[1,3,48,256]{3,2,1,0:T(8,128)(2,1)S(1)}, bf16[1,3,48,256]{3,2,1,0:T(8,128)(2,1)S(1)}, u32[]{:S(2)}, u32[]{:S(2)}) collective-permute-start(bf16[1,3,48,256]{3,2,1,0:T(8,128)(2,1)S(1)} %bitcast.45), channel_id=1, source_target_pairs={{0,12},{4,8},{8,4},{12,0},{16,28},{20,24},{24,20},{28,16},{1,13},{... | collective-permute-start | bytes 221192 | tf_op jit(solution)/shard_map/ppermute | solution.py:31
  12.9 4.6 %collective-permute-start.5 = (bf16[1,3,48,256]{3,2,1,0:T(8,128)(2,1)S(1)}, bf16[1,3,48,256]{3,2,1,0:T(8,128)(2,1)S(1)}, u32[]{:S(2)}, u32[]{:S(2)}) collective-permute-start(bf16[1,3,48,256]{3,2,1,0:T(8,128)(2,1)S(1)} %bitcast.46), channel_id=1, source_target_pairs={{0,8},{4,12},{8,0},{12,4},{16,24},{20,28},{24,16},{28,20},{1,9},{5... | collective-permute-start | bytes 221192 | tf_op jit(solution)/shard_map/ppermute | solution.py:31
  13.9 4.4 %collective-permute-start.4 = (bf16[1,3,48,256]{3,2,1,0:T(8,128)(2,1)S(1)}, bf16[1,3,48,256]{3,2,1,0:T(8,128)(2,1)S(1)}, u32[]{:S(2)}, u32[]{:S(2)}) collective-permute-start(bf16[1,3,48,256]{3,2,1,0:T(8,128)(2,1)S(1)} %bitcast.47), channel_id=1, source_target_pairs={{0,4},{4,0},{8,12},{12,8},{16,20},{20,16},{24,28},{28,24},{1,5},{5... | collective-permute-start | bytes 221192 | tf_op jit(solution)/shard_map/ppermute | solution.py:31
  14.6 3.7 %collective-permute-start.9 = (bf16[3,48,256]{2,1,0:T(8,128)(2,1)S(1)}, bf16[3,48,256]{2,1,0:T(8,128)(2,1)S(1)}, u32[]{:S(2)}, u32[]{:S(2)}) collective-permute-start(bf16[3,48,256]{2,1,0:T(8,128)(2,1)S(1)} %collective-permute-done.7), channel_id=1, source_target_pairs={{0,1},{1,0},{2,3},{3,2},{4,5},{5,4},{6,7},{7,6},{8,9},{9,8},{10,11... | collective-permute-start | bytes 221192 | tf_op jit(solution)/shard_map/ppermute | solution.py:31
  20.2 1.5 %collective-permute-start.10 = (bf16[4,96,256]{2,1,0:T(8,128)(2,1)S(1)}, bf16[4,96,256]{2,1,0:T(8,128)(2,1)S(1)}, u32[]{:S(2)}, u32[]{:S(2)}) collective-permute-start(bf16[4,96,256]{2,1,0:T(8,128)(2,1)S(1)} %get-tuple-element.25), channel_id=1, source_target_pairs={{0,1},{1,0},{2,3},{3,2},{4,5},{5,4},{6,7},{7,6},{8,9},{9,8},{10,11... | collective-permute-start | bytes 589832 | tf_op jit(solution)/shard_map/ppermute | solution.py:31
  21.8 5.3 %collective-permute-start.12 = (bf16[96,256]{1,0:T(8,128)(2,1)S(1)}, bf16[96,256]{1,0:T(8,128)(2,1)S(1)}, u32[]{:S(2)}, u32[]{:S(2)}) collective-permute-start(bf16[96,256]{1,0:T(8,128)(2,1)S(1)} %get-tuple-element.32), channel_id=1, source_target_pairs={{0,6},{1,7},{2,4},{3,5},{4,2},{5,3},{6,0},{7,1},{8,14},{9,15},{10,... | collective-permute-start | bytes 147464 | tf_op jit(solution)/shard_map/ppermute | solution.py:31
  23.5 4.1 %collective-permute-start.14 = (bf16[96,256]{1,0:T(8,128)(2,1)S(1)}, bf16[96,256]{1,0:T(8,128)(2,1)S(1)}, u32[]{:S(2)}, u32[]{:S(2)}) collective-permute-start(bf16[96,256]{1,0:T(8,128)(2,1)S(1)} %get-tuple-element.33), channel_id=1, source_target_pairs={{0,4},{1,5},{2,6},{3,7},{4,0},{5,1},{6,2},{7,3},{8,12},{9,13},{10,... | collective-permute-start | bytes 147464 | tf_op jit(solution)/shard_map/ppermute | solution.py:31
  24.8 4.1 %collective-permute-start.13 = (bf16[96,256]{1,0:T(8,128)(2,1)S(1)}, bf16[96,256]{1,0:T(8,128)(2,1)S(1)}, u32[]{:S(2)}, u32[]{:S(2)}) collective-permute-start(bf16[96,256]{1,0:T(8,128)(2,1)S(1)} %get-tuple-element.34), channel_id=1, source_target_pairs={{0,2},{1,3},{2,0},{3,1},{4,6},{5,7},{6,4},{7,5},{8,10},{9,11},{10,... | collective-permute-start | bytes 147464 | tf_op jit(solution)/shard_map/ppermute | solution.py:31
  25.4 3.5 %collective-permute-start.11 = (bf16[2,3,48,256]{3,2,1,0:T(8,128)(2,1)S(1)}, bf16[2,3,48,256]{3,2,1,0:T(8,128)(2,1)S(1)}, u32[]{:S(2)}, u32[]{:S(2)}) collective-permute-start(bf16[2,3,48,256]{3,2,1,0:T(8,128)(2,1)S(1)} %get-tuple-element.26), channel_id=1, source_target_pairs={{0,1},{1,0},{2,3},{3,2},{4,5},{5,4},{6,7},{7,6},{8,9},{9,8},{10,11... | collective-permute-start | bytes 442376 | tf_op jit(solution)/shard_map/ppermute | solution.py:31
  28.9 6.2 %collective-permute-start.18 = (bf16[96,256]{1,0:T(8,128)(2,1)S(1)}, bf16[96,256]{1,0:T(8,128)(2,1)S(1)}, u32[]{:S(2)}, u32[]{:S(2)}) collective-permute-start(bf16[96,256]{1,0:T(8,128)(2,1)S(1)} %fusion.5), channel_id=1, source_target_pairs={{0,24},{4,28},{8,16},{12,20},{16,8},{20,12},{24,0},{28,4},{1,25},{... | collective-permute-start | bytes 147464 | tf_op jit(solution)/shard_map/ppermute | solution.py:31
  31.4 5.0 %collective-permute-start.17 = (bf16[96,256]{1,0:T(8,128)(2,1)S(1)}, bf16[96,256]{1,0:T(8,128)(2,1)S(1)}, u32[]{:S(2)}, u32[]{:S(2)}) collective-permute-start(bf16[96,256]{1,0:T(8,128)(2,1)S(1)} %fusion.5), channel_id=1, source_target_pairs={{0,16},{4,20},{8,24},{12,28},{16,0},{20,4},{24,8},{28,12},{1,17},{... | collective-permute-start | bytes 147464 | tf_op jit(solution)/shard_map/ppermute | solution.py:31
  31.5 5.0 %collective-permute-start.16 = (bf16[96,256]{1,0:T(8,128)(2,1)S(1)}, bf16[96,256]{1,0:T(8,128)(2,1)S(1)}, u32[]{:S(2)}, u32[]{:S(2)}) collective-permute-start(bf16[96,256]{1,0:T(8,128)(2,1)S(1)} %fusion.5), channel_id=1, source_target_pairs={{0,8},{4,12},{8,0},{12,4},{16,24},{20,28},{24,16},{28,20},{1,9},{5... | collective-permute-start | bytes 147464 | tf_op jit(solution)/shard_map/ppermute | solution.py:31
  33.4 4.4 %collective-permute-start.15 = (bf16[1,3,48,256]{3,2,1,0:T(8,128)(2,1)S(1)}, bf16[1,3,48,256]{3,2,1,0:T(8,128)(2,1)S(1)}, u32[]{:S(2)}, u32[]{:S(2)}) collective-permute-start(bf16[1,3,48,256]{3,2,1,0:T(8,128)(2,1)S(1)} %fusion.7), channel_id=1, source_target_pairs={{0,2},{1,3},{2,0},{3,1},{4,6},{5,7},{6,4},{7,5},{8,10},{9,11},{10,... | collective-permute-start | bytes 221192 | tf_op jit(solution)/shard_map/ppermute | solution.py:31
  37.8 5.1 %collective-permute-start.21 = (bf16[96,256]{1,0:T(8,128)(2,1)S(1)}, bf16[96,256]{1,0:T(8,128)(2,1)S(1)}, u32[]{:S(2)}, u32[]{:S(2)}) collective-permute-start(bf16[96,256]{1,0:T(8,128)(2,1)S(1)} %add_convert_fusion), channel_id=1, source_target_pairs={{0,6},{1,7},{2,4},{3,5},{4,2},{5,3},{6,0},{7,1},{8,14},{9,15},{10,... | collective-permute-start | bytes 147464 | tf_op jit(solution)/shard_map/ppermute | solution.py:31
  38.6 4.6 %collective-permute-start.20 = (bf16[96,256]{1,0:T(8,128)(2,1)S(1)}, bf16[96,256]{1,0:T(8,128)(2,1)S(1)}, u32[]{:S(2)}, u32[]{:S(2)}) collective-permute-start(bf16[96,256]{1,0:T(8,128)(2,1)S(1)} %add_convert_fusion), channel_id=1, source_target_pairs={{0,2},{1,3},{2,0},{3,1},{4,6},{5,7},{6,4},{7,5},{8,10},{9,11},{10,... | collective-permute-start | bytes 147464 | tf_op jit(solution)/shard_map/ppermute | solution.py:31
  40.1 4.1 %collective-permute-start.19 = (bf16[96,256]{1,0:T(8,128)(2,1)S(1)}, bf16[96,256]{1,0:T(8,128)(2,1)S(1)}, u32[]{:S(2)}, u32[]{:S(2)}) collective-permute-start(bf16[96,256]{1,0:T(8,128)(2,1)S(1)} %add_convert_fusion), channel_id=1, source_target_pairs={{0,4},{1,5},{2,6},{3,7},{4,0},{5,1},{6,2},{7,3},{8,12},{9,13},{10,... | collective-permute-start | bytes 147464 | tf_op jit(solution)/shard_map/ppermute | solution.py:31
  44.2 1.5 %collective-permute-start.22 = (bf16[4,96,256]{2,1,0:T(8,128)(2,1)S(1)}, bf16[4,96,256]{2,1,0:T(8,128)(2,1)S(1)}, u32[]{:S(2)}, u32[]{:S(2)}) collective-permute-start(bf16[4,96,256]{2,1,0:T(8,128)(2,1)S(1)} %pad_maximum_fusion.here_ref), channel_id=1, source_target_pairs={{0,1},{1,0},{2,3},{3,2},{4,5},{5,4},{6,7},{7,6},{8,9},{9,8},{10,11... | collective-permute-start | bytes 589832 | tf_op jit(solution)/shard_map/ppermute | solution.py:31

commit v4 on v3

--- a/solution.py
+++ b/solution.py
@@ -165,6 +165,8 @@
         for bits, tile in held:
             along_col.append((bits ^ (1 << power),))
             sent = saved_panels if tile is None else tile[0]
+            if power == 0 and tile is None and len(held) > 1:
+                sent = after(sent, held[-1][1])
             col_tiles.append(swap(sent, ("col",), sizes, {"col": 1 << power})[None])
     for bits in near:
         along_row.append((bits,))
@@ -232,6 +234,9 @@
         from_first, from_second, from_both = [
             swap(mine, ("row",), sizes, {"row": bits}) for bits in (first, second, first ^ second)
         ]
+        from_second, from_first, from_both, arrived = lax.optimization_barrier(
+            (from_second, from_first, from_both, arrived)
+        )
         total = (mine.astype(F32) + from_first.astype(F32)) + (
             from_second.astype(F32) + from_both.astype(F32)
         )
@@ -239,7 +244,7 @@
         for bits in others:
             total = mine.astype(F32) + swap(mine, tuple(bits), sizes, bits).astype(F32)
             mine = total.astype(BF16)
-    mine = after(total.astype(BF16), arrived)
+    mine = total.astype(BF16)
     here = jnp.stack([mine] + [swap(mine, both, sizes, spots[bits]) for bits in range(1, 4)])
     there = swap(here, ("col",), sizes, {"col": 1})
     diag_cot = pl.pallas_call(

time: 46.8 us -> 45 us (0.962)
  waiting for transfers between devices: 15.9 us -> 12.2 us
  starting transfers between devices: 24.9 us -> 26.8 us
    ppermute x23, waiting for transfers between devices: 15.9 us -> 12.2 us  [swap(): return lax.ppermute(value, axes, pairs)]
    ppermute x23, starting transfers between devices: 24.9 us -> 26.8 us  [swap(): return lax.ppermute(value, axes, pairs)]
  transfers between devices with their start and end apart: 23 -> 23, of which waited for: 15 -> 13; matrix products, arithmetic and copies ran while one was open for 2% -> 2% of each run, Pallas kernels for 3% -> 3%
where the time goes in v4:
time: 45 us; the launch traced here: 44.8 us
  starting transfers between devices  26.8 us (60%)
  waiting for transfers between devices  12.2 us (27%)
  Pallas kernels  4.24 us (9%)
  other arithmetic  0.82 us (2%)
  between operations  0.74 us (2%)
    ppermute x23, starting transfers between devices, swap(): return lax.ppermute(value, axes, pairs)  26.8 us
    ppermute x23, waiting for transfers between devices, swap(): return lax.ppermute(value, axes, pairs)  12.2 us
    pallas_call x1, Pallas kernels, body(): pl.pallas_call(functools.partial(main_kernel, along_row, along_col), out_...  1.93 us
    pallas_call x1, Pallas kernels, body(): pl.pallas_call(prepare_kernel, out_shape=[jax.ShapeDtypeStruct(value.shap...  1.36 us
    pallas_call x1, Pallas kernels, body(): pl.pallas_call(finish_kernel, out_shape=jax.ShapeDtypeStruct((panels * wi...  0.94 us
  transfers between devices with their start and end apart: 23, of which 13 were waited for; matrix products, arithmetic and copies ran while one was open for 2% of the time, Pallas kernels for 3%

profile of v4, /device:TPU:0, one launch (start us, length us, event | category | flops | bytes accessed | tf_op | source)
XLA Modules:
  0.0 44.8 jit_solution(460843848903164277)
XLA Ops:
  0.6 4.1 %collective-permute-start.3 = (bf16[3,48,256]{2,1,0:T(8,128)(2,1)}, bf16[3,48,256]{2,1,0:T(8,128)(2,1)S(1)}, u32[]{:S(2)}, u32[]{:S(2)}) collective-permute-start(bf16[3,48,256]{2,1,0:T(8,128)(2,1)} %refs_2_.1), channel_id=1, source_target_pairs={{0,16},{4,20},{8,24},{12,28},{16,0},{20,4},{24,8},{28,12},{1,17},{... | collective-permute-start | bytes 221192 | tf_op jit(solution)/shard_map/ppermute | solution.py:31
  4.7 1.5 %collective-permute-start.7 = (bf16[3,48,256]{2,1,0:T(8,128)(2,1)}, bf16[3,48,256]{2,1,0:T(8,128)(2,1)S(1)}, u32[]{:S(2)}, u32[]{:S(2)}) collective-permute-start(bf16[3,48,256]{2,1,0:T(8,128)(2,1)} %refs_2_.1), channel_id=1, source_target_pairs={{0,2},{1,3},{2,0},{3,1},{4,6},{5,7},{6,4},{7,5},{8,10},{9,11},{10,... | collective-permute-start | bytes 221192 | tf_op jit(solution)/shard_map/ppermute | solution.py:31
  6.3 2.5 %collective-permute-start.2 = (bf16[3,48,256]{2,1,0:T(8,128)(2,1)}, bf16[3,48,256]{2,1,0:T(8,128)(2,1)S(1)}, u32[]{:S(2)}, u32[]{:S(2)}) collective-permute-start(bf16[3,48,256]{2,1,0:T(8,128)(2,1)} %refs_2_.1), channel_id=1, source_target_pairs={{0,12},{4,8},{8,4},{12,0},{16,28},{20,24},{24,20},{28,16},{1,13},{... | collective-permute-start | bytes 221192 | tf_op jit(solution)/shard_map/ppermute | solution.py:31
  8.8 0.4 %collective-permute-start.1 = (bf16[3,48,256]{2,1,0:T(8,128)(2,1)}, bf16[3,48,256]{2,1,0:T(8,128)(2,1)S(1)}, u32[]{:S(2)}, u32[]{:S(2)}) collective-permute-start(bf16[3,48,256]{2,1,0:T(8,128)(2,1)} %refs_2_.1), channel_id=1, source_target_pairs={{0,8},{4,12},{8,0},{12,4},{16,24},{20,28},{24,16},{28,20},{1,9},{5... | collective-permute-start | bytes 221192 | tf_op jit(solution)/shard_map/ppermute | solution.py:31
  9.2 0.5 %collective-permute-start = (bf16[3,48,256]{2,1,0:T(8,128)(2,1)}, bf16[3,48,256]{2,1,0:T(8,128)(2,1)S(1)}, u32[]{:S(2)}, u32[]{:S(2)}) collective-permute-start(bf16[3,48,256]{2,1,0:T(8,128)(2,1)} %refs_2_.1), channel_id=1, source_target_pairs={{0,4},{4,0},{8,12},{12,8},{16,20},{20,16},{24,28},{28,24},{1,5},{5... | collective-permute-start | bytes 221192 | tf_op jit(solution)/shard_map/ppermute | solution.py:31
  9.7 2.5 %collective-permute-start.6 = (bf16[1,3,48,256]{3,2,1,0:T(8,128)(2,1)S(1)}, bf16[1,3,48,256]{3,2,1,0:T(8,128)(2,1)S(1)}, u32[]{:S(2)}, u32[]{:S(2)}) collective-permute-start(bf16[1,3,48,256]{3,2,1,0:T(8,128)(2,1)S(1)} %bitcast.45), channel_id=1, source_target_pairs={{0,12},{4,8},{8,4},{12,0},{16,28},{20,24},{24,20},{28,16},{1,13},{... | collective-permute-start | bytes 221192 | tf_op jit(solution)/shard_map/ppermute | solution.py:31
  12.3 0.5 %collective-permute-start.5 = (bf16[1,3,48,256]{3,2,1,0:T(8,128)(2,1)S(1)}, bf16[1,3,48,256]{3,2,1,0:T(8,128)(2,1)S(1)}, u32[]{:S(2)}, u32[]{:S(2)}) collective-permute-start(bf16[1,3,48,256]{3,2,1,0:T(8,128)(2,1)S(1)} %bitcast.46), channel_id=1, source_target_pairs={{0,8},{4,12},{8,0},{12,4},{16,24},{20,28},{24,16},{28,20},{1,9},{5... | collective-permute-start | bytes 221192 | tf_op jit(solution)/shard_map/ppermute | solution.py:31
  12.7 1.2 %collective-permute-start.4 = (bf16[1,3,48,256]{3,2,1,0:T(8,128)(2,1)S(1)}, bf16[1,3,48,256]{3,2,1,0:T(8,128)(2,1)S(1)}, u32[]{:S(2)}, u32[]{:S(2)}) collective-permute-start(bf16[1,3,48,256]{3,2,1,0:T(8,128)(2,1)S(1)} %bitcast.47), channel_id=1, source_target_pairs={{0,4},{4,0},{8,12},{12,8},{16,20},{20,16},{24,28},{28,24},{1,5},{5... | collective-permute-start | bytes 221192 | tf_op jit(solution)/shard_map/ppermute | solution.py:31
  14.2 1.2 %collective-permute-done = bf16[3,48,256]{2,1,0:T(8,128)(2,1)S(1)} collective-permute-done((bf16[3,48,256]{2,1,0:T(8,128)(2,1)}, bf16[3,48,256]{2,1,0:T(8,128)(2,1)S(1)}, u32[]{:S(2)}, u32[]{:S(2)}) %collective-permute-start) | collective-permute-done | bytes 73760 | tf_op jit(solution)/shard_map/ppermute | solution.py:31
  15.4 1.4 %shard_map.68 = (bf16[192,384]{1,0:T(8,128)(2,1)S(1)}, bf16[3,48,256]{2,1,0:T(8,128)(2,1)S(1)}, bf16[3,48,256]{2,1,0:T(8,128)(2,1)S(1)}, bf16[3,256,256]{2,1,0:T...) custom-call(f32[3,256,256]{2,1,0:T(8,128)} %refs_0_.1, bf16[192,384]{1,0:T(8,128)(2,1)} %refs_1_.1, ...), custom_call_target="tpu_custom_call" | custom-call | tf_op jit(solution)/shard_map/pallas_call | solution.py:184
  17.1 1.9 %shard_map.69 = (f32[2,3,48,256]{3,2,1,0:T(8,128)S(1)}, bf16[2,3,48,256]{3,2,1,0:T(8,128)(2,1)S(1)}, f32[4,96,256]{2,1,0:T(8,128)S(1)}, bf16[4,96,256]{2,1,0:T(8,128)(2,1)S(1)}) custom-call(bf16[1,3,48,256]{3,2,1,0:T(8,128)(2,1)S(1)} %bitcast.43, bf16[1,3,48,256]{3,2,1,0:T(8,128)(2,1)S(1)} %bitcast.52, bf16[1,3,48,256]{3,2,1,0:T(8,128)(2,1)S(1)} %bitcast.51, ...), custom_call_target="tpu_custom_call" | custom-call | tf_op jit(solution)/shard_map/pallas_call | solution.py:196
  19.3 1.2 %collective-permute-done.10 = bf16[4,96,256]{2,1,0:T(8,128)(2,1)S(1)} collective-permute-done((bf16[4,96,256]{2,1,0:T(8,128)(2,1)S(1)}, bf16[4,96,256]{2,1,0:T(8,128)(2,1)S(1)}, u32[]{:S(2)}, u32[]{:S(2)}) %collective-permute-start.10) | collective-permute-done | bytes 196640 | tf_op jit(solution)/shard_map/ppermute | solution.py:31
  20.6 1.3 %collective-permute-start.12 = (bf16[96,256]{1,0:T(8,128)(2,1)S(1)}, bf16[96,256]{1,0:T(8,128)(2,1)S(1)}, u32[]{:S(2)}, u32[]{:S(2)}) collective-permute-start(bf16[96,256]{1,0:T(8,128)(2,1)S(1)} %get-tuple-element.38), channel_id=1, source_target_pairs={{0,6},{1,7},{2,4},{3,5},{4,2},{5,3},{6,0},{7,1},{8,14},{9,15},{10,... | collective-permute-start | bytes 147464 | tf_op jit(solution)/shard_map/ppermute | solution.py:31
  21.9 0.8 %collective-permute-start.14 = (bf16[96,256]{1,0:T(8,128)(2,1)S(1)}, bf16[96,256]{1,0:T(8,128)(2,1)S(1)}, u32[]{:S(2)}, u32[]{:S(2)}) collective-permute-start(bf16[96,256]{1,0:T(8,128)(2,1)S(1)} %get-tuple-element.39), channel_id=1, source_target_pairs={{0,4},{1,5},{2,6},{3,7},{4,0},{5,1},{6,2},{7,3},{8,12},{9,13},{10,... | collective-permute-start | bytes 147464 | tf_op jit(solution)/shard_map/ppermute | solution.py:31
  22.6 1.5 %collective-permute-start.13 = (bf16[96,256]{1,0:T(8,128)(2,1)S(1)}, bf16[96,256]{1,0:T(8,128)(2,1)S(1)}, u32[]{:S(2)}, u32[]{:S(2)}) collective-permute-start(bf16[96,256]{1,0:T(8,128)(2,1)S(1)} %get-tuple-element.40), channel_id=1, source_target_pairs={{0,2},{1,3},{2,0},{3,1},{4,6},{5,7},{6,4},{7,5},{8,10},{9,11},{10,... | collective-permute-start | bytes 147464 | tf_op jit(solution)/shard_map/ppermute | solution.py:31
  24.2 1.9 %collective-permute-done.12 = bf16[96,256]{1,0:T(8,128)(2,1)S(1)} collective-permute-done((bf16[96,256]{1,0:T(8,128)(2,1)S(1)}, bf16[96,256]{1,0:T(8,128)(2,1)S(1)}, u32[]{:S(2)}, u32[]{:S(2)}) %collective-permute-start.12) | collective-permute-done | bytes 49184 | tf_op jit(solution)/shard_map/ppermute | solution.py:31
  26.1 0.7 %collective-permute-done.13 = bf16[96,256]{1,0:T(8,128)(2,1)S(1)} collective-permute-done((bf16[96,256]{1,0:T(8,128)(2,1)S(1)}, bf16[96,256]{1,0:T(8,128)(2,1)S(1)}, u32[]{:S(2)}, u32[]{:S(2)}) %collective-permute-start.13) | collective-permute-done | bytes 49184 | tf_op jit(solution)/shard_map/ppermute | solution.py:31
  26.8 1.6 %collective-permute-start.15 = (bf16[1,3,48,256]{3,2,1,0:T(8,128)(2,1)S(1)}, bf16[1,3,48,256]{3,2,1,0:T(8,128)(2,1)S(1)}, u32[]{:S(2)}, u32[]{:S(2)}) collective-permute-start(bf16[1,3,48,256]{3,2,1,0:T(8,128)(2,1)S(1)} %fusion.7), channel_id=1, source_target_pairs={{0,2},{1,3},{2,0},{3,1},{4,6},{5,7},{6,4},{7,5},{8,10},{9,11},{10,... | collective-permute-start | bytes 221192 | tf_op jit(solution)/shard_map/ppermute | solution.py:31
  28.4 2.7 %collective-permute-start.18 = (bf16[96,256]{1,0:T(8,128)(2,1)S(1)}, bf16[96,256]{1,0:T(8,128)(2,1)S(1)}, u32[]{:S(2)}, u32[]{:S(2)}) collective-permute-start(bf16[96,256]{1,0:T(8,128)(2,1)S(1)} %fusion.5), channel_id=1, source_target_pairs={{0,24},{4,28},{8,16},{12,20},{16,8},{20,12},{24,0},{28,4},{1,25},{... | collective-permute-start | bytes 147464 | tf_op jit(solution)/shard_map/ppermute | solution.py:31
  31.1 1.7 %collective-permute-start.16 = (bf16[96,256]{1,0:T(8,128)(2,1)S(1)}, bf16[96,256]{1,0:T(8,128)(2,1)S(1)}, u32[]{:S(2)}, u32[]{:S(2)}) collective-permute-start(bf16[96,256]{1,0:T(8,128)(2,1)S(1)} %fusion.5), channel_id=1, source_target_pairs={{0,16},{4,20},{8,24},{12,28},{16,0},{20,4},{24,8},{28,12},{1,17},{... | collective-permute-start | bytes 147464 | tf_op jit(solution)/shard_map/ppermute | solution.py:31
  32.8 1.6 %collective-permute-done.18 = bf16[96,256]{1,0:T(8,128)(2,1)S(1)} collective-permute-done((bf16[96,256]{1,0:T(8,128)(2,1)S(1)}, bf16[96,256]{1,0:T(8,128)(2,1)S(1)}, u32[]{:S(2)}, u32[]{:S(2)}) %collective-permute-start.18) | collective-permute-done | bytes 49184 | tf_op jit(solution)/shard_map/ppermute | solution.py:31
  34.4 0.9 %collective-permute-done.17 = bf16[96,256]{1,0:T(8,128)(2,1)S(1)} collective-permute-done((bf16[96,256]{1,0:T(8,128)(2,1)S(1)}, bf16[96,256]{1,0:T(8,128)(2,1)S(1)}, u32[]{:S(2)}, u32[]{:S(2)}) %collective-permute-start.17) | collective-permute-done | bytes 49184 | tf_op jit(solution)/shard_map/ppermute | solution.py:31
  35.3 0.8 %collective-permute-done.16 = bf16[96,256]{1,0:T(8,128)(2,1)S(1)} collective-permute-done((bf16[96,256]{1,0:T(8,128)(2,1)S(1)}, bf16[96,256]{1,0:T(8,128)(2,1)S(1)}, u32[]{:S(2)}, u32[]{:S(2)}) %collective-permute-start.16) | collective-permute-done | bytes 49184 | tf_op jit(solution)/shard_map/ppermute | solution.py:31
  36.1 1.6 %collective-permute-start.21 = (bf16[96,256]{1,0:T(8,128)(2,1)S(1)}, bf16[96,256]{1,0:T(8,128)(2,1)S(1)}, u32[]{:S(2)}, u32[]{:S(2)}) collective-permute-start(bf16[96,256]{1,0:T(8,128)(2,1)S(1)} %add_convert_fusion), channel_id=1, source_target_pairs={{0,6},{1,7},{2,4},{3,5},{4,2},{5,3},{6,0},{7,1},{8,14},{9,15},{10,... | collective-permute-start | bytes 147464 | tf_op jit(solution)/shard_map/ppermute | solution.py:31
  37.7 0.6 %collective-permute-start.20 = (bf16[96,256]{1,0:T(8,128)(2,1)S(1)}, bf16[96,256]{1,0:T(8,128)(2,1)S(1)}, u32[]{:S(2)}, u32[]{:S(2)}) collective-permute-start(bf16[96,256]{1,0:T(8,128)(2,1)S(1)} %add_convert_fusion), channel_id=1, source_target_pairs={{0,2},{1,3},{2,0},{3,1},{4,6},{5,7},{6,4},{7,5},{8,10},{9,11},{10,... | collective-permute-start | bytes 147464 | tf_op jit(solution)/shard_map/ppermute | solution.py:31
  38.2 1.4 %collective-permute-start.19 = (bf16[96,256]{1,0:T(8,128)(2,1)S(1)}, bf16[96,256]{1,0:T(8,128)(2,1)S(1)}, u32[]{:S(2)}, u32[]{:S(2)}) collective-permute-start(bf16[96,256]{1,0:T(8,128)(2,1)S(1)} %add_convert_fusion), channel_id=1, source_target_pairs={{0,4},{1,5},{2,6},{3,7},{4,0},{5,1},{6,2},{7,3},{8,12},{9,13},{10,... | collective-permute-start | bytes 147464 | tf_op jit(solution)/shard_map/ppermute | solution.py:31
  39.7 1.5 %collective-permute-done.21 = bf16[96,256]{1,0:T(8,128)(2,1)S(1)} collective-permute-done((bf16[96,256]{1,0:T(8,128)(2,1)S(1)}, bf16[96,256]{1,0:T(8,128)(2,1)S(1)}, u32[]{:S(2)}, u32[]{:S(2)}) %collective-permute-start.21) | collective-permute-done | bytes 49184 | tf_op jit(solution)/shard_map/ppermute | solution.py:31
  41.2 0.6 %collective-permute-done.20 = bf16[96,256]{1,0:T(8,128)(2,1)S(1)} collective-permute-done((bf16[96,256]{1,0:T(8,128)(2,1)S(1)}, bf16[96,256]{1,0:T(8,128)(2,1)S(1)}, u32[]{:S(2)}, u32[]{:S(2)}) %collective-permute-start.20) | collective-permute-done | bytes 49184 | tf_op jit(solution)/shard_map/ppermute | solution.py:31
  41.8 0.6 %collective-permute-done.19 = bf16[96,256]{1,0:T(8,128)(2,1)S(1)} collective-permute-done((bf16[96,256]{1,0:T(8,128)(2,1)S(1)}, bf16[96,256]{1,0:T(8,128)(2,1)S(1)}, u32[]{:S(2)}, u32[]{:S(2)}) %collective-permute-start.19) | collective-permute-done | bytes 49184 | tf_op jit(solution)/shard_map/ppermute | solution.py:31
  42.4 0.6 %fusion.6 = bf16[3,48,256]{2,1,0:T(8,128)(2,1)} fusion(bf16[1,3,48,256]{3,2,1,0:T(8,128)(2,1)S(1)} %collective-permute-done.15, f32[1,2,3,48,256]{4,3,2,1,0:T(8,128)S(1)} %add_bitcast_fusion), kind=kLoop, calls=%fused_computation.13 | loop fusion | flops 110592 | bytes 294912 | tf_op jit(solution)/shard_map/convert_element_type | solution.py:228
  43.1 0.8 %collective-permute-done.22.there_ref = bf16[4,96,256]{2,1,0:T(8,128)(2,1)S(1)} collective-permute-done((bf16[4,96,256]{2,1,0:T(8,128)(2,1)S(1)}, bf16[4,96,256]{2,1,0:T(8,128)(2,1)S(1)}, u32[]{:S(2)}, u32[]{:S(2)}) %collective-permute-start.22) | collective-permute-done | bytes 196640 | tf_op jit(solution)/shard_map/ppermute | solution.py:31
  43.9 0.9 %shard_map.70 = f32[768,256]{1,0:T(8,128)} custom-call(bf16[4,96,256]{2,1,0:T(8,128)(2,1)S(1)} %pad_maximum_fusion.here_ref, bf16[4,96,256]{2,1,0:T(8,128)(2,1)S(1)} %collective-permute-done.22.there_ref), custom_call_target="tpu_custom_call" | custom-call | tf_op jit(solution)/shard_map/pallas_call | solution.py:250
  (25 shorter events, 1.1 us)
Async XLA Ops:
  0.6 9.1 %collective-permute-start.3 = (bf16[3,48,256]{2,1,0:T(8,128)(2,1)}, bf16[3,48,256]{2,1,0:T(8,128)(2,1)S(1)}, u32[]{:S(2)}, u32[]{:S(2)}) collective-permute-start(bf16[3,48,256]{2,1,0:T(8,128)(2,1)} %refs_2_.1), channel_id=1, source_target_pairs={{0,16},{4,20},{8,24},{12,28},{16,0},{20,4},{24,8},{28,12},{1,17},{... | collective-permute-start | bytes 221192 | tf_op jit(solution)/shard_map/ppermute | solution.py:31
  4.7 7.5 %collective-permute-start.7 = (bf16[3,48,256]{2,1,0:T(8,128)(2,1)}, bf16[3,48,256]{2,1,0:T(8,128)(2,1)S(1)}, u32[]{:S(2)}, u32[]{:S(2)}) collective-permute-start(bf16[3,48,256]{2,1,0:T(8,128)(2,1)} %refs_2_.1), channel_id=1, source_target_pairs={{0,2},{1,3},{2,0},{3,1},{4,6},{5,7},{6,4},{7,5},{8,10},{9,11},{10,... | collective-permute-start | bytes 221192 | tf_op jit(solution)/shard_map/ppermute | solution.py:31
  6.3 6.5 %collective-permute-start.2 = (bf16[3,48,256]{2,1,0:T(8,128)(2,1)}, bf16[3,48,256]{2,1,0:T(8,128)(2,1)S(1)}, u32[]{:S(2)}, u32[]{:S(2)}) collective-permute-start(bf16[3,48,256]{2,1,0:T(8,128)(2,1)} %refs_2_.1), channel_id=1, source_target_pairs={{0,12},{4,8},{8,4},{12,0},{16,28},{20,24},{24,20},{28,16},{1,13},{... | collective-permute-start | bytes 221192 | tf_op jit(solution)/shard_map/ppermute | solution.py:31
  8.8 5.4 %collective-permute-start.1 = (bf16[3,48,256]{2,1,0:T(8,128)(2,1)}, bf16[3,48,256]{2,1,0:T(8,128)(2,1)S(1)}, u32[]{:S(2)}, u32[]{:S(2)}) collective-permute-start(bf16[3,48,256]{2,1,0:T(8,128)(2,1)} %refs_2_.1), channel_id=1, source_target_pairs={{0,8},{4,12},{8,0},{12,4},{16,24},{20,28},{24,16},{28,20},{1,9},{5... | collective-permute-start | bytes 221192 | tf_op jit(solution)/shard_map/ppermute | solution.py:31
  9.2 6.2 %collective-permute-start = (bf16[3,48,256]{2,1,0:T(8,128)(2,1)}, bf16[3,48,256]{2,1,0:T(8,128)(2,1)S(1)}, u32[]{:S(2)}, u32[]{:S(2)}) collective-permute-start(bf16[3,48,256]{2,1,0:T(8,128)(2,1)} %refs_2_.1), channel_id=1, source_target_pairs={{0,4},{4,0},{8,12},{12,8},{16,20},{20,16},{24,28},{28,24},{1,5},{5... | collective-permute-start | bytes 221192 | tf_op jit(solution)/shard_map/ppermute | solution.py:31
  9.7 7.0 %collective-permute-start.6 = (bf16[1,3,48,256]{3,2,1,0:T(8,128)(2,1)S(1)}, bf16[1,3,48,256]{3,2,1,0:T(8,128)(2,1)S(1)}, u32[]{:S(2)}, u32[]{:S(2)}) collective-permute-start(bf16[1,3,48,256]{3,2,1,0:T(8,128)(2,1)S(1)} %bitcast.45), channel_id=1, source_target_pairs={{0,12},{4,8},{8,4},{12,0},{16,28},{20,24},{24,20},{28,16},{1,13},{... | collective-permute-start | bytes 221192 | tf_op jit(solution)/shard_map/ppermute | solution.py:31
  12.3 4.5 %collective-permute-start.5 = (bf16[1,3,48,256]{3,2,1,0:T(8,128)(2,1)S(1)}, bf16[1,3,48,256]{3,2,1,0:T(8,128)(2,1)S(1)}, u32[]{:S(2)}, u32[]{:S(2)}) collective-permute-start(bf16[1,3,48,256]{3,2,1,0:T(8,128)(2,1)S(1)} %bitcast.46), channel_id=1, source_target_pairs={{0,8},{4,12},{8,0},{12,4},{16,24},{20,28},{24,16},{28,20},{1,9},{5... | collective-permute-start | bytes 221192 | tf_op jit(solution)/shard_map/ppermute | solution.py:31
  12.7 4.4 %collective-permute-start.4 = (bf16[1,3,48,256]{3,2,1,0:T(8,128)(2,1)S(1)}, bf16[1,3,48,256]{3,2,1,0:T(8,128)(2,1)S(1)}, u32[]{:S(2)}, u32[]{:S(2)}) collective-permute-start(bf16[1,3,48,256]{3,2,1,0:T(8,128)(2,1)S(1)} %bitcast.47), channel_id=1, source_target_pairs={{0,4},{4,0},{8,12},{12,8},{16,20},{20,16},{24,28},{28,24},{1,5},{5... | collective-permute-start | bytes 221192 | tf_op jit(solution)/shard_map/ppermute | solution.py:31
  14.2 2.9 %collective-permute-start.8 = (bf16[3,48,256]{2,1,0:T(8,128)(2,1)}, bf16[3,48,256]{2,1,0:T(8,128)(2,1)S(1)}, u32[]{:S(2)}, u32[]{:S(2)}) collective-permute-start(bf16[3,48,256]{2,1,0:T(8,128)(2,1)} %refs_2_.1), channel_id=1, source_target_pairs={{0,1},{1,0},{2,3},{3,2},{4,5},{5,4},{6,7},{7,6},{8,9},{9,8},{10,11... | collective-permute-start | bytes 221192 | tf_op jit(solution)/shard_map/ppermute | solution.py:31
  15.4 1.7 %collective-permute-start.9 = (bf16[3,48,256]{2,1,0:T(8,128)(2,1)S(1)}, bf16[3,48,256]{2,1,0:T(8,128)(2,1)S(1)}, u32[]{:S(2)}, u32[]{:S(2)}) collective-permute-start(bf16[3,48,256]{2,1,0:T(8,128)(2,1)S(1)} %collective-permute-done.7), channel_id=1, source_target_pairs={{0,1},{1,0},{2,3},{3,2},{4,5},{5,4},{6,7},{7,6},{8,9},{9,8},{10,11... | collective-permute-start | bytes 221192 | tf_op jit(solution)/shard_map/ppermute | solution.py:31
  19.0 1.5 %collective-permute-start.10 = (bf16[4,96,256]{2,1,0:T(8,128)(2,1)S(1)}, bf16[4,96,256]{2,1,0:T(8,128)(2,1)S(1)}, u32[]{:S(2)}, u32[]{:S(2)}) collective-permute-start(bf16[4,96,256]{2,1,0:T(8,128)(2,1)S(1)} %get-tuple-element.29), channel_id=1, source_target_pairs={{0,1},{1,0},{2,3},{3,2},{4,5},{5,4},{6,7},{7,6},{8,9},{9,8},{10,11... | collective-permute-start | bytes 589832 | tf_op jit(solution)/shard_map/ppermute | solution.py:31
  20.6 5.5 %collective-permute-start.12 = (bf16[96,256]{1,0:T(8,128)(2,1)S(1)}, bf16[96,256]{1,0:T(8,128)(2,1)S(1)}, u32[]{:S(2)}, u32[]{:S(2)}) collective-permute-start(bf16[96,256]{1,0:T(8,128)(2,1)S(1)} %get-tuple-element.38), channel_id=1, source_target_pairs={{0,6},{1,7},{2,4},{3,5},{4,2},{5,3},{6,0},{7,1},{8,14},{9,15},{10,... | collective-permute-start | bytes 147464 | tf_op jit(solution)/shard_map/ppermute | solution.py:31
  21.9 4.2 %collective-permute-start.14 = (bf16[96,256]{1,0:T(8,128)(2,1)S(1)}, bf16[96,256]{1,0:T(8,128)(2,1)S(1)}, u32[]{:S(2)}, u32[]{:S(2)}) collective-permute-start(bf16[96,256]{1,0:T(8,128)(2,1)S(1)} %get-tuple-element.39), channel_id=1, source_target_pairs={{0,4},{1,5},{2,6},{3,7},{4,0},{5,1},{6,2},{7,3},{8,12},{9,13},{10,... | collective-permute-start | bytes 147464 | tf_op jit(solution)/shard_map/ppermute | solution.py:31
  22.6 4.1 %collective-permute-start.13 = (bf16[96,256]{1,0:T(8,128)(2,1)S(1)}, bf16[96,256]{1,0:T(8,128)(2,1)S(1)}, u32[]{:S(2)}, u32[]{:S(2)}) collective-permute-start(bf16[96,256]{1,0:T(8,128)(2,1)S(1)} %get-tuple-element.40), channel_id=1, source_target_pairs={{0,2},{1,3},{2,0},{3,1},{4,6},{5,7},{6,4},{7,5},{8,10},{9,11},{10,... | collective-permute-start | bytes 147464 | tf_op jit(solution)/shard_map/ppermute | solution.py:31
  24.2 2.6 %collective-permute-start.11 = (bf16[2,3,48,256]{3,2,1,0:T(8,128)(2,1)S(1)}, bf16[2,3,48,256]{3,2,1,0:T(8,128)(2,1)S(1)}, u32[]{:S(2)}, u32[]{:S(2)}) collective-permute-start(bf16[2,3,48,256]{3,2,1,0:T(8,128)(2,1)S(1)} %get-tuple-element.30), channel_id=1, source_target_pairs={{0,1},{1,0},{2,3},{3,2},{4,5},{5,4},{6,7},{7,6},{8,9},{9,8},{10,11... | collective-permute-start | bytes 442376 | tf_op jit(solution)/shard_map/ppermute | solution.py:31
  26.8 9.3 %collective-permute-start.15 = (bf16[1,3,48,256]{3,2,1,0:T(8,128)(2,1)S(1)}, bf16[1,3,48,256]{3,2,1,0:T(8,128)(2,1)S(1)}, u32[]{:S(2)}, u32[]{:S(2)}) collective-permute-start(bf16[1,3,48,256]{3,2,1,0:T(8,128)(2,1)S(1)} %fusion.7), channel_id=1, source_target_pairs={{0,2},{1,3},{2,0},{3,1},{4,6},{5,7},{6,4},{7,5},{8,10},{9,11},{10,... | collective-permute-start | bytes 221192 | tf_op jit(solution)/shard_map/ppermute | solution.py:31
  28.4 6.0 %collective-permute-start.18 = (bf16[96,256]{1,0:T(8,128)(2,1)S(1)}, bf16[96,256]{1,0:T(8,128)(2,1)S(1)}, u32[]{:S(2)}, u32[]{:S(2)}) collective-permute-start(bf16[96,256]{1,0:T(8,128)(2,1)S(1)} %fusion.5), channel_id=1, source_target_pairs={{0,24},{4,28},{8,16},{12,20},{16,8},{20,12},{24,0},{28,4},{1,25},{... | collective-permute-start | bytes 147464 | tf_op jit(solution)/shard_map/ppermute | solution.py:31
  31.1 4.2 %collective-permute-start.17 = (bf16[96,256]{1,0:T(8,128)(2,1)S(1)}, bf16[96,256]{1,0:T(8,128)(2,1)S(1)}, u32[]{:S(2)}, u32[]{:S(2)}) collective-permute-start(bf16[96,256]{1,0:T(8,128)(2,1)S(1)} %fusion.5), channel_id=1, source_target_pairs={{0,8},{4,12},{8,0},{12,4},{16,24},{20,28},{24,16},{28,20},{1,9},{5... | collective-permute-start | bytes 147464 | tf_op jit(solution)/shard_map/ppermute | solution.py:31
  31.1 5.0 %collective-permute-start.16 = (bf16[96,256]{1,0:T(8,128)(2,1)S(1)}, bf16[96,256]{1,0:T(8,128)(2,1)S(1)}, u32[]{:S(2)}, u32[]{:S(2)}) collective-permute-start(bf16[96,256]{1,0:T(8,128)(2,1)S(1)} %fusion.5), channel_id=1, source_target_pairs={{0,16},{4,20},{8,24},{12,28},{16,0},{20,4},{24,8},{28,12},{1,17},{... | collective-permute-start | bytes 147464 | tf_op jit(solution)/shard_map/ppermute | solution.py:31
  36.1 5.1 %collective-permute-start.21 = (bf16[96,256]{1,0:T(8,128)(2,1)S(1)}, bf16[96,256]{1,0:T(8,128)(2,1)S(1)}, u32[]{:S(2)}, u32[]{:S(2)}) collective-permute-start(bf16[96,256]{1,0:T(8,128)(2,1)S(1)} %add_convert_fusion), channel_id=1, source_target_pairs={{0,6},{1,7},{2,4},{3,5},{4,2},{5,3},{6,0},{7,1},{8,14},{9,15},{10,... | collective-permute-start | bytes 147464 | tf_op jit(solution)/shard_map/ppermute | solution.py:31
  37.7 4.1 %collective-permute-start.20 = (bf16[96,256]{1,0:T(8,128)(2,1)S(1)}, bf16[96,256]{1,0:T(8,128)(2,1)S(1)}, u32[]{:S(2)}, u32[]{:S(2)}) collective-permute-start(bf16[96,256]{1,0:T(8,128)(2,1)S(1)} %add_convert_fusion), channel_id=1, source_target_pairs={{0,2},{1,3},{2,0},{3,1},{4,6},{5,7},{6,4},{7,5},{8,10},{9,11},{10,... | collective-permute-start | bytes 147464 | tf_op jit(solution)/shard_map/ppermute | solution.py:31
  38.2 4.1 %collective-permute-start.19 = (bf16[96,256]{1,0:T(8,128)(2,1)S(1)}, bf16[96,256]{1,0:T(8,128)(2,1)S(1)}, u32[]{:S(2)}, u32[]{:S(2)}) collective-permute-start(bf16[96,256]{1,0:T(8,128)(2,1)S(1)} %add_convert_fusion), channel_id=1, source_target_pairs={{0,4},{1,5},{2,6},{3,7},{4,0},{5,1},{6,2},{7,3},{8,12},{9,13},{10,... | collective-permute-start | bytes 147464 | tf_op jit(solution)/shard_map/ppermute | solution.py:31
  42.4 1.5 %collective-permute-start.22 = (bf16[4,96,256]{2,1,0:T(8,128)(2,1)S(1)}, bf16[4,96,256]{2,1,0:T(8,128)(2,1)S(1)}, u32[]{:S(2)}, u32[]{:S(2)}) collective-permute-start(bf16[4,96,256]{2,1,0:T(8,128)(2,1)S(1)} %pad_maximum_fusion.here_ref), channel_id=1, source_target_pairs={{0,1},{1,0},{2,3},{3,2},{4,5},{5,4},{6,7},{7,6},{8,9},{9,8},{10,11... | collective-permute-start | bytes 589832 | tf_op jit(solution)/shard_map/ppermute | solution.py:31

commit v5 on v4

--- a/solution.py
+++ b/solution.py
@@ -31,11 +31,6 @@
     return lax.ppermute(value, axes, pairs)
 
 
-def split(value):
-    high = value.astype(BF16)
-    return high, (value - high.astype(F32)).astype(BF16)
-
-
 def dot(left, right):
     return jnp.dot(left, right, preferred_element_type=F32)
 
@@ -45,7 +40,7 @@
 
 
 def prepare_kernel(*refs):
-    sources, outs, (high_out, low_out, solver, sems) = refs[:5], refs[5:9], refs[9:]
+    sources, outs, (solver_out, solver, sems) = refs[:5], refs[5:9], refs[9:]
     copies = [
         pltpu.make_async_copy(source, target, sems.at[index])
         for index, (source, target) in enumerate(zip(sources, (solver, *outs)))
@@ -53,9 +48,7 @@
     for copy in copies:
         copy.start()
     copies[0].wait()
-    high, low = split(solver[...])
-    high_out[...] = high
-    low_out[...] = low
+    solver_out[...] = solver[...].astype(BF16)
     for copy in copies[1:]:
         copy.wait()
 
@@ -63,8 +56,8 @@
 def main_kernel(along_row, along_col, *refs):
     row_refs, refs = refs[: len(along_row)], refs[len(along_row) :]
     col_refs, refs = refs[: len(along_col)], refs[len(along_col) :]
-    cot_ref, upstream_ref, high_ref, low_ref, tops_ref = refs[:5]
-    columns_keep, columns_send, keep_ref, send_ref, joined, own, total, diag = refs[5:]
+    cot_ref, upstream_ref, solver_ref, tops_ref = refs[:4]
+    columns_keep, columns_send, keep_ref, send_ref, joined, own, total, diag = refs[4:]
     row, col = lax.axis_index("row"), lax.axis_index("col")
     panels, height, width = upstream_ref.shape
 
@@ -97,21 +90,22 @@
             appended = term if appended is None else appended + term
         if appended is not None:
             combined = combined - 2.0 * appended
-        high, low = split(combined)
+        combined = combined.astype(BF16)
         if appended is None:
-            first = dot(jnp.concatenate([high, low]), high_ref[index])
-            second = dot(high, low_ref[index])
+            now = dot(combined, solver_ref[index])
         else:
-            first = dot(jnp.concatenate([high, low, panel]), high_ref[index])
-            second = dot(jnp.concatenate([high, panel]), low_ref[index])
-        now = first[:tall] + (first[tall : 2 * tall] + second[:tall])
+            solved = dot(jnp.concatenate([combined, panel]), solver_ref[index])
+            now, solved = solved[:tall], 2.0 * solved[tall:]
         total[:, span] = now
         now = now.astype(BF16)
         columns.append(now)
-        result = -dot_rows(panel, now)
-        if appended is not None:
-            solved = 2.0 * (first[2 * tall :] + second[tall:])
-            result = result + dot_rows(appended.astype(BF16), solved.astype(BF16))
+        if appended is None:
+            result = dot_rows(panel, -now)
+        else:
+            result = dot_rows(
+                jnp.concatenate([panel, appended.astype(BF16)]),
+                jnp.concatenate([-now, solved.astype(BF16)]),
+            )
         diag[span, :] = result
 
     piece = keep_ref.shape[1]
@@ -180,12 +174,11 @@
             row_tiles.append(swap(sent, ("row",), sizes, {"row": bits}))
 
     arguments = (inverse_diag, cotangent, saved_panels, upstream, panel_tops)
-    halves = [jax.ShapeDtypeStruct(inverse_diag.shape, BF16)] * 2
-    cot, saved, upstream_here, tops, high, low = pl.pallas_call(
+    cot, saved, upstream_here, tops, solver = pl.pallas_call(
         prepare_kernel,
-        out_shape=[jax.ShapeDtypeStruct(value.shape, BF16) for value in arguments[1:]] + halves,
+        out_shape=[jax.ShapeDtypeStruct(value.shape, BF16) for value in arguments[1:] + arguments[:1]],
         in_specs=[pl.BlockSpec(memory_space=pl.ANY)] * 5,
-        out_specs=[VMEM] * 6,
+        out_specs=[VMEM] * 5,
         scratch_shapes=[pltpu.VMEM(inverse_diag.shape, F32), pltpu.SemaphoreType.DMA((5,))],
         compiler_params=limit,
     )(*[pltpu.with_memory_space_constraint(value, pltpu.HBM) for value in arguments])
@@ -201,7 +194,7 @@
             jax.ShapeDtypeStruct((4, piece, width), F32),
             jax.ShapeDtypeStruct((4, piece, width), BF16),
         ],
-        in_specs=[VMEM] * (len(row_tiles) + len(col_tiles) + 5),
+        in_specs=[VMEM] * (len(row_tiles) + len(col_tiles) + 4),
         out_specs=[VMEM] * 4,
         scratch_shapes=[
             pltpu.VMEM((rows * height, panels * width), BF16),
@@ -210,21 +203,21 @@
             pltpu.VMEM((panels * width, width), F32),
         ],
         compiler_params=limit,
-    )(*row_tiles, *col_tiles, cot, upstream_here, high, low, tops)
+    )(*row_tiles, *col_tiles, cot, upstream_here, solver, tops)
 
     both = ("row", "col")
     half = keep + swap(send, ("col",), sizes, {"col": 1}).astype(F32)
     spots = [{"col": (bits >> 1) * 2, "row": bits & 1} for bits in range(4)]
     total = half[0]
-    for bits in range(3, 0, -1):
+    for bits in (3, 1, 2):
         total = total + swap(half[bits].astype(BF16), both, sizes, spots[bits]).astype(F32)
-    arrived = swap(after(columns_send, half), ("col",), sizes, {"col": 1})
+    arrived = swap(columns_send, ("col",), sizes, {"col": 1})
     columns = columns_keep + arrived.astype(F32)
-    mine = after(total.astype(BF16), arrived)
     for power in range(1, cols.bit_length() - 1):
         halves = columns.reshape(-1, 2, panels, height, width)
-        arrived = swap(after(halves[:, 1].astype(BF16), mine), ("col",), sizes, {"col": 1 << power})
+        arrived = swap(after(halves[:, 1].astype(BF16), half), ("col",), sizes, {"col": 1 << power})
         columns = halves[:, 0] + arrived.astype(F32)
+    mine = total.astype(BF16)
     columns = columns[0].astype(BF16)
 
     others = [{"row": 1 << power} for power in range(1, rows.bit_length() - 1)]

time: 45 us -> 44 us (0.978)
  starting transfers between devices: 26.8 us -> 26 us
  Pallas kernels: 4.24 us -> 3.74 us
    ppermute x23, starting transfers between devices: 26.8 us -> 26 us  [swap(): return lax.ppermute(value, axes, pairs)]
    pallas_call x1, Pallas kernels: 1.93 us -> 1.43 us  [body(): pl.pallas_call(functools.partial(main_kernel, along_row, along_col), out_...]
  transfers between devices with their start and end apart: 23 -> 23, of which waited for: 13 -> 15; matrix products, arithmetic and copies ran while one was open for 2% -> 2% of each run, Pallas kernels for 3% -> 3%
where the time goes in v5:
time: 44 us; the launch traced here: 43.9 us
  starting transfers between devices  26 us (59%)
  waiting for transfers between devices  12.5 us (28%)
  Pallas kernels  3.74 us (8%)
  other arithmetic  0.81 us (2%)
  between operations  0.73 us (2%)
    ppermute x23, starting transfers between devices, swap(): return lax.ppermute(value, axes, pairs)  26 us
    ppermute x23, waiting for transfers between devices, swap(): return lax.ppermute(value, axes, pairs)  12.5 us
    pallas_call x1, Pallas kernels, body(): pl.pallas_call(functools.partial(main_kernel, along_row, along_col), out_...  1.43 us
    pallas_call x1, Pallas kernels, body(): pl.pallas_call(prepare_kernel, out_shape=[jax.ShapeDtypeStruct(value.shap...  1.36 us
    pallas_call x1, Pallas kernels, body(): pl.pallas_call(finish_kernel, out_shape=jax.ShapeDtypeStruct((panels * wi...  0.94 us
  transfers between devices with their start and end apart: 23, of which 15 were waited for; matrix products, arithmetic and copies ran while one was open for 2% of the time, Pallas kernels for 3%

profile of v5, /device:TPU:0, one launch (start us, length us, event | category | flops | bytes accessed | tf_op | source)
XLA Modules:
  0.0 43.9 jit_solution(5525913590508999183)
XLA Ops:
  0.6 4.1 %collective-permute-start.3 = (bf16[3,48,256]{2,1,0:T(8,128)(2,1)}, bf16[3,48,256]{2,1,0:T(8,128)(2,1)S(1)}, u32[]{:S(2)}, u32[]{:S(2)}) collective-permute-start(bf16[3,48,256]{2,1,0:T(8,128)(2,1)} %refs_2_.1), channel_id=1, source_target_pairs={{0,16},{4,20},{8,24},{12,28},{16,0},{20,4},{24,8},{28,12},{1,17},{... | collective-permute-start | bytes 221192 | tf_op jit(solution)/shard_map/ppermute | solution.py:31
  4.7 1.5 %collective-permute-start.7 = (bf16[3,48,256]{2,1,0:T(8,128)(2,1)}, bf16[3,48,256]{2,1,0:T(8,128)(2,1)S(1)}, u32[]{:S(2)}, u32[]{:S(2)}) collective-permute-start(bf16[3,48,256]{2,1,0:T(8,128)(2,1)} %refs_2_.1), channel_id=1, source_target_pairs={{0,2},{1,3},{2,0},{3,1},{4,6},{5,7},{6,4},{7,5},{8,10},{9,11},{10,... | collective-permute-start | bytes 221192 | tf_op jit(solution)/shard_map/ppermute | solution.py:31
  6.3 2.5 %collective-permute-start.2 = (bf16[3,48,256]{2,1,0:T(8,128)(2,1)}, bf16[3,48,256]{2,1,0:T(8,128)(2,1)S(1)}, u32[]{:S(2)}, u32[]{:S(2)}) collective-permute-start(bf16[3,48,256]{2,1,0:T(8,128)(2,1)} %refs_2_.1), channel_id=1, source_target_pairs={{0,12},{4,8},{8,4},{12,0},{16,28},{20,24},{24,20},{28,16},{1,13},{... | collective-permute-start | bytes 221192 | tf_op jit(solution)/shard_map/ppermute | solution.py:31
  9.2 0.5 %collective-permute-start = (bf16[3,48,256]{2,1,0:T(8,128)(2,1)}, bf16[3,48,256]{2,1,0:T(8,128)(2,1)S(1)}, u32[]{:S(2)}, u32[]{:S(2)}) collective-permute-start(bf16[3,48,256]{2,1,0:T(8,128)(2,1)} %refs_2_.1), channel_id=1, source_target_pairs={{0,4},{4,0},{8,12},{12,8},{16,20},{20,16},{24,28},{28,24},{1,5},{5... | collective-permute-start | bytes 221192 | tf_op jit(solution)/shard_map/ppermute | solution.py:31
  9.7 2.5 %collective-permute-start.6 = (bf16[1,3,48,256]{3,2,1,0:T(8,128)(2,1)S(1)}, bf16[1,3,48,256]{3,2,1,0:T(8,128)(2,1)S(1)}, u32[]{:S(2)}, u32[]{:S(2)}) collective-permute-start(bf16[1,3,48,256]{3,2,1,0:T(8,128)(2,1)S(1)} %bitcast.45), channel_id=1, source_target_pairs={{0,12},{4,8},{8,4},{12,0},{16,28},{20,24},{24,20},{28,16},{1,13},{... | collective-permute-start | bytes 221192 | tf_op jit(solution)/shard_map/ppermute | solution.py:31
  12.3 0.5 %collective-permute-start.5 = (bf16[1,3,48,256]{3,2,1,0:T(8,128)(2,1)S(1)}, bf16[1,3,48,256]{3,2,1,0:T(8,128)(2,1)S(1)}, u32[]{:S(2)}, u32[]{:S(2)}) collective-permute-start(bf16[1,3,48,256]{3,2,1,0:T(8,128)(2,1)S(1)} %bitcast.46), channel_id=1, source_target_pairs={{0,8},{4,12},{8,0},{12,4},{16,24},{20,28},{24,16},{28,20},{1,9},{5... | collective-permute-start | bytes 221192 | tf_op jit(solution)/shard_map/ppermute | solution.py:31
  12.7 1.2 %collective-permute-start.4 = (bf16[1,3,48,256]{3,2,1,0:T(8,128)(2,1)S(1)}, bf16[1,3,48,256]{3,2,1,0:T(8,128)(2,1)S(1)}, u32[]{:S(2)}, u32[]{:S(2)}) collective-permute-start(bf16[1,3,48,256]{3,2,1,0:T(8,128)(2,1)S(1)} %bitcast.47), channel_id=1, source_target_pairs={{0,4},{4,0},{8,12},{12,8},{16,20},{20,16},{24,28},{28,24},{1,5},{5... | collective-permute-start | bytes 221192 | tf_op jit(solution)/shard_map/ppermute | solution.py:31
  14.2 1.2 %collective-permute-done = bf16[3,48,256]{2,1,0:T(8,128)(2,1)S(1)} collective-permute-done((bf16[3,48,256]{2,1,0:T(8,128)(2,1)}, bf16[3,48,256]{2,1,0:T(8,128)(2,1)S(1)}, u32[]{:S(2)}, u32[]{:S(2)}) %collective-permute-start) | collective-permute-done | bytes 73760 | tf_op jit(solution)/shard_map/ppermute | solution.py:31
  15.4 1.4 %shard_map.68 = (bf16[192,384]{1,0:T(8,128)(2,1)S(1)}, bf16[3,48,256]{2,1,0:T(8,128)(2,1)S(1)}, bf16[3,48,256]{2,1,0:T(8,128)(2,1)S(1)}, bf16[3,256,256]{2,1,0:T(8,128)(2,1)S(1)}, bf16[3,256,256]{2,1,0:T(8,128)(2,1)S(1)}) custom-call(f32[3,256,256]{2,1,0:T(8,128)} %refs_0_.1, bf16[192,384]{1,0:T(8,128)(2,1)} %refs_1_.1, bf16[3,48,256]{2,1,0:T(8,128)(2,1)} %refs_2_.1, ...), custom_call_target="tpu_custom_call" | custom-call | tf_op jit(solution)/shard_map/pallas_call | solution.py:177
  17.1 1.4 %shard_map.69 = (f32[2,3,48,256]{3,2,1,0:T(8,128)S(1)}, bf16[2,3,48,256]{3,2,1,0:T(8,128)(2,1)S(1)}, f32[4,96,256]{2,1,0:T(8,128)S(1)}, bf16[4,96,256]{2,1,0:T(8,128)(2,1)S(1)}) custom-call(bf16[1,3,48,256]{3,2,1,0:T(8,128)(2,1)S(1)} %bitcast.43, bf16[1,3,48,256]{3,2,1,0:T(8,128)(2,1)S(1)} %bitcast.52, bf16[1,3,48,256]{3,2,1,0:T(8,128)(2,1)S(1)} %bitcast.51, ...), custom_call_target="tpu_custom_call" | custom-call | tf_op jit(solution)/shard_map/pallas_call | solution.py:189
  19.1 0.9 %collective-permute-done.10 = bf16[2,3,48,256]{3,2,1,0:T(8,128)(2,1)S(1)} collective-permute-done((bf16[2,3,48,256]{3,2,1,0:T(8,128)(2,1)S(1)}, bf16[2,3,48,256]{3,2,1,0:T(8,128)(2,1)S(1)}, u32[]{:S(2)}, u32[]{:S(2)}) %collective-permute-start.10) | collective-permute-done | bytes 147488 | tf_op jit(solution)/shard_map/ppermute | solution.py:31
  20.3 1.2 %collective-permute-start.13 = (bf16[96,256]{1,0:T(8,128)(2,1)S(1)}, bf16[96,256]{1,0:T(8,128)(2,1)S(1)}, u32[]{:S(2)}, u32[]{:S(2)}) collective-permute-start(bf16[96,256]{1,0:T(8,128)(2,1)S(1)} %get-tuple-element.32), channel_id=1, source_target_pairs={{0,6},{1,7},{2,4},{3,5},{4,2},{5,3},{6,0},{7,1},{8,14},{9,15},{10,... | collective-permute-start | bytes 147464 | tf_op jit(solution)/shard_map/ppermute | solution.py:31
  21.6 1.5 %collective-permute-start.15 = (bf16[96,256]{1,0:T(8,128)(2,1)S(1)}, bf16[96,256]{1,0:T(8,128)(2,1)S(1)}, u32[]{:S(2)}, u32[]{:S(2)}) collective-permute-start(bf16[96,256]{1,0:T(8,128)(2,1)S(1)} %get-tuple-element.33), channel_id=1, source_target_pairs={{0,2},{1,3},{2,0},{3,1},{4,6},{5,7},{6,4},{7,5},{8,10},{9,11},{10,... | collective-permute-start | bytes 147464 | tf_op jit(solution)/shard_map/ppermute | solution.py:31
  23.1 0.8 %collective-permute-start.14 = (bf16[96,256]{1,0:T(8,128)(2,1)S(1)}, bf16[96,256]{1,0:T(8,128)(2,1)S(1)}, u32[]{:S(2)}, u32[]{:S(2)}) collective-permute-start(bf16[96,256]{1,0:T(8,128)(2,1)S(1)} %get-tuple-element.34), channel_id=1, source_target_pairs={{0,4},{1,5},{2,6},{3,7},{4,0},{5,1},{6,2},{7,3},{8,12},{9,13},{10,... | collective-permute-start | bytes 147464 | tf_op jit(solution)/shard_map/ppermute | solution.py:31
  23.9 0.5 %collective-permute-start.12 = (bf16[1,3,48,256]{3,2,1,0:T(8,128)(2,1)S(1)}, bf16[1,3,48,256]{3,2,1,0:T(8,128)(2,1)S(1)}, u32[]{:S(2)}, u32[]{:S(2)}) collective-permute-start(bf16[1,3,48,256]{3,2,1,0:T(8,128)(2,1)S(1)} %fusion.7), channel_id=1, source_target_pairs={{0,2},{1,3},{2,0},{3,1},{4,6},{5,7},{6,4},{7,5},{8,10},{9,11},{10,... | collective-permute-start | bytes 221192 | tf_op jit(solution)/shard_map/ppermute | solution.py:31
  24.4 1.1 %collective-permute-done.13 = bf16[96,256]{1,0:T(8,128)(2,1)S(1)} collective-permute-done((bf16[96,256]{1,0:T(8,128)(2,1)S(1)}, bf16[96,256]{1,0:T(8,128)(2,1)S(1)}, u32[]{:S(2)}, u32[]{:S(2)}) %collective-permute-start.13) | collective-permute-done | bytes 49184 | tf_op jit(solution)/shard_map/ppermute | solution.py:31
  25.5 0.9 %collective-permute-done.15 = bf16[96,256]{1,0:T(8,128)(2,1)S(1)} collective-permute-done((bf16[96,256]{1,0:T(8,128)(2,1)S(1)}, bf16[96,256]{1,0:T(8,128)(2,1)S(1)}, u32[]{:S(2)}, u32[]{:S(2)}) %collective-permute-start.15) | collective-permute-done | bytes 49184 | tf_op jit(solution)/shard_map/ppermute | solution.py:31
  26.5 0.7 %collective-permute-done.14 = bf16[96,256]{1,0:T(8,128)(2,1)S(1)} collective-permute-done((bf16[96,256]{1,0:T(8,128)(2,1)S(1)}, bf16[96,256]{1,0:T(8,128)(2,1)S(1)}, u32[]{:S(2)}, u32[]{:S(2)}) %collective-permute-start.14) | collective-permute-done | bytes 49184 | tf_op jit(solution)/shard_map/ppermute | solution.py:31
  27.2 2.1 %collective-permute-start.18 = (bf16[96,256]{1,0:T(8,128)(2,1)S(1)}, bf16[96,256]{1,0:T(8,128)(2,1)S(1)}, u32[]{:S(2)}, u32[]{:S(2)}) collective-permute-start(bf16[96,256]{1,0:T(8,128)(2,1)S(1)} %fusion.5), channel_id=1, source_target_pairs={{0,24},{4,28},{8,16},{12,20},{16,8},{20,12},{24,0},{28,4},{1,25},{... | collective-permute-start | bytes 147464 | tf_op jit(solution)/shard_map/ppermute | solution.py:31
  29.3 2.4 %collective-permute-start.16 = (bf16[96,256]{1,0:T(8,128)(2,1)S(1)}, bf16[96,256]{1,0:T(8,128)(2,1)S(1)}, u32[]{:S(2)}, u32[]{:S(2)}) collective-permute-start(bf16[96,256]{1,0:T(8,128)(2,1)S(1)} %fusion.5), channel_id=1, source_target_pairs={{0,16},{4,20},{8,24},{12,28},{16,0},{20,4},{24,8},{28,12},{1,17},{... | collective-permute-start | bytes 147464 | tf_op jit(solution)/shard_map/ppermute | solution.py:31
  31.6 1.6 %collective-permute-done.18 = bf16[96,256]{1,0:T(8,128)(2,1)S(1)} collective-permute-done((bf16[96,256]{1,0:T(8,128)(2,1)S(1)}, bf16[96,256]{1,0:T(8,128)(2,1)S(1)}, u32[]{:S(2)}, u32[]{:S(2)}) %collective-permute-start.18) | collective-permute-done | bytes 49184 | tf_op jit(solution)/shard_map/ppermute | solution.py:31
  33.3 0.5 %collective-permute-done.17 = bf16[96,256]{1,0:T(8,128)(2,1)S(1)} collective-permute-done((bf16[96,256]{1,0:T(8,128)(2,1)S(1)}, bf16[96,256]{1,0:T(8,128)(2,1)S(1)}, u32[]{:S(2)}, u32[]{:S(2)}) %collective-permute-start.17) | collective-permute-done | bytes 49184 | tf_op jit(solution)/shard_map/ppermute | solution.py:31
  33.8 0.8 %collective-permute-done.16 = bf16[96,256]{1,0:T(8,128)(2,1)S(1)} collective-permute-done((bf16[96,256]{1,0:T(8,128)(2,1)S(1)}, bf16[96,256]{1,0:T(8,128)(2,1)S(1)}, u32[]{:S(2)}, u32[]{:S(2)}) %collective-permute-start.16) | collective-permute-done | bytes 49184 | tf_op jit(solution)/shard_map/ppermute | solution.py:31
  34.6 2.1 %collective-permute-start.21 = (bf16[96,256]{1,0:T(8,128)(2,1)S(1)}, bf16[96,256]{1,0:T(8,128)(2,1)S(1)}, u32[]{:S(2)}, u32[]{:S(2)}) collective-permute-start(bf16[96,256]{1,0:T(8,128)(2,1)S(1)} %add_convert_fusion), channel_id=1, source_target_pairs={{0,6},{1,7},{2,4},{3,5},{4,2},{5,3},{6,0},{7,1},{8,14},{9,15},{10,... | collective-permute-start | bytes 147464 | tf_op jit(solution)/shard_map/ppermute | solution.py:31
  36.7 0.6 %collective-permute-start.20 = (bf16[96,256]{1,0:T(8,128)(2,1)S(1)}, bf16[96,256]{1,0:T(8,128)(2,1)S(1)}, u32[]{:S(2)}, u32[]{:S(2)}) collective-permute-start(bf16[96,256]{1,0:T(8,128)(2,1)S(1)} %add_convert_fusion), channel_id=1, source_target_pairs={{0,2},{1,3},{2,0},{3,1},{4,6},{5,7},{6,4},{7,5},{8,10},{9,11},{10,... | collective-permute-start | bytes 147464 | tf_op jit(solution)/shard_map/ppermute | solution.py:31
  37.3 0.9 %collective-permute-start.19 = (bf16[96,256]{1,0:T(8,128)(2,1)S(1)}, bf16[96,256]{1,0:T(8,128)(2,1)S(1)}, u32[]{:S(2)}, u32[]{:S(2)}) collective-permute-start(bf16[96,256]{1,0:T(8,128)(2,1)S(1)} %add_convert_fusion), channel_id=1, source_target_pairs={{0,4},{1,5},{2,6},{3,7},{4,0},{5,1},{6,2},{7,3},{8,12},{9,13},{10,... | collective-permute-start | bytes 147464 | tf_op jit(solution)/shard_map/ppermute | solution.py:31
  38.2 1.5 %collective-permute-done.21 = bf16[96,256]{1,0:T(8,128)(2,1)S(1)} collective-permute-done((bf16[96,256]{1,0:T(8,128)(2,1)S(1)}, bf16[96,256]{1,0:T(8,128)(2,1)S(1)}, u32[]{:S(2)}, u32[]{:S(2)}) %collective-permute-start.21) | collective-permute-done | bytes 49184 | tf_op jit(solution)/shard_map/ppermute | solution.py:31
  39.7 1.1 %collective-permute-done.20 = bf16[96,256]{1,0:T(8,128)(2,1)S(1)} collective-permute-done((bf16[96,256]{1,0:T(8,128)(2,1)S(1)}, bf16[96,256]{1,0:T(8,128)(2,1)S(1)}, u32[]{:S(2)}, u32[]{:S(2)}) %collective-permute-start.20) | collective-permute-done | bytes 49184 | tf_op jit(solution)/shard_map/ppermute | solution.py:31
  40.8 0.6 %collective-permute-done.19 = bf16[96,256]{1,0:T(8,128)(2,1)S(1)} collective-permute-done((bf16[96,256]{1,0:T(8,128)(2,1)S(1)}, bf16[96,256]{1,0:T(8,128)(2,1)S(1)}, u32[]{:S(2)}, u32[]{:S(2)}) %collective-permute-start.19) | collective-permute-done | bytes 49184 | tf_op jit(solution)/shard_map/ppermute | solution.py:31
  41.5 0.6 %fusion.6 = bf16[3,48,256]{2,1,0:T(8,128)(2,1)} fusion(bf16[1,3,48,256]{3,2,1,0:T(8,128)(2,1)S(1)} %collective-permute-done.12, f32[1,2,3,48,256]{4,3,2,1,0:T(8,128)S(1)} %add_bitcast_fusion), kind=kLoop, calls=%fused_computation.13 | loop fusion | flops 110592 | bytes 294912 | tf_op jit(solution)/shard_map/convert_element_type | solution.py:221
  42.1 0.8 %collective-permute-done.22.there_ref = bf16[4,96,256]{2,1,0:T(8,128)(2,1)S(1)} collective-permute-done((bf16[4,96,256]{2,1,0:T(8,128)(2,1)S(1)}, bf16[4,96,256]{2,1,0:T(8,128)(2,1)S(1)}, u32[]{:S(2)}, u32[]{:S(2)}) %collective-permute-start.22) | collective-permute-done | bytes 196640 | tf_op jit(solution)/shard_map/ppermute | solution.py:31
  42.9 0.9 %shard_map.70 = f32[768,256]{1,0:T(8,128)} custom-call(bf16[4,96,256]{2,1,0:T(8,128)(2,1)S(1)} %pad_maximum_fusion.here_ref, bf16[4,96,256]{2,1,0:T(8,128)(2,1)S(1)} %collective-permute-done.22.there_ref), custom_call_target="tpu_custom_call" | custom-call | tf_op jit(solution)/shard_map/pallas_call | solution.py:243
  (25 shorter events, 2.1 us)
Async XLA Ops:
  0.6 9.1 %collective-permute-start.3 = (bf16[3,48,256]{2,1,0:T(8,128)(2,1)}, bf16[3,48,256]{2,1,0:T(8,128)(2,1)S(1)}, u32[]{:S(2)}, u32[]{:S(2)}) collective-permute-start(bf16[3,48,256]{2,1,0:T(8,128)(2,1)} %refs_2_.1), channel_id=1, source_target_pairs={{0,16},{4,20},{8,24},{12,28},{16,0},{20,4},{24,8},{28,12},{1,17},{... | collective-permute-start | bytes 221192 | tf_op jit(solution)/shard_map/ppermute | solution.py:31
  4.7 7.5 %collective-permute-start.7 = (bf16[3,48,256]{2,1,0:T(8,128)(2,1)}, bf16[3,48,256]{2,1,0:T(8,128)(2,1)S(1)}, u32[]{:S(2)}, u32[]{:S(2)}) collective-permute-start(bf16[3,48,256]{2,1,0:T(8,128)(2,1)} %refs_2_.1), channel_id=1, source_target_pairs={{0,2},{1,3},{2,0},{3,1},{4,6},{5,7},{6,4},{7,5},{8,10},{9,11},{10,... | collective-permute-start | bytes 221192 | tf_op jit(solution)/shard_map/ppermute | solution.py:31
  6.3 6.5 %collective-permute-start.2 = (bf16[3,48,256]{2,1,0:T(8,128)(2,1)}, bf16[3,48,256]{2,1,0:T(8,128)(2,1)S(1)}, u32[]{:S(2)}, u32[]{:S(2)}) collective-permute-start(bf16[3,48,256]{2,1,0:T(8,128)(2,1)} %refs_2_.1), channel_id=1, source_target_pairs={{0,12},{4,8},{8,4},{12,0},{16,28},{20,24},{24,20},{28,16},{1,13},{... | collective-permute-start | bytes 221192 | tf_op jit(solution)/shard_map/ppermute | solution.py:31
  8.8 5.4 %collective-permute-start.1 = (bf16[3,48,256]{2,1,0:T(8,128)(2,1)}, bf16[3,48,256]{2,1,0:T(8,128)(2,1)S(1)}, u32[]{:S(2)}, u32[]{:S(2)}) collective-permute-start(bf16[3,48,256]{2,1,0:T(8,128)(2,1)} %refs_2_.1), channel_id=1, source_target_pairs={{0,8},{4,12},{8,0},{12,4},{16,24},{20,28},{24,16},{28,20},{1,9},{5... | collective-permute-start | bytes 221192 | tf_op jit(solution)/shard_map/ppermute | solution.py:31
  9.2 6.2 %collective-permute-start = (bf16[3,48,256]{2,1,0:T(8,128)(2,1)}, bf16[3,48,256]{2,1,0:T(8,128)(2,1)S(1)}, u32[]{:S(2)}, u32[]{:S(2)}) collective-permute-start(bf16[3,48,256]{2,1,0:T(8,128)(2,1)} %refs_2_.1), channel_id=1, source_target_pairs={{0,4},{4,0},{8,12},{12,8},{16,20},{20,16},{24,28},{28,24},{1,5},{5... | collective-permute-start | bytes 221192 | tf_op jit(solution)/shard_map/ppermute | solution.py:31
  9.7 7.0 %collective-permute-start.6 = (bf16[1,3,48,256]{3,2,1,0:T(8,128)(2,1)S(1)}, bf16[1,3,48,256]{3,2,1,0:T(8,128)(2,1)S(1)}, u32[]{:S(2)}, u32[]{:S(2)}) collective-permute-start(bf16[1,3,48,256]{3,2,1,0:T(8,128)(2,1)S(1)} %bitcast.45), channel_id=1, source_target_pairs={{0,12},{4,8},{8,4},{12,0},{16,28},{20,24},{24,20},{28,16},{1,13},{... | collective-permute-start | bytes 221192 | tf_op jit(solution)/shard_map/ppermute | solution.py:31
  12.3 4.5 %collective-permute-start.5 = (bf16[1,3,48,256]{3,2,1,0:T(8,128)(2,1)S(1)}, bf16[1,3,48,256]{3,2,1,0:T(8,128)(2,1)S(1)}, u32[]{:S(2)}, u32[]{:S(2)}) collective-permute-start(bf16[1,3,48,256]{3,2,1,0:T(8,128)(2,1)S(1)} %bitcast.46), channel_id=1, source_target_pairs={{0,8},{4,12},{8,0},{12,4},{16,24},{20,28},{24,16},{28,20},{1,9},{5... | collective-permute-start | bytes 221192 | tf_op jit(solution)/shard_map/ppermute | solution.py:31
  12.7 4.4 %collective-permute-start.4 = (bf16[1,3,48,256]{3,2,1,0:T(8,128)(2,1)S(1)}, bf16[1,3,48,256]{3,2,1,0:T(8,128)(2,1)S(1)}, u32[]{:S(2)}, u32[]{:S(2)}) collective-permute-start(bf16[1,3,48,256]{3,2,1,0:T(8,128)(2,1)S(1)} %bitcast.47), channel_id=1, source_target_pairs={{0,4},{4,0},{8,12},{12,8},{16,20},{20,16},{24,28},{28,24},{1,5},{5... | collective-permute-start | bytes 221192 | tf_op jit(solution)/shard_map/ppermute | solution.py:31
  14.2 2.9 %collective-permute-start.8 = (bf16[3,48,256]{2,1,0:T(8,128)(2,1)}, bf16[3,48,256]{2,1,0:T(8,128)(2,1)S(1)}, u32[]{:S(2)}, u32[]{:S(2)}) collective-permute-start(bf16[3,48,256]{2,1,0:T(8,128)(2,1)} %refs_2_.1), channel_id=1, source_target_pairs={{0,1},{1,0},{2,3},{3,2},{4,5},{5,4},{6,7},{7,6},{8,9},{9,8},{10,11... | collective-permute-start | bytes 221192 | tf_op jit(solution)/shard_map/ppermute | solution.py:31
  15.4 1.7 %collective-permute-start.9 = (bf16[3,48,256]{2,1,0:T(8,128)(2,1)S(1)}, bf16[3,48,256]{2,1,0:T(8,128)(2,1)S(1)}, u32[]{:S(2)}, u32[]{:S(2)}) collective-permute-start(bf16[3,48,256]{2,1,0:T(8,128)(2,1)S(1)} %collective-permute-done.7), channel_id=1, source_target_pairs={{0,1},{1,0},{2,3},{3,2},{4,5},{5,4},{6,7},{7,6},{8,9},{9,8},{10,11... | collective-permute-start | bytes 221192 | tf_op jit(solution)/shard_map/ppermute | solution.py:31
  18.5 1.4 %collective-permute-start.10 = (bf16[2,3,48,256]{3,2,1,0:T(8,128)(2,1)S(1)}, bf16[2,3,48,256]{3,2,1,0:T(8,128)(2,1)S(1)}, u32[]{:S(2)}, u32[]{:S(2)}) collective-permute-start(bf16[2,3,48,256]{3,2,1,0:T(8,128)(2,1)S(1)} %get-tuple-element.23), channel_id=1, source_target_pairs={{0,1},{1,0},{2,3},{3,2},{4,5},{5,4},{6,7},{7,6},{8,9},{9,8},{10,11... | collective-permute-start | bytes 442376 | tf_op jit(solution)/shard_map/ppermute | solution.py:31
  18.8 1.4 %collective-permute-start.11 = (bf16[4,96,256]{2,1,0:T(8,128)(2,1)S(1)}, bf16[4,96,256]{2,1,0:T(8,128)(2,1)S(1)}, u32[]{:S(2)}, u32[]{:S(2)}) collective-permute-start(bf16[4,96,256]{2,1,0:T(8,128)(2,1)S(1)} %get-tuple-element.25), channel_id=1, source_target_pairs={{0,1},{1,0},{2,3},{3,2},{4,5},{5,4},{6,7},{7,6},{8,9},{9,8},{10,11... | collective-permute-start | bytes 589832 | tf_op jit(solution)/shard_map/ppermute | solution.py:31
  20.3 5.2 %collective-permute-start.13 = (bf16[96,256]{1,0:T(8,128)(2,1)S(1)}, bf16[96,256]{1,0:T(8,128)(2,1)S(1)}, u32[]{:S(2)}, u32[]{:S(2)}) collective-permute-start(bf16[96,256]{1,0:T(8,128)(2,1)S(1)} %get-tuple-element.32), channel_id=1, source_target_pairs={{0,6},{1,7},{2,4},{3,5},{4,2},{5,3},{6,0},{7,1},{8,14},{9,15},{10,... | collective-permute-start | bytes 147464 | tf_op jit(solution)/shard_map/ppermute | solution.py:31
  21.6 4.9 %collective-permute-start.15 = (bf16[96,256]{1,0:T(8,128)(2,1)S(1)}, bf16[96,256]{1,0:T(8,128)(2,1)S(1)}, u32[]{:S(2)}, u32[]{:S(2)}) collective-permute-start(bf16[96,256]{1,0:T(8,128)(2,1)S(1)} %get-tuple-element.33), channel_id=1, source_target_pairs={{0,2},{1,3},{2,0},{3,1},{4,6},{5,7},{6,4},{7,5},{8,10},{9,11},{10,... | collective-permute-start | bytes 147464 | tf_op jit(solution)/shard_map/ppermute | solution.py:31
  23.1 4.1 %collective-permute-start.14 = (bf16[96,256]{1,0:T(8,128)(2,1)S(1)}, bf16[96,256]{1,0:T(8,128)(2,1)S(1)}, u32[]{:S(2)}, u32[]{:S(2)}) collective-permute-start(bf16[96,256]{1,0:T(8,128)(2,1)S(1)} %get-tuple-element.34), channel_id=1, source_target_pairs={{0,4},{1,5},{2,6},{3,7},{4,0},{5,1},{6,2},{7,3},{8,12},{9,13},{10,... | collective-permute-start | bytes 147464 | tf_op jit(solution)/shard_map/ppermute | solution.py:31
  23.9 7.7 %collective-permute-start.12 = (bf16[1,3,48,256]{3,2,1,0:T(8,128)(2,1)S(1)}, bf16[1,3,48,256]{3,2,1,0:T(8,128)(2,1)S(1)}, u32[]{:S(2)}, u32[]{:S(2)}) collective-permute-start(bf16[1,3,48,256]{3,2,1,0:T(8,128)(2,1)S(1)} %fusion.7), channel_id=1, source_target_pairs={{0,2},{1,3},{2,0},{3,1},{4,6},{5,7},{6,4},{7,5},{8,10},{9,11},{10,... | collective-permute-start | bytes 221192 | tf_op jit(solution)/shard_map/ppermute | solution.py:31
  27.2 6.1 %collective-permute-start.18 = (bf16[96,256]{1,0:T(8,128)(2,1)S(1)}, bf16[96,256]{1,0:T(8,128)(2,1)S(1)}, u32[]{:S(2)}, u32[]{:S(2)}) collective-permute-start(bf16[96,256]{1,0:T(8,128)(2,1)S(1)} %fusion.5), channel_id=1, source_target_pairs={{0,24},{4,28},{8,16},{12,20},{16,8},{20,12},{24,0},{28,4},{1,25},{... | collective-permute-start | bytes 147464 | tf_op jit(solution)/shard_map/ppermute | solution.py:31
  29.3 4.5 %collective-permute-start.17 = (bf16[96,256]{1,0:T(8,128)(2,1)S(1)}, bf16[96,256]{1,0:T(8,128)(2,1)S(1)}, u32[]{:S(2)}, u32[]{:S(2)}) collective-permute-start(bf16[96,256]{1,0:T(8,128)(2,1)S(1)} %fusion.5), channel_id=1, source_target_pairs={{0,8},{4,12},{8,0},{12,4},{16,24},{20,28},{24,16},{28,20},{1,9},{5... | collective-permute-start | bytes 147464 | tf_op jit(solution)/shard_map/ppermute | solution.py:31
  29.3 5.3 %collective-permute-start.16 = (bf16[96,256]{1,0:T(8,128)(2,1)S(1)}, bf16[96,256]{1,0:T(8,128)(2,1)S(1)}, u32[]{:S(2)}, u32[]{:S(2)}) collective-permute-start(bf16[96,256]{1,0:T(8,128)(2,1)S(1)} %fusion.5), channel_id=1, source_target_pairs={{0,16},{4,20},{8,24},{12,28},{16,0},{20,4},{24,8},{28,12},{1,17},{... | collective-permute-start | bytes 147464 | tf_op jit(solution)/shard_map/ppermute | solution.py:31
  34.6 5.1 %collective-permute-start.21 = (bf16[96,256]{1,0:T(8,128)(2,1)S(1)}, bf16[96,256]{1,0:T(8,128)(2,1)S(1)}, u32[]{:S(2)}, u32[]{:S(2)}) collective-permute-start(bf16[96,256]{1,0:T(8,128)(2,1)S(1)} %add_convert_fusion), channel_id=1, source_target_pairs={{0,6},{1,7},{2,4},{3,5},{4,2},{5,3},{6,0},{7,1},{8,14},{9,15},{10,... | collective-permute-start | bytes 147464 | tf_op jit(solution)/shard_map/ppermute | solution.py:31
  36.7 4.1 %collective-permute-start.20 = (bf16[96,256]{1,0:T(8,128)(2,1)S(1)}, bf16[96,256]{1,0:T(8,128)(2,1)S(1)}, u32[]{:S(2)}, u32[]{:S(2)}) collective-permute-start(bf16[96,256]{1,0:T(8,128)(2,1)S(1)} %add_convert_fusion), channel_id=1, source_target_pairs={{0,2},{1,3},{2,0},{3,1},{4,6},{5,7},{6,4},{7,5},{8,10},{9,11},{10,... | collective-permute-start | bytes 147464 | tf_op jit(solution)/shard_map/ppermute | solution.py:31
  37.3 4.1 %collective-permute-start.19 = (bf16[96,256]{1,0:T(8,128)(2,1)S(1)}, bf16[96,256]{1,0:T(8,128)(2,1)S(1)}, u32[]{:S(2)}, u32[]{:S(2)}) collective-permute-start(bf16[96,256]{1,0:T(8,128)(2,1)S(1)} %add_convert_fusion), channel_id=1, source_target_pairs={{0,4},{1,5},{2,6},{3,7},{4,0},{5,1},{6,2},{7,3},{8,12},{9,13},{10,... | collective-permute-start | bytes 147464 | tf_op jit(solution)/shard_map/ppermute | solution.py:31
  41.4 1.5 %collective-permute-start.22 = (bf16[4,96,256]{2,1,0:T(8,128)(2,1)S(1)}, bf16[4,96,256]{2,1,0:T(8,128)(2,1)S(1)}, u32[]{:S(2)}, u32[]{:S(2)}) collective-permute-start(bf16[4,96,256]{2,1,0:T(8,128)(2,1)S(1)} %pad_maximum_fusion.here_ref), channel_id=1, source_target_pairs={{0,1},{1,0},{2,3},{3,2},{4,5},{5,4},{6,7},{7,6},{8,9},{9,8},{10,11... | collective-permute-start | bytes 589832 | tf_op jit(solution)/shard_map/ppermute | solution.py:31

commit v6 on v5

--- a/solution.py
+++ b/solution.py
@@ -190,7 +190,7 @@
         functools.partial(main_kernel, along_row, along_col),
         out_shape=[
             jax.ShapeDtypeStruct((cols // 2, panels, height, width), F32),
-            jax.ShapeDtypeStruct((cols // 2, panels, height, width), BF16),
+            jax.ShapeDtypeStruct((cols // 2, panels, height, width), F32),
             jax.ShapeDtypeStruct((4, piece, width), F32),
             jax.ShapeDtypeStruct((4, piece, width), BF16),
         ],

time: 44 us -> 43.8 us (level)
  transfers between devices with their start and end apart: 23 -> 23, of which waited for: 15 -> 14; matrix products, arithmetic and copies ran while one was open for 2% -> 2% of each run, Pallas kernels for 3% -> 3%
where the time goes in v6:
time: 43.8 us; the launch traced here: 43.7 us
  starting transfers between devices  26.1 us (60%)
  waiting for transfers between devices  12.3 us (28%)
  Pallas kernels  3.74 us (9%)
  other arithmetic  0.83 us (2%)
  between operations  0.73 us (2%)
    ppermute x23, starting transfers between devices, swap(): return lax.ppermute(value, axes, pairs)  26.1 us
    ppermute x23, waiting for transfers between devices, swap(): return lax.ppermute(value, axes, pairs)  12.3 us
    pallas_call x1, Pallas kernels, body(): pl.pallas_call(functools.partial(main_kernel, along_row, along_col), out_...  1.43 us
    pallas_call x1, Pallas kernels, body(): pl.pallas_call(prepare_kernel, out_shape=[jax.ShapeDtypeStruct(value.shap...  1.36 us
    pallas_call x1, Pallas kernels, body(): pl.pallas_call(finish_kernel, out_shape=jax.ShapeDtypeStruct((panels * wi...  0.94 us
  transfers between devices with their start and end apart: 23, of which 14 were waited for; matrix products, arithmetic and copies ran while one was open for 2% of the time, Pallas kernels for 3%

profile of v6, /device:TPU:0, one launch (start us, length us, event | category | flops | bytes accessed | tf_op | source)
XLA Modules:
  0.0 43.7 jit_solution(9164576213968228764)
XLA Ops:
  0.6 4.1 %collective-permute-start.3 = (bf16[3,48,256]{2,1,0:T(8,128)(2,1)}, bf16[3,48,256]{2,1,0:T(8,128)(2,1)S(1)}, u32[]{:S(2)}, u32[]{:S(2)}) collective-permute-start(bf16[3,48,256]{2,1,0:T(8,128)(2,1)} %refs_2_.1), channel_id=1, source_target_pairs={{0,16},{4,20},{8,24},{12,28},{16,0},{20,4},{24,8},{28,12},{1,17},{... | collective-permute-start | bytes 221192 | tf_op jit(solution)/shard_map/ppermute | solution.py:31
  4.7 1.5 %collective-permute-start.7 = (bf16[3,48,256]{2,1,0:T(8,128)(2,1)}, bf16[3,48,256]{2,1,0:T(8,128)(2,1)S(1)}, u32[]{:S(2)}, u32[]{:S(2)}) collective-permute-start(bf16[3,48,256]{2,1,0:T(8,128)(2,1)} %refs_2_.1), channel_id=1, source_target_pairs={{0,2},{1,3},{2,0},{3,1},{4,6},{5,7},{6,4},{7,5},{8,10},{9,11},{10,... | collective-permute-start | bytes 221192 | tf_op jit(solution)/shard_map/ppermute | solution.py:31
  6.3 2.5 %collective-permute-start.2 = (bf16[3,48,256]{2,1,0:T(8,128)(2,1)}, bf16[3,48,256]{2,1,0:T(8,128)(2,1)S(1)}, u32[]{:S(2)}, u32[]{:S(2)}) collective-permute-start(bf16[3,48,256]{2,1,0:T(8,128)(2,1)} %refs_2_.1), channel_id=1, source_target_pairs={{0,12},{4,8},{8,4},{12,0},{16,28},{20,24},{24,20},{28,16},{1,13},{... | collective-permute-start | bytes 221192 | tf_op jit(solution)/shard_map/ppermute | solution.py:31
  8.8 0.4 %collective-permute-start.1 = (bf16[3,48,256]{2,1,0:T(8,128)(2,1)}, bf16[3,48,256]{2,1,0:T(8,128)(2,1)S(1)}, u32[]{:S(2)}, u32[]{:S(2)}) collective-permute-start(bf16[3,48,256]{2,1,0:T(8,128)(2,1)} %refs_2_.1), channel_id=1, source_target_pairs={{0,8},{4,12},{8,0},{12,4},{16,24},{20,28},{24,16},{28,20},{1,9},{5... | collective-permute-start | bytes 221192 | tf_op jit(solution)/shard_map/ppermute | solution.py:31
  9.2 0.5 %collective-permute-start = (bf16[3,48,256]{2,1,0:T(8,128)(2,1)}, bf16[3,48,256]{2,1,0:T(8,128)(2,1)S(1)}, u32[]{:S(2)}, u32[]{:S(2)}) collective-permute-start(bf16[3,48,256]{2,1,0:T(8,128)(2,1)} %refs_2_.1), channel_id=1, source_target_pairs={{0,4},{4,0},{8,12},{12,8},{16,20},{20,16},{24,28},{28,24},{1,5},{5... | collective-permute-start | bytes 221192 | tf_op jit(solution)/shard_map/ppermute | solution.py:31
  9.7 2.5 %collective-permute-start.6 = (bf16[1,3,48,256]{3,2,1,0:T(8,128)(2,1)S(1)}, bf16[1,3,48,256]{3,2,1,0:T(8,128)(2,1)S(1)}, u32[]{:S(2)}, u32[]{:S(2)}) collective-permute-start(bf16[1,3,48,256]{3,2,1,0:T(8,128)(2,1)S(1)} %bitcast.45), channel_id=1, source_target_pairs={{0,12},{4,8},{8,4},{12,0},{16,28},{20,24},{24,20},{28,16},{1,13},{... | collective-permute-start | bytes 221192 | tf_op jit(solution)/shard_map/ppermute | solution.py:31
  12.3 0.5 %collective-permute-start.5 = (bf16[1,3,48,256]{3,2,1,0:T(8,128)(2,1)S(1)}, bf16[1,3,48,256]{3,2,1,0:T(8,128)(2,1)S(1)}, u32[]{:S(2)}, u32[]{:S(2)}) collective-permute-start(bf16[1,3,48,256]{3,2,1,0:T(8,128)(2,1)S(1)} %bitcast.46), channel_id=1, source_target_pairs={{0,8},{4,12},{8,0},{12,4},{16,24},{20,28},{24,16},{28,20},{1,9},{5... | collective-permute-start | bytes 221192 | tf_op jit(solution)/shard_map/ppermute | solution.py:31
  12.7 1.2 %collective-permute-start.4 = (bf16[1,3,48,256]{3,2,1,0:T(8,128)(2,1)S(1)}, bf16[1,3,48,256]{3,2,1,0:T(8,128)(2,1)S(1)}, u32[]{:S(2)}, u32[]{:S(2)}) collective-permute-start(bf16[1,3,48,256]{3,2,1,0:T(8,128)(2,1)S(1)} %bitcast.47), channel_id=1, source_target_pairs={{0,4},{4,0},{8,12},{12,8},{16,20},{20,16},{24,28},{28,24},{1,5},{5... | collective-permute-start | bytes 221192 | tf_op jit(solution)/shard_map/ppermute | solution.py:31
  14.2 1.2 %collective-permute-done = bf16[3,48,256]{2,1,0:T(8,128)(2,1)S(1)} collective-permute-done((bf16[3,48,256]{2,1,0:T(8,128)(2,1)}, bf16[3,48,256]{2,1,0:T(8,128)(2,1)S(1)}, u32[]{:S(2)}, u32[]{:S(2)}) %collective-permute-start) | collective-permute-done | bytes 73760 | tf_op jit(solution)/shard_map/ppermute | solution.py:31
  15.4 1.4 %shard_map.68 = (bf16[192,384]{1,0:T(8,128)(2,1)S(1)}, bf16[3,48,256]{2,1,0:T(8,128)(2,1)S(1)}, bf16[3,48,256]{2,1,0:T(8,128)(2,1)S(1)}, bf16[3,256,256]{2,1,0:T(8,128)(2,1)S(1)}, bf16[3,256,256]{2,1,0:T(8,128)(2,1)S(1)}) custom-call(f32[3,256,256]{2,1,0:T(8,128)} %refs_0_.1, bf16[192,384]{1,0:T(8,128)(2,1)} %refs_1_.1, bf16[3,48,256]{2,1,0:T(8,128)(2,1)} %refs_2_.1, ...), custom_call_target="tpu_custom_call" | custom-call | tf_op jit(solution)/shard_map/pallas_call | solution.py:177
  17.1 1.4 %shard_map.69 = (f32[2,3,48,256]{3,2,1,0:T(8,128)S(1)}, f32[2,3,48,256]{3,2,1,0:T(8,128)S(1)}, f32[4,96,256]{2,1,0:T(8,128)S(1)}, bf16[4,96,256]{2,1,0:T(8,128)(2,1)S(1)}) custom-call(bf16[1,3,48,256]{3,2,1,0:T(8,128)(2,1)S(1)} %bitcast.43, bf16[1,3,48,256]{3,2,1,0:T(8,128)(2,1)S(1)} %bitcast.52, bf16[1,3,48,256]{3,2,1,0:T(8,128)(2,1)S(1)} %bitcast.51, ...), custom_call_target="tpu_custom_call" | custom-call | tf_op jit(solution)/shard_map/pallas_call | solution.py:189
  19.1 0.9 %collective-permute-done.11 = bf16[4,96,256]{2,1,0:T(8,128)(2,1)S(1)} collective-permute-done((bf16[4,96,256]{2,1,0:T(8,128)(2,1)S(1)}, bf16[4,96,256]{2,1,0:T(8,128)(2,1)S(1)}, u32[]{:S(2)}, u32[]{:S(2)}) %collective-permute-start.11) | collective-permute-done | bytes 196640 | tf_op jit(solution)/shard_map/ppermute | solution.py:31
  20.1 1.3 %collective-permute-start.13 = (bf16[96,256]{1,0:T(8,128)(2,1)S(1)}, bf16[96,256]{1,0:T(8,128)(2,1)S(1)}, u32[]{:S(2)}, u32[]{:S(2)}) collective-permute-start(bf16[96,256]{1,0:T(8,128)(2,1)S(1)} %get-tuple-element.32), channel_id=1, source_target_pairs={{0,6},{1,7},{2,4},{3,5},{4,2},{5,3},{6,0},{7,1},{8,14},{9,15},{10,... | collective-permute-start | bytes 147464 | tf_op jit(solution)/shard_map/ppermute | solution.py:31
  21.4 1.5 %collective-permute-start.15 = (bf16[96,256]{1,0:T(8,128)(2,1)S(1)}, bf16[96,256]{1,0:T(8,128)(2,1)S(1)}, u32[]{:S(2)}, u32[]{:S(2)}) collective-permute-start(bf16[96,256]{1,0:T(8,128)(2,1)S(1)} %get-tuple-element.33), channel_id=1, source_target_pairs={{0,2},{1,3},{2,0},{3,1},{4,6},{5,7},{6,4},{7,5},{8,10},{9,11},{10,... | collective-permute-start | bytes 147464 | tf_op jit(solution)/shard_map/ppermute | solution.py:31
  22.9 0.8 %collective-permute-start.14 = (bf16[96,256]{1,0:T(8,128)(2,1)S(1)}, bf16[96,256]{1,0:T(8,128)(2,1)S(1)}, u32[]{:S(2)}, u32[]{:S(2)}) collective-permute-start(bf16[96,256]{1,0:T(8,128)(2,1)S(1)} %get-tuple-element.34), channel_id=1, source_target_pairs={{0,4},{1,5},{2,6},{3,7},{4,0},{5,1},{6,2},{7,3},{8,12},{9,13},{10,... | collective-permute-start | bytes 147464 | tf_op jit(solution)/shard_map/ppermute | solution.py:31
  23.7 0.6 %collective-permute-start.12 = (bf16[1,3,48,256]{3,2,1,0:T(8,128)(2,1)S(1)}, bf16[1,3,48,256]{3,2,1,0:T(8,128)(2,1)S(1)}, u32[]{:S(2)}, u32[]{:S(2)}) collective-permute-start(bf16[1,3,48,256]{3,2,1,0:T(8,128)(2,1)S(1)} %fusion.7), channel_id=1, source_target_pairs={{0,2},{1,3},{2,0},{3,1},{4,6},{5,7},{6,4},{7,5},{8,10},{9,11},{10,... | collective-permute-start | bytes 221192 | tf_op jit(solution)/shard_map/ppermute | solution.py:31
  24.3 1.1 %collective-permute-done.13 = bf16[96,256]{1,0:T(8,128)(2,1)S(1)} collective-permute-done((bf16[96,256]{1,0:T(8,128)(2,1)S(1)}, bf16[96,256]{1,0:T(8,128)(2,1)S(1)}, u32[]{:S(2)}, u32[]{:S(2)}) %collective-permute-start.13) | collective-permute-done | bytes 49184 | tf_op jit(solution)/shard_map/ppermute | solution.py:31
  25.4 0.6 %collective-permute-done.15 = bf16[96,256]{1,0:T(8,128)(2,1)S(1)} collective-permute-done((bf16[96,256]{1,0:T(8,128)(2,1)S(1)}, bf16[96,256]{1,0:T(8,128)(2,1)S(1)}, u32[]{:S(2)}, u32[]{:S(2)}) %collective-permute-start.15) | collective-permute-done | bytes 49184 | tf_op jit(solution)/shard_map/ppermute | solution.py:31
  26.1 0.9 %collective-permute-done.14 = bf16[96,256]{1,0:T(8,128)(2,1)S(1)} collective-permute-done((bf16[96,256]{1,0:T(8,128)(2,1)S(1)}, bf16[96,256]{1,0:T(8,128)(2,1)S(1)}, u32[]{:S(2)}, u32[]{:S(2)}) %collective-permute-start.14) | collective-permute-done | bytes 49184 | tf_op jit(solution)/shard_map/ppermute | solution.py:31
  27.0 2.0 %collective-permute-start.18 = (bf16[96,256]{1,0:T(8,128)(2,1)S(1)}, bf16[96,256]{1,0:T(8,128)(2,1)S(1)}, u32[]{:S(2)}, u32[]{:S(2)}) collective-permute-start(bf16[96,256]{1,0:T(8,128)(2,1)S(1)} %fusion.5), channel_id=1, source_target_pairs={{0,24},{4,28},{8,16},{12,20},{16,8},{20,12},{24,0},{28,4},{1,25},{... | collective-permute-start | bytes 147464 | tf_op jit(solution)/shard_map/ppermute | solution.py:31
  29.0 2.4 %collective-permute-start.16 = (bf16[96,256]{1,0:T(8,128)(2,1)S(1)}, bf16[96,256]{1,0:T(8,128)(2,1)S(1)}, u32[]{:S(2)}, u32[]{:S(2)}) collective-permute-start(bf16[96,256]{1,0:T(8,128)(2,1)S(1)} %fusion.5), channel_id=1, source_target_pairs={{0,16},{4,20},{8,24},{12,28},{16,0},{20,4},{24,8},{28,12},{1,17},{... | collective-permute-start | bytes 147464 | tf_op jit(solution)/shard_map/ppermute | solution.py:31
  31.4 1.7 %collective-permute-done.18 = bf16[96,256]{1,0:T(8,128)(2,1)S(1)} collective-permute-done((bf16[96,256]{1,0:T(8,128)(2,1)S(1)}, bf16[96,256]{1,0:T(8,128)(2,1)S(1)}, u32[]{:S(2)}, u32[]{:S(2)}) %collective-permute-start.18) | collective-permute-done | bytes 49184 | tf_op jit(solution)/shard_map/ppermute | solution.py:31
  33.5 0.7 %collective-permute-done.16 = bf16[96,256]{1,0:T(8,128)(2,1)S(1)} collective-permute-done((bf16[96,256]{1,0:T(8,128)(2,1)S(1)}, bf16[96,256]{1,0:T(8,128)(2,1)S(1)}, u32[]{:S(2)}, u32[]{:S(2)}) %collective-permute-start.16) | collective-permute-done | bytes 49184 | tf_op jit(solution)/shard_map/ppermute | solution.py:31
  34.2 2.3 %collective-permute-start.21 = (bf16[96,256]{1,0:T(8,128)(2,1)S(1)}, bf16[96,256]{1,0:T(8,128)(2,1)S(1)}, u32[]{:S(2)}, u32[]{:S(2)}) collective-permute-start(bf16[96,256]{1,0:T(8,128)(2,1)S(1)} %add_convert_fusion), channel_id=1, source_target_pairs={{0,6},{1,7},{2,4},{3,5},{4,2},{5,3},{6,0},{7,1},{8,14},{9,15},{10,... | collective-permute-start | bytes 147464 | tf_op jit(solution)/shard_map/ppermute | solution.py:31
  36.5 0.6 %collective-permute-start.20 = (bf16[96,256]{1,0:T(8,128)(2,1)S(1)}, bf16[96,256]{1,0:T(8,128)(2,1)S(1)}, u32[]{:S(2)}, u32[]{:S(2)}) collective-permute-start(bf16[96,256]{1,0:T(8,128)(2,1)S(1)} %add_convert_fusion), channel_id=1, source_target_pairs={{0,2},{1,3},{2,0},{3,1},{4,6},{5,7},{6,4},{7,5},{8,10},{9,11},{10,... | collective-permute-start | bytes 147464 | tf_op jit(solution)/shard_map/ppermute | solution.py:31
  37.1 0.7 %collective-permute-start.19 = (bf16[96,256]{1,0:T(8,128)(2,1)S(1)}, bf16[96,256]{1,0:T(8,128)(2,1)S(1)}, u32[]{:S(2)}, u32[]{:S(2)}) collective-permute-start(bf16[96,256]{1,0:T(8,128)(2,1)S(1)} %add_convert_fusion), channel_id=1, source_target_pairs={{0,4},{1,5},{2,6},{3,7},{4,0},{5,1},{6,2},{7,3},{8,12},{9,13},{10,... | collective-permute-start | bytes 147464 | tf_op jit(solution)/shard_map/ppermute | solution.py:31
  37.8 1.5 %collective-permute-done.21 = bf16[96,256]{1,0:T(8,128)(2,1)S(1)} collective-permute-done((bf16[96,256]{1,0:T(8,128)(2,1)S(1)}, bf16[96,256]{1,0:T(8,128)(2,1)S(1)}, u32[]{:S(2)}, u32[]{:S(2)}) %collective-permute-start.21) | collective-permute-done | bytes 49184 | tf_op jit(solution)/shard_map/ppermute | solution.py:31
  39.3 1.3 %collective-permute-done.20 = bf16[96,256]{1,0:T(8,128)(2,1)S(1)} collective-permute-done((bf16[96,256]{1,0:T(8,128)(2,1)S(1)}, bf16[96,256]{1,0:T(8,128)(2,1)S(1)}, u32[]{:S(2)}, u32[]{:S(2)}) %collective-permute-start.20) | collective-permute-done | bytes 49184 | tf_op jit(solution)/shard_map/ppermute | solution.py:31
  40.6 0.6 %collective-permute-done.19 = bf16[96,256]{1,0:T(8,128)(2,1)S(1)} collective-permute-done((bf16[96,256]{1,0:T(8,128)(2,1)S(1)}, bf16[96,256]{1,0:T(8,128)(2,1)S(1)}, u32[]{:S(2)}, u32[]{:S(2)}) %collective-permute-start.19) | collective-permute-done | bytes 49184 | tf_op jit(solution)/shard_map/ppermute | solution.py:31
  41.3 0.6 %fusion.6 = bf16[3,48,256]{2,1,0:T(8,128)(2,1)} fusion(bf16[1,3,48,256]{3,2,1,0:T(8,128)(2,1)S(1)} %collective-permute-done.12, f32[1,2,3,48,256]{4,3,2,1,0:T(8,128)S(1)} %add_bitcast_fusion), kind=kLoop, calls=%fused_computation.13 | loop fusion | flops 110592 | bytes 294912 | tf_op jit(solution)/shard_map/convert_element_type | solution.py:221
  41.9 0.8 %collective-permute-done.22.there_ref = bf16[4,96,256]{2,1,0:T(8,128)(2,1)S(1)} collective-permute-done((bf16[4,96,256]{2,1,0:T(8,128)(2,1)S(1)}, bf16[4,96,256]{2,1,0:T(8,128)(2,1)S(1)}, u32[]{:S(2)}, u32[]{:S(2)}) %collective-permute-start.22) | collective-permute-done | bytes 196640 | tf_op jit(solution)/shard_map/ppermute | solution.py:31
  42.7 0.9 %shard_map.70 = f32[768,256]{1,0:T(8,128)} custom-call(bf16[4,96,256]{2,1,0:T(8,128)(2,1)S(1)} %pad_maximum_fusion.here_ref, bf16[4,96,256]{2,1,0:T(8,128)(2,1)S(1)} %collective-permute-done.22.there_ref), custom_call_target="tpu_custom_call" | custom-call | tf_op jit(solution)/shard_map/pallas_call | solution.py:243
  (25 shorter events, 1.7 us)
Async XLA Ops:
  0.6 9.1 %collective-permute-start.3 = (bf16[3,48,256]{2,1,0:T(8,128)(2,1)}, bf16[3,48,256]{2,1,0:T(8,128)(2,1)S(1)}, u32[]{:S(2)}, u32[]{:S(2)}) collective-permute-start(bf16[3,48,256]{2,1,0:T(8,128)(2,1)} %refs_2_.1), channel_id=1, source_target_pairs={{0,16},{4,20},{8,24},{12,28},{16,0},{20,4},{24,8},{28,12},{1,17},{... | collective-permute-start | bytes 221192 | tf_op jit(solution)/shard_map/ppermute | solution.py:31
  4.7 7.5 %collective-permute-start.7 = (bf16[3,48,256]{2,1,0:T(8,128)(2,1)}, bf16[3,48,256]{2,1,0:T(8,128)(2,1)S(1)}, u32[]{:S(2)}, u32[]{:S(2)}) collective-permute-start(bf16[3,48,256]{2,1,0:T(8,128)(2,1)} %refs_2_.1), channel_id=1, source_target_pairs={{0,2},{1,3},{2,0},{3,1},{4,6},{5,7},{6,4},{7,5},{8,10},{9,11},{10,... | collective-permute-start | bytes 221192 | tf_op jit(solution)/shard_map/ppermute | solution.py:31
  6.3 6.5 %collective-permute-start.2 = (bf16[3,48,256]{2,1,0:T(8,128)(2,1)}, bf16[3,48,256]{2,1,0:T(8,128)(2,1)S(1)}, u32[]{:S(2)}, u32[]{:S(2)}) collective-permute-start(bf16[3,48,256]{2,1,0:T(8,128)(2,1)} %refs_2_.1), channel_id=1, source_target_pairs={{0,12},{4,8},{8,4},{12,0},{16,28},{20,24},{24,20},{28,16},{1,13},{... | collective-permute-start | bytes 221192 | tf_op jit(solution)/shard_map/ppermute | solution.py:31
  8.8 5.4 %collective-permute-start.1 = (bf16[3,48,256]{2,1,0:T(8,128)(2,1)}, bf16[3,48,256]{2,1,0:T(8,128)(2,1)S(1)}, u32[]{:S(2)}, u32[]{:S(2)}) collective-permute-start(bf16[3,48,256]{2,1,0:T(8,128)(2,1)} %refs_2_.1), channel_id=1, source_target_pairs={{0,8},{4,12},{8,0},{12,4},{16,24},{20,28},{24,16},{28,20},{1,9},{5... | collective-permute-start | bytes 221192 | tf_op jit(solution)/shard_map/ppermute | solution.py:31
  9.2 6.2 %collective-permute-start = (bf16[3,48,256]{2,1,0:T(8,128)(2,1)}, bf16[3,48,256]{2,1,0:T(8,128)(2,1)S(1)}, u32[]{:S(2)}, u32[]{:S(2)}) collective-permute-start(bf16[3,48,256]{2,1,0:T(8,128)(2,1)} %refs_2_.1), channel_id=1, source_target_pairs={{0,4},{4,0},{8,12},{12,8},{16,20},{20,16},{24,28},{28,24},{1,5},{5... | collective-permute-start | bytes 221192 | tf_op jit(solution)/shard_map/ppermute | solution.py:31
  9.7 7.0 %collective-permute-start.6 = (bf16[1,3,48,256]{3,2,1,0:T(8,128)(2,1)S(1)}, bf16[1,3,48,256]{3,2,1,0:T(8,128)(2,1)S(1)}, u32[]{:S(2)}, u32[]{:S(2)}) collective-permute-start(bf16[1,3,48,256]{3,2,1,0:T(8,128)(2,1)S(1)} %bitcast.45), channel_id=1, source_target_pairs={{0,12},{4,8},{8,4},{12,0},{16,28},{20,24},{24,20},{28,16},{1,13},{... | collective-permute-start | bytes 221192 | tf_op jit(solution)/shard_map/ppermute | solution.py:31
  12.3 4.5 %collective-permute-start.5 = (bf16[1,3,48,256]{3,2,1,0:T(8,128)(2,1)S(1)}, bf16[1,3,48,256]{3,2,1,0:T(8,128)(2,1)S(1)}, u32[]{:S(2)}, u32[]{:S(2)}) collective-permute-start(bf16[1,3,48,256]{3,2,1,0:T(8,128)(2,1)S(1)} %bitcast.46), channel_id=1, source_target_pairs={{0,8},{4,12},{8,0},{12,4},{16,24},{20,28},{24,16},{28,20},{1,9},{5... | collective-permute-start | bytes 221192 | tf_op jit(solution)/shard_map/ppermute | solution.py:31
  12.7 4.4 %collective-permute-start.4 = (bf16[1,3,48,256]{3,2,1,0:T(8,128)(2,1)S(1)}, bf16[1,3,48,256]{3,2,1,0:T(8,128)(2,1)S(1)}, u32[]{:S(2)}, u32[]{:S(2)}) collective-permute-start(bf16[1,3,48,256]{3,2,1,0:T(8,128)(2,1)S(1)} %bitcast.47), channel_id=1, source_target_pairs={{0,4},{4,0},{8,12},{12,8},{16,20},{20,16},{24,28},{28,24},{1,5},{5... | collective-permute-start | bytes 221192 | tf_op jit(solution)/shard_map/ppermute | solution.py:31
  14.2 2.9 %collective-permute-start.8 = (bf16[3,48,256]{2,1,0:T(8,128)(2,1)}, bf16[3,48,256]{2,1,0:T(8,128)(2,1)S(1)}, u32[]{:S(2)}, u32[]{:S(2)}) collective-permute-start(bf16[3,48,256]{2,1,0:T(8,128)(2,1)} %refs_2_.1), channel_id=1, source_target_pairs={{0,1},{1,0},{2,3},{3,2},{4,5},{5,4},{6,7},{7,6},{8,9},{9,8},{10,11... | collective-permute-start | bytes 221192 | tf_op jit(solution)/shard_map/ppermute | solution.py:31
  15.4 1.7 %collective-permute-start.9 = (bf16[3,48,256]{2,1,0:T(8,128)(2,1)S(1)}, bf16[3,48,256]{2,1,0:T(8,128)(2,1)S(1)}, u32[]{:S(2)}, u32[]{:S(2)}) collective-permute-start(bf16[3,48,256]{2,1,0:T(8,128)(2,1)S(1)} %collective-permute-done.7), channel_id=1, source_target_pairs={{0,1},{1,0},{2,3},{3,2},{4,5},{5,4},{6,7},{7,6},{8,9},{9,8},{10,11... | collective-permute-start | bytes 221192 | tf_op jit(solution)/shard_map/ppermute | solution.py:31
  18.5 1.5 %collective-permute-start.11 = (bf16[4,96,256]{2,1,0:T(8,128)(2,1)S(1)}, bf16[4,96,256]{2,1,0:T(8,128)(2,1)S(1)}, u32[]{:S(2)}, u32[]{:S(2)}) collective-permute-start(bf16[4,96,256]{2,1,0:T(8,128)(2,1)S(1)} %get-tuple-element.25), channel_id=1, source_target_pairs={{0,1},{1,0},{2,3},{3,2},{4,5},{5,4},{6,7},{7,6},{8,9},{9,8},{10,11... | collective-permute-start | bytes 589832 | tf_op jit(solution)/shard_map/ppermute | solution.py:31
  18.8 4.8 %collective-permute-start.10 = (f32[2,3,48,256]{3,2,1,0:T(8,128)S(1)}, f32[2,3,48,256]{3,2,1,0:T(8,128)S(1)}, u32[]{:S(2)}, u32[]{:S(2)}) collective-permute-start(f32[2,3,48,256]{3,2,1,0:T(8,128)S(1)} %get-tuple-element.23), channel_id=1, source_target_pairs={{0,1},{1,0},{2,3},{3,2},{4,5},{5,4},{6,7},{7,6},{8,9},{9,8},{10,11... | collective-permute-start | bytes 884744 | tf_op jit(solution)/shard_map/ppermute | solution.py:31
  20.1 5.3 %collective-permute-start.13 = (bf16[96,256]{1,0:T(8,128)(2,1)S(1)}, bf16[96,256]{1,0:T(8,128)(2,1)S(1)}, u32[]{:S(2)}, u32[]{:S(2)}) collective-permute-start(bf16[96,256]{1,0:T(8,128)(2,1)S(1)} %get-tuple-element.32), channel_id=1, source_target_pairs={{0,6},{1,7},{2,4},{3,5},{4,2},{5,3},{6,0},{7,1},{8,14},{9,15},{10,... | collective-permute-start | bytes 147464 | tf_op jit(solution)/shard_map/ppermute | solution.py:31
  21.4 4.7 %collective-permute-start.15 = (bf16[96,256]{1,0:T(8,128)(2,1)S(1)}, bf16[96,256]{1,0:T(8,128)(2,1)S(1)}, u32[]{:S(2)}, u32[]{:S(2)}) collective-permute-start(bf16[96,256]{1,0:T(8,128)(2,1)S(1)} %get-tuple-element.33), channel_id=1, source_target_pairs={{0,2},{1,3},{2,0},{3,1},{4,6},{5,7},{6,4},{7,5},{8,10},{9,11},{10,... | collective-permute-start | bytes 147464 | tf_op jit(solution)/shard_map/ppermute | solution.py:31
  22.9 4.1 %collective-permute-start.14 = (bf16[96,256]{1,0:T(8,128)(2,1)S(1)}, bf16[96,256]{1,0:T(8,128)(2,1)S(1)}, u32[]{:S(2)}, u32[]{:S(2)}) collective-permute-start(bf16[96,256]{1,0:T(8,128)(2,1)S(1)} %get-tuple-element.34), channel_id=1, source_target_pairs={{0,4},{1,5},{2,6},{3,7},{4,0},{5,1},{6,2},{7,3},{8,12},{9,13},{10,... | collective-permute-start | bytes 147464 | tf_op jit(solution)/shard_map/ppermute | solution.py:31
  23.7 10.4 %collective-permute-start.12 = (bf16[1,3,48,256]{3,2,1,0:T(8,128)(2,1)S(1)}, bf16[1,3,48,256]{3,2,1,0:T(8,128)(2,1)S(1)}, u32[]{:S(2)}, u32[]{:S(2)}) collective-permute-start(bf16[1,3,48,256]{3,2,1,0:T(8,128)(2,1)S(1)} %fusion.7), channel_id=1, source_target_pairs={{0,2},{1,3},{2,0},{3,1},{4,6},{5,7},{6,4},{7,5},{8,10},{9,11},{10,... | collective-permute-start | bytes 221192 | tf_op jit(solution)/shard_map/ppermute | solution.py:31
  27.0 6.2 %collective-permute-start.18 = (bf16[96,256]{1,0:T(8,128)(2,1)S(1)}, bf16[96,256]{1,0:T(8,128)(2,1)S(1)}, u32[]{:S(2)}, u32[]{:S(2)}) collective-permute-start(bf16[96,256]{1,0:T(8,128)(2,1)S(1)} %fusion.5), channel_id=1, source_target_pairs={{0,24},{4,28},{8,16},{12,20},{16,8},{20,12},{24,0},{28,4},{1,25},{... | collective-permute-start | bytes 147464 | tf_op jit(solution)/shard_map/ppermute | solution.py:31
  29.0 4.4 %collective-permute-start.17 = (bf16[96,256]{1,0:T(8,128)(2,1)S(1)}, bf16[96,256]{1,0:T(8,128)(2,1)S(1)}, u32[]{:S(2)}, u32[]{:S(2)}) collective-permute-start(bf16[96,256]{1,0:T(8,128)(2,1)S(1)} %fusion.5), channel_id=1, source_target_pairs={{0,8},{4,12},{8,0},{12,4},{16,24},{20,28},{24,16},{28,20},{1,9},{5... | collective-permute-start | bytes 147464 | tf_op jit(solution)/shard_map/ppermute | solution.py:31
  29.0 5.1 %collective-permute-start.16 = (bf16[96,256]{1,0:T(8,128)(2,1)S(1)}, bf16[96,256]{1,0:T(8,128)(2,1)S(1)}, u32[]{:S(2)}, u32[]{:S(2)}) collective-permute-start(bf16[96,256]{1,0:T(8,128)(2,1)S(1)} %fusion.5), channel_id=1, source_target_pairs={{0,16},{4,20},{8,24},{12,28},{16,0},{20,4},{24,8},{28,12},{1,17},{... | collective-permute-start | bytes 147464 | tf_op jit(solution)/shard_map/ppermute | solution.py:31
  34.2 5.1 %collective-permute-start.21 = (bf16[96,256]{1,0:T(8,128)(2,1)S(1)}, bf16[96,256]{1,0:T(8,128)(2,1)S(1)}, u32[]{:S(2)}, u32[]{:S(2)}) collective-permute-start(bf16[96,256]{1,0:T(8,128)(2,1)S(1)} %add_convert_fusion), channel_id=1, source_target_pairs={{0,6},{1,7},{2,4},{3,5},{4,2},{5,3},{6,0},{7,1},{8,14},{9,15},{10,... | collective-permute-start | bytes 147464 | tf_op jit(solution)/shard_map/ppermute | solution.py:31
  36.5 4.1 %collective-permute-start.20 = (bf16[96,256]{1,0:T(8,128)(2,1)S(1)}, bf16[96,256]{1,0:T(8,128)(2,1)S(1)}, u32[]{:S(2)}, u32[]{:S(2)}) collective-permute-start(bf16[96,256]{1,0:T(8,128)(2,1)S(1)} %add_convert_fusion), channel_id=1, source_target_pairs={{0,2},{1,3},{2,0},{3,1},{4,6},{5,7},{6,4},{7,5},{8,10},{9,11},{10,... | collective-permute-start | bytes 147464 | tf_op jit(solution)/shard_map/ppermute | solution.py:31
  37.1 4.1 %collective-permute-start.19 = (bf16[96,256]{1,0:T(8,128)(2,1)S(1)}, bf16[96,256]{1,0:T(8,128)(2,1)S(1)}, u32[]{:S(2)}, u32[]{:S(2)}) collective-permute-start(bf16[96,256]{1,0:T(8,128)(2,1)S(1)} %add_convert_fusion), channel_id=1, source_target_pairs={{0,4},{1,5},{2,6},{3,7},{4,0},{5,1},{6,2},{7,3},{8,12},{9,13},{10,... | collective-permute-start | bytes 147464 | tf_op jit(solution)/shard_map/ppermute | solution.py:31
  41.2 1.5 %collective-permute-start.22 = (bf16[4,96,256]{2,1,0:T(8,128)(2,1)S(1)}, bf16[4,96,256]{2,1,0:T(8,128)(2,1)S(1)}, u32[]{:S(2)}, u32[]{:S(2)}) collective-permute-start(bf16[4,96,256]{2,1,0:T(8,128)(2,1)S(1)} %pad_maximum_fusion.here_ref), channel_id=1, source_target_pairs={{0,1},{1,0},{2,3},{3,2},{4,5},{5,4},{6,7},{7,6},{8,9},{9,8},{10,11... | collective-permute-start | bytes 589832 | tf_op jit(solution)/shard_map/ppermute | solution.py:31

commit v7 on v6

--- a/solution.py
+++ b/solution.py
@@ -147,7 +147,7 @@
     limit = pltpu.CompilerParams(vmem_limit_bytes=32 * 1024 * 1024)
     tile_shape = jax.ShapeDtypeStruct(saved_panels.shape, BF16)
 
-    near = [bits for bits in (1, 2, 3) if bits < rows]
+    near = [bits for bits in (2, 3, 1) if bits < rows]
     along_row, row_tiles = [(0,)], [None]
     far = [bits for bits in range(4, rows, 4)]
     crossed = [swap(saved_panels, ("row",), sizes, {"row": bits}) for bits in far]

time: 43.8 us -> 43.4 us (level)
  transfers between devices with their start and end apart: 23 -> 23, of which waited for: 14 -> 15; matrix products, arithmetic and copies ran while one was open for 2% -> 2% of each run, Pallas kernels for 3% -> 3%
where the time goes in v7:
time: 43.4 us; the launch traced here: 43.3 us
  starting transfers between devices  25.7 us (59%)
  waiting for transfers between devices  12.3 us (28%)
  Pallas kernels  3.74 us (9%)
  other arithmetic  0.83 us (2%)
  between operations  0.73 us (2%)
    ppermute x23, starting transfers between devices, swap(): return lax.ppermute(value, axes, pairs)  25.7 us
    ppermute x23, waiting for transfers between devices, swap(): return lax.ppermute(value, axes, pairs)  12.3 us
    pallas_call x1, Pallas kernels, body(): pl.pallas_call(functools.partial(main_kernel, along_row, along_col), out_...  1.44 us
    pallas_call x1, Pallas kernels, body(): pl.pallas_call(prepare_kernel, out_shape=[jax.ShapeDtypeStruct(value.shap...  1.36 us
    pallas_call x1, Pallas kernels, body(): pl.pallas_call(finish_kernel, out_shape=jax.ShapeDtypeStruct((panels * wi...  0.94 us
  transfers between devices with their start and end apart: 23, of which 15 were waited for; matrix products, arithmetic and copies ran while one was open for 2% of the time, Pallas kernels for 3%

profile of v7, /device:TPU:0, one launch (start us, length us, event | category | flops | bytes accessed | tf_op | source)
XLA Modules:
  0.0 43.3 jit_solution(7455370791722600287)
XLA Ops:
  0.6 4.1 %collective-permute-start.3 = (bf16[3,48,256]{2,1,0:T(8,128)(2,1)}, bf16[3,48,256]{2,1,0:T(8,128)(2,1)S(1)}, u32[]{:S(2)}, u32[]{:S(2)}) collective-permute-start(bf16[3,48,256]{2,1,0:T(8,128)(2,1)} %refs_2_.1), channel_id=1, source_target_pairs={{0,16},{4,20},{8,24},{12,28},{16,0},{20,4},{24,8},{28,12},{1,17},{... | collective-permute-start | bytes 221192 | tf_op jit(solution)/shard_map/ppermute | solution.py:31
  4.7 1.5 %collective-permute-start.7 = (bf16[3,48,256]{2,1,0:T(8,128)(2,1)}, bf16[3,48,256]{2,1,0:T(8,128)(2,1)S(1)}, u32[]{:S(2)}, u32[]{:S(2)}) collective-permute-start(bf16[3,48,256]{2,1,0:T(8,128)(2,1)} %refs_2_.1), channel_id=1, source_target_pairs={{0,2},{1,3},{2,0},{3,1},{4,6},{5,7},{6,4},{7,5},{8,10},{9,11},{10,... | collective-permute-start | bytes 221192 | tf_op jit(solution)/shard_map/ppermute | solution.py:31
  6.3 1.5 %collective-permute-start.2 = (bf16[3,48,256]{2,1,0:T(8,128)(2,1)}, bf16[3,48,256]{2,1,0:T(8,128)(2,1)S(1)}, u32[]{:S(2)}, u32[]{:S(2)}) collective-permute-start(bf16[3,48,256]{2,1,0:T(8,128)(2,1)} %refs_2_.1), channel_id=1, source_target_pairs={{0,4},{4,0},{8,12},{12,8},{16,20},{20,16},{24,28},{28,24},{1,5},{5... | collective-permute-start | bytes 221192 | tf_op jit(solution)/shard_map/ppermute | solution.py:31
  7.7 1.5 %collective-permute-start.1 = (bf16[3,48,256]{2,1,0:T(8,128)(2,1)}, bf16[3,48,256]{2,1,0:T(8,128)(2,1)S(1)}, u32[]{:S(2)}, u32[]{:S(2)}) collective-permute-start(bf16[3,48,256]{2,1,0:T(8,128)(2,1)} %refs_2_.1), channel_id=1, source_target_pairs={{0,12},{4,8},{8,4},{12,0},{16,28},{20,24},{24,20},{28,16},{1,13},{... | collective-permute-start | bytes 221192 | tf_op jit(solution)/shard_map/ppermute | solution.py:31
  9.7 1.5 %collective-permute-start.6 = (bf16[1,3,48,256]{3,2,1,0:T(8,128)(2,1)S(1)}, bf16[1,3,48,256]{3,2,1,0:T(8,128)(2,1)S(1)}, u32[]{:S(2)}, u32[]{:S(2)}) collective-permute-start(bf16[1,3,48,256]{3,2,1,0:T(8,128)(2,1)S(1)} %bitcast.45), channel_id=1, source_target_pairs={{0,4},{4,0},{8,12},{12,8},{16,20},{20,16},{24,28},{28,24},{1,5},{5... | collective-permute-start | bytes 221192 | tf_op jit(solution)/shard_map/ppermute | solution.py:31
  11.2 1.5 %collective-permute-start.5 = (bf16[1,3,48,256]{3,2,1,0:T(8,128)(2,1)S(1)}, bf16[1,3,48,256]{3,2,1,0:T(8,128)(2,1)S(1)}, u32[]{:S(2)}, u32[]{:S(2)}) collective-permute-start(bf16[1,3,48,256]{3,2,1,0:T(8,128)(2,1)S(1)} %bitcast.46), channel_id=1, source_target_pairs={{0,12},{4,8},{8,4},{12,0},{16,28},{20,24},{24,20},{28,16},{1,13},{... | collective-permute-start | bytes 221192 | tf_op jit(solution)/shard_map/ppermute | solution.py:31
  12.8 0.7 %collective-permute-start.4 = (bf16[1,3,48,256]{3,2,1,0:T(8,128)(2,1)S(1)}, bf16[1,3,48,256]{3,2,1,0:T(8,128)(2,1)S(1)}, u32[]{:S(2)}, u32[]{:S(2)}) collective-permute-start(bf16[1,3,48,256]{3,2,1,0:T(8,128)(2,1)S(1)} %bitcast.47), channel_id=1, source_target_pairs={{0,8},{4,12},{8,0},{12,4},{16,24},{20,28},{24,16},{28,20},{1,9},{5... | collective-permute-start | bytes 221192 | tf_op jit(solution)/shard_map/ppermute | solution.py:31
  13.9 0.8 %collective-permute-done = bf16[3,48,256]{2,1,0:T(8,128)(2,1)S(1)} collective-permute-done((bf16[3,48,256]{2,1,0:T(8,128)(2,1)}, bf16[3,48,256]{2,1,0:T(8,128)(2,1)S(1)}, u32[]{:S(2)}, u32[]{:S(2)}) %collective-permute-start) | collective-permute-done | bytes 73760 | tf_op jit(solution)/shard_map/ppermute | solution.py:31
  14.7 1.4 %shard_map.68 = (bf16[192,384]{1,0:T(8,128)(2,1)S(1)}, bf16[3,48,256]{2,1,0:T(8,128)(2,1)S(1)}, bf16[3,48,256]{2,1,0:T(8,128)(2,1)S(1)}, bf16[3,256,256]{2,1,0:T(8,128)(2,1)S(1)}, bf16[3,256,256]{2,1,0:T(8,128)(2,1)S(1)}) custom-call(f32[3,256,256]{2,1,0:T(8,128)} %refs_0_.1, bf16[192,384]{1,0:T(8,128)(2,1)} %refs_1_.1, bf16[3,48,256]{2,1,0:T(8,128)(2,1)} %refs_2_.1, ...), custom_call_target="tpu_custom_call" | custom-call | tf_op jit(solution)/shard_map/pallas_call | solution.py:177
  16.5 0.7 %collective-permute-done.4.refs_5_ = bf16[1,3,48,256]{3,2,1,0:T(8,128)(2,1)S(1)} collective-permute-done((bf16[1,3,48,256]{3,2,1,0:T(8,128)(2,1)S(1)}, bf16[1,3,48,256]{3,2,1,0:T(8,128)(2,1)S(1)}, u32[]{:S(2)}, u32[]{:S(2)}) %collective-permute-start.4) | collective-permute-done | bytes 73760 | tf_op jit(solution)/shard_map/ppermute | solution.py:31
  17.2 1.4 %shard_map.69 = (f32[2,3,48,256]{3,2,1,0:T(8,128)S(1)}, f32[2,3,48,256]{3,2,1,0:T(8,128)S(1)}, f32[4,96,256]{2,1,0:T(8,128)S(1)}, bf16[4,96,256]{2,1,0:T(8,128)(2,1)S(1)}) custom-call(bf16[1,3,48,256]{3,2,1,0:T(8,128)(2,1)S(1)} %bitcast.43, bf16[1,3,48,256]{3,2,1,0:T(8,128)(2,1)S(1)} %bitcast.52, bf16[1,3,48,256]{3,2,1,0:T(8,128)(2,1)S(1)} %bitcast.51, ...), custom_call_target="tpu_custom_call" | custom-call | tf_op jit(solution)/shard_map/pallas_call | solution.py:189
  18.7 0.5 %collective-permute-start.10 = (f32[2,3,48,256]{3,2,1,0:T(8,128)S(1)}, f32[2,3,48,256]{3,2,1,0:T(8,128)S(1)}, u32[]{:S(2)}, u32[]{:S(2)}) collective-permute-start(f32[2,3,48,256]{3,2,1,0:T(8,128)S(1)} %get-tuple-element.23), channel_id=1, source_target_pairs={{0,1},{1,0},{2,3},{3,2},{4,5},{5,4},{6,7},{7,6},{8,9},{9,8},{10,11... | collective-permute-start | bytes 884744 | tf_op jit(solution)/shard_map/ppermute | solution.py:31
  19.2 0.9 %collective-permute-done.11 = bf16[4,96,256]{2,1,0:T(8,128)(2,1)S(1)} collective-permute-done((bf16[4,96,256]{2,1,0:T(8,128)(2,1)S(1)}, bf16[4,96,256]{2,1,0:T(8,128)(2,1)S(1)}, u32[]{:S(2)}, u32[]{:S(2)}) %collective-permute-start.11) | collective-permute-done | bytes 196640 | tf_op jit(solution)/shard_map/ppermute | solution.py:31
  20.2 2.0 %collective-permute-start.13 = (bf16[96,256]{1,0:T(8,128)(2,1)S(1)}, bf16[96,256]{1,0:T(8,128)(2,1)S(1)}, u32[]{:S(2)}, u32[]{:S(2)}) collective-permute-start(bf16[96,256]{1,0:T(8,128)(2,1)S(1)} %get-tuple-element.32), channel_id=1, source_target_pairs={{0,6},{1,7},{2,4},{3,5},{4,2},{5,3},{6,0},{7,1},{8,14},{9,15},{10,... | collective-permute-start | bytes 147464 | tf_op jit(solution)/shard_map/ppermute | solution.py:31
  22.2 1.0 %collective-permute-start.15 = (bf16[96,256]{1,0:T(8,128)(2,1)S(1)}, bf16[96,256]{1,0:T(8,128)(2,1)S(1)}, u32[]{:S(2)}, u32[]{:S(2)}) collective-permute-start(bf16[96,256]{1,0:T(8,128)(2,1)S(1)} %get-tuple-element.33), channel_id=1, source_target_pairs={{0,2},{1,3},{2,0},{3,1},{4,6},{5,7},{6,4},{7,5},{8,10},{9,11},{10,... | collective-permute-start | bytes 147464 | tf_op jit(solution)/shard_map/ppermute | solution.py:31
  23.2 0.5 %collective-permute-start.14 = (bf16[96,256]{1,0:T(8,128)(2,1)S(1)}, bf16[96,256]{1,0:T(8,128)(2,1)S(1)}, u32[]{:S(2)}, u32[]{:S(2)}) collective-permute-start(bf16[96,256]{1,0:T(8,128)(2,1)S(1)} %get-tuple-element.34), channel_id=1, source_target_pairs={{0,4},{1,5},{2,6},{3,7},{4,0},{5,1},{6,2},{7,3},{8,12},{9,13},{10,... | collective-permute-start | bytes 147464 | tf_op jit(solution)/shard_map/ppermute | solution.py:31
  23.8 0.6 %collective-permute-start.12 = (bf16[1,3,48,256]{3,2,1,0:T(8,128)(2,1)S(1)}, bf16[1,3,48,256]{3,2,1,0:T(8,128)(2,1)S(1)}, u32[]{:S(2)}, u32[]{:S(2)}) collective-permute-start(bf16[1,3,48,256]{3,2,1,0:T(8,128)(2,1)S(1)} %fusion.7), channel_id=1, source_target_pairs={{0,2},{1,3},{2,0},{3,1},{4,6},{5,7},{6,4},{7,5},{8,10},{9,11},{10,... | collective-permute-start | bytes 221192 | tf_op jit(solution)/shard_map/ppermute | solution.py:31
  24.4 0.9 %collective-permute-done.13 = bf16[96,256]{1,0:T(8,128)(2,1)S(1)} collective-permute-done((bf16[96,256]{1,0:T(8,128)(2,1)S(1)}, bf16[96,256]{1,0:T(8,128)(2,1)S(1)}, u32[]{:S(2)}, u32[]{:S(2)}) %collective-permute-start.13) | collective-permute-done | bytes 49184 | tf_op jit(solution)/shard_map/ppermute | solution.py:31
  25.4 1.5 %collective-permute-done.15 = bf16[96,256]{1,0:T(8,128)(2,1)S(1)} collective-permute-done((bf16[96,256]{1,0:T(8,128)(2,1)S(1)}, bf16[96,256]{1,0:T(8,128)(2,1)S(1)}, u32[]{:S(2)}, u32[]{:S(2)}) %collective-permute-start.15) | collective-permute-done | bytes 49184 | tf_op jit(solution)/shard_map/ppermute | solution.py:31
  27.3 2.0 %collective-permute-start.18 = (bf16[96,256]{1,0:T(8,128)(2,1)S(1)}, bf16[96,256]{1,0:T(8,128)(2,1)S(1)}, u32[]{:S(2)}, u32[]{:S(2)}) collective-permute-start(bf16[96,256]{1,0:T(8,128)(2,1)S(1)} %fusion.5), channel_id=1, source_target_pairs={{0,24},{4,28},{8,16},{12,20},{16,8},{20,12},{24,0},{28,4},{1,25},{... | collective-permute-start | bytes 147464 | tf_op jit(solution)/shard_map/ppermute | solution.py:31
  29.6 2.2 %collective-permute-start.16 = (bf16[96,256]{1,0:T(8,128)(2,1)S(1)}, bf16[96,256]{1,0:T(8,128)(2,1)S(1)}, u32[]{:S(2)}, u32[]{:S(2)}) collective-permute-start(bf16[96,256]{1,0:T(8,128)(2,1)S(1)} %fusion.5), channel_id=1, source_target_pairs={{0,16},{4,20},{8,24},{12,28},{16,0},{20,4},{24,8},{28,12},{1,17},{... | collective-permute-start | bytes 147464 | tf_op jit(solution)/shard_map/ppermute | solution.py:31
  31.8 1.5 %collective-permute-done.18 = bf16[96,256]{1,0:T(8,128)(2,1)S(1)} collective-permute-done((bf16[96,256]{1,0:T(8,128)(2,1)S(1)}, bf16[96,256]{1,0:T(8,128)(2,1)S(1)}, u32[]{:S(2)}, u32[]{:S(2)}) %collective-permute-start.18) | collective-permute-done | bytes 49184 | tf_op jit(solution)/shard_map/ppermute | solution.py:31
  33.8 0.8 %collective-permute-done.16 = bf16[96,256]{1,0:T(8,128)(2,1)S(1)} collective-permute-done((bf16[96,256]{1,0:T(8,128)(2,1)S(1)}, bf16[96,256]{1,0:T(8,128)(2,1)S(1)}, u32[]{:S(2)}, u32[]{:S(2)}) %collective-permute-start.16) | collective-permute-done | bytes 49184 | tf_op jit(solution)/shard_map/ppermute | solution.py:31
  34.7 1.6 %collective-permute-start.21 = (bf16[96,256]{1,0:T(8,128)(2,1)S(1)}, bf16[96,256]{1,0:T(8,128)(2,1)S(1)}, u32[]{:S(2)}, u32[]{:S(2)}) collective-permute-start(bf16[96,256]{1,0:T(8,128)(2,1)S(1)} %add_convert_fusion), channel_id=1, source_target_pairs={{0,6},{1,7},{2,4},{3,5},{4,2},{5,3},{6,0},{7,1},{8,14},{9,15},{10,... | collective-permute-start | bytes 147464 | tf_op jit(solution)/shard_map/ppermute | solution.py:31
  36.2 0.5 %collective-permute-start.20 = (bf16[96,256]{1,0:T(8,128)(2,1)S(1)}, bf16[96,256]{1,0:T(8,128)(2,1)S(1)}, u32[]{:S(2)}, u32[]{:S(2)}) collective-permute-start(bf16[96,256]{1,0:T(8,128)(2,1)S(1)} %add_convert_fusion), channel_id=1, source_target_pairs={{0,2},{1,3},{2,0},{3,1},{4,6},{5,7},{6,4},{7,5},{8,10},{9,11},{10,... | collective-permute-start | bytes 147464 | tf_op jit(solution)/shard_map/ppermute | solution.py:31
  36.7 1.5 %collective-permute-start.19 = (bf16[96,256]{1,0:T(8,128)(2,1)S(1)}, bf16[96,256]{1,0:T(8,128)(2,1)S(1)}, u32[]{:S(2)}, u32[]{:S(2)}) collective-permute-start(bf16[96,256]{1,0:T(8,128)(2,1)S(1)} %add_convert_fusion), channel_id=1, source_target_pairs={{0,4},{1,5},{2,6},{3,7},{4,0},{5,1},{6,2},{7,3},{8,12},{9,13},{10,... | collective-permute-start | bytes 147464 | tf_op jit(solution)/shard_map/ppermute | solution.py:31
  38.2 1.5 %collective-permute-done.21 = bf16[96,256]{1,0:T(8,128)(2,1)S(1)} collective-permute-done((bf16[96,256]{1,0:T(8,128)(2,1)S(1)}, bf16[96,256]{1,0:T(8,128)(2,1)S(1)}, u32[]{:S(2)}, u32[]{:S(2)}) %collective-permute-start.21) | collective-permute-done | bytes 49184 | tf_op jit(solution)/shard_map/ppermute | solution.py:31
  39.7 0.6 %collective-permute-done.20 = bf16[96,256]{1,0:T(8,128)(2,1)S(1)} collective-permute-done((bf16[96,256]{1,0:T(8,128)(2,1)S(1)}, bf16[96,256]{1,0:T(8,128)(2,1)S(1)}, u32[]{:S(2)}, u32[]{:S(2)}) %collective-permute-start.20) | collective-permute-done | bytes 49184 | tf_op jit(solution)/shard_map/ppermute | solution.py:31
  40.3 0.5 %collective-permute-done.19 = bf16[96,256]{1,0:T(8,128)(2,1)S(1)} collective-permute-done((bf16[96,256]{1,0:T(8,128)(2,1)S(1)}, bf16[96,256]{1,0:T(8,128)(2,1)S(1)}, u32[]{:S(2)}, u32[]{:S(2)}) %collective-permute-start.19) | collective-permute-done | bytes 49184 | tf_op jit(solution)/shard_map/ppermute | solution.py:31
  40.9 0.6 %fusion.6 = bf16[3,48,256]{2,1,0:T(8,128)(2,1)} fusion(bf16[1,3,48,256]{3,2,1,0:T(8,128)(2,1)S(1)} %collective-permute-done.12, f32[1,2,3,48,256]{4,3,2,1,0:T(8,128)S(1)} %add_bitcast_fusion), kind=kLoop, calls=%fused_computation.13 | loop fusion | flops 110592 | bytes 294912 | tf_op jit(solution)/shard_map/convert_element_type | solution.py:221
  41.6 0.8 %collective-permute-done.22.there_ref = bf16[4,96,256]{2,1,0:T(8,128)(2,1)S(1)} collective-permute-done((bf16[4,96,256]{2,1,0:T(8,128)(2,1)S(1)}, bf16[4,96,256]{2,1,0:T(8,128)(2,1)S(1)}, u32[]{:S(2)}, u32[]{:S(2)}) %collective-permute-start.22) | collective-permute-done | bytes 196640 | tf_op jit(solution)/shard_map/ppermute | solution.py:31
  42.4 0.9 %shard_map.70 = f32[768,256]{1,0:T(8,128)} custom-call(bf16[4,96,256]{2,1,0:T(8,128)(2,1)S(1)} %pad_maximum_fusion.here_ref, bf16[4,96,256]{2,1,0:T(8,128)(2,1)S(1)} %collective-permute-done.22.there_ref), custom_call_target="tpu_custom_call" | custom-call | tf_op jit(solution)/shard_map/pallas_call | solution.py:243
  (25 shorter events, 3.0 us)
Async XLA Ops:
  0.6 9.1 %collective-permute-start.3 = (bf16[3,48,256]{2,1,0:T(8,128)(2,1)}, bf16[3,48,256]{2,1,0:T(8,128)(2,1)S(1)}, u32[]{:S(2)}, u32[]{:S(2)}) collective-permute-start(bf16[3,48,256]{2,1,0:T(8,128)(2,1)} %refs_2_.1), channel_id=1, source_target_pairs={{0,16},{4,20},{8,24},{12,28},{16,0},{20,4},{24,8},{28,12},{1,17},{... | collective-permute-start | bytes 221192 | tf_op jit(solution)/shard_map/ppermute | solution.py:31
  4.7 6.5 %collective-permute-start.7 = (bf16[3,48,256]{2,1,0:T(8,128)(2,1)}, bf16[3,48,256]{2,1,0:T(8,128)(2,1)S(1)}, u32[]{:S(2)}, u32[]{:S(2)}) collective-permute-start(bf16[3,48,256]{2,1,0:T(8,128)(2,1)} %refs_2_.1), channel_id=1, source_target_pairs={{0,2},{1,3},{2,0},{3,1},{4,6},{5,7},{6,4},{7,5},{8,10},{9,11},{10,... | collective-permute-start | bytes 221192 | tf_op jit(solution)/shard_map/ppermute | solution.py:31
  6.3 6.5 %collective-permute-start.2 = (bf16[3,48,256]{2,1,0:T(8,128)(2,1)}, bf16[3,48,256]{2,1,0:T(8,128)(2,1)S(1)}, u32[]{:S(2)}, u32[]{:S(2)}) collective-permute-start(bf16[3,48,256]{2,1,0:T(8,128)(2,1)} %refs_2_.1), channel_id=1, source_target_pairs={{0,4},{4,0},{8,12},{12,8},{16,20},{20,16},{24,28},{28,24},{1,5},{5... | collective-permute-start | bytes 221192 | tf_op jit(solution)/shard_map/ppermute | solution.py:31
  7.7 6.1 %collective-permute-start.1 = (bf16[3,48,256]{2,1,0:T(8,128)(2,1)}, bf16[3,48,256]{2,1,0:T(8,128)(2,1)S(1)}, u32[]{:S(2)}, u32[]{:S(2)}) collective-permute-start(bf16[3,48,256]{2,1,0:T(8,128)(2,1)} %refs_2_.1), channel_id=1, source_target_pairs={{0,12},{4,8},{8,4},{12,0},{16,28},{20,24},{24,20},{28,16},{1,13},{... | collective-permute-start | bytes 221192 | tf_op jit(solution)/shard_map/ppermute | solution.py:31
  9.3 5.4 %collective-permute-start = (bf16[3,48,256]{2,1,0:T(8,128)(2,1)}, bf16[3,48,256]{2,1,0:T(8,128)(2,1)S(1)}, u32[]{:S(2)}, u32[]{:S(2)}) collective-permute-start(bf16[3,48,256]{2,1,0:T(8,128)(2,1)} %refs_2_.1), channel_id=1, source_target_pairs={{0,8},{4,12},{8,0},{12,4},{16,24},{20,28},{24,16},{28,20},{1,9},{5... | collective-permute-start | bytes 221192 | tf_op jit(solution)/shard_map/ppermute | solution.py:31
  9.7 6.3 %collective-permute-start.6 = (bf16[1,3,48,256]{3,2,1,0:T(8,128)(2,1)S(1)}, bf16[1,3,48,256]{3,2,1,0:T(8,128)(2,1)S(1)}, u32[]{:S(2)}, u32[]{:S(2)}) collective-permute-start(bf16[1,3,48,256]{3,2,1,0:T(8,128)(2,1)S(1)} %bitcast.45), channel_id=1, source_target_pairs={{0,4},{4,0},{8,12},{12,8},{16,20},{20,16},{24,28},{28,24},{1,5},{5... | collective-permute-start | bytes 221192 | tf_op jit(solution)/shard_map/ppermute | solution.py:31
  11.2 5.3 %collective-permute-start.5 = (bf16[1,3,48,256]{3,2,1,0:T(8,128)(2,1)S(1)}, bf16[1,3,48,256]{3,2,1,0:T(8,128)(2,1)S(1)}, u32[]{:S(2)}, u32[]{:S(2)}) collective-permute-start(bf16[1,3,48,256]{3,2,1,0:T(8,128)(2,1)S(1)} %bitcast.46), channel_id=1, source_target_pairs={{0,12},{4,8},{8,4},{12,0},{16,28},{20,24},{24,20},{28,16},{1,13},{... | collective-permute-start | bytes 221192 | tf_op jit(solution)/shard_map/ppermute | solution.py:31
  12.8 4.4 %collective-permute-start.4 = (bf16[1,3,48,256]{3,2,1,0:T(8,128)(2,1)S(1)}, bf16[1,3,48,256]{3,2,1,0:T(8,128)(2,1)S(1)}, u32[]{:S(2)}, u32[]{:S(2)}) collective-permute-start(bf16[1,3,48,256]{3,2,1,0:T(8,128)(2,1)S(1)} %bitcast.47), channel_id=1, source_target_pairs={{0,8},{4,12},{8,0},{12,4},{16,24},{20,28},{24,16},{28,20},{1,9},{5... | collective-permute-start | bytes 221192 | tf_op jit(solution)/shard_map/ppermute | solution.py:31
  13.9 3.3 %collective-permute-start.8 = (bf16[3,48,256]{2,1,0:T(8,128)(2,1)}, bf16[3,48,256]{2,1,0:T(8,128)(2,1)S(1)}, u32[]{:S(2)}, u32[]{:S(2)}) collective-permute-start(bf16[3,48,256]{2,1,0:T(8,128)(2,1)} %refs_2_.1), channel_id=1, source_target_pairs={{0,1},{1,0},{2,3},{3,2},{4,5},{5,4},{6,7},{7,6},{8,9},{9,8},{10,11... | collective-permute-start | bytes 221192 | tf_op jit(solution)/shard_map/ppermute | solution.py:31
  14.7 2.5 %collective-permute-start.9 = (bf16[3,48,256]{2,1,0:T(8,128)(2,1)S(1)}, bf16[3,48,256]{2,1,0:T(8,128)(2,1)S(1)}, u32[]{:S(2)}, u32[]{:S(2)}) collective-permute-start(bf16[3,48,256]{2,1,0:T(8,128)(2,1)S(1)} %collective-permute-done.7), channel_id=1, source_target_pairs={{0,1},{1,0},{2,3},{3,2},{4,5},{5,4},{6,7},{7,6},{8,9},{9,8},{10,11... | collective-permute-start | bytes 221192 | tf_op jit(solution)/shard_map/ppermute | solution.py:31
  18.6 1.5 %collective-permute-start.11 = (bf16[4,96,256]{2,1,0:T(8,128)(2,1)S(1)}, bf16[4,96,256]{2,1,0:T(8,128)(2,1)S(1)}, u32[]{:S(2)}, u32[]{:S(2)}) collective-permute-start(bf16[4,96,256]{2,1,0:T(8,128)(2,1)S(1)} %get-tuple-element.25), channel_id=1, source_target_pairs={{0,1},{1,0},{2,3},{3,2},{4,5},{5,4},{6,7},{7,6},{8,9},{9,8},{10,11... | collective-permute-start | bytes 589832 | tf_op jit(solution)/shard_map/ppermute | solution.py:31
  18.7 5.1 %collective-permute-start.10 = (f32[2,3,48,256]{3,2,1,0:T(8,128)S(1)}, f32[2,3,48,256]{3,2,1,0:T(8,128)S(1)}, u32[]{:S(2)}, u32[]{:S(2)}) collective-permute-start(f32[2,3,48,256]{3,2,1,0:T(8,128)S(1)} %get-tuple-element.23), channel_id=1, source_target_pairs={{0,1},{1,0},{2,3},{3,2},{4,5},{5,4},{6,7},{7,6},{8,9},{9,8},{10,11... | collective-permute-start | bytes 884744 | tf_op jit(solution)/shard_map/ppermute | solution.py:31
  20.2 5.2 %collective-permute-start.13 = (bf16[96,256]{1,0:T(8,128)(2,1)S(1)}, bf16[96,256]{1,0:T(8,128)(2,1)S(1)}, u32[]{:S(2)}, u32[]{:S(2)}) collective-permute-start(bf16[96,256]{1,0:T(8,128)(2,1)S(1)} %get-tuple-element.32), channel_id=1, source_target_pairs={{0,6},{1,7},{2,4},{3,5},{4,2},{5,3},{6,0},{7,1},{8,14},{9,15},{10,... | collective-permute-start | bytes 147464 | tf_op jit(solution)/shard_map/ppermute | solution.py:31
  22.2 4.6 %collective-permute-start.15 = (bf16[96,256]{1,0:T(8,128)(2,1)S(1)}, bf16[96,256]{1,0:T(8,128)(2,1)S(1)}, u32[]{:S(2)}, u32[]{:S(2)}) collective-permute-start(bf16[96,256]{1,0:T(8,128)(2,1)S(1)} %get-tuple-element.33), channel_id=1, source_target_pairs={{0,2},{1,3},{2,0},{3,1},{4,6},{5,7},{6,4},{7,5},{8,10},{9,11},{10,... | collective-permute-start | bytes 147464 | tf_op jit(solution)/shard_map/ppermute | solution.py:31
  23.2 4.1 %collective-permute-start.14 = (bf16[96,256]{1,0:T(8,128)(2,1)S(1)}, bf16[96,256]{1,0:T(8,128)(2,1)S(1)}, u32[]{:S(2)}, u32[]{:S(2)}) collective-permute-start(bf16[96,256]{1,0:T(8,128)(2,1)S(1)} %get-tuple-element.34), channel_id=1, source_target_pairs={{0,4},{1,5},{2,6},{3,7},{4,0},{5,1},{6,2},{7,3},{8,12},{9,13},{10,... | collective-permute-start | bytes 147464 | tf_op jit(solution)/shard_map/ppermute | solution.py:31
  23.8 10.8 %collective-permute-start.12 = (bf16[1,3,48,256]{3,2,1,0:T(8,128)(2,1)S(1)}, bf16[1,3,48,256]{3,2,1,0:T(8,128)(2,1)S(1)}, u32[]{:S(2)}, u32[]{:S(2)}) collective-permute-start(bf16[1,3,48,256]{3,2,1,0:T(8,128)(2,1)S(1)} %fusion.7), channel_id=1, source_target_pairs={{0,2},{1,3},{2,0},{3,1},{4,6},{5,7},{6,4},{7,5},{8,10},{9,11},{10,... | collective-permute-start | bytes 221192 | tf_op jit(solution)/shard_map/ppermute | solution.py:31
  27.3 6.0 %collective-permute-start.18 = (bf16[96,256]{1,0:T(8,128)(2,1)S(1)}, bf16[96,256]{1,0:T(8,128)(2,1)S(1)}, u32[]{:S(2)}, u32[]{:S(2)}) collective-permute-start(bf16[96,256]{1,0:T(8,128)(2,1)S(1)} %fusion.5), channel_id=1, source_target_pairs={{0,24},{4,28},{8,16},{12,20},{16,8},{20,12},{24,0},{28,4},{1,25},{... | collective-permute-start | bytes 147464 | tf_op jit(solution)/shard_map/ppermute | solution.py:31
  29.3 4.5 %collective-permute-start.17 = (bf16[96,256]{1,0:T(8,128)(2,1)S(1)}, bf16[96,256]{1,0:T(8,128)(2,1)S(1)}, u32[]{:S(2)}, u32[]{:S(2)}) collective-permute-start(bf16[96,256]{1,0:T(8,128)(2,1)S(1)} %fusion.5), channel_id=1, source_target_pairs={{0,8},{4,12},{8,0},{12,4},{16,24},{20,28},{24,16},{28,20},{1,9},{5... | collective-permute-start | bytes 147464 | tf_op jit(solution)/shard_map/ppermute | solution.py:31
  29.6 5.0 %collective-permute-start.16 = (bf16[96,256]{1,0:T(8,128)(2,1)S(1)}, bf16[96,256]{1,0:T(8,128)(2,1)S(1)}, u32[]{:S(2)}, u32[]{:S(2)}) collective-permute-start(bf16[96,256]{1,0:T(8,128)(2,1)S(1)} %fusion.5), channel_id=1, source_target_pairs={{0,16},{4,20},{8,24},{12,28},{16,0},{20,4},{24,8},{28,12},{1,17},{... | collective-permute-start | bytes 147464 | tf_op jit(solution)/shard_map/ppermute | solution.py:31
  34.7 5.1 %collective-permute-start.21 = (bf16[96,256]{1,0:T(8,128)(2,1)S(1)}, bf16[96,256]{1,0:T(8,128)(2,1)S(1)}, u32[]{:S(2)}, u32[]{:S(2)}) collective-permute-start(bf16[96,256]{1,0:T(8,128)(2,1)S(1)} %add_convert_fusion), channel_id=1, source_target_pairs={{0,6},{1,7},{2,4},{3,5},{4,2},{5,3},{6,0},{7,1},{8,14},{9,15},{10,... | collective-permute-start | bytes 147464 | tf_op jit(solution)/shard_map/ppermute | solution.py:31
  36.2 4.1 %collective-permute-start.20 = (bf16[96,256]{1,0:T(8,128)(2,1)S(1)}, bf16[96,256]{1,0:T(8,128)(2,1)S(1)}, u32[]{:S(2)}, u32[]{:S(2)}) collective-permute-start(bf16[96,256]{1,0:T(8,128)(2,1)S(1)} %add_convert_fusion), channel_id=1, source_target_pairs={{0,2},{1,3},{2,0},{3,1},{4,6},{5,7},{6,4},{7,5},{8,10},{9,11},{10,... | collective-permute-start | bytes 147464 | tf_op jit(solution)/shard_map/ppermute | solution.py:31
  36.7 4.1 %collective-permute-start.19 = (bf16[96,256]{1,0:T(8,128)(2,1)S(1)}, bf16[96,256]{1,0:T(8,128)(2,1)S(1)}, u32[]{:S(2)}, u32[]{:S(2)}) collective-permute-start(bf16[96,256]{1,0:T(8,128)(2,1)S(1)} %add_convert_fusion), channel_id=1, source_target_pairs={{0,4},{1,5},{2,6},{3,7},{4,0},{5,1},{6,2},{7,3},{8,12},{9,13},{10,... | collective-permute-start | bytes 147464 | tf_op jit(solution)/shard_map/ppermute | solution.py:31
  40.8 1.5 %collective-permute-start.22 = (bf16[4,96,256]{2,1,0:T(8,128)(2,1)S(1)}, bf16[4,96,256]{2,1,0:T(8,128)(2,1)S(1)}, u32[]{:S(2)}, u32[]{:S(2)}) collective-permute-start(bf16[4,96,256]{2,1,0:T(8,128)(2,1)S(1)} %pad_maximum_fusion.here_ref), channel_id=1, source_target_pairs={{0,1},{1,0},{2,3},{3,2},{4,5},{5,4},{6,7},{7,6},{8,9},{9,8},{10,11... | collective-permute-start | bytes 589832 | tf_op jit(solution)/shard_map/ppermute | solution.py:31

commit v8 on v7

--- a/solution.py
+++ b/solution.py
@@ -53,11 +53,18 @@
         copy.wait()
 
 
-def main_kernel(along_row, along_col, *refs):
+def partner(row):
+    return row ^ (1 + 2 * (row & 1))
+
+
+def main_kernel(along_row, shared, along_col, *refs):
+    shared_refs, refs = refs[: len(shared)], refs[len(shared) :]
     row_refs, refs = refs[: len(along_row)], refs[len(along_row) :]
     col_refs, refs = refs[: len(along_col)], refs[len(along_col) :]
     cot_ref, upstream_ref, solver_ref, tops_ref = refs[:4]
-    columns_keep, columns_send, keep_ref, send_ref, joined, own, total, diag = refs[4:]
+    columns_keep, columns_send, keep_ref, send_ref = refs[4:8]
+    guests = [bits for bits_list in shared for bits in bits_list]
+    back_refs, (joined, own, total, across, diag) = refs[8 : 8 + len(guests)], refs[8 + len(guests) :]
     row, col = lax.axis_index("row"), lax.axis_index("col")
     panels, height, width = upstream_ref.shape
 
@@ -69,11 +76,24 @@
     for bits_list, ref in zip(along_row, row_refs):
         for spot, bits in enumerate(bits_list):
             place(joined, row ^ bits, ref.at[spot])
+    def tile_rows(index):
+        return pl.ds(pl.multiple_of(index * height, height), height)
+
+    base = len(along_col)
+    tall = base * height
     for bits_list, ref in zip(along_col, col_refs):
         for spot, bits in enumerate(bits_list):
             place(own, col ^ bits, ref.at[spot])
-    total[...] = -2.0 * dot(cot_ref[...], joined[...])
-    mine = pl.ds(pl.multiple_of(col * height, height), height)
+    for bits_list, ref in zip(shared, shared_refs):
+        for spot, bits in enumerate(bits_list):
+            place(joined, partner(row) ^ bits, ref.at[spot])
+            place(own, base + guests.index(bits), ref.at[spot])
+            joined[tile_rows(partner(row) ^ bits ^ 2), :] = jnp.zeros((height, joined.shape[1]), BF16)
+    total[:tall, :] = -2.0 * dot(cot_ref[...], joined[...])
+    across[...] = -2.0 * dot_rows(cot_ref[...], own[:tall, :])
+    for spot, bits in enumerate(guests):
+        total[tall + spot * height : tall + (spot + 1) * height, :] = across[tile_rows(partner(row) ^ bits), :]
+    mine = tile_rows(col)
     for index in range(panels):
         span = slice(index * width, (index + 1) * width)
         total[mine, span] += upstream_ref[index].astype(F32)
@@ -120,6 +140,11 @@
             tile = pl.ds(pl.multiple_of((col ^ bits) * height, height), height)
             for index in range(panels):
                 ref[pair, index] = total[tile, index * width : (index + 1) * width].astype(ref.dtype)
+    for spot, ref in enumerate(back_refs):
+        start = (base + spot) * height
+        for index in range(panels):
+            tile = total[start : start + height, index * width : (index + 1) * width]
+            ref[index] = tile.astype(BF16)
 
 
 def place_of():
@@ -147,11 +172,15 @@
     limit = pltpu.CompilerParams(vmem_limit_bytes=32 * 1024 * 1024)
     tile_shape = jax.ShapeDtypeStruct(saved_panels.shape, BF16)
 
-    near = [bits for bits in (2, 3, 1) if bits < rows]
-    along_row, row_tiles = [(0,)], [None]
     far = [bits for bits in range(4, rows, 4)]
+
+    def guest(value, bits=0, back=False):
+        pairs = [(partner(row) ^ bits, row) for row in range(rows)]
+        return lax.ppermute(value, "row", [pair[::-1] for pair in pairs] if back else pairs)
+
     crossed = [swap(saved_panels, ("row",), sizes, {"row": bits}) for bits in far]
-    nearby = {bits: swap(saved_panels, ("row",), sizes, {"row": bits}) for bits in near}
+    along_row, row_tiles = [(0,), (2,)], [None, swap(saved_panels, ("row",), sizes, {"row": 2})[None]]
+    shared, shared_tiles = [(0,)], [guest(saved_panels)[None]]
     along_col = [(0,)]
     col_tiles = [None]
     for power in list(range(1, cols.bit_length() - 1)) + [0]:
@@ -162,14 +191,11 @@
             if power == 0 and tile is None and len(held) > 1:
                 sent = after(sent, held[-1][1])
             col_tiles.append(swap(sent, ("col",), sizes, {"col": 1 << power})[None])
-    for bits in near:
-        along_row.append((bits,))
-        row_tiles.append(nearby[bits][None])
     if far:
         sent = jnp.stack(crossed)
         along_row.append(tuple(far))
         row_tiles.append(sent)
-        for bits in near:
+        for bits in (1, 2, 3):
             along_row.append(tuple(other ^ bits for other in far))
             row_tiles.append(swap(sent, ("row",), sizes, {"row": bits}))
 
@@ -186,24 +212,27 @@
     col_tiles[0] = saved[None]
 
     piece = panels * width // 8
-    columns_keep, columns_send, keep, send = pl.pallas_call(
-        functools.partial(main_kernel, along_row, along_col),
+    tall = (cols + 1) * height
+    columns_keep, columns_send, keep, send, *backs = pl.pallas_call(
+        functools.partial(main_kernel, along_row, shared, along_col),
         out_shape=[
             jax.ShapeDtypeStruct((cols // 2, panels, height, width), F32),
             jax.ShapeDtypeStruct((cols // 2, panels, height, width), F32),
             jax.ShapeDtypeStruct((4, piece, width), F32),
             jax.ShapeDtypeStruct((4, piece, width), BF16),
-        ],
-        in_specs=[VMEM] * (len(row_tiles) + len(col_tiles) + 4),
-        out_specs=[VMEM] * 4,
+        ]
+        + [tile_shape],
+        in_specs=[VMEM] * (len(row_tiles) + len(shared_tiles) + len(col_tiles) + 4),
+        out_specs=[VMEM] * 5,
         scratch_shapes=[
             pltpu.VMEM((rows * height, panels * width), BF16),
-            pltpu.VMEM((cols * height, panels * width), BF16),
-            pltpu.VMEM((cols * height, panels * width), F32),
+            pltpu.VMEM((tall, panels * width), BF16),
+            pltpu.VMEM((tall, panels * width), F32),
+            pltpu.VMEM((rows * height, panels * width), F32),
             pltpu.VMEM((panels * width, width), F32),
         ],
         compiler_params=limit,
-    )(*row_tiles, *col_tiles, cot, upstream_here, solver, tops)
+    )(*shared_tiles, *row_tiles, *col_tiles, cot, upstream_here, solver, tops)
 
     both = ("row", "col")
     half = keep + swap(send, ("col",), sizes, {"col": 1}).astype(F32)
@@ -211,6 +240,7 @@
     total = half[0]
     for bits in (3, 1, 2):
         total = total + swap(half[bits].astype(BF16), both, sizes, spots[bits]).astype(F32)
+    returned = guest(after(backs[0], half), back=True)
     arrived = swap(columns_send, ("col",), sizes, {"col": 1})
     columns = columns_keep + arrived.astype(F32)
     for power in range(1, cols.bit_length() - 1):
@@ -218,7 +248,8 @@
         arrived = swap(after(halves[:, 1].astype(BF16), half), ("col",), sizes, {"col": 1 << power})
         columns = halves[:, 0] + arrived.astype(F32)
     mine = total.astype(BF16)
-    columns = columns[0].astype(BF16)
+    columns = columns[0]
+    columns = (columns + returned.astype(F32)).astype(BF16)
 
     others = [{"row": 1 << power} for power in range(1, rows.bit_length() - 1)]
     others += [{"col": 1 << power} for power in range(2, cols.bit_length() - 1)]
@@ -227,8 +258,8 @@
         from_first, from_second, from_both = [
             swap(mine, ("row",), sizes, {"row": bits}) for bits in (first, second, first ^ second)
         ]
-        from_second, from_first, from_both, arrived = lax.optimization_barrier(
-            (from_second, from_first, from_both, arrived)
+        from_second, from_first, from_both, arrived, returned = lax.optimization_barrier(
+            (from_second, from_first, from_both, arrived, returned)
         )
         total = (mine.astype(F32) + from_first.astype(F32)) + (
             from_second.astype(F32) + from_both.astype(F32)

time: 43.4 us -> 44.1 us (1.016)
    ppermute x0 -> x2, starting transfers between devices: none -> 2.21 us  [guest(): lax.ppermute(value, 'row', [pair[::-1] for pair in pairs] if back else pa...]
    ppermute x23 -> x21, starting transfers between devices: 25.7 us -> 23.9 us  [swap(): return lax.ppermute(value, axes, pairs)]
    ppermute x0 -> x2, waiting for transfers between devices: none -> 0.76 us  [guest(): lax.ppermute(value, 'row', [pair[::-1] for pair in pairs] if back else pa...]
    ppermute x23 -> x21, waiting for transfers between devices: 12.3 us -> 11.6 us  [swap(): return lax.ppermute(value, axes, pairs)]
  transfers between devices with their start and end apart: 23 -> 23, of which waited for: 15 -> 13; matrix products, arithmetic and copies ran while one was open for 2% -> 2% of each run, Pallas kernels for 3% -> 3%
where the time goes in v8:
time: 44.1 us; the launch traced here: 44 us
  starting transfers between devices  26.1 us (59%)
  waiting for transfers between devices  12.4 us (28%)
  Pallas kernels  3.95 us (9%)
  other arithmetic  0.85 us (2%)
  between operations  0.73 us (2%)
    ppermute x21, starting transfers between devices, swap(): return lax.ppermute(value, axes, pairs)  23.9 us
    ppermute x21, waiting for transfers between devices, swap(): return lax.ppermute(value, axes, pairs)  11.6 us
    ppermute x2, starting transfers between devices, guest(): lax.ppermute(value, 'row', [pair[::-1] for pair in pairs] if back else pa...  2.21 us
    pallas_call x1, Pallas kernels, body(): pl.pallas_call(functools.partial(main_kernel, along_row, shared, along_co...  1.64 us
    pallas_call x1, Pallas kernels, body(): pl.pallas_call(prepare_kernel, out_shape=[jax.ShapeDtypeStruct(value.shap...  1.36 us
    pallas_call x1, Pallas kernels, body(): pl.pallas_call(finish_kernel, out_shape=jax.ShapeDtypeStruct((panels * wi...  0.94 us
  transfers between devices with their start and end apart: 23, of which 13 were waited for; matrix products, arithmetic and copies ran while one was open for 2% of the time, Pallas kernels for 3%

profile of v8, /device:TPU:0, one launch (start us, length us, event | category | flops | bytes accessed | tf_op | source)
XLA Modules:
  0.0 44.0 jit_solution(9649726593534560507)
XLA Ops:
  0.6 4.1 %collective-permute-start.2 = (bf16[3,48,256]{2,1,0:T(8,128)(2,1)}, bf16[3,48,256]{2,1,0:T(8,128)(2,1)S(1)}, u32[]{:S(2)}, u32[]{:S(2)}) collective-permute-start(bf16[3,48,256]{2,1,0:T(8,128)(2,1)} %refs_2_.1), channel_id=1, source_target_pairs={{0,16},{4,20},{8,24},{12,28},{16,0},{20,4},{24,8},{28,12},{1,17},{... | collective-permute-start | bytes 221192 | tf_op jit(solution)/shard_map/ppermute | solution.py:31
  4.7 1.5 %collective-permute-start.6 = (bf16[3,48,256]{2,1,0:T(8,128)(2,1)}, bf16[3,48,256]{2,1,0:T(8,128)(2,1)S(1)}, u32[]{:S(2)}, u32[]{:S(2)}) collective-permute-start(bf16[3,48,256]{2,1,0:T(8,128)(2,1)} %refs_2_.1), channel_id=1, source_target_pairs={{0,2},{1,3},{2,0},{3,1},{4,6},{5,7},{6,4},{7,5},{8,10},{9,11},{10,... | collective-permute-start | bytes 221192 | tf_op jit(solution)/shard_map/ppermute | solution.py:31
  6.3 1.6 %collective-permute-start.1 = (bf16[3,48,256]{2,1,0:T(8,128)(2,1)}, bf16[3,48,256]{2,1,0:T(8,128)(2,1)S(1)}, u32[]{:S(2)}, u32[]{:S(2)}) collective-permute-start(bf16[3,48,256]{2,1,0:T(8,128)(2,1)} %refs_2_.1), channel_id=1, source_target_pairs={{0,8},{4,12},{8,0},{12,4},{16,24},{20,28},{24,16},{28,20},{1,9},{5... | collective-permute-start | bytes 221192 | tf_op jit(solution)/shard_map/ppermute | solution.py:31
  7.8 1.4 %collective-permute-start = (bf16[3,48,256]{2,1,0:T(8,128)(2,1)}, bf16[3,48,256]{2,1,0:T(8,128)(2,1)S(1)}, u32[]{:S(2)}, u32[]{:S(2)}) collective-permute-start(bf16[3,48,256]{2,1,0:T(8,128)(2,1)} %refs_2_.1), channel_id=1, source_target_pairs={{4,0},{8,4},{12,8},{0,12},{20,16},{24,20},{28,24},{16,28},{5,1},{9... | collective-permute-start | bytes 221192 | tf_op jit(solution)/shard_map/ppermute | solution.py:179
  9.2 1.4 %collective-permute-start.5 = (bf16[1,3,48,256]{3,2,1,0:T(8,128)(2,1)S(1)}, bf16[1,3,48,256]{3,2,1,0:T(8,128)(2,1)S(1)}, u32[]{:S(2)}, u32[]{:S(2)}) collective-permute-start(bf16[1,3,48,256]{3,2,1,0:T(8,128)(2,1)S(1)} %bitcast.50), channel_id=1, source_target_pairs={{0,12},{4,8},{8,4},{12,0},{16,28},{20,24},{24,20},{28,16},{1,13},{... | collective-permute-start | bytes 221192 | tf_op jit(solution)/shard_map/ppermute | solution.py:31
  10.6 1.4 %collective-permute-start.4 = (bf16[1,3,48,256]{3,2,1,0:T(8,128)(2,1)S(1)}, bf16[1,3,48,256]{3,2,1,0:T(8,128)(2,1)S(1)}, u32[]{:S(2)}, u32[]{:S(2)}) collective-permute-start(bf16[1,3,48,256]{3,2,1,0:T(8,128)(2,1)S(1)} %bitcast.51), channel_id=1, source_target_pairs={{0,8},{4,12},{8,0},{12,4},{16,24},{20,28},{24,16},{28,20},{1,9},{5... | collective-permute-start | bytes 221192 | tf_op jit(solution)/shard_map/ppermute | solution.py:31
  12.0 0.7 %collective-permute-start.3 = (bf16[1,3,48,256]{3,2,1,0:T(8,128)(2,1)S(1)}, bf16[1,3,48,256]{3,2,1,0:T(8,128)(2,1)S(1)}, u32[]{:S(2)}, u32[]{:S(2)}) collective-permute-start(bf16[1,3,48,256]{3,2,1,0:T(8,128)(2,1)S(1)} %bitcast.52), channel_id=1, source_target_pairs={{0,4},{4,0},{8,12},{12,8},{16,20},{20,16},{24,28},{28,24},{1,5},{5... | collective-permute-start | bytes 221192 | tf_op jit(solution)/shard_map/ppermute | solution.py:31
  12.7 0.8 %collective-permute-done = bf16[3,48,256]{2,1,0:T(8,128)(2,1)S(1)} collective-permute-done((bf16[3,48,256]{2,1,0:T(8,128)(2,1)}, bf16[3,48,256]{2,1,0:T(8,128)(2,1)S(1)}, u32[]{:S(2)}, u32[]{:S(2)}) %collective-permute-start) | collective-permute-done | bytes 73760 | tf_op jit(solution)/shard_map/ppermute | solution.py:179
  13.5 1.4 %shard_map.68 = (bf16[192,384]{1,0:T(8,128)(2,1)S(1)}, bf16[3,48,256]{2,1,0:T(8,128)(2,1)S(1)}, bf16[3,48,256]{2,1,0:T(8,128)(2,1)S(1)}, bf16[3,256,256]{2,1,0:T(8,128)(2,1)S(1)}, bf16[3,256,256]{2,1,0:T(8,128)(2,1)S(1)}) custom-call(f32[3,256,256]{2,1,0:T(8,128)} %refs_0_.1, bf16[192,384]{1,0:T(8,128)(2,1)} %refs_1_.1, bf16[3,48,256]{2,1,0:T(8,128)(2,1)} %refs_2_.1, ...), custom_call_target="tpu_custom_call" | custom-call | tf_op jit(solution)/shard_map/pallas_call | solution.py:203
  14.8 0.8 %collective-permute-done.4.refs_5_ = bf16[1,3,48,256]{3,2,1,0:T(8,128)(2,1)S(1)} collective-permute-done((bf16[1,3,48,256]{3,2,1,0:T(8,128)(2,1)S(1)}, bf16[1,3,48,256]{3,2,1,0:T(8,128)(2,1)S(1)}, u32[]{:S(2)}, u32[]{:S(2)}) %collective-permute-start.4) | collective-permute-done | bytes 73760 | tf_op jit(solution)/shard_map/ppermute | solution.py:31
  15.7 0.6 %collective-permute-done.3.refs_4_ = bf16[1,3,48,256]{3,2,1,0:T(8,128)(2,1)S(1)} collective-permute-done((bf16[1,3,48,256]{3,2,1,0:T(8,128)(2,1)S(1)}, bf16[1,3,48,256]{3,2,1,0:T(8,128)(2,1)S(1)}, u32[]{:S(2)}, u32[]{:S(2)}) %collective-permute-start.3) | collective-permute-done | bytes 73760 | tf_op jit(solution)/shard_map/ppermute | solution.py:31
  16.3 1.6 %shard_map.69 = (f32[2,3,48,256]{3,2,1,0:T(8,128)S(1)}, f32[2,3,48,256]{3,2,1,0:T(8,128)S(1)}, f32[4,96,256]{2,1,0:T(8,128)S(1)}, bf16[4,96,256]{2,1,0:T(8,128)(2,1)S(1)}, bf16[3,48,256]{2,1,0:T(8,128)(2,1)S(1)}) custom-call(bf16[1,3,48,256]{3,2,1,0:T(8,128)(2,1)S(1)} %bitcast.56, bf16[1,3,48,256]{3,2,1,0:T(8,128)(2,1)S(1)} %bitcast.48, ...), custom_call_target="tpu_custom_call" | custom-call | tf_op jit(solution)/shard_map/pallas_call | solution.py:216
  18.6 0.9 %collective-permute-done.10 = bf16[4,96,256]{2,1,0:T(8,128)(2,1)S(1)} collective-permute-done((bf16[4,96,256]{2,1,0:T(8,128)(2,1)S(1)}, bf16[4,96,256]{2,1,0:T(8,128)(2,1)S(1)}, u32[]{:S(2)}, u32[]{:S(2)}) %collective-permute-start.10) | collective-permute-done | bytes 196640 | tf_op jit(solution)/shard_map/ppermute | solution.py:31
  19.6 1.3 %collective-permute-start.13 = (bf16[96,256]{1,0:T(8,128)(2,1)S(1)}, bf16[96,256]{1,0:T(8,128)(2,1)S(1)}, u32[]{:S(2)}, u32[]{:S(2)}) collective-permute-start(bf16[96,256]{1,0:T(8,128)(2,1)S(1)} %get-tuple-element.36), channel_id=1, source_target_pairs={{0,6},{1,7},{2,4},{3,5},{4,2},{5,3},{6,0},{7,1},{8,14},{9,15},{10,... | collective-permute-start | bytes 147464 | tf_op jit(solution)/shard_map/ppermute | solution.py:31
  20.8 1.1 %collective-permute-start.15 = (bf16[96,256]{1,0:T(8,128)(2,1)S(1)}, bf16[96,256]{1,0:T(8,128)(2,1)S(1)}, u32[]{:S(2)}, u32[]{:S(2)}) collective-permute-start(bf16[96,256]{1,0:T(8,128)(2,1)S(1)} %get-tuple-element.37), channel_id=1, source_target_pairs={{0,2},{1,3},{2,0},{3,1},{4,6},{5,7},{6,4},{7,5},{8,10},{9,11},{10,... | collective-permute-start | bytes 147464 | tf_op jit(solution)/shard_map/ppermute | solution.py:31
  21.9 1.2 %collective-permute-start.14 = (bf16[96,256]{1,0:T(8,128)(2,1)S(1)}, bf16[96,256]{1,0:T(8,128)(2,1)S(1)}, u32[]{:S(2)}, u32[]{:S(2)}) collective-permute-start(bf16[96,256]{1,0:T(8,128)(2,1)S(1)} %get-tuple-element.38), channel_id=1, source_target_pairs={{0,4},{1,5},{2,6},{3,7},{4,0},{5,1},{6,2},{7,3},{8,12},{9,13},{10,... | collective-permute-start | bytes 147464 | tf_op jit(solution)/shard_map/ppermute | solution.py:31
  23.1 0.8 %collective-permute-start.12 = (bf16[3,48,256]{2,1,0:T(8,128)(2,1)S(1)}, bf16[3,48,256]{2,1,0:T(8,128)(2,1)S(1)}, u32[]{:S(2)}, u32[]{:S(2)}) collective-permute-start(bf16[3,48,256]{2,1,0:T(8,128)(2,1)S(1)} %get-tuple-element.30), channel_id=1, source_target_pairs={{0,4},{4,8},{8,12},{12,0},{16,20},{20,24},{24,28},{28,16},{1,5},{5... | collective-permute-start | bytes 221192 | tf_op jit(solution)/shard_map/ppermute | solution.py:179
  24.0 1.0 %collective-permute-start.11 = (bf16[1,3,48,256]{3,2,1,0:T(8,128)(2,1)S(1)}, bf16[1,3,48,256]{3,2,1,0:T(8,128)(2,1)S(1)}, u32[]{:S(2)}, u32[]{:S(2)}) collective-permute-start(bf16[1,3,48,256]{3,2,1,0:T(8,128)(2,1)S(1)} %fusion.8), channel_id=1, source_target_pairs={{0,2},{1,3},{2,0},{3,1},{4,6},{5,7},{6,4},{7,5},{8,10},{9,11},{10,... | collective-permute-start | bytes 221192 | tf_op jit(solution)/shard_map/ppermute | solution.py:31
  25.4 1.4 %collective-permute-done.14 = bf16[96,256]{1,0:T(8,128)(2,1)S(1)} collective-permute-done((bf16[96,256]{1,0:T(8,128)(2,1)S(1)}, bf16[96,256]{1,0:T(8,128)(2,1)S(1)}, u32[]{:S(2)}, u32[]{:S(2)}) %collective-permute-start.14) | collective-permute-done | bytes 49184 | tf_op jit(solution)/shard_map/ppermute | solution.py:31
  26.8 2.4 %collective-permute-start.18 = (bf16[96,256]{1,0:T(8,128)(2,1)S(1)}, bf16[96,256]{1,0:T(8,128)(2,1)S(1)}, u32[]{:S(2)}, u32[]{:S(2)}) collective-permute-start(bf16[96,256]{1,0:T(8,128)(2,1)S(1)} %fusion.7), channel_id=1, source_target_pairs={{0,24},{4,28},{8,16},{12,20},{16,8},{20,12},{24,0},{28,4},{1,25},{... | collective-permute-start | bytes 147464 | tf_op jit(solution)/shard_map/ppermute | solution.py:31
  29.2 2.1 %collective-permute-start.16 = (bf16[96,256]{1,0:T(8,128)(2,1)S(1)}, bf16[96,256]{1,0:T(8,128)(2,1)S(1)}, u32[]{:S(2)}, u32[]{:S(2)}) collective-permute-start(bf16[96,256]{1,0:T(8,128)(2,1)S(1)} %fusion.7), channel_id=1, source_target_pairs={{0,16},{4,20},{8,24},{12,28},{16,0},{20,4},{24,8},{28,12},{1,17},{... | collective-permute-start | bytes 147464 | tf_op jit(solution)/shard_map/ppermute | solution.py:31
  31.3 1.6 %collective-permute-done.18 = bf16[96,256]{1,0:T(8,128)(2,1)S(1)} collective-permute-done((bf16[96,256]{1,0:T(8,128)(2,1)S(1)}, bf16[96,256]{1,0:T(8,128)(2,1)S(1)}, u32[]{:S(2)}, u32[]{:S(2)}) %collective-permute-start.18) | collective-permute-done | bytes 49184 | tf_op jit(solution)/shard_map/ppermute | solution.py:31
  33.4 0.9 %collective-permute-done.16 = bf16[96,256]{1,0:T(8,128)(2,1)S(1)} collective-permute-done((bf16[96,256]{1,0:T(8,128)(2,1)S(1)}, bf16[96,256]{1,0:T(8,128)(2,1)S(1)}, u32[]{:S(2)}, u32[]{:S(2)}) %collective-permute-start.16) | collective-permute-done | bytes 49184 | tf_op jit(solution)/shard_map/ppermute | solution.py:31
  34.4 2.3 %collective-permute-start.21 = (bf16[96,256]{1,0:T(8,128)(2,1)S(1)}, bf16[96,256]{1,0:T(8,128)(2,1)S(1)}, u32[]{:S(2)}, u32[]{:S(2)}) collective-permute-start(bf16[96,256]{1,0:T(8,128)(2,1)S(1)} %add_convert_fusion), channel_id=1, source_target_pairs={{0,6},{1,7},{2,4},{3,5},{4,2},{5,3},{6,0},{7,1},{8,14},{9,15},{10,... | collective-permute-start | bytes 147464 | tf_op jit(solution)/shard_map/ppermute | solution.py:31
  36.7 0.7 %collective-permute-start.20 = (bf16[96,256]{1,0:T(8,128)(2,1)S(1)}, bf16[96,256]{1,0:T(8,128)(2,1)S(1)}, u32[]{:S(2)}, u32[]{:S(2)}) collective-permute-start(bf16[96,256]{1,0:T(8,128)(2,1)S(1)} %add_convert_fusion), channel_id=1, source_target_pairs={{0,2},{1,3},{2,0},{3,1},{4,6},{5,7},{6,4},{7,5},{8,10},{9,11},{10,... | collective-permute-start | bytes 147464 | tf_op jit(solution)/shard_map/ppermute | solution.py:31
  37.4 0.5 %collective-permute-start.19 = (bf16[96,256]{1,0:T(8,128)(2,1)S(1)}, bf16[96,256]{1,0:T(8,128)(2,1)S(1)}, u32[]{:S(2)}, u32[]{:S(2)}) collective-permute-start(bf16[96,256]{1,0:T(8,128)(2,1)S(1)} %add_convert_fusion), channel_id=1, source_target_pairs={{0,4},{1,5},{2,6},{3,7},{4,0},{5,1},{6,2},{7,3},{8,12},{9,13},{10,... | collective-permute-start | bytes 147464 | tf_op jit(solution)/shard_map/ppermute | solution.py:31
  38.0 1.5 %collective-permute-done.21 = bf16[96,256]{1,0:T(8,128)(2,1)S(1)} collective-permute-done((bf16[96,256]{1,0:T(8,128)(2,1)S(1)}, bf16[96,256]{1,0:T(8,128)(2,1)S(1)}, u32[]{:S(2)}, u32[]{:S(2)}) %collective-permute-start.21) | collective-permute-done | bytes 49184 | tf_op jit(solution)/shard_map/ppermute | solution.py:31
  39.5 1.4 %collective-permute-done.20 = bf16[96,256]{1,0:T(8,128)(2,1)S(1)} collective-permute-done((bf16[96,256]{1,0:T(8,128)(2,1)S(1)}, bf16[96,256]{1,0:T(8,128)(2,1)S(1)}, u32[]{:S(2)}, u32[]{:S(2)}) %collective-permute-start.20) | collective-permute-done | bytes 49184 | tf_op jit(solution)/shard_map/ppermute | solution.py:31
  40.8 0.7 %collective-permute-done.19 = bf16[96,256]{1,0:T(8,128)(2,1)S(1)} collective-permute-done((bf16[96,256]{1,0:T(8,128)(2,1)S(1)}, bf16[96,256]{1,0:T(8,128)(2,1)S(1)}, u32[]{:S(2)}, u32[]{:S(2)}) %collective-permute-start.19) | collective-permute-done | bytes 49184 | tf_op jit(solution)/shard_map/ppermute | solution.py:31
  41.6 0.7 %fusion.3 = bf16[3,48,256]{2,1,0:T(8,128)(2,1)} fusion(f32[1,2,3,48,256]{4,3,2,1,0:T(8,128)S(1)} %add_bitcast_fusion, bf16[3,48,256]{2,1,0:T(8,128)(2,1)S(1)} %collective-permute-done.12, bf16[1,3,48,256]{3,2,1,0:T(8,128)(2,1)S(1)} %collective-permute-done.11), kind=kLoop, calls=%fused_computation.8 | loop fusion | flops 184320 | bytes 368640 | tf_op jit(solution)/shard_map/convert_element_type | solution.py:252
  42.3 0.8 %collective-permute-done.22.there_ref = bf16[4,96,256]{2,1,0:T(8,128)(2,1)S(1)} collective-permute-done((bf16[4,96,256]{2,1,0:T(8,128)(2,1)S(1)}, bf16[4,96,256]{2,1,0:T(8,128)(2,1)S(1)}, u32[]{:S(2)}, u32[]{:S(2)}) %collective-permute-start.22) | collective-permute-done | bytes 196640 | tf_op jit(solution)/shard_map/ppermute | solution.py:31
  43.0 0.9 %shard_map.70 = f32[768,256]{1,0:T(8,128)} custom-call(bf16[4,96,256]{2,1,0:T(8,128)(2,1)S(1)} %pad_maximum_fusion.here_ref, bf16[4,96,256]{2,1,0:T(8,128)(2,1)S(1)} %collective-permute-done.22.there_ref), custom_call_target="tpu_custom_call" | custom-call | tf_op jit(solution)/shard_map/pallas_call | solution.py:274
  (25 shorter events, 1.8 us)
Async XLA Ops:
  0.6 8.6 %collective-permute-start.2 = (bf16[3,48,256]{2,1,0:T(8,128)(2,1)}, bf16[3,48,256]{2,1,0:T(8,128)(2,1)S(1)}, u32[]{:S(2)}, u32[]{:S(2)}) collective-permute-start(bf16[3,48,256]{2,1,0:T(8,128)(2,1)} %refs_2_.1), channel_id=1, source_target_pairs={{0,16},{4,20},{8,24},{12,28},{16,0},{20,4},{24,8},{28,12},{1,17},{... | collective-permute-start | bytes 221192 | tf_op jit(solution)/shard_map/ppermute | solution.py:31
  4.7 7.2 %collective-permute-start.6 = (bf16[3,48,256]{2,1,0:T(8,128)(2,1)}, bf16[3,48,256]{2,1,0:T(8,128)(2,1)S(1)}, u32[]{:S(2)}, u32[]{:S(2)}) collective-permute-start(bf16[3,48,256]{2,1,0:T(8,128)(2,1)} %refs_2_.1), channel_id=1, source_target_pairs={{0,2},{1,3},{2,0},{3,1},{4,6},{5,7},{6,4},{7,5},{8,10},{9,11},{10,... | collective-permute-start | bytes 221192 | tf_op jit(solution)/shard_map/ppermute | solution.py:31
  6.3 6.5 %collective-permute-start.1 = (bf16[3,48,256]{2,1,0:T(8,128)(2,1)}, bf16[3,48,256]{2,1,0:T(8,128)(2,1)S(1)}, u32[]{:S(2)}, u32[]{:S(2)}) collective-permute-start(bf16[3,48,256]{2,1,0:T(8,128)(2,1)} %refs_2_.1), channel_id=1, source_target_pairs={{0,8},{4,12},{8,0},{12,4},{16,24},{20,28},{24,16},{28,20},{1,9},{5... | collective-permute-start | bytes 221192 | tf_op jit(solution)/shard_map/ppermute | solution.py:31
  7.8 5.6 %collective-permute-start = (bf16[3,48,256]{2,1,0:T(8,128)(2,1)}, bf16[3,48,256]{2,1,0:T(8,128)(2,1)S(1)}, u32[]{:S(2)}, u32[]{:S(2)}) collective-permute-start(bf16[3,48,256]{2,1,0:T(8,128)(2,1)} %refs_2_.1), channel_id=1, source_target_pairs={{4,0},{8,4},{12,8},{0,12},{20,16},{24,20},{28,24},{16,28},{5,1},{9... | collective-permute-start | bytes 221192 | tf_op jit(solution)/shard_map/ppermute | solution.py:179
  9.2 5.6 %collective-permute-start.5 = (bf16[1,3,48,256]{3,2,1,0:T(8,128)(2,1)S(1)}, bf16[1,3,48,256]{3,2,1,0:T(8,128)(2,1)S(1)}, u32[]{:S(2)}, u32[]{:S(2)}) collective-permute-start(bf16[1,3,48,256]{3,2,1,0:T(8,128)(2,1)S(1)} %bitcast.50), channel_id=1, source_target_pairs={{0,12},{4,8},{8,4},{12,0},{16,28},{20,24},{24,20},{28,16},{1,13},{... | collective-permute-start | bytes 221192 | tf_op jit(solution)/shard_map/ppermute | solution.py:31
  10.6 5.1 %collective-permute-start.4 = (bf16[1,3,48,256]{3,2,1,0:T(8,128)(2,1)S(1)}, bf16[1,3,48,256]{3,2,1,0:T(8,128)(2,1)S(1)}, u32[]{:S(2)}, u32[]{:S(2)}) collective-permute-start(bf16[1,3,48,256]{3,2,1,0:T(8,128)(2,1)S(1)} %bitcast.51), channel_id=1, source_target_pairs={{0,8},{4,12},{8,0},{12,4},{16,24},{20,28},{24,16},{28,20},{1,9},{5... | collective-permute-start | bytes 221192 | tf_op jit(solution)/shard_map/ppermute | solution.py:31
  12.0 4.4 %collective-permute-start.3 = (bf16[1,3,48,256]{3,2,1,0:T(8,128)(2,1)S(1)}, bf16[1,3,48,256]{3,2,1,0:T(8,128)(2,1)S(1)}, u32[]{:S(2)}, u32[]{:S(2)}) collective-permute-start(bf16[1,3,48,256]{3,2,1,0:T(8,128)(2,1)S(1)} %bitcast.52), channel_id=1, source_target_pairs={{0,4},{4,0},{8,12},{12,8},{16,20},{20,16},{24,28},{28,24},{1,5},{5... | collective-permute-start | bytes 221192 | tf_op jit(solution)/shard_map/ppermute | solution.py:31
  12.7 3.6 %collective-permute-start.7 = (bf16[3,48,256]{2,1,0:T(8,128)(2,1)}, bf16[3,48,256]{2,1,0:T(8,128)(2,1)S(1)}, u32[]{:S(2)}, u32[]{:S(2)}) collective-permute-start(bf16[3,48,256]{2,1,0:T(8,128)(2,1)} %refs_2_.1), channel_id=1, source_target_pairs={{0,1},{1,0},{2,3},{3,2},{4,5},{5,4},{6,7},{7,6},{8,9},{9,8},{10,11... | collective-permute-start | bytes 221192 | tf_op jit(solution)/shard_map/ppermute | solution.py:31
  13.5 2.9 %collective-permute-start.8 = (bf16[3,48,256]{2,1,0:T(8,128)(2,1)S(1)}, bf16[3,48,256]{2,1,0:T(8,128)(2,1)S(1)}, u32[]{:S(2)}, u32[]{:S(2)}) collective-permute-start(bf16[3,48,256]{2,1,0:T(8,128)(2,1)S(1)} %collective-permute-done.6), channel_id=1, source_target_pairs={{0,1},{1,0},{2,3},{3,2},{4,5},{5,4},{6,7},{7,6},{8,9},{9,8},{10,11... | collective-permute-start | bytes 221192 | tf_op jit(solution)/shard_map/ppermute | solution.py:31
  18.0 1.5 %collective-permute-start.10 = (bf16[4,96,256]{2,1,0:T(8,128)(2,1)S(1)}, bf16[4,96,256]{2,1,0:T(8,128)(2,1)S(1)}, u32[]{:S(2)}, u32[]{:S(2)}) collective-permute-start(bf16[4,96,256]{2,1,0:T(8,128)(2,1)S(1)} %get-tuple-element.27), channel_id=1, source_target_pairs={{0,1},{1,0},{2,3},{3,2},{4,5},{5,4},{6,7},{7,6},{8,9},{9,8},{10,11... | collective-permute-start | bytes 589832 | tf_op jit(solution)/shard_map/ppermute | solution.py:31
  18.1 5.9 %collective-permute-start.9 = (f32[2,3,48,256]{3,2,1,0:T(8,128)S(1)}, f32[2,3,48,256]{3,2,1,0:T(8,128)S(1)}, u32[]{:S(2)}, u32[]{:S(2)}) collective-permute-start(f32[2,3,48,256]{3,2,1,0:T(8,128)S(1)} %get-tuple-element.25), channel_id=1, source_target_pairs={{0,1},{1,0},{2,3},{3,2},{4,5},{5,4},{6,7},{7,6},{8,9},{9,8},{10,11... | collective-permute-start | bytes 884744 | tf_op jit(solution)/shard_map/ppermute | solution.py:31
  19.6 5.4 %collective-permute-start.13 = (bf16[96,256]{1,0:T(8,128)(2,1)S(1)}, bf16[96,256]{1,0:T(8,128)(2,1)S(1)}, u32[]{:S(2)}, u32[]{:S(2)}) collective-permute-start(bf16[96,256]{1,0:T(8,128)(2,1)S(1)} %get-tuple-element.36), channel_id=1, source_target_pairs={{0,6},{1,7},{2,4},{3,5},{4,2},{5,3},{6,0},{7,1},{8,14},{9,15},{10,... | collective-permute-start | bytes 147464 | tf_op jit(solution)/shard_map/ppermute | solution.py:31
  20.8 4.5 %collective-permute-start.15 = (bf16[96,256]{1,0:T(8,128)(2,1)S(1)}, bf16[96,256]{1,0:T(8,128)(2,1)S(1)}, u32[]{:S(2)}, u32[]{:S(2)}) collective-permute-start(bf16[96,256]{1,0:T(8,128)(2,1)S(1)} %get-tuple-element.37), channel_id=1, source_target_pairs={{0,2},{1,3},{2,0},{3,1},{4,6},{5,7},{6,4},{7,5},{8,10},{9,11},{10,... | collective-permute-start | bytes 147464 | tf_op jit(solution)/shard_map/ppermute | solution.py:31
  21.9 4.9 %collective-permute-start.14 = (bf16[96,256]{1,0:T(8,128)(2,1)S(1)}, bf16[96,256]{1,0:T(8,128)(2,1)S(1)}, u32[]{:S(2)}, u32[]{:S(2)}) collective-permute-start(bf16[96,256]{1,0:T(8,128)(2,1)S(1)} %get-tuple-element.38), channel_id=1, source_target_pairs={{0,4},{1,5},{2,6},{3,7},{4,0},{5,1},{6,2},{7,3},{8,12},{9,13},{10,... | collective-permute-start | bytes 147464 | tf_op jit(solution)/shard_map/ppermute | solution.py:31
  23.1 8.2 %collective-permute-start.12 = (bf16[3,48,256]{2,1,0:T(8,128)(2,1)S(1)}, bf16[3,48,256]{2,1,0:T(8,128)(2,1)S(1)}, u32[]{:S(2)}, u32[]{:S(2)}) collective-permute-start(bf16[3,48,256]{2,1,0:T(8,128)(2,1)S(1)} %get-tuple-element.30), channel_id=1, source_target_pairs={{0,4},{4,8},{8,12},{12,0},{16,20},{20,24},{24,28},{28,16},{1,5},{5... | collective-permute-start | bytes 221192 | tf_op jit(solution)/shard_map/ppermute | solution.py:179
  24.0 10.3 %collective-permute-start.11 = (bf16[1,3,48,256]{3,2,1,0:T(8,128)(2,1)S(1)}, bf16[1,3,48,256]{3,2,1,0:T(8,128)(2,1)S(1)}, u32[]{:S(2)}, u32[]{:S(2)}) collective-permute-start(bf16[1,3,48,256]{3,2,1,0:T(8,128)(2,1)S(1)} %fusion.8), channel_id=1, source_target_pairs={{0,2},{1,3},{2,0},{3,1},{4,6},{5,7},{6,4},{7,5},{8,10},{9,11},{10,... | collective-permute-start | bytes 221192 | tf_op jit(solution)/shard_map/ppermute | solution.py:31
  26.8 6.1 %collective-permute-start.18 = (bf16[96,256]{1,0:T(8,128)(2,1)S(1)}, bf16[96,256]{1,0:T(8,128)(2,1)S(1)}, u32[]{:S(2)}, u32[]{:S(2)}) collective-permute-start(bf16[96,256]{1,0:T(8,128)(2,1)S(1)} %fusion.7), channel_id=1, source_target_pairs={{0,24},{4,28},{8,16},{12,20},{16,8},{20,12},{24,0},{28,4},{1,25},{... | collective-permute-start | bytes 147464 | tf_op jit(solution)/shard_map/ppermute | solution.py:31
  29.2 4.2 %collective-permute-start.17 = (bf16[96,256]{1,0:T(8,128)(2,1)S(1)}, bf16[96,256]{1,0:T(8,128)(2,1)S(1)}, u32[]{:S(2)}, u32[]{:S(2)}) collective-permute-start(bf16[96,256]{1,0:T(8,128)(2,1)S(1)} %fusion.7), channel_id=1, source_target_pairs={{0,8},{4,12},{8,0},{12,4},{16,24},{20,28},{24,16},{28,20},{1,9},{5... | collective-permute-start | bytes 147464 | tf_op jit(solution)/shard_map/ppermute | solution.py:31
  29.2 5.1 %collective-permute-start.16 = (bf16[96,256]{1,0:T(8,128)(2,1)S(1)}, bf16[96,256]{1,0:T(8,128)(2,1)S(1)}, u32[]{:S(2)}, u32[]{:S(2)}) collective-permute-start(bf16[96,256]{1,0:T(8,128)(2,1)S(1)} %fusion.7), channel_id=1, source_target_pairs={{0,16},{4,20},{8,24},{12,28},{16,0},{20,4},{24,8},{28,12},{1,17},{... | collective-permute-start | bytes 147464 | tf_op jit(solution)/shard_map/ppermute | solution.py:31
  34.4 5.1 %collective-permute-start.21 = (bf16[96,256]{1,0:T(8,128)(2,1)S(1)}, bf16[96,256]{1,0:T(8,128)(2,1)S(1)}, u32[]{:S(2)}, u32[]{:S(2)}) collective-permute-start(bf16[96,256]{1,0:T(8,128)(2,1)S(1)} %add_convert_fusion), channel_id=1, source_target_pairs={{0,6},{1,7},{2,4},{3,5},{4,2},{5,3},{6,0},{7,1},{8,14},{9,15},{10,... | collective-permute-start | bytes 147464 | tf_op jit(solution)/shard_map/ppermute | solution.py:31
  36.7 4.1 %collective-permute-start.20 = (bf16[96,256]{1,0:T(8,128)(2,1)S(1)}, bf16[96,256]{1,0:T(8,128)(2,1)S(1)}, u32[]{:S(2)}, u32[]{:S(2)}) collective-permute-start(bf16[96,256]{1,0:T(8,128)(2,1)S(1)} %add_convert_fusion), channel_id=1, source_target_pairs={{0,2},{1,3},{2,0},{3,1},{4,6},{5,7},{6,4},{7,5},{8,10},{9,11},{10,... | collective-permute-start | bytes 147464 | tf_op jit(solution)/shard_map/ppermute | solution.py:31
  37.4 4.1 %collective-permute-start.19 = (bf16[96,256]{1,0:T(8,128)(2,1)S(1)}, bf16[96,256]{1,0:T(8,128)(2,1)S(1)}, u32[]{:S(2)}, u32[]{:S(2)}) collective-permute-start(bf16[96,256]{1,0:T(8,128)(2,1)S(1)} %add_convert_fusion), channel_id=1, source_target_pairs={{0,4},{1,5},{2,6},{3,7},{4,0},{5,1},{6,2},{7,3},{8,12},{9,13},{10,... | collective-permute-start | bytes 147464 | tf_op jit(solution)/shard_map/ppermute | solution.py:31
  41.5 1.5 %collective-permute-start.22 = (bf16[4,96,256]{2,1,0:T(8,128)(2,1)S(1)}, bf16[4,96,256]{2,1,0:T(8,128)(2,1)S(1)}, u32[]{:S(2)}, u32[]{:S(2)}) collective-permute-start(bf16[4,96,256]{2,1,0:T(8,128)(2,1)S(1)} %pad_maximum_fusion.here_ref), channel_id=1, source_target_pairs={{0,1},{1,0},{2,3},{3,2},{4,5},{5,4},{6,7},{7,6},{8,9},{9,8},{10,11... | collective-permute-start | bytes 589832 | tf_op jit(solution)/shard_map/ppermute | solution.py:31

commit v9 on v7

--- a/solution.py
+++ b/solution.py
@@ -147,7 +147,7 @@
     limit = pltpu.CompilerParams(vmem_limit_bytes=32 * 1024 * 1024)
     tile_shape = jax.ShapeDtypeStruct(saved_panels.shape, BF16)
 
-    near = [bits for bits in (2, 3, 1) if bits < rows]
+    near = [bits for bits in (2, 1, 3) if bits < rows]
     along_row, row_tiles = [(0,)], [None]
     far = [bits for bits in range(4, rows, 4)]
     crossed = [swap(saved_panels, ("row",), sizes, {"row": bits}) for bits in far]

time: 43.4 us -> 43.5 us (level)
  starting transfers between devices: 25.7 us -> 26.8 us
  waiting for transfers between devices: 12.3 us -> 11.2 us
    ppermute x23, starting transfers between devices: 25.7 us -> 26.8 us  [swap(): return lax.ppermute(value, axes, pairs)]
    ppermute x23, waiting for transfers between devices: 12.3 us -> 11.2 us  [swap(): return lax.ppermute(value, axes, pairs)]
  transfers between devices with their start and end apart: 23 -> 23, of which waited for: 15 -> 12; matrix products, arithmetic and copies ran while one was open for 2% -> 2% of each run, Pallas kernels for 3% -> 3%
where the time goes in v9:
time: 43.5 us; the launch traced here: 43.4 us
  starting transfers between devices  26.8 us (62%)
  waiting for transfers between devices  11.2 us (26%)
  Pallas kernels  3.76 us (9%)
  other arithmetic  0.83 us (2%)
  between operations  0.73 us (2%)
    ppermute x23, starting transfers between devices, swap(): return lax.ppermute(value, axes, pairs)  26.8 us
    ppermute x23, waiting for transfers between devices, swap(): return lax.ppermute(value, axes, pairs)  11.2 us
    pallas_call x1, Pallas kernels, body(): pl.pallas_call(functools.partial(main_kernel, along_row, along_col), out_...  1.45 us
    pallas_call x1, Pallas kernels, body(): pl.pallas_call(prepare_kernel, out_shape=[jax.ShapeDtypeStruct(value.shap...  1.36 us
    pallas_call x1, Pallas kernels, body(): pl.pallas_call(finish_kernel, out_shape=jax.ShapeDtypeStruct((panels * wi...  0.94 us
  transfers between devices with their start and end apart: 23, of which 12 were waited for; matrix products, arithmetic and copies ran while one was open for 2% of the time, Pallas kernels for 3%

profile of v9, /device:TPU:0, one launch (start us, length us, event | category | flops | bytes accessed | tf_op | source)
XLA Modules:
  0.0 43.4 jit_solution(2522387802216499024)
XLA Ops:
  0.6 4.1 %collective-permute-start.3 = (bf16[3,48,256]{2,1,0:T(8,128)(2,1)}, bf16[3,48,256]{2,1,0:T(8,128)(2,1)S(1)}, u32[]{:S(2)}, u32[]{:S(2)}) collective-permute-start(bf16[3,48,256]{2,1,0:T(8,128)(2,1)} %refs_2_.1), channel_id=1, source_target_pairs={{0,16},{4,20},{8,24},{12,28},{16,0},{20,4},{24,8},{28,12},{1,17},{... | collective-permute-start | bytes 221192 | tf_op jit(solution)/shard_map/ppermute | solution.py:31
  4.7 1.5 %collective-permute-start.7 = (bf16[3,48,256]{2,1,0:T(8,128)(2,1)}, bf16[3,48,256]{2,1,0:T(8,128)(2,1)S(1)}, u32[]{:S(2)}, u32[]{:S(2)}) collective-permute-start(bf16[3,48,256]{2,1,0:T(8,128)(2,1)} %refs_2_.1), channel_id=1, source_target_pairs={{0,2},{1,3},{2,0},{3,1},{4,6},{5,7},{6,4},{7,5},{8,10},{9,11},{10,... | collective-permute-start | bytes 221192 | tf_op jit(solution)/shard_map/ppermute | solution.py:31
  6.3 2.5 %collective-permute-start.2 = (bf16[3,48,256]{2,1,0:T(8,128)(2,1)}, bf16[3,48,256]{2,1,0:T(8,128)(2,1)S(1)}, u32[]{:S(2)}, u32[]{:S(2)}) collective-permute-start(bf16[3,48,256]{2,1,0:T(8,128)(2,1)} %refs_2_.1), channel_id=1, source_target_pairs={{0,12},{4,8},{8,4},{12,0},{16,28},{20,24},{24,20},{28,16},{1,13},{... | collective-permute-start | bytes 221192 | tf_op jit(solution)/shard_map/ppermute | solution.py:31
  8.8 0.5 %collective-permute-start.1 = (bf16[3,48,256]{2,1,0:T(8,128)(2,1)}, bf16[3,48,256]{2,1,0:T(8,128)(2,1)S(1)}, u32[]{:S(2)}, u32[]{:S(2)}) collective-permute-start(bf16[3,48,256]{2,1,0:T(8,128)(2,1)} %refs_2_.1), channel_id=1, source_target_pairs={{0,4},{4,0},{8,12},{12,8},{16,20},{20,16},{24,28},{28,24},{1,5},{5... | collective-permute-start | bytes 221192 | tf_op jit(solution)/shard_map/ppermute | solution.py:31
  9.7 2.5 %collective-permute-start.6 = (bf16[1,3,48,256]{3,2,1,0:T(8,128)(2,1)S(1)}, bf16[1,3,48,256]{3,2,1,0:T(8,128)(2,1)S(1)}, u32[]{:S(2)}, u32[]{:S(2)}) collective-permute-start(bf16[1,3,48,256]{3,2,1,0:T(8,128)(2,1)S(1)} %bitcast.45), channel_id=1, source_target_pairs={{0,12},{4,8},{8,4},{12,0},{16,28},{20,24},{24,20},{28,16},{1,13},{... | collective-permute-start | bytes 221192 | tf_op jit(solution)/shard_map/ppermute | solution.py:31
  12.3 0.5 %collective-permute-start.5 = (bf16[1,3,48,256]{3,2,1,0:T(8,128)(2,1)S(1)}, bf16[1,3,48,256]{3,2,1,0:T(8,128)(2,1)S(1)}, u32[]{:S(2)}, u32[]{:S(2)}) collective-permute-start(bf16[1,3,48,256]{3,2,1,0:T(8,128)(2,1)S(1)} %bitcast.46), channel_id=1, source_target_pairs={{0,4},{4,0},{8,12},{12,8},{16,20},{20,16},{24,28},{28,24},{1,5},{5... | collective-permute-start | bytes 221192 | tf_op jit(solution)/shard_map/ppermute | solution.py:31
  12.8 1.4 %collective-permute-start.4 = (bf16[1,3,48,256]{3,2,1,0:T(8,128)(2,1)S(1)}, bf16[1,3,48,256]{3,2,1,0:T(8,128)(2,1)S(1)}, u32[]{:S(2)}, u32[]{:S(2)}) collective-permute-start(bf16[1,3,48,256]{3,2,1,0:T(8,128)(2,1)S(1)} %bitcast.47), channel_id=1, source_target_pairs={{0,8},{4,12},{8,0},{12,4},{16,24},{20,28},{24,16},{28,20},{1,9},{5... | collective-permute-start | bytes 221192 | tf_op jit(solution)/shard_map/ppermute | solution.py:31
  14.2 0.7 %collective-permute-done.1 = bf16[3,48,256]{2,1,0:T(8,128)(2,1)S(1)} collective-permute-done((bf16[3,48,256]{2,1,0:T(8,128)(2,1)}, bf16[3,48,256]{2,1,0:T(8,128)(2,1)S(1)}, u32[]{:S(2)}, u32[]{:S(2)}) %collective-permute-start.1) | collective-permute-done | bytes 73760 | tf_op jit(solution)/shard_map/ppermute | solution.py:31
  15.4 1.4 %shard_map.68 = (bf16[192,384]{1,0:T(8,128)(2,1)S(1)}, bf16[3,48,256]{2,1,0:T(8,128)(2,1)S(1)}, bf16[3,48,256]{2,1,0:T(8,128)(2,1)S(1)}, bf16[3,256,256]{2,1,0:T(8,128)(2,1)S(1)}, bf16[3,256,256]{2,1,0:T(8,128)(2,1)S(1)}) custom-call(f32[3,256,256]{2,1,0:T(8,128)} %refs_0_.1, bf16[192,384]{1,0:T(8,128)(2,1)} %refs_1_.1, bf16[3,48,256]{2,1,0:T(8,128)(2,1)} %refs_2_.1, ...), custom_call_target="tpu_custom_call" | custom-call | tf_op jit(solution)/shard_map/pallas_call | solution.py:177
  17.2 1.4 %shard_map.69 = (f32[2,3,48,256]{3,2,1,0:T(8,128)S(1)}, f32[2,3,48,256]{3,2,1,0:T(8,128)S(1)}, f32[4,96,256]{2,1,0:T(8,128)S(1)}, bf16[4,96,256]{2,1,0:T(8,128)(2,1)S(1)}) custom-call(bf16[1,3,48,256]{3,2,1,0:T(8,128)(2,1)S(1)} %bitcast.43, bf16[1,3,48,256]{3,2,1,0:T(8,128)(2,1)S(1)} %bitcast.52, bf16[1,3,48,256]{3,2,1,0:T(8,128)(2,1)S(1)} %bitcast.51, ...), custom_call_target="tpu_custom_call" | custom-call | tf_op jit(solution)/shard_map/pallas_call | solution.py:189
  19.2 0.9 %collective-permute-done.11 = bf16[4,96,256]{2,1,0:T(8,128)(2,1)S(1)} collective-permute-done((bf16[4,96,256]{2,1,0:T(8,128)(2,1)S(1)}, bf16[4,96,256]{2,1,0:T(8,128)(2,1)S(1)}, u32[]{:S(2)}, u32[]{:S(2)}) %collective-permute-start.11) | collective-permute-done | bytes 196640 | tf_op jit(solution)/shard_map/ppermute | solution.py:31
  20.2 1.5 %collective-permute-start.13 = (bf16[96,256]{1,0:T(8,128)(2,1)S(1)}, bf16[96,256]{1,0:T(8,128)(2,1)S(1)}, u32[]{:S(2)}, u32[]{:S(2)}) collective-permute-start(bf16[96,256]{1,0:T(8,128)(2,1)S(1)} %get-tuple-element.32), channel_id=1, source_target_pairs={{0,6},{1,7},{2,4},{3,5},{4,2},{5,3},{6,0},{7,1},{8,14},{9,15},{10,... | collective-permute-start | bytes 147464 | tf_op jit(solution)/shard_map/ppermute | solution.py:31
  21.7 1.5 %collective-permute-start.15 = (bf16[96,256]{1,0:T(8,128)(2,1)S(1)}, bf16[96,256]{1,0:T(8,128)(2,1)S(1)}, u32[]{:S(2)}, u32[]{:S(2)}) collective-permute-start(bf16[96,256]{1,0:T(8,128)(2,1)S(1)} %get-tuple-element.33), channel_id=1, source_target_pairs={{0,2},{1,3},{2,0},{3,1},{4,6},{5,7},{6,4},{7,5},{8,10},{9,11},{10,... | collective-permute-start | bytes 147464 | tf_op jit(solution)/shard_map/ppermute | solution.py:31
  23.2 0.6 %collective-permute-start.14 = (bf16[96,256]{1,0:T(8,128)(2,1)S(1)}, bf16[96,256]{1,0:T(8,128)(2,1)S(1)}, u32[]{:S(2)}, u32[]{:S(2)}) collective-permute-start(bf16[96,256]{1,0:T(8,128)(2,1)S(1)} %get-tuple-element.34), channel_id=1, source_target_pairs={{0,4},{1,5},{2,6},{3,7},{4,0},{5,1},{6,2},{7,3},{8,12},{9,13},{10,... | collective-permute-start | bytes 147464 | tf_op jit(solution)/shard_map/ppermute | solution.py:31
  23.8 0.5 %collective-permute-start.12 = (bf16[1,3,48,256]{3,2,1,0:T(8,128)(2,1)S(1)}, bf16[1,3,48,256]{3,2,1,0:T(8,128)(2,1)S(1)}, u32[]{:S(2)}, u32[]{:S(2)}) collective-permute-start(bf16[1,3,48,256]{3,2,1,0:T(8,128)(2,1)S(1)} %fusion.7), channel_id=1, source_target_pairs={{0,2},{1,3},{2,0},{3,1},{4,6},{5,7},{6,4},{7,5},{8,10},{9,11},{10,... | collective-permute-start | bytes 221192 | tf_op jit(solution)/shard_map/ppermute | solution.py:31
  24.4 0.9 %collective-permute-done.13 = bf16[96,256]{1,0:T(8,128)(2,1)S(1)} collective-permute-done((bf16[96,256]{1,0:T(8,128)(2,1)S(1)}, bf16[96,256]{1,0:T(8,128)(2,1)S(1)}, u32[]{:S(2)}, u32[]{:S(2)}) %collective-permute-start.13) | collective-permute-done | bytes 49184 | tf_op jit(solution)/shard_map/ppermute | solution.py:31
  25.3 0.9 %collective-permute-done.15 = bf16[96,256]{1,0:T(8,128)(2,1)S(1)} collective-permute-done((bf16[96,256]{1,0:T(8,128)(2,1)S(1)}, bf16[96,256]{1,0:T(8,128)(2,1)S(1)}, u32[]{:S(2)}, u32[]{:S(2)}) %collective-permute-start.15) | collective-permute-done | bytes 49184 | tf_op jit(solution)/shard_map/ppermute | solution.py:31
  26.2 1.1 %collective-permute-done.14 = bf16[96,256]{1,0:T(8,128)(2,1)S(1)} collective-permute-done((bf16[96,256]{1,0:T(8,128)(2,1)S(1)}, bf16[96,256]{1,0:T(8,128)(2,1)S(1)}, u32[]{:S(2)}, u32[]{:S(2)}) %collective-permute-start.14) | collective-permute-done | bytes 49184 | tf_op jit(solution)/shard_map/ppermute | solution.py:31
  27.3 1.3 %collective-permute-start.18 = (bf16[96,256]{1,0:T(8,128)(2,1)S(1)}, bf16[96,256]{1,0:T(8,128)(2,1)S(1)}, u32[]{:S(2)}, u32[]{:S(2)}) collective-permute-start(bf16[96,256]{1,0:T(8,128)(2,1)S(1)} %fusion.5), channel_id=1, source_target_pairs={{0,24},{4,28},{8,16},{12,20},{16,8},{20,12},{24,0},{28,4},{1,25},{... | collective-permute-start | bytes 147464 | tf_op jit(solution)/shard_map/ppermute | solution.py:31
  28.6 1.0 %collective-permute-start.17 = (bf16[96,256]{1,0:T(8,128)(2,1)S(1)}, bf16[96,256]{1,0:T(8,128)(2,1)S(1)}, u32[]{:S(2)}, u32[]{:S(2)}) collective-permute-start(bf16[96,256]{1,0:T(8,128)(2,1)S(1)} %fusion.5), channel_id=1, source_target_pairs={{0,8},{4,12},{8,0},{12,4},{16,24},{20,28},{24,16},{28,20},{1,9},{5... | collective-permute-start | bytes 147464 | tf_op jit(solution)/shard_map/ppermute | solution.py:31
  29.6 2.2 %collective-permute-start.16 = (bf16[96,256]{1,0:T(8,128)(2,1)S(1)}, bf16[96,256]{1,0:T(8,128)(2,1)S(1)}, u32[]{:S(2)}, u32[]{:S(2)}) collective-permute-start(bf16[96,256]{1,0:T(8,128)(2,1)S(1)} %fusion.5), channel_id=1, source_target_pairs={{0,16},{4,20},{8,24},{12,28},{16,0},{20,4},{24,8},{28,12},{1,17},{... | collective-permute-start | bytes 147464 | tf_op jit(solution)/shard_map/ppermute | solution.py:31
  31.8 1.5 %collective-permute-done.18 = bf16[96,256]{1,0:T(8,128)(2,1)S(1)} collective-permute-done((bf16[96,256]{1,0:T(8,128)(2,1)S(1)}, bf16[96,256]{1,0:T(8,128)(2,1)S(1)}, u32[]{:S(2)}, u32[]{:S(2)}) %collective-permute-start.18) | collective-permute-done | bytes 49184 | tf_op jit(solution)/shard_map/ppermute | solution.py:31
  33.3 1.3 %collective-permute-done.16 = bf16[96,256]{1,0:T(8,128)(2,1)S(1)} collective-permute-done((bf16[96,256]{1,0:T(8,128)(2,1)S(1)}, bf16[96,256]{1,0:T(8,128)(2,1)S(1)}, u32[]{:S(2)}, u32[]{:S(2)}) %collective-permute-start.16) | collective-permute-done | bytes 49184 | tf_op jit(solution)/shard_map/ppermute | solution.py:31
  34.7 1.5 %collective-permute-start.21 = (bf16[96,256]{1,0:T(8,128)(2,1)S(1)}, bf16[96,256]{1,0:T(8,128)(2,1)S(1)}, u32[]{:S(2)}, u32[]{:S(2)}) collective-permute-start(bf16[96,256]{1,0:T(8,128)(2,1)S(1)} %add_convert_fusion), channel_id=1, source_target_pairs={{0,6},{1,7},{2,4},{3,5},{4,2},{5,3},{6,0},{7,1},{8,14},{9,15},{10,... | collective-permute-start | bytes 147464 | tf_op jit(solution)/shard_map/ppermute | solution.py:31
  36.2 0.6 %collective-permute-start.20 = (bf16[96,256]{1,0:T(8,128)(2,1)S(1)}, bf16[96,256]{1,0:T(8,128)(2,1)S(1)}, u32[]{:S(2)}, u32[]{:S(2)}) collective-permute-start(bf16[96,256]{1,0:T(8,128)(2,1)S(1)} %add_convert_fusion), channel_id=1, source_target_pairs={{0,2},{1,3},{2,0},{3,1},{4,6},{5,7},{6,4},{7,5},{8,10},{9,11},{10,... | collective-permute-start | bytes 147464 | tf_op jit(solution)/shard_map/ppermute | solution.py:31
  36.8 1.4 %collective-permute-start.19 = (bf16[96,256]{1,0:T(8,128)(2,1)S(1)}, bf16[96,256]{1,0:T(8,128)(2,1)S(1)}, u32[]{:S(2)}, u32[]{:S(2)}) collective-permute-start(bf16[96,256]{1,0:T(8,128)(2,1)S(1)} %add_convert_fusion), channel_id=1, source_target_pairs={{0,4},{1,5},{2,6},{3,7},{4,0},{5,1},{6,2},{7,3},{8,12},{9,13},{10,... | collective-permute-start | bytes 147464 | tf_op jit(solution)/shard_map/ppermute | solution.py:31
  38.2 1.5 %collective-permute-done.21 = bf16[96,256]{1,0:T(8,128)(2,1)S(1)} collective-permute-done((bf16[96,256]{1,0:T(8,128)(2,1)S(1)}, bf16[96,256]{1,0:T(8,128)(2,1)S(1)}, u32[]{:S(2)}, u32[]{:S(2)}) %collective-permute-start.21) | collective-permute-done | bytes 49184 | tf_op jit(solution)/shard_map/ppermute | solution.py:31
  39.7 0.6 %collective-permute-done.20 = bf16[96,256]{1,0:T(8,128)(2,1)S(1)} collective-permute-done((bf16[96,256]{1,0:T(8,128)(2,1)S(1)}, bf16[96,256]{1,0:T(8,128)(2,1)S(1)}, u32[]{:S(2)}, u32[]{:S(2)}) %collective-permute-start.20) | collective-permute-done | bytes 49184 | tf_op jit(solution)/shard_map/ppermute | solution.py:31
  40.3 0.6 %collective-permute-done.19 = bf16[96,256]{1,0:T(8,128)(2,1)S(1)} collective-permute-done((bf16[96,256]{1,0:T(8,128)(2,1)S(1)}, bf16[96,256]{1,0:T(8,128)(2,1)S(1)}, u32[]{:S(2)}, u32[]{:S(2)}) %collective-permute-start.19) | collective-permute-done | bytes 49184 | tf_op jit(solution)/shard_map/ppermute | solution.py:31
  41.0 0.6 %fusion.6 = bf16[3,48,256]{2,1,0:T(8,128)(2,1)} fusion(bf16[1,3,48,256]{3,2,1,0:T(8,128)(2,1)S(1)} %collective-permute-done.12, f32[1,2,3,48,256]{4,3,2,1,0:T(8,128)S(1)} %add_bitcast_fusion), kind=kLoop, calls=%fused_computation.13 | loop fusion | flops 110592 | bytes 294912 | tf_op jit(solution)/shard_map/convert_element_type | solution.py:221
  41.7 0.8 %collective-permute-done.22.there_ref = bf16[4,96,256]{2,1,0:T(8,128)(2,1)S(1)} collective-permute-done((bf16[4,96,256]{2,1,0:T(8,128)(2,1)S(1)}, bf16[4,96,256]{2,1,0:T(8,128)(2,1)S(1)}, u32[]{:S(2)}, u32[]{:S(2)}) %collective-permute-start.22) | collective-permute-done | bytes 196640 | tf_op jit(solution)/shard_map/ppermute | solution.py:31
  42.4 0.9 %shard_map.70 = f32[768,256]{1,0:T(8,128)} custom-call(bf16[4,96,256]{2,1,0:T(8,128)(2,1)S(1)} %pad_maximum_fusion.here_ref, bf16[4,96,256]{2,1,0:T(8,128)(2,1)S(1)} %collective-permute-done.22.there_ref), custom_call_target="tpu_custom_call" | custom-call | tf_op jit(solution)/shard_map/pallas_call | solution.py:243
  (25 shorter events, 2.2 us)
Async XLA Ops:
  0.6 9.1 %collective-permute-start.3 = (bf16[3,48,256]{2,1,0:T(8,128)(2,1)}, bf16[3,48,256]{2,1,0:T(8,128)(2,1)S(1)}, u32[]{:S(2)}, u32[]{:S(2)}) collective-permute-start(bf16[3,48,256]{2,1,0:T(8,128)(2,1)} %refs_2_.1), channel_id=1, source_target_pairs={{0,16},{4,20},{8,24},{12,28},{16,0},{20,4},{24,8},{28,12},{1,17},{... | collective-permute-start | bytes 221192 | tf_op jit(solution)/shard_map/ppermute | solution.py:31
  4.7 7.5 %collective-permute-start.7 = (bf16[3,48,256]{2,1,0:T(8,128)(2,1)}, bf16[3,48,256]{2,1,0:T(8,128)(2,1)S(1)}, u32[]{:S(2)}, u32[]{:S(2)}) collective-permute-start(bf16[3,48,256]{2,1,0:T(8,128)(2,1)} %refs_2_.1), channel_id=1, source_target_pairs={{0,2},{1,3},{2,0},{3,1},{4,6},{5,7},{6,4},{7,5},{8,10},{9,11},{10,... | collective-permute-start | bytes 221192 | tf_op jit(solution)/shard_map/ppermute | solution.py:31
  6.3 6.5 %collective-permute-start.2 = (bf16[3,48,256]{2,1,0:T(8,128)(2,1)}, bf16[3,48,256]{2,1,0:T(8,128)(2,1)S(1)}, u32[]{:S(2)}, u32[]{:S(2)}) collective-permute-start(bf16[3,48,256]{2,1,0:T(8,128)(2,1)} %refs_2_.1), channel_id=1, source_target_pairs={{0,12},{4,8},{8,4},{12,0},{16,28},{20,24},{24,20},{28,16},{1,13},{... | collective-permute-start | bytes 221192 | tf_op jit(solution)/shard_map/ppermute | solution.py:31
  8.8 6.1 %collective-permute-start.1 = (bf16[3,48,256]{2,1,0:T(8,128)(2,1)}, bf16[3,48,256]{2,1,0:T(8,128)(2,1)S(1)}, u32[]{:S(2)}, u32[]{:S(2)}) collective-permute-start(bf16[3,48,256]{2,1,0:T(8,128)(2,1)} %refs_2_.1), channel_id=1, source_target_pairs={{0,4},{4,0},{8,12},{12,8},{16,20},{20,16},{24,28},{28,24},{1,5},{5... | collective-permute-start | bytes 221192 | tf_op jit(solution)/shard_map/ppermute | solution.py:31
  9.3 5.6 %collective-permute-start = (bf16[3,48,256]{2,1,0:T(8,128)(2,1)}, bf16[3,48,256]{2,1,0:T(8,128)(2,1)S(1)}, u32[]{:S(2)}, u32[]{:S(2)}) collective-permute-start(bf16[3,48,256]{2,1,0:T(8,128)(2,1)} %refs_2_.1), channel_id=1, source_target_pairs={{0,8},{4,12},{8,0},{12,4},{16,24},{20,28},{24,16},{28,20},{1,9},{5... | collective-permute-start | bytes 221192 | tf_op jit(solution)/shard_map/ppermute | solution.py:31
  9.7 7.0 %collective-permute-start.6 = (bf16[1,3,48,256]{3,2,1,0:T(8,128)(2,1)S(1)}, bf16[1,3,48,256]{3,2,1,0:T(8,128)(2,1)S(1)}, u32[]{:S(2)}, u32[]{:S(2)}) collective-permute-start(bf16[1,3,48,256]{3,2,1,0:T(8,128)(2,1)S(1)} %bitcast.45), channel_id=1, source_target_pairs={{0,12},{4,8},{8,4},{12,0},{16,28},{20,24},{24,20},{28,16},{1,13},{... | collective-permute-start | bytes 221192 | tf_op jit(solution)/shard_map/ppermute | solution.py:31
  12.3 4.9 %collective-permute-start.5 = (bf16[1,3,48,256]{3,2,1,0:T(8,128)(2,1)S(1)}, bf16[1,3,48,256]{3,2,1,0:T(8,128)(2,1)S(1)}, u32[]{:S(2)}, u32[]{:S(2)}) collective-permute-start(bf16[1,3,48,256]{3,2,1,0:T(8,128)(2,1)S(1)} %bitcast.46), channel_id=1, source_target_pairs={{0,4},{4,0},{8,12},{12,8},{16,20},{20,16},{24,28},{28,24},{1,5},{5... | collective-permute-start | bytes 221192 | tf_op jit(solution)/shard_map/ppermute | solution.py:31
  12.8 4.4 %collective-permute-start.4 = (bf16[1,3,48,256]{3,2,1,0:T(8,128)(2,1)S(1)}, bf16[1,3,48,256]{3,2,1,0:T(8,128)(2,1)S(1)}, u32[]{:S(2)}, u32[]{:S(2)}) collective-permute-start(bf16[1,3,48,256]{3,2,1,0:T(8,128)(2,1)S(1)} %bitcast.47), channel_id=1, source_target_pairs={{0,8},{4,12},{8,0},{12,4},{16,24},{20,28},{24,16},{28,20},{1,9},{5... | collective-permute-start | bytes 221192 | tf_op jit(solution)/shard_map/ppermute | solution.py:31
  14.9 2.3 %collective-permute-start.8 = (bf16[3,48,256]{2,1,0:T(8,128)(2,1)}, bf16[3,48,256]{2,1,0:T(8,128)(2,1)S(1)}, u32[]{:S(2)}, u32[]{:S(2)}) collective-permute-start(bf16[3,48,256]{2,1,0:T(8,128)(2,1)} %refs_2_.1), channel_id=1, source_target_pairs={{0,1},{1,0},{2,3},{3,2},{4,5},{5,4},{6,7},{7,6},{8,9},{9,8},{10,11... | collective-permute-start | bytes 221192 | tf_op jit(solution)/shard_map/ppermute | solution.py:31
  14.9 2.3 %collective-permute-start.9 = (bf16[3,48,256]{2,1,0:T(8,128)(2,1)S(1)}, bf16[3,48,256]{2,1,0:T(8,128)(2,1)S(1)}, u32[]{:S(2)}, u32[]{:S(2)}) collective-permute-start(bf16[3,48,256]{2,1,0:T(8,128)(2,1)S(1)} %collective-permute-done.7), channel_id=1, source_target_pairs={{0,1},{1,0},{2,3},{3,2},{4,5},{5,4},{6,7},{7,6},{8,9},{9,8},{10,11... | collective-permute-start | bytes 221192 | tf_op jit(solution)/shard_map/ppermute | solution.py:31
  18.6 1.5 %collective-permute-start.11 = (bf16[4,96,256]{2,1,0:T(8,128)(2,1)S(1)}, bf16[4,96,256]{2,1,0:T(8,128)(2,1)S(1)}, u32[]{:S(2)}, u32[]{:S(2)}) collective-permute-start(bf16[4,96,256]{2,1,0:T(8,128)(2,1)S(1)} %get-tuple-element.25), channel_id=1, source_target_pairs={{0,1},{1,0},{2,3},{3,2},{4,5},{5,4},{6,7},{7,6},{8,9},{9,8},{10,11... | collective-permute-start | bytes 589832 | tf_op jit(solution)/shard_map/ppermute | solution.py:31
  18.7 5.1 %collective-permute-start.10 = (f32[2,3,48,256]{3,2,1,0:T(8,128)S(1)}, f32[2,3,48,256]{3,2,1,0:T(8,128)S(1)}, u32[]{:S(2)}, u32[]{:S(2)}) collective-permute-start(f32[2,3,48,256]{3,2,1,0:T(8,128)S(1)} %get-tuple-element.23), channel_id=1, source_target_pairs={{0,1},{1,0},{2,3},{3,2},{4,5},{5,4},{6,7},{7,6},{8,9},{9,8},{10,11... | collective-permute-start | bytes 884744 | tf_op jit(solution)/shard_map/ppermute | solution.py:31
  20.2 5.1 %collective-permute-start.13 = (bf16[96,256]{1,0:T(8,128)(2,1)S(1)}, bf16[96,256]{1,0:T(8,128)(2,1)S(1)}, u32[]{:S(2)}, u32[]{:S(2)}) collective-permute-start(bf16[96,256]{1,0:T(8,128)(2,1)S(1)} %get-tuple-element.32), channel_id=1, source_target_pairs={{0,6},{1,7},{2,4},{3,5},{4,2},{5,3},{6,0},{7,1},{8,14},{9,15},{10,... | collective-permute-start | bytes 147464 | tf_op jit(solution)/shard_map/ppermute | solution.py:31
  21.7 4.5 %collective-permute-start.15 = (bf16[96,256]{1,0:T(8,128)(2,1)S(1)}, bf16[96,256]{1,0:T(8,128)(2,1)S(1)}, u32[]{:S(2)}, u32[]{:S(2)}) collective-permute-start(bf16[96,256]{1,0:T(8,128)(2,1)S(1)} %get-tuple-element.33), channel_id=1, source_target_pairs={{0,2},{1,3},{2,0},{3,1},{4,6},{5,7},{6,4},{7,5},{8,10},{9,11},{10,... | collective-permute-start | bytes 147464 | tf_op jit(solution)/shard_map/ppermute | solution.py:31
  23.2 4.1 %collective-permute-start.14 = (bf16[96,256]{1,0:T(8,128)(2,1)S(1)}, bf16[96,256]{1,0:T(8,128)(2,1)S(1)}, u32[]{:S(2)}, u32[]{:S(2)}) collective-permute-start(bf16[96,256]{1,0:T(8,128)(2,1)S(1)} %get-tuple-element.34), channel_id=1, source_target_pairs={{0,4},{1,5},{2,6},{3,7},{4,0},{5,1},{6,2},{7,3},{8,12},{9,13},{10,... | collective-permute-start | bytes 147464 | tf_op jit(solution)/shard_map/ppermute | solution.py:31
  23.8 10.8 %collective-permute-start.12 = (bf16[1,3,48,256]{3,2,1,0:T(8,128)(2,1)S(1)}, bf16[1,3,48,256]{3,2,1,0:T(8,128)(2,1)S(1)}, u32[]{:S(2)}, u32[]{:S(2)}) collective-permute-start(bf16[1,3,48,256]{3,2,1,0:T(8,128)(2,1)S(1)} %fusion.7), channel_id=1, source_target_pairs={{0,2},{1,3},{2,0},{3,1},{4,6},{5,7},{6,4},{7,5},{8,10},{9,11},{10,... | collective-permute-start | bytes 221192 | tf_op jit(solution)/shard_map/ppermute | solution.py:31
  27.3 6.0 %collective-permute-start.18 = (bf16[96,256]{1,0:T(8,128)(2,1)S(1)}, bf16[96,256]{1,0:T(8,128)(2,1)S(1)}, u32[]{:S(2)}, u32[]{:S(2)}) collective-permute-start(bf16[96,256]{1,0:T(8,128)(2,1)S(1)} %fusion.5), channel_id=1, source_target_pairs={{0,24},{4,28},{8,16},{12,20},{16,8},{20,12},{24,0},{28,4},{1,25},{... | collective-permute-start | bytes 147464 | tf_op jit(solution)/shard_map/ppermute | solution.py:31
  28.6 4.6 %collective-permute-start.17 = (bf16[96,256]{1,0:T(8,128)(2,1)S(1)}, bf16[96,256]{1,0:T(8,128)(2,1)S(1)}, u32[]{:S(2)}, u32[]{:S(2)}) collective-permute-start(bf16[96,256]{1,0:T(8,128)(2,1)S(1)} %fusion.5), channel_id=1, source_target_pairs={{0,8},{4,12},{8,0},{12,4},{16,24},{20,28},{24,16},{28,20},{1,9},{5... | collective-permute-start | bytes 147464 | tf_op jit(solution)/shard_map/ppermute | solution.py:31
  29.6 5.0 %collective-permute-start.16 = (bf16[96,256]{1,0:T(8,128)(2,1)S(1)}, bf16[96,256]{1,0:T(8,128)(2,1)S(1)}, u32[]{:S(2)}, u32[]{:S(2)}) collective-permute-start(bf16[96,256]{1,0:T(8,128)(2,1)S(1)} %fusion.5), channel_id=1, source_target_pairs={{0,16},{4,20},{8,24},{12,28},{16,0},{20,4},{24,8},{28,12},{1,17},{... | collective-permute-start | bytes 147464 | tf_op jit(solution)/shard_map/ppermute | solution.py:31
  34.7 5.1 %collective-permute-start.21 = (bf16[96,256]{1,0:T(8,128)(2,1)S(1)}, bf16[96,256]{1,0:T(8,128)(2,1)S(1)}, u32[]{:S(2)}, u32[]{:S(2)}) collective-permute-start(bf16[96,256]{1,0:T(8,128)(2,1)S(1)} %add_convert_fusion), channel_id=1, source_target_pairs={{0,6},{1,7},{2,4},{3,5},{4,2},{5,3},{6,0},{7,1},{8,14},{9,15},{10,... | collective-permute-start | bytes 147464 | tf_op jit(solution)/shard_map/ppermute | solution.py:31
  36.2 4.1 %collective-permute-start.20 = (bf16[96,256]{1,0:T(8,128)(2,1)S(1)}, bf16[96,256]{1,0:T(8,128)(2,1)S(1)}, u32[]{:S(2)}, u32[]{:S(2)}) collective-permute-start(bf16[96,256]{1,0:T(8,128)(2,1)S(1)} %add_convert_fusion), channel_id=1, source_target_pairs={{0,2},{1,3},{2,0},{3,1},{4,6},{5,7},{6,4},{7,5},{8,10},{9,11},{10,... | collective-permute-start | bytes 147464 | tf_op jit(solution)/shard_map/ppermute | solution.py:31
  36.8 4.1 %collective-permute-start.19 = (bf16[96,256]{1,0:T(8,128)(2,1)S(1)}, bf16[96,256]{1,0:T(8,128)(2,1)S(1)}, u32[]{:S(2)}, u32[]{:S(2)}) collective-permute-start(bf16[96,256]{1,0:T(8,128)(2,1)S(1)} %add_convert_fusion), channel_id=1, source_target_pairs={{0,4},{1,5},{2,6},{3,7},{4,0},{5,1},{6,2},{7,3},{8,12},{9,13},{10,... | collective-permute-start | bytes 147464 | tf_op jit(solution)/shard_map/ppermute | solution.py:31
  40.9 1.5 %collective-permute-start.22 = (bf16[4,96,256]{2,1,0:T(8,128)(2,1)S(1)}, bf16[4,96,256]{2,1,0:T(8,128)(2,1)S(1)}, u32[]{:S(2)}, u32[]{:S(2)}) collective-permute-start(bf16[4,96,256]{2,1,0:T(8,128)(2,1)S(1)} %pad_maximum_fusion.here_ref), channel_id=1, source_target_pairs={{0,1},{1,0},{2,3},{3,2},{4,5},{5,4},{6,7},{7,6},{8,9},{9,8},{10,11... | collective-permute-start | bytes 589832 | tf_op jit(solution)/shard_map/ppermute | solution.py:31

commit v10 on v7

--- a/solution.py
+++ b/solution.py
@@ -227,8 +227,8 @@
         from_first, from_second, from_both = [
             swap(mine, ("row",), sizes, {"row": bits}) for bits in (first, second, first ^ second)
         ]
-        from_second, from_first, from_both, arrived = lax.optimization_barrier(
-            (from_second, from_first, from_both, arrived)
+        arrived, from_first, from_second, from_both = lax.optimization_barrier(
+            (arrived, from_first, from_second, from_both)
         )
         total = (mine.astype(F32) + from_first.astype(F32)) + (
             from_second.astype(F32) + from_both.astype(F32)

time: 43.4 us -> 43.6 us (level)
  transfers between devices with their start and end apart: 23 -> 23, of which waited for: 15 -> 14; matrix products, arithmetic and copies ran while one was open for 2% -> 2% of each run, Pallas kernels for 3% -> 3%
where the time goes in v10:
time: 43.6 us; the launch traced here: 43.5 us
  starting transfers between devices  25.7 us (59%)
  waiting for transfers between devices  12.5 us (29%)
  Pallas kernels  3.74 us (9%)
  other arithmetic  0.83 us (2%)
  between operations  0.73 us (2%)
    ppermute x23, starting transfers between devices, swap(): return lax.ppermute(value, axes, pairs)  25.7 us
    ppermute x23, waiting for transfers between devices, swap(): return lax.ppermute(value, axes, pairs)  12.5 us
    pallas_call x1, Pallas kernels, body(): pl.pallas_call(functools.partial(main_kernel, along_row, along_col), out_...  1.44 us
    pallas_call x1, Pallas kernels, body(): pl.pallas_call(prepare_kernel, out_shape=[jax.ShapeDtypeStruct(value.shap...  1.36 us
    pallas_call x1, Pallas kernels, body(): pl.pallas_call(finish_kernel, out_shape=jax.ShapeDtypeStruct((panels * wi...  0.94 us
  transfers between devices with their start and end apart: 23, of which 14 were waited for; matrix products, arithmetic and copies ran while one was open for 2% of the time, Pallas kernels for 3%

profile of v10, /device:TPU:0, one launch (start us, length us, event | category | flops | bytes accessed | tf_op | source)
XLA Modules:
  0.0 43.5 jit_solution(18345742852129270516)
XLA Ops:
  0.6 4.1 %collective-permute-start.3 = (bf16[3,48,256]{2,1,0:T(8,128)(2,1)}, bf16[3,48,256]{2,1,0:T(8,128)(2,1)S(1)}, u32[]{:S(2)}, u32[]{:S(2)}) collective-permute-start(bf16[3,48,256]{2,1,0:T(8,128)(2,1)} %refs_2_.1), channel_id=1, source_target_pairs={{0,16},{4,20},{8,24},{12,28},{16,0},{20,4},{24,8},{28,12},{1,17},{... | collective-permute-start | bytes 221192 | tf_op jit(solution)/shard_map/ppermute | solution.py:31
  4.7 1.5 %collective-permute-start.7 = (bf16[3,48,256]{2,1,0:T(8,128)(2,1)}, bf16[3,48,256]{2,1,0:T(8,128)(2,1)S(1)}, u32[]{:S(2)}, u32[]{:S(2)}) collective-permute-start(bf16[3,48,256]{2,1,0:T(8,128)(2,1)} %refs_2_.1), channel_id=1, source_target_pairs={{0,2},{1,3},{2,0},{3,1},{4,6},{5,7},{6,4},{7,5},{8,10},{9,11},{10,... | collective-permute-start | bytes 221192 | tf_op jit(solution)/shard_map/ppermute | solution.py:31
  6.3 1.5 %collective-permute-start.2 = (bf16[3,48,256]{2,1,0:T(8,128)(2,1)}, bf16[3,48,256]{2,1,0:T(8,128)(2,1)S(1)}, u32[]{:S(2)}, u32[]{:S(2)}) collective-permute-start(bf16[3,48,256]{2,1,0:T(8,128)(2,1)} %refs_2_.1), channel_id=1, source_target_pairs={{0,4},{4,0},{8,12},{12,8},{16,20},{20,16},{24,28},{28,24},{1,5},{5... | collective-permute-start | bytes 221192 | tf_op jit(solution)/shard_map/ppermute | solution.py:31
  7.7 1.5 %collective-permute-start.1 = (bf16[3,48,256]{2,1,0:T(8,128)(2,1)}, bf16[3,48,256]{2,1,0:T(8,128)(2,1)S(1)}, u32[]{:S(2)}, u32[]{:S(2)}) collective-permute-start(bf16[3,48,256]{2,1,0:T(8,128)(2,1)} %refs_2_.1), channel_id=1, source_target_pairs={{0,12},{4,8},{8,4},{12,0},{16,28},{20,24},{24,20},{28,16},{1,13},{... | collective-permute-start | bytes 221192 | tf_op jit(solution)/shard_map/ppermute | solution.py:31
  9.7 1.5 %collective-permute-start.6 = (bf16[1,3,48,256]{3,2,1,0:T(8,128)(2,1)S(1)}, bf16[1,3,48,256]{3,2,1,0:T(8,128)(2,1)S(1)}, u32[]{:S(2)}, u32[]{:S(2)}) collective-permute-start(bf16[1,3,48,256]{3,2,1,0:T(8,128)(2,1)S(1)} %bitcast.45), channel_id=1, source_target_pairs={{0,4},{4,0},{8,12},{12,8},{16,20},{20,16},{24,28},{28,24},{1,5},{5... | collective-permute-start | bytes 221192 | tf_op jit(solution)/shard_map/ppermute | solution.py:31
  11.2 1.5 %collective-permute-start.5 = (bf16[1,3,48,256]{3,2,1,0:T(8,128)(2,1)S(1)}, bf16[1,3,48,256]{3,2,1,0:T(8,128)(2,1)S(1)}, u32[]{:S(2)}, u32[]{:S(2)}) collective-permute-start(bf16[1,3,48,256]{3,2,1,0:T(8,128)(2,1)S(1)} %bitcast.46), channel_id=1, source_target_pairs={{0,12},{4,8},{8,4},{12,0},{16,28},{20,24},{24,20},{28,16},{1,13},{... | collective-permute-start | bytes 221192 | tf_op jit(solution)/shard_map/ppermute | solution.py:31
  12.8 0.7 %collective-permute-start.4 = (bf16[1,3,48,256]{3,2,1,0:T(8,128)(2,1)S(1)}, bf16[1,3,48,256]{3,2,1,0:T(8,128)(2,1)S(1)}, u32[]{:S(2)}, u32[]{:S(2)}) collective-permute-start(bf16[1,3,48,256]{3,2,1,0:T(8,128)(2,1)S(1)} %bitcast.47), channel_id=1, source_target_pairs={{0,8},{4,12},{8,0},{12,4},{16,24},{20,28},{24,16},{28,20},{1,9},{5... | collective-permute-start | bytes 221192 | tf_op jit(solution)/shard_map/ppermute | solution.py:31
  13.9 0.8 %collective-permute-done = bf16[3,48,256]{2,1,0:T(8,128)(2,1)S(1)} collective-permute-done((bf16[3,48,256]{2,1,0:T(8,128)(2,1)}, bf16[3,48,256]{2,1,0:T(8,128)(2,1)S(1)}, u32[]{:S(2)}, u32[]{:S(2)}) %collective-permute-start) | collective-permute-done | bytes 73760 | tf_op jit(solution)/shard_map/ppermute | solution.py:31
  14.7 1.4 %shard_map.68 = (bf16[192,384]{1,0:T(8,128)(2,1)S(1)}, bf16[3,48,256]{2,1,0:T(8,128)(2,1)S(1)}, bf16[3,48,256]{2,1,0:T(8,128)(2,1)S(1)}, bf16[3,256,256]{2,1,0:T(8,128)(2,1)S(1)}, bf16[3,256,256]{2,1,0:T(8,128)(2,1)S(1)}) custom-call(f32[3,256,256]{2,1,0:T(8,128)} %refs_0_.1, bf16[192,384]{1,0:T(8,128)(2,1)} %refs_1_.1, bf16[3,48,256]{2,1,0:T(8,128)(2,1)} %refs_2_.1, ...), custom_call_target="tpu_custom_call" | custom-call | tf_op jit(solution)/shard_map/pallas_call | solution.py:177
  16.5 0.7 %collective-permute-done.4.refs_5_ = bf16[1,3,48,256]{3,2,1,0:T(8,128)(2,1)S(1)} collective-permute-done((bf16[1,3,48,256]{3,2,1,0:T(8,128)(2,1)S(1)}, bf16[1,3,48,256]{3,2,1,0:T(8,128)(2,1)S(1)}, u32[]{:S(2)}, u32[]{:S(2)}) %collective-permute-start.4) | collective-permute-done | bytes 73760 | tf_op jit(solution)/shard_map/ppermute | solution.py:31
  17.2 1.4 %shard_map.69 = (f32[2,3,48,256]{3,2,1,0:T(8,128)S(1)}, f32[2,3,48,256]{3,2,1,0:T(8,128)S(1)}, f32[4,96,256]{2,1,0:T(8,128)S(1)}, bf16[4,96,256]{2,1,0:T(8,128)(2,1)S(1)}) custom-call(bf16[1,3,48,256]{3,2,1,0:T(8,128)(2,1)S(1)} %bitcast.43, bf16[1,3,48,256]{3,2,1,0:T(8,128)(2,1)S(1)} %bitcast.52, bf16[1,3,48,256]{3,2,1,0:T(8,128)(2,1)S(1)} %bitcast.51, ...), custom_call_target="tpu_custom_call" | custom-call | tf_op jit(solution)/shard_map/pallas_call | solution.py:189
  18.7 0.5 %collective-permute-start.10 = (f32[2,3,48,256]{3,2,1,0:T(8,128)S(1)}, f32[2,3,48,256]{3,2,1,0:T(8,128)S(1)}, u32[]{:S(2)}, u32[]{:S(2)}) collective-permute-start(f32[2,3,48,256]{3,2,1,0:T(8,128)S(1)} %get-tuple-element.23), channel_id=1, source_target_pairs={{0,1},{1,0},{2,3},{3,2},{4,5},{5,4},{6,7},{7,6},{8,9},{9,8},{10,11... | collective-permute-start | bytes 884744 | tf_op jit(solution)/shard_map/ppermute | solution.py:31
  19.2 0.9 %collective-permute-done.11 = bf16[4,96,256]{2,1,0:T(8,128)(2,1)S(1)} collective-permute-done((bf16[4,96,256]{2,1,0:T(8,128)(2,1)S(1)}, bf16[4,96,256]{2,1,0:T(8,128)(2,1)S(1)}, u32[]{:S(2)}, u32[]{:S(2)}) %collective-permute-start.11) | collective-permute-done | bytes 196640 | tf_op jit(solution)/shard_map/ppermute | solution.py:31
  20.2 2.0 %collective-permute-start.13 = (bf16[96,256]{1,0:T(8,128)(2,1)S(1)}, bf16[96,256]{1,0:T(8,128)(2,1)S(1)}, u32[]{:S(2)}, u32[]{:S(2)}) collective-permute-start(bf16[96,256]{1,0:T(8,128)(2,1)S(1)} %get-tuple-element.32), channel_id=1, source_target_pairs={{0,6},{1,7},{2,4},{3,5},{4,2},{5,3},{6,0},{7,1},{8,14},{9,15},{10,... | collective-permute-start | bytes 147464 | tf_op jit(solution)/shard_map/ppermute | solution.py:31
  22.2 1.0 %collective-permute-start.15 = (bf16[96,256]{1,0:T(8,128)(2,1)S(1)}, bf16[96,256]{1,0:T(8,128)(2,1)S(1)}, u32[]{:S(2)}, u32[]{:S(2)}) collective-permute-start(bf16[96,256]{1,0:T(8,128)(2,1)S(1)} %get-tuple-element.33), channel_id=1, source_target_pairs={{0,2},{1,3},{2,0},{3,1},{4,6},{5,7},{6,4},{7,5},{8,10},{9,11},{10,... | collective-permute-start | bytes 147464 | tf_op jit(solution)/shard_map/ppermute | solution.py:31
  23.2 0.5 %collective-permute-start.14 = (bf16[96,256]{1,0:T(8,128)(2,1)S(1)}, bf16[96,256]{1,0:T(8,128)(2,1)S(1)}, u32[]{:S(2)}, u32[]{:S(2)}) collective-permute-start(bf16[96,256]{1,0:T(8,128)(2,1)S(1)} %get-tuple-element.34), channel_id=1, source_target_pairs={{0,4},{1,5},{2,6},{3,7},{4,0},{5,1},{6,2},{7,3},{8,12},{9,13},{10,... | collective-permute-start | bytes 147464 | tf_op jit(solution)/shard_map/ppermute | solution.py:31
  23.8 0.6 %collective-permute-start.12 = (bf16[1,3,48,256]{3,2,1,0:T(8,128)(2,1)S(1)}, bf16[1,3,48,256]{3,2,1,0:T(8,128)(2,1)S(1)}, u32[]{:S(2)}, u32[]{:S(2)}) collective-permute-start(bf16[1,3,48,256]{3,2,1,0:T(8,128)(2,1)S(1)} %fusion.7), channel_id=1, source_target_pairs={{0,2},{1,3},{2,0},{3,1},{4,6},{5,7},{6,4},{7,5},{8,10},{9,11},{10,... | collective-permute-start | bytes 221192 | tf_op jit(solution)/shard_map/ppermute | solution.py:31
  24.4 0.9 %collective-permute-done.13 = bf16[96,256]{1,0:T(8,128)(2,1)S(1)} collective-permute-done((bf16[96,256]{1,0:T(8,128)(2,1)S(1)}, bf16[96,256]{1,0:T(8,128)(2,1)S(1)}, u32[]{:S(2)}, u32[]{:S(2)}) %collective-permute-start.13) | collective-permute-done | bytes 49184 | tf_op jit(solution)/shard_map/ppermute | solution.py:31
  25.4 1.5 %collective-permute-done.15 = bf16[96,256]{1,0:T(8,128)(2,1)S(1)} collective-permute-done((bf16[96,256]{1,0:T(8,128)(2,1)S(1)}, bf16[96,256]{1,0:T(8,128)(2,1)S(1)}, u32[]{:S(2)}, u32[]{:S(2)}) %collective-permute-start.15) | collective-permute-done | bytes 49184 | tf_op jit(solution)/shard_map/ppermute | solution.py:31
  27.3 2.0 %collective-permute-start.18 = (bf16[96,256]{1,0:T(8,128)(2,1)S(1)}, bf16[96,256]{1,0:T(8,128)(2,1)S(1)}, u32[]{:S(2)}, u32[]{:S(2)}) collective-permute-start(bf16[96,256]{1,0:T(8,128)(2,1)S(1)} %fusion.5), channel_id=1, source_target_pairs={{0,24},{4,28},{8,16},{12,20},{16,8},{20,12},{24,0},{28,4},{1,25},{... | collective-permute-start | bytes 147464 | tf_op jit(solution)/shard_map/ppermute | solution.py:31
  29.6 2.1 %collective-permute-start.16 = (bf16[96,256]{1,0:T(8,128)(2,1)S(1)}, bf16[96,256]{1,0:T(8,128)(2,1)S(1)}, u32[]{:S(2)}, u32[]{:S(2)}) collective-permute-start(bf16[96,256]{1,0:T(8,128)(2,1)S(1)} %fusion.5), channel_id=1, source_target_pairs={{0,8},{4,12},{8,0},{12,4},{16,24},{20,28},{24,16},{28,20},{1,9},{5... | collective-permute-start | bytes 147464 | tf_op jit(solution)/shard_map/ppermute | solution.py:31
  31.8 1.5 %collective-permute-done.18 = bf16[96,256]{1,0:T(8,128)(2,1)S(1)} collective-permute-done((bf16[96,256]{1,0:T(8,128)(2,1)S(1)}, bf16[96,256]{1,0:T(8,128)(2,1)S(1)}, u32[]{:S(2)}, u32[]{:S(2)}) %collective-permute-start.18) | collective-permute-done | bytes 49184 | tf_op jit(solution)/shard_map/ppermute | solution.py:31
  33.3 1.3 %collective-permute-done.17 = bf16[96,256]{1,0:T(8,128)(2,1)S(1)} collective-permute-done((bf16[96,256]{1,0:T(8,128)(2,1)S(1)}, bf16[96,256]{1,0:T(8,128)(2,1)S(1)}, u32[]{:S(2)}, u32[]{:S(2)}) %collective-permute-start.17) | collective-permute-done | bytes 49184 | tf_op jit(solution)/shard_map/ppermute | solution.py:31
  34.6 1.6 %collective-permute-start.21 = (bf16[96,256]{1,0:T(8,128)(2,1)S(1)}, bf16[96,256]{1,0:T(8,128)(2,1)S(1)}, u32[]{:S(2)}, u32[]{:S(2)}) collective-permute-start(bf16[96,256]{1,0:T(8,128)(2,1)S(1)} %add_convert_fusion), channel_id=1, source_target_pairs={{0,6},{1,7},{2,4},{3,5},{4,2},{5,3},{6,0},{7,1},{8,14},{9,15},{10,... | collective-permute-start | bytes 147464 | tf_op jit(solution)/shard_map/ppermute | solution.py:31
  36.2 0.7 %collective-permute-start.20 = (bf16[96,256]{1,0:T(8,128)(2,1)S(1)}, bf16[96,256]{1,0:T(8,128)(2,1)S(1)}, u32[]{:S(2)}, u32[]{:S(2)}) collective-permute-start(bf16[96,256]{1,0:T(8,128)(2,1)S(1)} %add_convert_fusion), channel_id=1, source_target_pairs={{0,2},{1,3},{2,0},{3,1},{4,6},{5,7},{6,4},{7,5},{8,10},{9,11},{10,... | collective-permute-start | bytes 147464 | tf_op jit(solution)/shard_map/ppermute | solution.py:31
  36.9 1.3 %collective-permute-start.19 = (bf16[96,256]{1,0:T(8,128)(2,1)S(1)}, bf16[96,256]{1,0:T(8,128)(2,1)S(1)}, u32[]{:S(2)}, u32[]{:S(2)}) collective-permute-start(bf16[96,256]{1,0:T(8,128)(2,1)S(1)} %add_convert_fusion), channel_id=1, source_target_pairs={{0,4},{1,5},{2,6},{3,7},{4,0},{5,1},{6,2},{7,3},{8,12},{9,13},{10,... | collective-permute-start | bytes 147464 | tf_op jit(solution)/shard_map/ppermute | solution.py:31
  38.2 1.5 %collective-permute-done.21 = bf16[96,256]{1,0:T(8,128)(2,1)S(1)} collective-permute-done((bf16[96,256]{1,0:T(8,128)(2,1)S(1)}, bf16[96,256]{1,0:T(8,128)(2,1)S(1)}, u32[]{:S(2)}, u32[]{:S(2)}) %collective-permute-start.21) | collective-permute-done | bytes 49184 | tf_op jit(solution)/shard_map/ppermute | solution.py:31
  39.7 0.6 %collective-permute-done.20 = bf16[96,256]{1,0:T(8,128)(2,1)S(1)} collective-permute-done((bf16[96,256]{1,0:T(8,128)(2,1)S(1)}, bf16[96,256]{1,0:T(8,128)(2,1)S(1)}, u32[]{:S(2)}, u32[]{:S(2)}) %collective-permute-start.20) | collective-permute-done | bytes 49184 | tf_op jit(solution)/shard_map/ppermute | solution.py:31
  40.3 0.7 %collective-permute-done.19 = bf16[96,256]{1,0:T(8,128)(2,1)S(1)} collective-permute-done((bf16[96,256]{1,0:T(8,128)(2,1)S(1)}, bf16[96,256]{1,0:T(8,128)(2,1)S(1)}, u32[]{:S(2)}, u32[]{:S(2)}) %collective-permute-start.19) | collective-permute-done | bytes 49184 | tf_op jit(solution)/shard_map/ppermute | solution.py:31
  41.1 0.6 %fusion.6 = bf16[3,48,256]{2,1,0:T(8,128)(2,1)} fusion(bf16[1,3,48,256]{3,2,1,0:T(8,128)(2,1)S(1)} %collective-permute-done.12, f32[1,2,3,48,256]{4,3,2,1,0:T(8,128)S(1)} %add_bitcast_fusion), kind=kLoop, calls=%fused_computation.13 | loop fusion | flops 110592 | bytes 294912 | tf_op jit(solution)/shard_map/convert_element_type | solution.py:221
  41.8 0.8 %collective-permute-done.22.there_ref = bf16[4,96,256]{2,1,0:T(8,128)(2,1)S(1)} collective-permute-done((bf16[4,96,256]{2,1,0:T(8,128)(2,1)S(1)}, bf16[4,96,256]{2,1,0:T(8,128)(2,1)S(1)}, u32[]{:S(2)}, u32[]{:S(2)}) %collective-permute-start.22) | collective-permute-done | bytes 196640 | tf_op jit(solution)/shard_map/ppermute | solution.py:31
  42.5 0.9 %shard_map.70 = f32[768,256]{1,0:T(8,128)} custom-call(bf16[4,96,256]{2,1,0:T(8,128)(2,1)S(1)} %pad_maximum_fusion.here_ref, bf16[4,96,256]{2,1,0:T(8,128)(2,1)S(1)} %collective-permute-done.22.there_ref), custom_call_target="tpu_custom_call" | custom-call | tf_op jit(solution)/shard_map/pallas_call | solution.py:243
  (25 shorter events, 2.5 us)
Async XLA Ops:
  0.6 9.1 %collective-permute-start.3 = (bf16[3,48,256]{2,1,0:T(8,128)(2,1)}, bf16[3,48,256]{2,1,0:T(8,128)(2,1)S(1)}, u32[]{:S(2)}, u32[]{:S(2)}) collective-permute-start(bf16[3,48,256]{2,1,0:T(8,128)(2,1)} %refs_2_.1), channel_id=1, source_target_pairs={{0,16},{4,20},{8,24},{12,28},{16,0},{20,4},{24,8},{28,12},{1,17},{... | collective-permute-start | bytes 221192 | tf_op jit(solution)/shard_map/ppermute | solution.py:31
  4.7 6.5 %collective-permute-start.7 = (bf16[3,48,256]{2,1,0:T(8,128)(2,1)}, bf16[3,48,256]{2,1,0:T(8,128)(2,1)S(1)}, u32[]{:S(2)}, u32[]{:S(2)}) collective-permute-start(bf16[3,48,256]{2,1,0:T(8,128)(2,1)} %refs_2_.1), channel_id=1, source_target_pairs={{0,2},{1,3},{2,0},{3,1},{4,6},{5,7},{6,4},{7,5},{8,10},{9,11},{10,... | collective-permute-start | bytes 221192 | tf_op jit(solution)/shard_map/ppermute | solution.py:31
  6.3 6.5 %collective-permute-start.2 = (bf16[3,48,256]{2,1,0:T(8,128)(2,1)}, bf16[3,48,256]{2,1,0:T(8,128)(2,1)S(1)}, u32[]{:S(2)}, u32[]{:S(2)}) collective-permute-start(bf16[3,48,256]{2,1,0:T(8,128)(2,1)} %refs_2_.1), channel_id=1, source_target_pairs={{0,4},{4,0},{8,12},{12,8},{16,20},{20,16},{24,28},{28,24},{1,5},{5... | collective-permute-start | bytes 221192 | tf_op jit(solution)/shard_map/ppermute | solution.py:31
  7.7 6.1 %collective-permute-start.1 = (bf16[3,48,256]{2,1,0:T(8,128)(2,1)}, bf16[3,48,256]{2,1,0:T(8,128)(2,1)S(1)}, u32[]{:S(2)}, u32[]{:S(2)}) collective-permute-start(bf16[3,48,256]{2,1,0:T(8,128)(2,1)} %refs_2_.1), channel_id=1, source_target_pairs={{0,12},{4,8},{8,4},{12,0},{16,28},{20,24},{24,20},{28,16},{1,13},{... | collective-permute-start | bytes 221192 | tf_op jit(solution)/shard_map/ppermute | solution.py:31
  9.3 5.4 %collective-permute-start = (bf16[3,48,256]{2,1,0:T(8,128)(2,1)}, bf16[3,48,256]{2,1,0:T(8,128)(2,1)S(1)}, u32[]{:S(2)}, u32[]{:S(2)}) collective-permute-start(bf16[3,48,256]{2,1,0:T(8,128)(2,1)} %refs_2_.1), channel_id=1, source_target_pairs={{0,8},{4,12},{8,0},{12,4},{16,24},{20,28},{24,16},{28,20},{1,9},{5... | collective-permute-start | bytes 221192 | tf_op jit(solution)/shard_map/ppermute | solution.py:31
  9.7 6.3 %collective-permute-start.6 = (bf16[1,3,48,256]{3,2,1,0:T(8,128)(2,1)S(1)}, bf16[1,3,48,256]{3,2,1,0:T(8,128)(2,1)S(1)}, u32[]{:S(2)}, u32[]{:S(2)}) collective-permute-start(bf16[1,3,48,256]{3,2,1,0:T(8,128)(2,1)S(1)} %bitcast.45), channel_id=1, source_target_pairs={{0,4},{4,0},{8,12},{12,8},{16,20},{20,16},{24,28},{28,24},{1,5},{5... | collective-permute-start | bytes 221192 | tf_op jit(solution)/shard_map/ppermute | solution.py:31
  11.2 5.3 %collective-permute-start.5 = (bf16[1,3,48,256]{3,2,1,0:T(8,128)(2,1)S(1)}, bf16[1,3,48,256]{3,2,1,0:T(8,128)(2,1)S(1)}, u32[]{:S(2)}, u32[]{:S(2)}) collective-permute-start(bf16[1,3,48,256]{3,2,1,0:T(8,128)(2,1)S(1)} %bitcast.46), channel_id=1, source_target_pairs={{0,12},{4,8},{8,4},{12,0},{16,28},{20,24},{24,20},{28,16},{1,13},{... | collective-permute-start | bytes 221192 | tf_op jit(solution)/shard_map/ppermute | solution.py:31
  12.8 4.4 %collective-permute-start.4 = (bf16[1,3,48,256]{3,2,1,0:T(8,128)(2,1)S(1)}, bf16[1,3,48,256]{3,2,1,0:T(8,128)(2,1)S(1)}, u32[]{:S(2)}, u32[]{:S(2)}) collective-permute-start(bf16[1,3,48,256]{3,2,1,0:T(8,128)(2,1)S(1)} %bitcast.47), channel_id=1, source_target_pairs={{0,8},{4,12},{8,0},{12,4},{16,24},{20,28},{24,16},{28,20},{1,9},{5... | collective-permute-start | bytes 221192 | tf_op jit(solution)/shard_map/ppermute | solution.py:31
  13.9 3.3 %collective-permute-start.8 = (bf16[3,48,256]{2,1,0:T(8,128)(2,1)}, bf16[3,48,256]{2,1,0:T(8,128)(2,1)S(1)}, u32[]{:S(2)}, u32[]{:S(2)}) collective-permute-start(bf16[3,48,256]{2,1,0:T(8,128)(2,1)} %refs_2_.1), channel_id=1, source_target_pairs={{0,1},{1,0},{2,3},{3,2},{4,5},{5,4},{6,7},{7,6},{8,9},{9,8},{10,11... | collective-permute-start | bytes 221192 | tf_op jit(solution)/shard_map/ppermute | solution.py:31
  14.7 2.5 %collective-permute-start.9 = (bf16[3,48,256]{2,1,0:T(8,128)(2,1)S(1)}, bf16[3,48,256]{2,1,0:T(8,128)(2,1)S(1)}, u32[]{:S(2)}, u32[]{:S(2)}) collective-permute-start(bf16[3,48,256]{2,1,0:T(8,128)(2,1)S(1)} %collective-permute-done.7), channel_id=1, source_target_pairs={{0,1},{1,0},{2,3},{3,2},{4,5},{5,4},{6,7},{7,6},{8,9},{9,8},{10,11... | collective-permute-start | bytes 221192 | tf_op jit(solution)/shard_map/ppermute | solution.py:31
  18.6 1.5 %collective-permute-start.11 = (bf16[4,96,256]{2,1,0:T(8,128)(2,1)S(1)}, bf16[4,96,256]{2,1,0:T(8,128)(2,1)S(1)}, u32[]{:S(2)}, u32[]{:S(2)}) collective-permute-start(bf16[4,96,256]{2,1,0:T(8,128)(2,1)S(1)} %get-tuple-element.25), channel_id=1, source_target_pairs={{0,1},{1,0},{2,3},{3,2},{4,5},{5,4},{6,7},{7,6},{8,9},{9,8},{10,11... | collective-permute-start | bytes 589832 | tf_op jit(solution)/shard_map/ppermute | solution.py:31
  18.7 5.1 %collective-permute-start.10 = (f32[2,3,48,256]{3,2,1,0:T(8,128)S(1)}, f32[2,3,48,256]{3,2,1,0:T(8,128)S(1)}, u32[]{:S(2)}, u32[]{:S(2)}) collective-permute-start(f32[2,3,48,256]{3,2,1,0:T(8,128)S(1)} %get-tuple-element.23), channel_id=1, source_target_pairs={{0,1},{1,0},{2,3},{3,2},{4,5},{5,4},{6,7},{7,6},{8,9},{9,8},{10,11... | collective-permute-start | bytes 884744 | tf_op jit(solution)/shard_map/ppermute | solution.py:31
  20.2 5.2 %collective-permute-start.13 = (bf16[96,256]{1,0:T(8,128)(2,1)S(1)}, bf16[96,256]{1,0:T(8,128)(2,1)S(1)}, u32[]{:S(2)}, u32[]{:S(2)}) collective-permute-start(bf16[96,256]{1,0:T(8,128)(2,1)S(1)} %get-tuple-element.32), channel_id=1, source_target_pairs={{0,6},{1,7},{2,4},{3,5},{4,2},{5,3},{6,0},{7,1},{8,14},{9,15},{10,... | collective-permute-start | bytes 147464 | tf_op jit(solution)/shard_map/ppermute | solution.py:31
  22.2 4.6 %collective-permute-start.15 = (bf16[96,256]{1,0:T(8,128)(2,1)S(1)}, bf16[96,256]{1,0:T(8,128)(2,1)S(1)}, u32[]{:S(2)}, u32[]{:S(2)}) collective-permute-start(bf16[96,256]{1,0:T(8,128)(2,1)S(1)} %get-tuple-element.33), channel_id=1, source_target_pairs={{0,2},{1,3},{2,0},{3,1},{4,6},{5,7},{6,4},{7,5},{8,10},{9,11},{10,... | collective-permute-start | bytes 147464 | tf_op jit(solution)/shard_map/ppermute | solution.py:31
  23.2 4.1 %collective-permute-start.14 = (bf16[96,256]{1,0:T(8,128)(2,1)S(1)}, bf16[96,256]{1,0:T(8,128)(2,1)S(1)}, u32[]{:S(2)}, u32[]{:S(2)}) collective-permute-start(bf16[96,256]{1,0:T(8,128)(2,1)S(1)} %get-tuple-element.34), channel_id=1, source_target_pairs={{0,4},{1,5},{2,6},{3,7},{4,0},{5,1},{6,2},{7,3},{8,12},{9,13},{10,... | collective-permute-start | bytes 147464 | tf_op jit(solution)/shard_map/ppermute | solution.py:31
  23.8 10.8 %collective-permute-start.12 = (bf16[1,3,48,256]{3,2,1,0:T(8,128)(2,1)S(1)}, bf16[1,3,48,256]{3,2,1,0:T(8,128)(2,1)S(1)}, u32[]{:S(2)}, u32[]{:S(2)}) collective-permute-start(bf16[1,3,48,256]{3,2,1,0:T(8,128)(2,1)S(1)} %fusion.7), channel_id=1, source_target_pairs={{0,2},{1,3},{2,0},{3,1},{4,6},{5,7},{6,4},{7,5},{8,10},{9,11},{10,... | collective-permute-start | bytes 221192 | tf_op jit(solution)/shard_map/ppermute | solution.py:31
  27.3 6.0 %collective-permute-start.18 = (bf16[96,256]{1,0:T(8,128)(2,1)S(1)}, bf16[96,256]{1,0:T(8,128)(2,1)S(1)}, u32[]{:S(2)}, u32[]{:S(2)}) collective-permute-start(bf16[96,256]{1,0:T(8,128)(2,1)S(1)} %fusion.5), channel_id=1, source_target_pairs={{0,24},{4,28},{8,16},{12,20},{16,8},{20,12},{24,0},{28,4},{1,25},{... | collective-permute-start | bytes 147464 | tf_op jit(solution)/shard_map/ppermute | solution.py:31
  29.3 5.3 %collective-permute-start.17 = (bf16[96,256]{1,0:T(8,128)(2,1)S(1)}, bf16[96,256]{1,0:T(8,128)(2,1)S(1)}, u32[]{:S(2)}, u32[]{:S(2)}) collective-permute-start(bf16[96,256]{1,0:T(8,128)(2,1)S(1)} %fusion.5), channel_id=1, source_target_pairs={{0,16},{4,20},{8,24},{12,28},{16,0},{20,4},{24,8},{28,12},{1,17},{... | collective-permute-start | bytes 147464 | tf_op jit(solution)/shard_map/ppermute | solution.py:31
  29.6 4.9 %collective-permute-start.16 = (bf16[96,256]{1,0:T(8,128)(2,1)S(1)}, bf16[96,256]{1,0:T(8,128)(2,1)S(1)}, u32[]{:S(2)}, u32[]{:S(2)}) collective-permute-start(bf16[96,256]{1,0:T(8,128)(2,1)S(1)} %fusion.5), channel_id=1, source_target_pairs={{0,8},{4,12},{8,0},{12,4},{16,24},{20,28},{24,16},{28,20},{1,9},{5... | collective-permute-start | bytes 147464 | tf_op jit(solution)/shard_map/ppermute | solution.py:31
  34.6 5.1 %collective-permute-start.21 = (bf16[96,256]{1,0:T(8,128)(2,1)S(1)}, bf16[96,256]{1,0:T(8,128)(2,1)S(1)}, u32[]{:S(2)}, u32[]{:S(2)}) collective-permute-start(bf16[96,256]{1,0:T(8,128)(2,1)S(1)} %add_convert_fusion), channel_id=1, source_target_pairs={{0,6},{1,7},{2,4},{3,5},{4,2},{5,3},{6,0},{7,1},{8,14},{9,15},{10,... | collective-permute-start | bytes 147464 | tf_op jit(solution)/shard_map/ppermute | solution.py:31
  36.2 4.1 %collective-permute-start.20 = (bf16[96,256]{1,0:T(8,128)(2,1)S(1)}, bf16[96,256]{1,0:T(8,128)(2,1)S(1)}, u32[]{:S(2)}, u32[]{:S(2)}) collective-permute-start(bf16[96,256]{1,0:T(8,128)(2,1)S(1)} %add_convert_fusion), channel_id=1, source_target_pairs={{0,2},{1,3},{2,0},{3,1},{4,6},{5,7},{6,4},{7,5},{8,10},{9,11},{10,... | collective-permute-start | bytes 147464 | tf_op jit(solution)/shard_map/ppermute | solution.py:31
  36.9 4.1 %collective-permute-start.19 = (bf16[96,256]{1,0:T(8,128)(2,1)S(1)}, bf16[96,256]{1,0:T(8,128)(2,1)S(1)}, u32[]{:S(2)}, u32[]{:S(2)}) collective-permute-start(bf16[96,256]{1,0:T(8,128)(2,1)S(1)} %add_convert_fusion), channel_id=1, source_target_pairs={{0,4},{1,5},{2,6},{3,7},{4,0},{5,1},{6,2},{7,3},{8,12},{9,13},{10,... | collective-permute-start | bytes 147464 | tf_op jit(solution)/shard_map/ppermute | solution.py:31
  41.0 1.5 %collective-permute-start.22 = (bf16[4,96,256]{2,1,0:T(8,128)(2,1)S(1)}, bf16[4,96,256]{2,1,0:T(8,128)(2,1)S(1)}, u32[]{:S(2)}, u32[]{:S(2)}) collective-permute-start(bf16[4,96,256]{2,1,0:T(8,128)(2,1)S(1)} %pad_maximum_fusion.here_ref), channel_id=1, source_target_pairs={{0,1},{1,0},{2,3},{3,2},{4,5},{5,4},{6,7},{7,6},{8,9},{9,8},{10,11... | collective-permute-start | bytes 589832 | tf_op jit(solution)/shard_map/ppermute | solution.py:31
